TPU v7x, 32 devices: a whole 2x2x4 slice. The times are simulated.
32 devices in a mesh: row: 16 (over z, y, core), ch: 2 (over x).
Axes of the slice: x: 2, y: 2, z: 4, core: 2. Of those that a mesh axis runs over, the one named last changes fastest.
Arguments:
- pair_act: bfloat16 [256, 256, 128], P('row', 'ch'), may hold values from -240 to 240
- cotangent: bfloat16 [256, 256, 128], P('row', 'ch'), may hold values from -6 to 6
- in_gain: float32 [128], replicated, may hold values from 0.25 to 1.75
- in_bias: float32 [128], replicated, may hold values from -3 to 3
- proj_weight: bfloat16 [128, 640], replicated, may hold values from -0.5 to 0.5
- out_gain: float32 [128], replicated, may hold values from 0.25 to 1.75
- out_bias: float32 [128], replicated, may hold values from -3 to 3
- out_weight: bfloat16 [128, 128], replicated, may hold values from -0.5 to 0.5
Outputs:
- grad_pair: bfloat16 [256, 256, 128], P('row', 'ch')
All inputs are finite; a program needn't handle non-finite values.
Results may differ from a plain program's by a relative error of at most 0.0072.
Values may be sent and summed in bfloat16 or wider, within the bound.
No kernel may reach another device: no remote copies, remote signals or barrier semaphores. Data moves between devices by JAX's collectives and lax.ppermute only.
A program may use at most 64 MiB of HBM per device.

v0:
```python
import jax
import jax.numpy as jnp
from jax import lax
from jax.sharding import PartitionSpec as P

EPSILON = 1e-05


def normalize(values, axis):
    center = jnp.mean(values, axis=axis, keepdims=True)
    shifted = values - center
    scale_inv = lax.rsqrt(jnp.mean(shifted * shifted, axis=axis, keepdims=True) + EPSILON)
    return (shifted * scale_inv, scale_inv)


def norm_back(grad_hat, normed, scale_inv, axis):
    first = jnp.mean(grad_hat, axis=axis, keepdims=True)
    second = jnp.mean(grad_hat * normed, axis=axis, keepdims=True)
    return scale_inv * (grad_hat - first - normed * second)


def on_device(pair_act, cotangent, in_gain, in_bias, proj_weight, out_gain, out_bias, out_weight):
    rows_here, cols_here, width = pair_act.shape
    flat = pair_act.astype(jnp.float32).reshape(rows_here * cols_here, width)
    normed, scale_inv = normalize(flat, -1)
    normal_in = (normed * in_gain + in_bias).astype(jnp.bfloat16)
    projected = jnp.einsum("pd,de->ep", normal_in, proj_weight, preferred_element_type=jnp.float32)
    blocks = jnp.split(projected, 5, axis=0)
    left_sig = jax.nn.sigmoid(blocks[1])
    right_sig = jax.nn.sigmoid(blocks[3])
    left_fac = (left_sig * blocks[0]).astype(jnp.bfloat16).reshape(width, rows_here, cols_here)
    right_fac = (right_sig * blocks[2]).astype(jnp.bfloat16).reshape(width, rows_here, cols_here)
    left_chan, right_chan = (
        lax.all_to_all(left_fac, "ch", split_axis=0, concat_axis=2, tiled=True),
        lax.all_to_all(right_fac, "ch", split_axis=0, concat_axis=2, tiled=True),
    )
    tri_chan = jnp.einsum(
        "cik,cjk->cij",
        left_chan,
        lax.all_gather(right_chan, "row", axis=1, tiled=True),
        preferred_element_type=jnp.float32,
    ).astype(jnp.bfloat16)
    tri_back = lax.all_to_all(tri_chan, "ch", split_axis=2, concat_axis=0, tiled=True)
    tri_hat, tri_inv = normalize(tri_back.astype(jnp.float32).reshape(width, -1), 0)
    normal_out = (tri_hat * out_gain[:, None] + out_bias[:, None]).astype(jnp.bfloat16)
    mixed = jnp.einsum("cp,ce->ep", normal_out, out_weight, preferred_element_type=jnp.float32)
    out_gate = jax.nn.sigmoid(blocks[4])
    grad_out = cotangent.astype(jnp.float32).reshape(rows_here * cols_here, width).T
    grad_mixed = (grad_out * out_gate).astype(jnp.bfloat16)
    grad_logit = grad_out * mixed * out_gate * (1.0 - out_gate)
    grad_normal = jnp.einsum(
        "ep,ce->cp", grad_mixed, out_weight, preferred_element_type=jnp.float32
    )
    grad_tri = norm_back(grad_normal * out_gain[:, None], tri_hat, tri_inv, 0)
    grad_tri = grad_tri.astype(jnp.bfloat16).reshape(width, rows_here, cols_here)
    grad_chan = lax.all_to_all(grad_tri, "ch", split_axis=0, concat_axis=2, tiled=True)
    grad_cols = lax.all_to_all(grad_chan, "row", split_axis=2, concat_axis=1, tiled=True)
    block = grad_chan
    grad_left = jnp.einsum(
        "cij,cjk->cik",
        block,
        lax.all_gather(right_chan, "row", axis=1, tiled=True),
        preferred_element_type=jnp.float32,
    )
    block = grad_cols
    grad_right = jnp.einsum(
        "cij,cik->cjk",
        block,
        lax.all_gather(left_chan, "row", axis=1, tiled=True),
        preferred_element_type=jnp.float32,
    )
    left_back, right_back = (
        lax.all_to_all(
            grad_left.astype(jnp.bfloat16), "ch", split_axis=2, concat_axis=0, tiled=True
        ),
        lax.all_to_all(
            grad_right.astype(jnp.bfloat16), "ch", split_axis=2, concat_axis=0, tiled=True
        ),
    )
    left_grad = left_back.astype(jnp.float32).reshape(width, -1)
    right_grad = right_back.astype(jnp.float32).reshape(width, -1)
    grad_proj = jnp.concatenate(
        [
            left_grad * left_sig,
            left_grad * blocks[0] * left_sig * (1.0 - left_sig),
            right_grad * right_sig,
            right_grad * blocks[2] * right_sig * (1.0 - right_sig),
            grad_logit,
        ],
        axis=0,
    ).astype(jnp.bfloat16)
    grad_in = jnp.einsum("ep,de->pd", grad_proj, proj_weight, preferred_element_type=jnp.float32)
    grad_pair = norm_back(grad_in * in_gain, normed, scale_inv, -1)
    return grad_pair.astype(jnp.bfloat16).reshape(rows_here, cols_here, width)


def solution(mesh):
    placed = (P("row", "ch", None), P("row", "ch", None), P(), P(), P(), P(), P(), P())
    return jax.shard_map(
        on_device, mesh=mesh, in_specs=placed, out_specs=P("row", "ch", None), check_vma=False
    )
```

profile of v0, /device:TPU:0, one launch (start us, length us, event | category | flops | bytes accessed | tf_op | source)
XLA Modules:
  0.0 238.1 jit_solution(12858767312660383392)
XLA Ops:
  6.5 1.3 convert_reduce_fusion
  7.8 1.7 multiply_reduce_fusion.1
  9.5 1.7 add_convert_fusion.1
  11.2 0.8 convolution_bitcast_fusion
  12.1 2.3 copy-done.1
  14.4 0.6 multiply_convert_fusion.6
  14.9 0.4 copy.57
  15.3 12.0 %all_to_all.99 = bf16[128,16,128]{2,1,0:T(8,128)(2,1)S(1)} all-to-all(bf16[128,16,128]{2,1,0:T(8,128)(2,1)S(1)} %copy.57), channel_id=1, replica_groups=mesh['row'=16,'ch'=2] {'ch'}, dimensions={0} | all-to-all | bytes 1048576 | tf_op jit(solution)/shard_map/all_to_all | solution.py:35
  27.3 0.9 copy.97
  28.2 0.0 all-gather.3.cloned.1.call-update
  28.2 0.0 all-gather.5.cloned.1.call-start
  28.3 0.4 copy.55
  28.7 9.5 %all_to_all.100 = bf16[128,16,128]{2,1,0:T(8,128)(2,1)S(1)} all-to-all(bf16[128,16,128]{2,1,0:T(8,128)(2,1)S(1)} %copy.55), channel_id=1, replica_groups=mesh['row'=16,'ch'=2] {'ch'}, dimensions={0} | all-to-all | bytes 1048576 | tf_op jit(solution)/shard_map/all_to_all | solution.py:34
  38.2 0.9 copy.98
  39.1 67.8 %all-gather.3.cloned.1.call-done = bf16[64,256,256]{2,1,0:T(8,128)(2,1)} async-done(((bf16[64,16,256]{2,1,0:T(8,128)(2,1)}), bf16[64,256,256]{2,1,0:T(8,128)(2,1)}) %all-gather.3.cloned.1.call-update) | async-done | bytes 8388624 | tf_op jit(solution)/shard_map/all_gather | solution.py:40
  106.9 5.7 %convolution_convert_fusion.2 = bf16[64,16,256]{2,1,0:T(8,128)(2,1)S(1)} fusion(bf16[64,256,256]{2,1,0:T(8,128)(2,1)} %all-gather.3.cloned.1.call-done, bf16[2,64,2,8,128]{4,3,2,1,0:T(8,128)(2,1)S(1)} %bitcast.139), kind=kOutput, calls=%fused_computation.11 | convolution fusion | flops 134479872 | bytes 9437184 | tf_op jit(solution)/shard_map/cik,cjk->cij/dot_general | solution.py:37
  112.6 1.3 copy.59
  113.9 0.8 reshape.137
  114.8 11.1 %all_to_all.101 = bf16[2,2,65536]{2,1,0:T(2,128)(2,1)S(1)} all-to-all(bf16[2,2,65536]{2,1,0:T(2,128)(2,1)S(1)} %reshape.137), channel_id=1, replica_groups=mesh['row'=16,'ch'=2] {'ch'}, dimensions={0} | all-to-all | bytes 1048576 | tf_op jit(solution)/shard_map/all_to_all | solution.py:43
  125.9 0.7 reshape.138
  126.6 1.1 copy.60
  127.7 0.3 copy.95
  128.0 0.3 copy.61
  128.4 0.1 bitcast_reduce_fusion
  128.5 0.2 fusion.21
  128.7 2.2 fusion.19
  130.9 0.3 reduce_sum.76
  131.3 1.6 fusion.18
  132.9 0.4 copy.62
  133.4 10.2 %all_to_all.102 = bf16[128,16,128]{2,1,0:T(8,128)(2,1)S(1)} all-to-all(bf16[128,16,128]{2,1,0:T(8,128)(2,1)S(1)} %copy.62), channel_id=1, replica_groups=mesh['row'=16,'ch'=2] {'ch'}, dimensions={0} | all-to-all | bytes 1048576 | tf_op jit(solution)/shard_map/all_to_all | solution.py:56
  143.6 4.8 %convolution_convert_fusion.1 = bf16[64,16,256]{2,1,0:T(8,128)(2,1)S(1)} fusion(bf16[64,256,256]{2,1,0:T(8,128)(2,1)} %all-gather.3.cloned.1.call-done, bf16[2,64,2,8,128]{4,3,2,1,0:T(8,128)(2,1)S(1)} %bitcast.136), kind=kOutput, calls=%fused_computation.10 | convolution fusion | flops 134479872 | bytes 9437184 | tf_op jit(solution)/shard_map/cij,cjk->cik/dot_general | solution.py:59
  148.4 1.3 copy.64
  149.7 1.5 reshape.139
  151.2 3.5 %all-to-all-start.4 = ((bf16[2,2,65536]{2,1,0:T(2,128)(2,1)}), bf16[2,2,65536]{2,1,0:T(2,128)(2,1)S(1)}, u32[]{:S(2)}, u32[]{:S(2)}) async-start(bf16[2,2,65536]{2,1,0:T(2,128)(2,1)} %reshape.139), calls=%async_computation.4 | async-start | bytes 1048576 | tf_op jit(solution)/shard_map/all_to_all | solution.py:73
  154.7 0.1 copy.96
  154.8 1.3 copy.68
  156.1 1.5 reshape.141
  157.6 4.7 %all-to-all-done.4 = bf16[2,2,65536]{2,1,0:T(2,128)(2,1)S(1)} async-done(((bf16[2,2,65536]{2,1,0:T(2,128)(2,1)}), bf16[2,2,65536]{2,1,0:T(2,128)(2,1)S(1)}, u32[]{:S(2)}, u32[]{:S(2)}) %all-to-all-start.4) | async-done | bytes 524320 | tf_op jit(solution)/shard_map/all_to_all | solution.py:73
  162.3 4.2 %all-to-all-start.5 = ((bf16[16,2,8192]{2,1,0:T(2,128)(2,1)}), bf16[16,2,8192]{2,1,0:T(2,128)(2,1)}, u32[]{:S(2)}, u32[]{:S(2)}) async-start(bf16[16,2,8192]{2,1,0:T(2,128)(2,1)} %reshape.141), calls=%async_computation.5 | async-start | bytes 1048576 | tf_op jit(solution)/shard_map/all_to_all | solution.py:57
  166.6 0.7 reshape.140
  167.3 1.1 copy.65
  168.4 0.3 copy.94
  168.8 0.3 copy.66
  169.1 2.4 fusion.23
  171.5 17.7 %all-to-all-done.5 = bf16[16,2,8192]{2,1,0:T(2,128)(2,1)} async-done(((bf16[16,2,8192]{2,1,0:T(2,128)(2,1)}), bf16[16,2,8192]{2,1,0:T(2,128)(2,1)}, u32[]{:S(2)}, u32[]{:S(2)}) %all-to-all-start.5) | async-done | bytes 524320 | tf_op jit(solution)/shard_map/all_to_all | solution.py:57
  189.2 2.3 reshape.142
  191.5 0.3 copy.70
  191.8 1.3 copy.71
  193.1 3.2 %all-gather.5.cloned.1.call-done = bf16[64,256,256]{2,1,0:T(8,128)(2,1)} async-done(((bf16[64,16,256]{2,1,0:T(8,128)(2,1)}), bf16[64,256,256]{2,1,0:T(8,128)(2,1)}) %all-gather.5.cloned.1.call-update) | async-done | bytes 8388624 | tf_op jit(solution)/shard_map/all_gather | solution.py:69
  196.3 4.6 %convolution_convert_fusion = bf16[64,16,256]{2,1,0:T(8,128)(2,1)S(1)} fusion(bf16[64,256,16]{1,2,0:T(8,128)(2,1)S(1)} %copy.71, bf16[64,256,256]{2,1,0:T(8,128)(2,1)} %all-gather.5.cloned.1.call-done), kind=kOutput, calls=%fused_computation.9 | convolution fusion | flops 134479872 | bytes 9437184 | tf_op jit(solution)/shard_map/cij,cik->cjk/dot_general | solution.py:66
  200.9 1.3 copy.72
  202.2 1.5 reshape.143
  203.8 3.7 %all-to-all-start.6 = ((bf16[2,2,65536]{2,1,0:T(2,128)(2,1)}), bf16[2,2,65536]{2,1,0:T(2,128)(2,1)S(1)}, u32[]{:S(2)}, u32[]{:S(2)}) async-start(bf16[2,2,65536]{2,1,0:T(2,128)(2,1)} %reshape.143), calls=%async_computation.6 | async-start | bytes 1048576 | tf_op jit(solution)/shard_map/all_to_all | solution.py:76
  207.5 2.7 %fusion.24 = bf16[640,2048]{0,1:T(8,128)(2,1)} fusion(bf16[640,2048]{0,1:T(8,128)(2,1)} %fusion.23, f32[128,2048]{0,1:T(8,128)S(1)} %copy.66, f32[640,2048]{0,1:T(8,128)} %copy-done.1), kind=kLoop, calls=%fused_computation.56 | loop fusion | flops 2097152 | bytes 3670016
  210.2 5.8 %all-to-all-done.6 = bf16[2,2,65536]{2,1,0:T(2,128)(2,1)S(1)} async-done(((bf16[2,2,65536]{2,1,0:T(2,128)(2,1)}), bf16[2,2,65536]{2,1,0:T(2,128)(2,1)S(1)}, u32[]{:S(2)}, u32[]{:S(2)}) %all-to-all-start.6) | async-done | bytes 524320 | tf_op jit(solution)/shard_map/all_to_all | solution.py:76
  215.9 0.7 reshape.144
  216.6 1.1 copy.73
  217.8 0.3 copy.93
  218.1 0.3 copy.74
  218.5 2.4 %fusion.25 = bf16[640,2048]{0,1:T(8,128)(2,1)} fusion(bf16[640,2048]{0,1:T(8,128)(2,1)} %fusion.24, f32[128,2048]{0,1:T(8,128)S(1)} %copy.74, f32[640,2048]{0,1:T(8,128)} %copy-done.1), kind=kLoop, calls=%fused_computation.57 | loop fusion | flops 1310720 | bytes 2621440
  220.9 2.8 %fusion.26 = bf16[640,2048]{0,1:T(8,128)(2,1)} fusion(bf16[640,2048]{0,1:T(8,128)(2,1)} %fusion.25, f32[128,2048]{0,1:T(8,128)S(1)} %copy.74, f32[640,2048]{0,1:T(8,128)} %copy-done.1), kind=kLoop, calls=%fused_computation.58 | loop fusion | flops 2097152 | bytes 3670016
  223.7 2.7 %fusion.4 = bf16[640,2048]{0,1:T(8,128)(2,1)} fusion(bf16[640,2048]{0,1:T(8,128)(2,1)} %fusion.26, bf16[128,128]{1,0:T(8,128)(2,1)S(1)} %copy-done.7, bf16[2048,128]{1,0:T(8,128)(2,1)S(1)} %bitcast.162, f32[128,2048]{0,1:T(8,128)S(1)} %copy-done.4, f32[128]{0:T(128)S(1)} %copy-done.9, f32[128]{0:T(128)S(1)} %copy-done.8, f32[2048]{0:T(1024)S(1)} %get-tuple-element.10, ...), kind=kOutput, calls=%fused_computation.8 | convolution fusion | flops 70778880 | bytes 3195904 | tf_op jit(solution)/shard_map/cp,ce->ep/dot_general | solution.py:46
  226.4 2.9 %fusion.36 = (f32[2048]{0:T(1024)S(1)}, f32[2048]{0:T(1024)S(1)}, f32[2048,128]{1,0:T(8,128)S(1)}) fusion(f32[2048]{0:T(1024)S(1)} %rsqrt_bitcast_fusion.1, f32[2048]{0:T(1024)S(1)} %get-tuple-element.12, bf16[16,128,128]{2,1,0:T(8,128)(2,1)S(1)} %copy-done.2, f32[128]{0:T(128)S(1)} %copy-done.5, bf16[640,2048]{0,1:T(8,128)(2,1)} %fusion.4, ...), kind=kOutput, calls=%fused_computation.77 | convolution fusion | flops 337375232 | bytes 4391424 | tf_op jit(solution)/shard_map/ep,de->pd/dot_general | solution.py:92
  229.3 2.0 multiply_convert_fusion
  (28 shorter events, 0.1 us)
Async XLA Ops:
  6.5 4.7 %copy-start = (bf16[128,640]{1,0:T(8,128)(2,1)S(1)}, bf16[128,640]{1,0:T(8,128)(2,1)}, u32[]{:S(2)}) copy-start(bf16[128,640]{1,0:T(8,128)(2,1)} %param.12) | copy-start | bytes 491524
  6.5 100.4 %all-gather.3.cloned.1.call-start = ((), (), s32[]{:S(2)}) async-start(), calls=%async_computation.7 | async-start | bytes 8912896 | tf_op jit(solution)/shard_map/all_gather | solution.py:40
  12.1 2.3 copy-start.1
  28.2 168.1 %all-gather.5.cloned.1.call-start = ((), (), s32[]{:S(2)}) async-start(), calls=%async_computation.8 | async-start | bytes 8912896 | tf_op jit(solution)/shard_map/all_gather | solution.py:69
  125.8 2.9 %copy-start.7 = (bf16[128,128]{1,0:T(8,128)(2,1)S(1)}, bf16[128,128]{1,0:T(8,128)(2,1)}, u32[]{:S(2)}) copy-start(bf16[128,128]{1,0:T(8,128)(2,1)} %param.15) | copy-start | bytes 98308
  125.9 2.9 %copy-start.8 = (f32[128]{0:T(128)S(1)}, f32[128]{0:T(128)}, u32[]{:S(2)}) copy-start(f32[128]{0:T(128)} %param.13) | copy-start | bytes 1540
  128.4 4.5 %copy-start.3 = (f32[128,2048]{0,1:T(8,128)}, f32[128,2048]{0,1:T(8,128)S(1)}, u32[]{:S(2)}) copy-start(f32[128,2048]{0,1:T(8,128)S(1)} %copy.61) | copy-start | bytes 3145732
  151.2 11.0 %all-to-all-start.4 = ((bf16[2,2,65536]{2,1,0:T(2,128)(2,1)}), bf16[2,2,65536]{2,1,0:T(2,128)(2,1)S(1)}, u32[]{:S(2)}, u32[]{:S(2)}) async-start(bf16[2,2,65536]{2,1,0:T(2,128)(2,1)} %reshape.139), calls=%async_computation.4 | async-start | bytes 1048576 | tf_op jit(solution)/shard_map/all_to_all | solution.py:73
  162.3 26.9 %all-to-all-start.5 = ((bf16[16,2,8192]{2,1,0:T(2,128)(2,1)}), bf16[16,2,8192]{2,1,0:T(2,128)(2,1)}, u32[]{:S(2)}, u32[]{:S(2)}) async-start(bf16[16,2,8192]{2,1,0:T(2,128)(2,1)} %reshape.141), calls=%async_computation.5 | async-start | bytes 1048576 | tf_op jit(solution)/shard_map/all_to_all | solution.py:57
  203.8 12.2 %all-to-all-start.6 = ((bf16[2,2,65536]{2,1,0:T(2,128)(2,1)}), bf16[2,2,65536]{2,1,0:T(2,128)(2,1)S(1)}, u32[]{:S(2)}, u32[]{:S(2)}) async-start(bf16[2,2,65536]{2,1,0:T(2,128)(2,1)} %reshape.143), calls=%async_computation.6 | async-start | bytes 1048576 | tf_op jit(solution)/shard_map/all_to_all | solution.py:76
  217.8 5.9 %copy-start.9 = (f32[128]{0:T(128)S(1)}, f32[128]{0:T(128)}, u32[]{:S(2)}) copy-start(f32[128]{0:T(128)} %param.14) | copy-start | bytes 1540
  218.1 5.6 %copy-start.4 = (f32[128,2048]{0,1:T(8,128)S(1)}, f32[128,2048]{0,1:T(8,128)}, u32[]{:S(2)}) copy-start(f32[128,2048]{0,1:T(8,128)} %copy-done.3) | copy-start | bytes 3145732
  218.5 5.2 %copy-start.6 = (bf16[16,128,128]{2,1,0:T(8,128)(2,1)S(1)}, bf16[16,128,128]{2,1,0:T(8,128)(2,1)}, u32[]{:S(2)}) copy-start(bf16[16,128,128]{2,1,0:T(8,128)(2,1)} %param.9) | copy-start | bytes 1572868
  220.9 5.5 %copy-start.2 = (bf16[16,128,128]{2,1,0:T(8,128)(2,1)S(1)}, bf16[16,128,128]{2,1,0:T(8,128)(2,1)}, u32[]{:S(2)}) copy-start(bf16[16,128,128]{2,1,0:T(8,128)(2,1)} %param.8) | copy-start | bytes 1572868
  220.9 5.5 %copy-start.5 = (f32[128]{0:T(128)S(1)}, f32[128]{0:T(128)}, u32[]{:S(2)}) copy-start(f32[128]{0:T(128)} %param.10) | copy-start | bytes 1540
Sparse Core Ops, SparseCore 0:
  28.3 78.5 all-gather.2
  109.1 87.2 all-gather.4
where the time goes:
time: 239 us; the launch traced here: 238 us
  waiting for transfers between devices  99.2 us (42%)
  blocking collectives  42.8 us (18%)
  local copies, waits for them, and re-layouts  27.5 us (12%)
  matrix products  23.6 us (10%)
  other arithmetic  19.7 us (8%)
  between operations  13.8 us (6%)
  starting transfers between devices  11.5 us (5%)
    all_gather x1, waiting for transfers between devices, on_device(): lax.all_gather(right_chan, 'row', axis=1, tiled=True)  67.8 us
    all_to_all x1, waiting for transfers between devices, on_device(): lax.all_to_all(grad_chan, 'row', split_axis=2, concat_axis=1, tiled=True)  17.7 us
    unnamed x31, local copies, waits for them, and re-layouts  13.2 us
    all_to_all x1, blocking collectives, on_device(): lax.all_to_all(right_fac, 'ch', split_axis=0, concat_axis=2, tiled=True)  12 us
    all_to_all x1, blocking collectives, on_device(): lax.all_to_all(tri_chan, 'ch', split_axis=2, concat_axis=0, tiled=True)  11.1 us
    unnamed x4, other arithmetic  10.3 us
    all_to_all x1, blocking collectives, on_device(): lax.all_to_all(grad_tri, 'ch', split_axis=0, concat_axis=2, tiled=True)  10.2 us
    all_to_all x1, blocking collectives, on_device(): lax.all_to_all(left_fac, 'ch', split_axis=0, concat_axis=2, tiled=True)  9.46 us
  transfers between devices with their start and end apart: 5, of which 5 were waited for; matrix products, arithmetic and copies ran while one was open for 16% of the time, Pallas kernels for 0%

commit v1 on v0

--- a/solution.py
+++ b/solution.py
@@ -1,9 +1,27 @@
+import functools
+import math
+
 import jax
 import jax.numpy as jnp
 from jax import lax
+from jax.experimental import pallas as pl
+from jax.experimental.pallas import tpu as pltpu
 from jax.sharding import PartitionSpec as P
 
 EPSILON = 1e-05
+F32 = jnp.float32
+BF16 = jnp.bfloat16
+UNROLL = 4
+BLOCK = 256
+PARTS = 4
+
+
+def dot(a, b, da, db):
+    return lax.dot_general(a, b, (((da,), (db,)), ((), ())), preferred_element_type=F32)
+
+
+def sigmoid(values):
+    return 0.5 * jnp.tanh(0.5 * values) + 0.5
 
 
 def normalize(values, axis):
@@ -19,7 +37,657 @@
     return scale_inv * (grad_hat - first - normed * second)
 
 
-def on_device(pair_act, cotangent, in_gain, in_bias, proj_weight, out_gain, out_bias, out_weight):
+def column(row, width):
+    return jnp.broadcast_to(row, (width, row.shape[-1])).T
+
+
+def call(kernel, outs, scratch, *args, hbm=0, limit=16):
+    single = not isinstance(outs, (list, tuple))
+    args = [pltpu.with_memory_space_constraint(a, pltpu.HBM) if n < hbm else a for n, a in enumerate(args)]
+    specs = [pl.BlockSpec(memory_space=pltpu.HBM if n < hbm else pltpu.VMEM) for n in range(len(args))]
+    out_specs = [
+        pl.BlockSpec(memory_space=getattr(out, "memory_space", pltpu.VMEM))
+        for out in ([outs] if single else outs)
+    ]
+    return pl.pallas_call(
+        kernel,
+        out_shape=outs if single else tuple(outs),
+        in_specs=specs,
+        out_specs=out_specs[0] if single else tuple(out_specs),
+        scratch_shapes=scratch,
+        compiler_params=pltpu.CompilerParams(vmem_limit_bytes=limit * 1024 * 1024),
+    )(*args)
+
+
+def permutation(outer, inner):
+    to = lax.broadcasted_iota(jnp.int32, (BLOCK, BLOCK), 0)
+    start = lax.broadcasted_iota(jnp.int32, (BLOCK, BLOCK), 1)
+    return (start == to % inner * outer + to // inner).astype(F32).astype(BF16)
+
+
+def identity(size):
+    first = lax.broadcasted_iota(jnp.int32, (size, size), 0)
+    return (first == lax.broadcasted_iota(jnp.int32, (size, size), 1)).astype(F32).astype(BF16)
+
+
+def swapped(swap, blocks):
+    cols = blocks[0].shape[-1]
+    wide = jnp.concatenate([block.reshape(BLOCK, cols) for block in blocks], axis=1)
+    wide = dot(swap, wide, 1, 0).astype(BF16)
+    return [wide[:, n * cols : (n + 1) * cols] for n in range(len(blocks))]
+
+
+def fetched(sources, targets, sems):
+    copies = [
+        pltpu.make_async_copy(source, target, sems.at[n])
+        for n, (source, target) in enumerate(zip(sources, targets))
+    ]
+    for copy in copies:
+        copy.start()
+    for copy in copies:
+        copy.wait()
+
+
+def weight_copies(w_hbm, w_ref, first, sems):
+    width = w_hbm.shape[0]
+    return [
+        pltpu.make_async_copy(
+            w_hbm.at[:, (first + n) * width : (first + n + 1) * width],
+            w_ref.at[:, n * width : (n + 1) * width],
+            sems.at[n],
+        )
+        for n in range(2)
+    ]
+
+
+def right_kernel(
+    lay, x_hbm, gain_hbm, bias_hbm, w_hbm, r_hbm, n_ref, x_ref, gain_ref, bias_ref, w_ref, wt_ref, r_ref, right_ref, sems, out_sems
+):
+    rows, cols, width = x_ref.shape
+    mine = width // lay.half
+    parts = sems.shape[0] - 4
+    size = rows // parts
+
+    def fetch(p):
+        here = pl.ds(p * size, size)
+        return pltpu.make_async_copy(x_hbm.at[here], x_ref.at[here], sems.at[4 + p])
+
+    small = [
+        pltpu.make_async_copy(gain_hbm, gain_ref, sems.at[2]),
+        pltpu.make_async_copy(bias_hbm, bias_ref, sems.at[3]),
+    ]
+    weights = weight_copies(w_hbm, w_ref, 2, sems)
+    fetch(0).start()
+    for copy in small + weights:
+        copy.start()
+    for p in range(1, parts):
+        fetch(p).start()
+    group = BLOCK // rows
+    swap = permutation(group, rows)
+
+    def normal(p):
+        fetch(p).wait()
+        for n in range(0, size, 2):
+            i = p * size + n
+            x = dot(eye, x_ref[pl.ds(i, 2)].reshape(2 * cols, width), 1, 1)
+            normed, _s = normalize(x, 0)
+            n_ref[p * size // 2 + n // 2] = (normed * gain + bias).astype(BF16)
+
+    def project(p):
+        for n in range(0, size, 2):
+            i = p * size + n
+            proj = dot(wt_ref[...], n_ref[p * size // 2 + n // 2], 1, 0)
+            right = (sigmoid(proj[width:]) * proj[:width]).astype(BF16)
+            for m in range(2):
+                r_ref[i + m] = right[:, m * cols : (m + 1) * cols]
+
+    def body(p, _):
+        normal(p)
+        project(p - 1)
+        return 0
+
+    eye = identity(width)
+    for copy in small:
+        copy.wait()
+    gain = column(gain_ref[...], 2 * cols)
+    bias = column(bias_ref[...], 2 * cols)
+    normal(0)
+    for copy in weights:
+        copy.wait()
+    wt_ref[...] = w_ref[...].astype(F32).T.astype(BF16)
+    lax.fori_loop(1, parts, body, 0)
+    project(parts - 1)
+    out = []
+    blocks = places(width, mine, rows)
+    for k in range(0, len(blocks), 2):
+        pair = blocks[k : k + 2]
+        for (to, _here), right in zip(pair, swapped(swap, [r_ref[:, here] for _to, here in pair])):
+            right_ref[to] = right.reshape(group // mine, mine, rows, cols)
+            for share in range(to.start, to.stop):
+                for n, device in enumerate(lay.order):
+                    if lay.inside.index(device % lay.half) == share:
+                        out.append(pltpu.make_async_copy(right_ref.at[share], r_hbm.at[n], out_sems.at[n]))
+                        out[-1].start()
+    for copy in out:
+        copy.wait()
+
+
+def left_kernel(lay, w_hbm, n_ref, mine_out, mate_out, w_ref, wt_ref, l_ref, left_ref, sems):
+    rows, width, cols = l_ref.shape
+    mine = width // lay.half
+    group = BLOCK // rows
+    weights = weight_copies(w_hbm, w_ref, 0, sems)
+    for copy in weights:
+        copy.start()
+    for copy in weights:
+        copy.wait()
+    wt_ref[...] = w_ref[...].astype(F32).T.astype(BF16)
+    swap = permutation(group, rows)
+
+    def body(n, _):
+        proj = dot(wt_ref[...], n_ref[n], 1, 0)
+        left = (sigmoid(proj[width:]) * proj[:width]).astype(BF16)
+        for m in range(2):
+            l_ref[2 * n + m] = left[:, m * cols : (m + 1) * cols]
+        return 0
+
+    lax.fori_loop(0, rows // 2, body, 0, unroll=2)
+    blocks = places(width, mine, rows)
+    for k in range(0, len(blocks), 2):
+        pair = blocks[k : k + 2]
+        for (to, _here), left in zip(pair, swapped(swap, [l_ref[:, here] for _to, here in pair])):
+            left_ref[to] = left.reshape(group // mine, mine, rows, cols)
+    for n, s in enumerate(lay.hops):
+        mine_out[n] = left_ref[lay.share(s)]
+        mate_out[n] = left_ref[lay.share(s ^ lay.mate)]
+
+
+def gate_kernel(*refs):
+    sources, (h_ref, fac_hbm, fac_ref, wt_ref), targets, (sems, out_sems) = (
+        refs[:7],
+        refs[7:11],
+        refs[11:18],
+        refs[18:],
+    )
+    x_ref, cot_ref, gain_ref, bias_ref, w_ref, ogain_ref, ow_ref = targets
+    rows, cols, width = x_ref.shape
+    fetched(sources, targets, sems)
+    wt_ref[...] = w_ref[:, : 4 * width].astype(F32).T.astype(BF16)
+    ogain = column(ogain_ref[...], cols)
+
+    def body(i, _):
+        normed, _s = normalize(x_ref[i].astype(F32), -1)
+        normal_in = (normed * gain_ref[...] + bias_ref[...]).astype(BF16)
+        proj = dot(wt_ref[...], normal_in, 1, 1)
+        for side in range(2):
+            val = proj[2 * side * width : (2 * side + 1) * width]
+            sig = sigmoid(proj[(2 * side + 1) * width : (2 * side + 2) * width])
+            fac_ref[i, 2 * side * width : (2 * side + 1) * width] = sig.astype(BF16)
+            fac_ref[i, (2 * side + 1) * width : (2 * side + 2) * width] = (
+                val * sig * (1.0 - sig)
+            ).astype(BF16)
+        out_gate = sigmoid(dot(normal_in, w_ref[:, 4 * width :], 1, 0))
+        grad_mixed = (cot_ref[i].astype(F32) * out_gate).astype(BF16)
+        h_ref[i] = dot(ow_ref[...], grad_mixed, 1, 1) * ogain
+        return 0
+
+    size = rows // PARTS
+
+    def send(p):
+        here = pl.ds(p * size, size)
+        return pltpu.make_async_copy(fac_ref.at[here], fac_hbm.at[here], out_sems.at[p])
+
+    def part(p, _):
+        for n in range(size):
+            body(p * size + n, 0)
+        send(p).start()
+        return 0
+
+    lax.fori_loop(0, PARTS, part, 0)
+    for p in range(PARTS):
+        send(p).wait()
+
+
+def places(n_channels, mine, rows):
+    group = BLOCK // rows
+    return [
+        (slice(c // mine, (c + group) // mine), slice(c, c + group)) for c in range(0, n_channels, group)
+    ]
+
+
+def to_rows(t_ref, ts_ref):
+    rows, width, cols = ts_ref.shape
+    mine = t_ref.shape[1]
+    group = BLOCK // rows
+    swap = permutation(rows, group)
+    blocks = places(width, mine, rows)
+    for n in range(0, len(blocks), 2):
+        pair = blocks[n : n + 2]
+        for (_to, here), block in zip(pair, swapped(swap, [t_ref[to] for to, _here in pair])):
+            ts_ref[:, here] = block.reshape(rows, group, cols)
+
+
+def tri_back_kernel(t_ref, h_ref, gt_ref, t_hbm, ts_ref, gs_ref, sem):
+    rows, width, cols = h_ref.shape
+    mine = t_ref.shape[1]
+    group = BLOCK // rows
+    copy = pltpu.make_async_copy(t_ref, t_hbm, sem)
+    copy.start()
+    back = permutation(group, rows)
+    to_rows(t_ref, ts_ref)
+
+    def body(i, _):
+        tri, h = ts_ref[i].astype(F32), h_ref[i]
+        shifted = tri - jnp.mean(tri, axis=0, keepdims=True)
+        first = jnp.mean(h, axis=0, keepdims=True)
+        both = jnp.mean(h * shifted, axis=0, keepdims=True)
+        tri_inv = lax.rsqrt(jnp.mean(shifted * shifted, axis=0, keepdims=True) + EPSILON)
+        gs_ref[i] = (tri_inv * (h - first - shifted * (both * tri_inv * tri_inv))).astype(BF16)
+        return 0
+
+    lax.fori_loop(0, rows, body, 0, unroll=UNROLL)
+    blocks = places(width, mine, rows)
+    for n in range(0, len(blocks), 2):
+        pair = blocks[n : n + 2]
+        for (to, _here), block in zip(pair, swapped(back, [gs_ref[:, here] for _to, here in pair])):
+            gt_ref[to] = block.reshape(group // mine, mine, rows, cols)
+    copy.wait()
+
+
+def logit_kernel(*refs):
+    (fac_hbm, *sources), refs = refs[:10], refs[10:]
+    (gin0_ref, nt0_ref, fac0_ref, gin_hbm, nt_hbm, s_ref), refs = refs[:6], refs[6:]
+    (ts_ref, gin_ref, nt_ref, out_sems), targets, sems = refs[:4], refs[4:13], refs[13]
+    t_ref, x_ref, cot_ref, gain_ref, bias_ref, w_ref, ogain_ref, obias_ref, ow_ref = targets
+    rows, cols, width = x_ref.shape
+    first = pl.ds(0, nt0_ref.shape[0])
+    fetched([*sources, fac_hbm.at[first]], [*targets, fac0_ref], sems)
+    to_rows(t_ref, ts_ref)
+    ogain = column(ogain_ref[...], cols)
+    obias = column(obias_ref[...], cols)
+
+    def body(i, _):
+        normed, scale_inv = normalize(x_ref[i].astype(F32), -1)
+        normal_in = (normed * gain_ref[...] + bias_ref[...]).astype(BF16)
+        out_gate = sigmoid(dot(normal_in, w_ref[:, 4 * width :], 1, 0))
+        tri_hat, _s = normalize(ts_ref[i].astype(F32), 0)
+        normal_out = (tri_hat * ogain + obias).astype(BF16)
+        mixed = dot(normal_out, ow_ref[...], 0, 0)
+        grad_logit = cot_ref[i].astype(F32) * mixed * out_gate * (1.0 - out_gate)
+        gin_ref[i] = dot(w_ref[:, 4 * width :], grad_logit.astype(BF16), 1, 1)
+        nt_ref[i] = normed.T.astype(BF16)
+        s_ref[pl.ds(i, 1), :] = jnp.broadcast_to(scale_inv, (cols, width)).T[:1]
+        return 0
+
+    lax.fori_loop(0, rows, body, 0, unroll=UNROLL)
+    gin0_ref[...] = gin_ref[first]
+    nt0_ref[...] = nt_ref[first]
+    copies = [
+        pltpu.make_async_copy(gin_ref, gin_hbm, out_sems.at[0]),
+        pltpu.make_async_copy(nt_ref, nt_hbm, out_sems.at[1]),
+    ]
+    for copy in copies:
+        copy.start()
+    for copy in copies:
+        copy.wait()
+
+
+def pair_kernel(
+    lay, fac_hbm, nt_hbm, gin_hbm, fac0_ref, nt0_ref, gin0_ref, r_ref, s_ref, gain_ref, w_ref, *refs
+):
+    l_refs, refs = refs[: lay.n_hops], refs[lay.n_hops :]
+    out_hbm, l_ref, ls_ref, rs_ref, fac_ref, nt_ref, gin_ref, out_ref, sems = refs
+    rows, cols, width = out_ref.shape
+    mine = width // lay.half
+    parts = sems.shape[1]
+    size = rows // parts
+
+    def fetch(p):
+        here = pl.ds(p * size, size)
+        return [
+            pltpu.make_async_copy(fac_hbm.at[here], fac_ref.at[here], sems.at[0, p]),
+            pltpu.make_async_copy(nt_hbm.at[here], nt_ref.at[here], sems.at[1, p]),
+            pltpu.make_async_copy(gin_hbm.at[here], gin_ref.at[here], sems.at[2, p]),
+        ]
+
+    def send(p):
+        here = pl.ds(p * size, size)
+        return pltpu.make_async_copy(out_ref.at[here], out_hbm.at[here], sems.at[3, p])
+
+    for p in range(1, parts):
+        for copy in fetch(p):
+            copy.start()
+    gain = column(gain_ref[...], cols)
+    eye = identity(cols)
+    group = BLOCK // rows
+    swap = permutation(rows, group)
+    for s, source in lay.received(l_refs):
+        l_ref[lay.share(s)] = source[...]
+    for to, here in places(width, mine, rows):
+        sums = []
+        for share in range(to.start, to.stop):
+            one, two = (
+                r_ref[n].astype(F32)
+                for n, device in enumerate(lay.order)
+                if lay.inside.index(device % lay.half) == share
+            )
+            sums.append((one + two).astype(BF16))
+        left, right = swapped(swap, [l_ref[to], jnp.stack(sums)])
+        ls_ref[:, here] = left.reshape(rows, group, cols)
+        rs_ref[:, here] = right.reshape(rows, group, cols)
+
+    def part(p, fac_here, nt_here, gin_here):
+        for n in range(0, size, 2):
+            i = p * size + n
+            blocks = []
+            for m in range(2):
+                left, right, fac = ls_ref[i + m], rs_ref[i + m], fac_here[i + m]
+                blocks.append(
+                    jnp.concatenate(
+                        [
+                            left * fac[:width],
+                            left * fac[width : 2 * width],
+                            right * fac[2 * width : 3 * width],
+                            right * fac[3 * width :],
+                        ],
+                        axis=0,
+                    )
+                )
+            grad_in = dot(w_ref[:, : 4 * width], jnp.concatenate(blocks, axis=1), 1, 0)
+            for m in range(2):
+                grad = (grad_in[:, m * cols : (m + 1) * cols] + gin_here[i + m]) * gain
+                scale_inv = s_ref[pl.ds(i + m, 1), :]
+                normed = nt_here[i + m].astype(F32)
+                result = norm_back(grad, normed, scale_inv, 0).astype(BF16)
+                out_ref[i + m] = dot(eye, result, 1, 1).astype(BF16)
+
+    def body(p, _):
+        for copy in fetch(p):
+            copy.wait()
+        part(p, fac_ref, nt_ref, gin_ref)
+        send(p).start()
+        return 0
+
+    part(0, fac0_ref, nt0_ref, gin0_ref)
+    send(0).start()
+    lax.fori_loop(1, parts, body, 0)
+    for p in range(parts):
+        send(p).wait()
+
+
+class Layout:
+    def __init__(self, n_row, n_ch):
+        self.n_row, self.n_ch = n_row, n_ch
+        self.devices = n_row * n_ch
+        self.half = self.devices // 2
+        outer = math.isqrt(n_row)
+        self.inner = self.devices // outer
+        self.order = [o * self.inner + n for n in range(self.inner) for o in range(outer)]
+        self.inside = [o * self.inner + n for n in range(self.inner) for o in range(outer // 2)]
+        self.mate = n_ch
+        self.hops = [s for s in range(self.half) if s & self.mate == 0]
+        self.hops[1:] = self.hops[:0:-1]
+        self.n_hops = len(self.hops) + 1
+        self.all_place = self.place(self.order, n_row)
+        self.half_place = self.place(self.inside, n_row // 2)
+        self.near_place = self.place(list(range(self.half)), n_row // 2)
+
+    def place(self, order, n_row):
+        return [[order.index(r * self.n_ch + b) for b in range(self.n_ch)] for r in range(n_row)]
+
+    def other(self, s):
+        me = lax.axis_index("row") * self.n_ch + lax.axis_index("ch")
+        return jnp.bitwise_xor(lax.rem(me, self.half), s)
+
+    def share(self, s):
+        other = self.other(s)
+        return lax.rem(other, self.inner) * (self.half // self.inner) + lax.div(other, self.inner)
+
+    def exchange_all(self, blocks):
+        return lax.all_to_all(
+            blocks, ("row", "ch"), split_axis=0, concat_axis=0, tiled=True, axis_index_groups=[self.order]
+        )
+
+    def exchange_half(self, blocks):
+        groups = [[first + n for n in self.inside] for first in (0, self.half)]
+        return lax.all_to_all(
+            blocks, ("row", "ch"), split_axis=0, concat_axis=0, tiled=True, axis_index_groups=groups
+        )
+
+    def swap(self, block, s):
+        return lax.ppermute(block, ("row", "ch"), [(n, n ^ s) for n in range(self.devices)])
+
+    def permute(self, mine, mates):
+        mates = self.swap(mates, self.mate)
+        shape = jax.ShapeDtypeStruct((2,) + mine.shape[1:], mine.dtype)
+        pairs = call(merge_kernel, [shape] * (len(self.hops) - 1), [], mine, mates)
+        return [mine, mates] + [self.swap(pair, s) for pair, s in zip(pairs, self.hops[1:])]
+
+    def received(self, refs):
+        mine, mates, *pairs = refs
+        found = [(0, mine.at[0]), (self.mate, mates.at[0])]
+        for s, pair in zip(self.hops[1:], pairs):
+            found += [(s, pair.at[0]), (s ^ self.mate, pair.at[1])]
+        return found
+
+
+def merge_kernel(mine_ref, mates_ref, *outs):
+    for n, out_ref in enumerate(outs, 1):
+        out_ref[0] = mine_ref[n]
+        out_ref[1] = mates_ref[n]
+
+
+def plane(ref, place, c):
+    return jnp.concatenate(
+        [
+            jnp.concatenate([ref[n, c] for n in column_of], axis=0)
+            for column_of in zip(*place)
+        ],
+        axis=1,
+    )
+
+
+def store_plane(ref, place, c, value):
+    rows, cols = ref.shape[-2:]
+    for r, row_of in enumerate(place):
+        for b, n in enumerate(row_of):
+            ref[n, c] = value[r * rows : (r + 1) * rows, b * cols : (b + 1) * cols]
+
+
+def tri_kernel(lay, r_ref, *refs):
+    l_refs, (t_ref, l_ref) = refs[: lay.n_hops], refs[lay.n_hops :]
+    for s, source in lay.received(l_refs):
+        l_ref[lay.other(s)] = source[...]
+    for c in range(t_ref.shape[1]):
+        tri = dot(plane(l_ref, lay.near_place, c), plane(r_ref, lay.all_place, c), 1, 1)
+        store_plane(t_ref, lay.half_place, c, tri.astype(BF16))
+
+
+def factor_back_kernel(lay, gt_ref, l_ref, r_ref, gr_hbm, *refs):
+    mine_out, mate_out, gl_ref, gr_ref, sems = refs
+    copies = []
+    for c in range(gt_ref.shape[1]):
+        right = dot(plane(gt_ref, lay.half_place, c), plane(l_ref, lay.near_place, c), 0, 0)
+        store_plane(gr_ref, lay.all_place, c, right.astype(BF16))
+        here = (slice(None), c)
+        copies.append(pltpu.make_async_copy(gr_ref.at[here], gr_hbm.at[here], sems.at[c]))
+        copies[-1].start()
+    for c in range(gt_ref.shape[1]):
+        left = dot(plane(gt_ref, lay.half_place, c), plane(r_ref, lay.all_place, c), 1, 0)
+        store_plane(gl_ref, lay.near_place, c, left.astype(BF16))
+    for n, s in enumerate(lay.hops):
+        mine_out[n] = gl_ref[lay.other(s)]
+        mate_out[n] = gl_ref[lay.other(s ^ lay.mate)]
+    for copy in copies:
+        copy.wait()
+
+
+def by_channel(
+    n_row, n_ch, pair_act, cotangent, in_gain, in_bias, proj_weight, out_gain, out_bias, out_weight
+):
+    lay = Layout(n_row, n_ch)
+    rows, cols, width = pair_act.shape
+    mine = width // lay.half
+    struct = jax.ShapeDtypeStruct
+    half = pltpu.VMEM((rows, width, cols), BF16)
+    weight_t = pltpu.VMEM((4 * width, width), BF16)
+    in_gain, in_bias, out_gain, out_bias = (
+        v.reshape(1, width) for v in (in_gain, in_bias, out_gain, out_bias)
+    )
+
+    some = struct((len(lay.hops), mine, rows, cols), BF16)
+    one = struct((lay.half, mine, rows, cols), BF16)
+    one_here = pltpu.VMEM(one.shape, BF16)
+    two_shape = (lay.devices, mine, rows, cols)
+    row = pltpu.VMEM((1, width), F32)
+    weight = pltpu.VMEM(proj_weight.shape, BF16)
+    out_weight_here = pltpu.VMEM((width, width), BF16)
+    both_weights = pltpu.VMEM((width, 2 * width), BF16)
+    both_turned = pltpu.VMEM((2 * width, width), BF16)
+    right, normal_in = call(
+        functools.partial(right_kernel, lay),
+        [pltpu.HBM(two_shape, BF16), struct((rows // 2, width, 2 * cols), BF16)],
+        [
+            half,
+            row,
+            row,
+            both_weights,
+            both_turned,
+            half,
+            one_here,
+            pltpu.SemaphoreType.DMA((4 + PARTS,)),
+            pltpu.SemaphoreType.DMA((lay.devices,)),
+        ],
+        pair_act,
+        in_gain,
+        in_bias,
+        proj_weight,
+        hbm=4,
+    )
+    left = call(
+        functools.partial(left_kernel, lay),
+        [some, some],
+        [both_weights, both_turned, half, one_here, pltpu.SemaphoreType.DMA((2,))],
+        proj_weight,
+        normal_in,
+        hbm=1,
+    )
+    right = lay.exchange_all(right)
+    left = lay.permute(*left)
+    h, fac = call(
+        gate_kernel,
+        [pltpu.VMEM((rows, width, cols), F32), pltpu.HBM((rows, 4 * width, cols), BF16)],
+        [
+            pltpu.VMEM((rows, 4 * width, cols), BF16),
+            weight_t,
+            half,
+            half,
+            row,
+            row,
+            weight,
+            row,
+            out_weight_here,
+            pltpu.SemaphoreType.DMA((7,)),
+            pltpu.SemaphoreType.DMA((PARTS,)),
+        ],
+        pair_act,
+        cotangent,
+        in_gain,
+        in_bias,
+        proj_weight,
+        out_gain,
+        out_weight,
+        hbm=7,
+    )
+    right, h, fac = lax.optimization_barrier((right, h, fac))
+    tri, left = call(functools.partial(tri_kernel, lay), [one, one], [], right, *left)
+    tri = lay.exchange_half(tri)
+    grad_tri, tri = call(
+        tri_back_kernel,
+        [one, pltpu.HBM(one.shape, BF16)],
+        [half, half, pltpu.SemaphoreType.DMA(())],
+        tri,
+        h,
+    )
+    grad_right, *grad_left = call(
+        functools.partial(factor_back_kernel, lay),
+        [pltpu.HBM(two_shape, BF16), some, some],
+        [one_here, pltpu.VMEM(two_shape, BF16), pltpu.SemaphoreType.DMA((mine,))],
+        lay.exchange_half(grad_tri),
+        left,
+        right,
+    )
+    grad_right = lay.exchange_all(grad_right)
+    grad_left = lay.permute(*grad_left)
+    grad_in_first, normed_first, fac_first, grad_in, normed_t, scale = call(
+        logit_kernel,
+        [
+            pltpu.VMEM((rows // PARTS, width, cols), F32),
+            pltpu.VMEM((rows // PARTS, width, cols), BF16),
+            pltpu.VMEM((rows // PARTS, 4 * width, cols), BF16),
+            pltpu.HBM((rows, width, cols), F32),
+            pltpu.HBM((rows, width, cols), BF16),
+            pltpu.VMEM((rows, cols), F32),
+        ],
+        [
+            half,
+            pltpu.VMEM((rows, width, cols), F32),
+            half,
+            pltpu.SemaphoreType.DMA((2,)),
+            one_here,
+            half,
+            half,
+            row,
+            row,
+            weight,
+            row,
+            row,
+            out_weight_here,
+            pltpu.SemaphoreType.DMA((10,)),
+        ],
+        fac,
+        tri,
+        pair_act,
+        cotangent,
+        in_gain,
+        in_bias,
+        proj_weight,
+        out_gain,
+        out_bias,
+        out_weight,
+        hbm=10,
+    )
+    return call(
+        functools.partial(pair_kernel, lay),
+        pltpu.HBM((rows, cols, width), BF16),
+        [
+            one_here,
+            half,
+            half,
+            pltpu.VMEM((rows, 4 * width, cols), BF16),
+            half,
+            pltpu.VMEM((rows, width, cols), F32),
+            half,
+            pltpu.SemaphoreType.DMA((4, PARTS)),
+        ],
+        fac,
+        normed_t,
+        grad_in,
+        fac_first,
+        normed_first,
+        grad_in_first,
+        grad_right,
+        scale,
+        in_gain,
+        proj_weight,
+        *grad_left,
+        hbm=3,
+    )
+
+
+def by_row(
+    pair_act, cotangent, in_gain, in_bias, proj_weight, out_gain, out_bias, out_weight
+):
     rows_here, cols_here, width = pair_act.shape
     flat = pair_act.astype(jnp.float32).reshape(rows_here * cols_here, width)
     normed, scale_inv = normalize(flat, -1)
@@ -55,17 +723,15 @@
     grad_tri = grad_tri.astype(jnp.bfloat16).reshape(width, rows_here, cols_here)
     grad_chan = lax.all_to_all(grad_tri, "ch", split_axis=0, concat_axis=2, tiled=True)
     grad_cols = lax.all_to_all(grad_chan, "row", split_axis=2, concat_axis=1, tiled=True)
-    block = grad_chan
     grad_left = jnp.einsum(
         "cij,cjk->cik",
-        block,
+        grad_chan,
         lax.all_gather(right_chan, "row", axis=1, tiled=True),
         preferred_element_type=jnp.float32,
     )
-    block = grad_cols
     grad_right = jnp.einsum(
         "cij,cik->cjk",
-        block,
+        grad_cols,
         lax.all_gather(left_chan, "row", axis=1, tiled=True),
         preferred_element_type=jnp.float32,
     )
@@ -95,7 +761,27 @@
 
 
 def solution(mesh):
+    n_row, n_ch = mesh.shape["row"], mesh.shape["ch"]
     placed = (P("row", "ch", None), P("row", "ch", None), P(), P(), P(), P(), P(), P())
+
+    def on_device(*args):
+        rows, cols, width = args[0].shape
+        devices, outer, group = n_row * n_ch, math.isqrt(n_row), BLOCK // rows
+        if (
+            devices & (devices - 1) == 0
+            and n_row >= 4
+            and n_row % outer == 0
+            and outer % 2 == 0
+            and width % (devices // 2) == 0
+            and rows % (2 * PARTS) == 0
+            and BLOCK % rows == 0
+            and group % (width // (devices // 2)) == 0
+            and width % (2 * group) == 0
+            and cols % 128 == 0
+        ):
+            return by_channel(n_row, n_ch, *args)
+        return by_row(*args)
+
     return jax.shard_map(
         on_device, mesh=mesh, in_specs=placed, out_specs=P("row", "ch", None), check_vma=False
     )

time: 239 us -> 110 us (0.46)
  waiting for transfers between devices: 99.2 us -> 18.7 us
  local copies, waits for them, and re-layouts: 27.5 us -> 0.01 us
  Pallas kernels: 0 us -> 25.5 us
  starting transfers between devices: 11.5 us -> 35.4 us
  matrix products: 23.6 us -> 0 us
  other arithmetic: 19.7 us -> 0 us
  blocking collectives: 42.8 us -> 28.1 us
  between operations: 13.8 us -> 0.2 us
    all_gather x2 -> x0, waiting for transfers between devices: 71.1 us -> none  [the longest x1 67.8 us: on_device(): lax.all_gather(right_chan, 'row', axis=1, tiled=True)]
    all_to_all x3 -> x2, waiting for transfers between devices: 28.2 us -> 0.01 us  [exchange_all(): lax.all_to_all(blocks, ('row', 'ch'), split_axis=0, concat_axis=0, tiled=...]
    pallas_call x0 -> x10, Pallas kernels: none -> 25.5 us  [call(): pl.pallas_call(kernel, out_shape=outs if single else tuple(outs), in_spec...]
    ppermute x0 -> x16, starting transfers between devices: none -> 24.4 us  [swap(): lax.ppermute(block, ('row', 'ch'), [(n, n ^ s) for n in range(self.device...]
    dot_general x7 -> x0, matrix products: 23.6 us -> none  [the longest x1 5.68 us: on_device(): jnp.einsum('cik,cjk->cij', left_chan, lax.all_gather(right_chan, 'row', a...]
    ppermute x0 -> x16, waiting for transfers between devices: none -> 18.7 us  [swap(): lax.ppermute(block, ('row', 'ch'), [(n, n ^ s) for n in range(self.device...]
    all_to_all x4 -> x2, blocking collectives: 42.8 us -> 28.1 us  [exchange_half(): lax.all_to_all(blocks, ('row', 'ch'), split_axis=0, concat_axis=0, tiled=...]
    unnamed x31 -> x4, local copies, waits for them, and re-layouts: 13.2 us -> 0.01 us
  transfers between devices with their start and end apart: 5 -> 18, of which waited for: 5 -> 4; matrix products, arithmetic and copies ran while one was open for 16% -> 0% of each run, Pallas kernels for 0% -> 13%
where the time goes in v1:
time: 110 us; the launch traced here: 108 us
  starting transfers between devices  35.4 us (32%)
  blocking collectives  28.1 us (26%)
  Pallas kernels  25.5 us (23%)
  waiting for transfers between devices  18.7 us (17%)
    all_to_all x2, blocking collectives, exchange_half(): lax.all_to_all(blocks, ('row', 'ch'), split_axis=0, concat_axis=0, tiled=...  28.1 us
    pallas_call x10, Pallas kernels, call(): pl.pallas_call(kernel, out_shape=outs if single else tuple(outs), in_spec...  25.5 us
    ppermute x16, starting transfers between devices, swap(): lax.ppermute(block, ('row', 'ch'), [(n, n ^ s) for n in range(self.device...  24.4 us
    ppermute x16, waiting for transfers between devices, swap(): lax.ppermute(block, ('row', 'ch'), [(n, n ^ s) for n in range(self.device...  18.7 us
    all_to_all x2, starting transfers between devices, exchange_all(): lax.all_to_all(blocks, ('row', 'ch'), split_axis=0, concat_axis=0, tiled=...  11.1 us
  transfers between devices with their start and end apart: 18, of which 4 were waited for; matrix products, arithmetic and copies ran while one was open for 0% of the time, Pallas kernels for 13%

profile of v1, /device:TPU:0, one launch (start us, length us, event | category | flops | bytes accessed | tf_op | source)
XLA Modules:
  0.0 107.9 jit_solution(2687892959843245417)
XLA Ops:
  0.0 4.6 %shard_map.82 = (bf16[32,8,16,128]{3,2,1,0:T(8,128)(2,1)}, bf16[8,128,256]{2,1,0:T(8,128)(2,1)S(1)}) custom-call(bf16[16,128,128]{2,1,0:T(8,128)(2,1)} %refs_2_.1, f32[1,128]{1,0:T(1,128)} %bitcast.4, f32[1,128]{1,0:T(1,128)} %bitcast.8, bf16[128,640]{1,0:T(8,128)(2,1)} %w_ref.1), custom_call_target="tpu_custom_call" | custom-call | tf_op jit(solution)/shard_map/pallas_call | solution.py:52
  4.6 7.3 %all-to-all-start = ((bf16[32,8,16,128]{3,2,1,0:T(8,128)(2,1)}), bf16[32,8,16,128]{3,2,1,0:T(8,128)(2,1)S(1)}, u32[]{:S(2)}, u32[]{:S(2)}) async-start(bf16[32,8,16,128]{3,2,1,0:T(8,128)(2,1)} %get-tuple-element.41), calls=%async_computation | async-start | bytes 2097152 | tf_op jit(solution)/shard_map/all_to_all | solution.py:447
  11.9 2.2 %shard_map.84 = (bf16[8,8,16,128]{3,2,1,0:T(8,128)(2,1)S(1)}, bf16[8,8,16,128]{3,2,1,0:T(8,128)(2,1)S(1)}) custom-call(bf16[128,640]{1,0:T(8,128)(2,1)} %w_ref.1, bf16[8,128,256]{2,1,0:T(8,128)(2,1)S(1)} %get-tuple-element.46.n_ref), custom_call_target="tpu_custom_call" | custom-call | tf_op jit(solution)/shard_map/pallas_call | solution.py:52
  14.1 0.3 collective-permute-start
  14.4 1.3 %collective-permute-done.mates_ref.refs_1_ = bf16[8,8,16,128]{3,2,1,0:T(8,128)(2,1)S(1)} collective-permute-done((bf16[8,8,16,128]{3,2,1,0:T(8,128)(2,1)S(1)}, bf16[8,8,16,128]{3,2,1,0:T(8,128)(2,1)S(1)}, u32[]{:S(2)}, u32[]{:S(2)}) %collective-permute-start) | collective-permute-done | bytes 262176 | tf_op jit(solution)/shard_map/ppermute | solution.py:458
  15.7 3.6 %collective-permute-start.1 = (bf16[2,8,16,128]{3,2,1,0:T(8,128)(2,1)S(1)}, bf16[2,8,16,128]{3,2,1,0:T(8,128)(2,1)S(1)}, u32[]{:S(2)}, u32[]{:S(2)}) collective-permute-start(bf16[2,8,16,128]{3,2,1,0:T(8,128)(2,1)S(1)} %get-tuple-element.49), channel_id=1, source_target_pairs={{0,13},{1,12},{2,15},{3,14},{4,9},{5,8},{6,11},{7,10},{8,5},{9,4},... | collective-permute-start | bytes 196616 | tf_op jit(solution)/shard_map/ppermute | solution.py:458
  19.4 0.5 collective-permute-start.2
  19.9 1.5 %collective-permute-start.3 = (bf16[2,8,16,128]{3,2,1,0:T(8,128)(2,1)S(1)}, bf16[2,8,16,128]{3,2,1,0:T(8,128)(2,1)S(1)}, u32[]{:S(2)}, u32[]{:S(2)}) collective-permute-start(bf16[2,8,16,128]{3,2,1,0:T(8,128)(2,1)S(1)} %get-tuple-element.51), channel_id=1, source_target_pairs={{0,9},{1,8},{2,11},{3,10},{4,13},{5,12},{6,15},{7,14},{8,1},{9,0},... | collective-permute-start | bytes 196616 | tf_op jit(solution)/shard_map/ppermute | solution.py:458
  21.4 0.3 collective-permute-start.4
  21.6 2.7 %collective-permute-start.5 = (bf16[2,8,16,128]{3,2,1,0:T(8,128)(2,1)S(1)}, bf16[2,8,16,128]{3,2,1,0:T(8,128)(2,1)S(1)}, u32[]{:S(2)}, u32[]{:S(2)}) collective-permute-start(bf16[2,8,16,128]{3,2,1,0:T(8,128)(2,1)S(1)} %get-tuple-element.53), channel_id=1, source_target_pairs={{0,5},{1,4},{2,7},{3,6},{4,1},{5,0},{6,3},{7,2},{8,13},{9,12},{10,... | collective-permute-start | bytes 196616 | tf_op jit(solution)/shard_map/ppermute | solution.py:458
  24.3 6.9 %collective-permute-done.1.refs_2_ = bf16[2,8,16,128]{3,2,1,0:T(8,128)(2,1)S(1)} collective-permute-done((bf16[2,8,16,128]{3,2,1,0:T(8,128)(2,1)S(1)}, bf16[2,8,16,128]{3,2,1,0:T(8,128)(2,1)S(1)}, u32[]{:S(2)}, u32[]{:S(2)}) %collective-permute-start.1) | collective-permute-done | bytes 65568 | tf_op jit(solution)/shard_map/ppermute | solution.py:458
  31.2 1.8 %collective-permute-start.6 = (bf16[2,8,16,128]{3,2,1,0:T(8,128)(2,1)S(1)}, bf16[2,8,16,128]{3,2,1,0:T(8,128)(2,1)S(1)}, u32[]{:S(2)}, u32[]{:S(2)}) collective-permute-start(bf16[2,8,16,128]{3,2,1,0:T(8,128)(2,1)S(1)} %get-tuple-element.54), channel_id=1, source_target_pairs={{0,4},{1,5},{2,6},{3,7},{4,0},{5,1},{6,2},{7,3},{8,12},{9,13},{10,... | collective-permute-start | bytes 196616 | tf_op jit(solution)/shard_map/ppermute | solution.py:458
  33.0 0.0 collective-permute-done.2.refs_3_
  33.0 1.5 %collective-permute-start.7 = (bf16[2,8,16,128]{3,2,1,0:T(8,128)(2,1)S(1)}, bf16[2,8,16,128]{3,2,1,0:T(8,128)(2,1)S(1)}, u32[]{:S(2)}, u32[]{:S(2)}) collective-permute-start(bf16[2,8,16,128]{3,2,1,0:T(8,128)(2,1)S(1)} %get-tuple-element.55), channel_id=1, source_target_pairs={{0,1},{1,0},{2,3},{3,2},{4,5},{5,4},{6,7},{7,6},{8,9},{9,8},{10,11... | collective-permute-start | bytes 196616 | tf_op jit(solution)/shard_map/ppermute | solution.py:458
  34.5 5.7 %shard_map.83 = (f32[16,128,128]{2,1,0:T(8,128)S(1)}, bf16[16,512,128]{2,1,0:T(8,128)(2,1)}) custom-call(bf16[16,128,128]{2,1,0:T(8,128)(2,1)} %refs_2_.1, bf16[16,128,128]{2,1,0:T(8,128)(2,1)} %refs_3_.1, f32[1,128]{1,0:T(1,128)} %bitcast.5, f32[1,128]{1,0:T(1,128)} %bitcast.9, bf16[128,640]{1,0:T(8,128)(2,1)} %w_ref.1, f32[1,128]{1,0:T(1,128)} %bitcast.11, ...), custom_call_target="tpu_custom_call" | custom-call | tf_op jit(solution)/shard_map/pallas_call | solution.py:52
  40.3 0.0 all-to-all-done.r_ref
  40.3 0.0 collective-permute-done.3.refs_4_
  40.3 0.0 collective-permute-done.4.refs_5_
  40.3 0.0 collective-permute-done.5.refs_6_
  40.3 0.0 collective-permute-done.6.refs_7_
  40.4 0.0 collective-permute-done.7.refs_8_
  40.4 0.5 shard_map.86
  40.8 15.8 %all_to_all.20.t_ref = bf16[16,8,16,128]{3,2,1,0:T(8,128)(2,1)S(1)} all-to-all(bf16[16,8,16,128]{3,2,1,0:T(8,128)(2,1)S(1)} %get-tuple-element.56), channel_id=1, replica_groups={{0,8,1,9,2,10,3,11,4,12,5,13,6,14,7,15},{16,24,17,25,18,26,19,27,20,28,..., dimensions={0} | all-to-all | bytes 1048576 | tf_op jit(solution)/shard_map/all_to_all | solution.py:453
  56.7 1.2 %shard_map.87 = (bf16[16,8,16,128]{3,2,1,0:T(8,128)(2,1)S(1)}, bf16[16,8,16,128]{3,2,1,0:T(8,128)(2,1)}) custom-call(bf16[16,8,16,128]{3,2,1,0:T(8,128)(2,1)S(1)} %all_to_all.20.t_ref, f32[16,128,128]{2,1,0:T(8,128)S(1)} %get-tuple-element.57.h_ref), custom_call_target="tpu_custom_call" | custom-call | tf_op jit(solution)/shard_map/pallas_call | solution.py:52
  57.9 12.3 %all_to_all.21.gt_ref = bf16[16,8,16,128]{3,2,1,0:T(8,128)(2,1)S(1)} all-to-all(bf16[16,8,16,128]{3,2,1,0:T(8,128)(2,1)S(1)} %get-tuple-element.64), channel_id=1, replica_groups={{0,8,1,9,2,10,3,11,4,12,5,13,6,14,7,15},{16,24,17,25,18,26,19,27,20,28,..., dimensions={0} | all-to-all | bytes 1048576 | tf_op jit(solution)/shard_map/all_to_all | solution.py:453
  70.2 1.3 %shard_map.89 = (bf16[32,8,16,128]{3,2,1,0:T(8,128)(2,1)}, bf16[8,8,16,128]{3,2,1,0:T(8,128)(2,1)S(1)}, bf16[8,8,16,128]{3,2,1,0:T(8,128)(2,1)S(1)}) custom-call(bf16[16,8,16,128]{3,2,1,0:T(8,128)(2,1)S(1)} %all_to_all.21.gt_ref, bf16[16,8,16,128]{3,2,1,0:T(8,128)(2,1)S(1)} %get-tuple-element.65.l_ref, bf16[32,8,16,128]{3,2,1,0:T(8,128)(2,1)S(1)} %all-to-all-done.r_ref), custom_call_target="tpu_custom_call" | custom-call | tf_op jit(solution)/shard_map/pallas_call | solution.py:52
  71.6 3.8 %all-to-all-start.3 = ((bf16[32,8,16,128]{3,2,1,0:T(8,128)(2,1)}), bf16[32,8,16,128]{3,2,1,0:T(8,128)(2,1)S(1)}, u32[]{:S(2)}, u32[]{:S(2)}) async-start(bf16[32,8,16,128]{3,2,1,0:T(8,128)(2,1)} %get-tuple-element.66), calls=%async_computation.3 | async-start | bytes 2097152 | tf_op jit(solution)/shard_map/all_to_all | solution.py:447
  75.4 0.3 collective-permute-start.8
  75.7 1.3 %collective-permute-done.8.mates_ref.refs_1_ = bf16[8,8,16,128]{3,2,1,0:T(8,128)(2,1)S(1)} collective-permute-done((bf16[8,8,16,128]{3,2,1,0:T(8,128)(2,1)S(1)}, bf16[8,8,16,128]{3,2,1,0:T(8,128)(2,1)S(1)}, u32[]{:S(2)}, u32[]{:S(2)}) %collective-permute-start.8) | collective-permute-done | bytes 262176 | tf_op jit(solution)/shard_map/ppermute | solution.py:458
  77.0 0.0 copy-start
  77.0 0.0 copy-start.1
  77.0 3.6 %collective-permute-start.9 = (bf16[2,8,16,128]{3,2,1,0:T(8,128)(2,1)S(1)}, bf16[2,8,16,128]{3,2,1,0:T(8,128)(2,1)S(1)}, u32[]{:S(2)}, u32[]{:S(2)}) collective-permute-start(bf16[2,8,16,128]{3,2,1,0:T(8,128)(2,1)S(1)} %get-tuple-element.70), channel_id=1, source_target_pairs={{0,13},{1,12},{2,15},{3,14},{4,9},{5,8},{6,11},{7,10},{8,5},{9,4},... | collective-permute-start | bytes 196616 | tf_op jit(solution)/shard_map/ppermute | solution.py:458
  80.6 0.6 collective-permute-start.10
  81.2 1.5 %collective-permute-start.11 = (bf16[2,8,16,128]{3,2,1,0:T(8,128)(2,1)S(1)}, bf16[2,8,16,128]{3,2,1,0:T(8,128)(2,1)S(1)}, u32[]{:S(2)}, u32[]{:S(2)}) collective-permute-start(bf16[2,8,16,128]{3,2,1,0:T(8,128)(2,1)S(1)} %get-tuple-element.72), channel_id=1, source_target_pairs={{0,9},{1,8},{2,11},{3,10},{4,13},{5,12},{6,15},{7,14},{8,1},{9,0},... | collective-permute-start | bytes 196616 | tf_op jit(solution)/shard_map/ppermute | solution.py:458
  82.7 0.3 collective-permute-start.12
  82.9 2.7 %collective-permute-start.13 = (bf16[2,8,16,128]{3,2,1,0:T(8,128)(2,1)S(1)}, bf16[2,8,16,128]{3,2,1,0:T(8,128)(2,1)S(1)}, u32[]{:S(2)}, u32[]{:S(2)}) collective-permute-start(bf16[2,8,16,128]{3,2,1,0:T(8,128)(2,1)S(1)} %get-tuple-element.74), channel_id=1, source_target_pairs={{0,5},{1,4},{2,7},{3,6},{4,1},{5,0},{6,3},{7,2},{8,13},{9,12},{10,... | collective-permute-start | bytes 196616 | tf_op jit(solution)/shard_map/ppermute | solution.py:458
  85.6 9.1 %collective-permute-done.9.refs_2_ = bf16[2,8,16,128]{3,2,1,0:T(8,128)(2,1)S(1)} collective-permute-done((bf16[2,8,16,128]{3,2,1,0:T(8,128)(2,1)S(1)}, bf16[2,8,16,128]{3,2,1,0:T(8,128)(2,1)S(1)}, u32[]{:S(2)}, u32[]{:S(2)}) %collective-permute-start.9) | collective-permute-done | bytes 65568 | tf_op jit(solution)/shard_map/ppermute | solution.py:458
  94.7 1.8 %collective-permute-start.14 = (bf16[2,8,16,128]{3,2,1,0:T(8,128)(2,1)S(1)}, bf16[2,8,16,128]{3,2,1,0:T(8,128)(2,1)S(1)}, u32[]{:S(2)}, u32[]{:S(2)}) collective-permute-start(bf16[2,8,16,128]{3,2,1,0:T(8,128)(2,1)S(1)} %get-tuple-element.75), channel_id=1, source_target_pairs={{0,4},{1,5},{2,6},{3,7},{4,0},{5,1},{6,2},{7,3},{8,12},{9,13},{10,... | collective-permute-start | bytes 196616 | tf_op jit(solution)/shard_map/ppermute | solution.py:458
  96.5 0.0 collective-permute-done.10.refs_3_
  96.5 1.5 %collective-permute-start.15 = (bf16[2,8,16,128]{3,2,1,0:T(8,128)(2,1)S(1)}, bf16[2,8,16,128]{3,2,1,0:T(8,128)(2,1)S(1)}, u32[]{:S(2)}, u32[]{:S(2)}) collective-permute-start(bf16[2,8,16,128]{3,2,1,0:T(8,128)(2,1)S(1)} %get-tuple-element.76), channel_id=1, source_target_pairs={{0,1},{1,0},{2,3},{3,2},{4,5},{5,4},{6,7},{7,6},{8,9},{9,8},{10,11... | collective-permute-start | bytes 196616 | tf_op jit(solution)/shard_map/ppermute | solution.py:458
  98.0 6.0 %shard_map.88 = (f32[4,128,128]{2,1,0:T(8,128)S(1)}, bf16[4,128,128]{2,1,0:T(8,128)(2,1)S(1)}, bf16[4,512,128]{2,1,0:T(8,128)(2,1)S(1)}, f32[16,128,128]{2,1,0:T...) custom-call(bf16[16,512,128]{2,1,0:T(8,128)(2,1)} %get-tuple-element.44.refs_0_.fac_hbm, ...), custom_call_target="tpu_custom_call" | custom-call | tf_op jit(solution)/shard_map/pallas_call | solution.py:52
  104.0 0.0 collective-permute-done.11.refs_4_
  104.0 0.0 collective-permute-done.12.refs_5_
  104.0 0.0 collective-permute-done.13.refs_6_
  104.0 0.0 collective-permute-done.14.refs_7_
  104.0 0.0 collective-permute-done.15.refs_8_
  104.0 0.0 all-to-all-done.3.r_ref
  104.0 0.0 copy-done
  104.0 0.0 copy-done.1
  104.1 3.9 %shard_map.91 = bf16[16,128,128]{2,1,0:T(8,128)(2,1)} custom-call(bf16[16,512,128]{2,1,0:T(8,128)(2,1)} %get-tuple-element.44.refs_0_.fac_hbm, bf16[16,128,128]{2,1,0:T(8,128)(2,1)} %get-tuple-element.59.nt_hbm, f32[16,128,128]{2,1,0:T(8,128)} %get-tuple-element.60.gin_hbm, bf16[4,512,128]{2,1,0:T(8,128)(2,1)S(1)} %get-tuple-element.61.fac0_ref, ...), custom_call_target="tpu_custom_call" | custom-call | tf_op jit(solution)/shard_map/pallas_call | solution.py:52
  (2 shorter events, 0.1 us)
Async XLA Ops:
  4.6 35.7 %all-to-all-start = ((bf16[32,8,16,128]{3,2,1,0:T(8,128)(2,1)}), bf16[32,8,16,128]{3,2,1,0:T(8,128)(2,1)S(1)}, u32[]{:S(2)}, u32[]{:S(2)}) async-start(bf16[32,8,16,128]{3,2,1,0:T(8,128)(2,1)} %get-tuple-element.41), calls=%async_computation | async-start | bytes 2097152 | tf_op jit(solution)/shard_map/all_to_all | solution.py:447
  14.1 1.6 %collective-permute-start = (bf16[8,8,16,128]{3,2,1,0:T(8,128)(2,1)S(1)}, bf16[8,8,16,128]{3,2,1,0:T(8,128)(2,1)S(1)}, u32[]{:S(2)}, u32[]{:S(2)}) collective-permute-start(bf16[8,8,16,128]{3,2,1,0:T(8,128)(2,1)S(1)} %get-tuple-element.48), channel_id=1, source_target_pairs={{0,2},{1,3},{2,0},{3,1},{4,6},{5,7},{6,4},{7,5},{8,10},{9,11},{10,... | collective-permute-start | bytes 786440 | tf_op jit(solution)/shard_map/ppermute | solution.py:458
  15.7 15.5 %collective-permute-start.1 = (bf16[2,8,16,128]{3,2,1,0:T(8,128)(2,1)S(1)}, bf16[2,8,16,128]{3,2,1,0:T(8,128)(2,1)S(1)}, u32[]{:S(2)}, u32[]{:S(2)}) collective-permute-start(bf16[2,8,16,128]{3,2,1,0:T(8,128)(2,1)S(1)} %get-tuple-element.49), channel_id=1, source_target_pairs={{0,13},{1,12},{2,15},{3,14},{4,9},{5,8},{6,11},{7,10},{8,5},{9,4},... | collective-permute-start | bytes 196616 | tf_op jit(solution)/shard_map/ppermute | solution.py:458
  19.4 13.7 %collective-permute-start.2 = (bf16[2,8,16,128]{3,2,1,0:T(8,128)(2,1)S(1)}, bf16[2,8,16,128]{3,2,1,0:T(8,128)(2,1)S(1)}, u32[]{:S(2)}, u32[]{:S(2)}) collective-permute-start(bf16[2,8,16,128]{3,2,1,0:T(8,128)(2,1)S(1)} %get-tuple-element.50), channel_id=1, source_target_pairs={{0,12},{1,13},{2,14},{3,15},{4,8},{5,9},{6,10},{7,11},{8,4},{9,5},... | collective-permute-start | bytes 196616 | tf_op jit(solution)/shard_map/ppermute | solution.py:458
  19.9 20.4 %collective-permute-start.3 = (bf16[2,8,16,128]{3,2,1,0:T(8,128)(2,1)S(1)}, bf16[2,8,16,128]{3,2,1,0:T(8,128)(2,1)S(1)}, u32[]{:S(2)}, u32[]{:S(2)}) collective-permute-start(bf16[2,8,16,128]{3,2,1,0:T(8,128)(2,1)S(1)} %get-tuple-element.51), channel_id=1, source_target_pairs={{0,9},{1,8},{2,11},{3,10},{4,13},{5,12},{6,15},{7,14},{8,1},{9,0},... | collective-permute-start | bytes 196616 | tf_op jit(solution)/shard_map/ppermute | solution.py:458
  21.4 19.0 %collective-permute-start.4 = (bf16[2,8,16,128]{3,2,1,0:T(8,128)(2,1)S(1)}, bf16[2,8,16,128]{3,2,1,0:T(8,128)(2,1)S(1)}, u32[]{:S(2)}, u32[]{:S(2)}) collective-permute-start(bf16[2,8,16,128]{3,2,1,0:T(8,128)(2,1)S(1)} %get-tuple-element.52), channel_id=1, source_target_pairs={{0,8},{1,9},{2,10},{3,11},{4,12},{5,13},{6,14},{7,15},{8,0},{9,1},... | collective-permute-start | bytes 196616 | tf_op jit(solution)/shard_map/ppermute | solution.py:458
  21.6 18.7 %collective-permute-start.5 = (bf16[2,8,16,128]{3,2,1,0:T(8,128)(2,1)S(1)}, bf16[2,8,16,128]{3,2,1,0:T(8,128)(2,1)S(1)}, u32[]{:S(2)}, u32[]{:S(2)}) collective-permute-start(bf16[2,8,16,128]{3,2,1,0:T(8,128)(2,1)S(1)} %get-tuple-element.53), channel_id=1, source_target_pairs={{0,5},{1,4},{2,7},{3,6},{4,1},{5,0},{6,3},{7,2},{8,13},{9,12},{10,... | collective-permute-start | bytes 196616 | tf_op jit(solution)/shard_map/ppermute | solution.py:458
  31.2 9.1 %collective-permute-start.6 = (bf16[2,8,16,128]{3,2,1,0:T(8,128)(2,1)S(1)}, bf16[2,8,16,128]{3,2,1,0:T(8,128)(2,1)S(1)}, u32[]{:S(2)}, u32[]{:S(2)}) collective-permute-start(bf16[2,8,16,128]{3,2,1,0:T(8,128)(2,1)S(1)} %get-tuple-element.54), channel_id=1, source_target_pairs={{0,4},{1,5},{2,6},{3,7},{4,0},{5,1},{6,2},{7,3},{8,12},{9,13},{10,... | collective-permute-start | bytes 196616 | tf_op jit(solution)/shard_map/ppermute | solution.py:458
  33.0 7.3 %collective-permute-start.7 = (bf16[2,8,16,128]{3,2,1,0:T(8,128)(2,1)S(1)}, bf16[2,8,16,128]{3,2,1,0:T(8,128)(2,1)S(1)}, u32[]{:S(2)}, u32[]{:S(2)}) collective-permute-start(bf16[2,8,16,128]{3,2,1,0:T(8,128)(2,1)S(1)} %get-tuple-element.55), channel_id=1, source_target_pairs={{0,1},{1,0},{2,3},{3,2},{4,5},{5,4},{6,7},{7,6},{8,9},{9,8},{10,11... | collective-permute-start | bytes 196616 | tf_op jit(solution)/shard_map/ppermute | solution.py:458
  71.6 32.5 %all-to-all-start.3 = ((bf16[32,8,16,128]{3,2,1,0:T(8,128)(2,1)}), bf16[32,8,16,128]{3,2,1,0:T(8,128)(2,1)S(1)}, u32[]{:S(2)}, u32[]{:S(2)}) async-start(bf16[32,8,16,128]{3,2,1,0:T(8,128)(2,1)} %get-tuple-element.66), calls=%async_computation.3 | async-start | bytes 2097152 | tf_op jit(solution)/shard_map/all_to_all | solution.py:447
  75.4 1.6 %collective-permute-start.8 = (bf16[8,8,16,128]{3,2,1,0:T(8,128)(2,1)S(1)}, bf16[8,8,16,128]{3,2,1,0:T(8,128)(2,1)S(1)}, u32[]{:S(2)}, u32[]{:S(2)}) collective-permute-start(bf16[8,8,16,128]{3,2,1,0:T(8,128)(2,1)S(1)} %get-tuple-element.69), channel_id=1, source_target_pairs={{0,2},{1,3},{2,0},{3,1},{4,6},{5,7},{6,4},{7,5},{8,10},{9,11},{10,... | collective-permute-start | bytes 786440 | tf_op jit(solution)/shard_map/ppermute | solution.py:458
  77.0 27.1 %copy-start = (bf16[128,640]{1,0:T(8,128)(2,1)S(1)}, bf16[128,640]{1,0:T(8,128)(2,1)}, u32[]{:S(2)}) copy-start(bf16[128,640]{1,0:T(8,128)(2,1)} %w_ref.1) | copy-start | bytes 491524
  77.0 27.1 %copy-start.1 = (f32[128]{0:T(128)S(1)}, f32[128]{0:T(128)}, u32[]{:S(2)}) copy-start(f32[128]{0:T(128)} %param.10) | copy-start | bytes 1540
  77.0 17.7 %collective-permute-start.9 = (bf16[2,8,16,128]{3,2,1,0:T(8,128)(2,1)S(1)}, bf16[2,8,16,128]{3,2,1,0:T(8,128)(2,1)S(1)}, u32[]{:S(2)}, u32[]{:S(2)}) collective-permute-start(bf16[2,8,16,128]{3,2,1,0:T(8,128)(2,1)S(1)} %get-tuple-element.70), channel_id=1, source_target_pairs={{0,13},{1,12},{2,15},{3,14},{4,9},{5,8},{6,11},{7,10},{8,5},{9,4},... | collective-permute-start | bytes 196616 | tf_op jit(solution)/shard_map/ppermute | solution.py:458
  80.6 15.9 %collective-permute-start.10 = (bf16[2,8,16,128]{3,2,1,0:T(8,128)(2,1)S(1)}, bf16[2,8,16,128]{3,2,1,0:T(8,128)(2,1)S(1)}, u32[]{:S(2)}, u32[]{:S(2)}) collective-permute-start(bf16[2,8,16,128]{3,2,1,0:T(8,128)(2,1)S(1)} %get-tuple-element.71), channel_id=1, source_target_pairs={{0,12},{1,13},{2,14},{3,15},{4,8},{5,9},{6,10},{7,11},{8,4},{9,5},... | collective-permute-start | bytes 196616 | tf_op jit(solution)/shard_map/ppermute | solution.py:458
  81.2 22.8 %collective-permute-start.11 = (bf16[2,8,16,128]{3,2,1,0:T(8,128)(2,1)S(1)}, bf16[2,8,16,128]{3,2,1,0:T(8,128)(2,1)S(1)}, u32[]{:S(2)}, u32[]{:S(2)}) collective-permute-start(bf16[2,8,16,128]{3,2,1,0:T(8,128)(2,1)S(1)} %get-tuple-element.72), channel_id=1, source_target_pairs={{0,9},{1,8},{2,11},{3,10},{4,13},{5,12},{6,15},{7,14},{8,1},{9,0},... | collective-permute-start | bytes 196616 | tf_op jit(solution)/shard_map/ppermute | solution.py:458
  82.7 21.3 %collective-permute-start.12 = (bf16[2,8,16,128]{3,2,1,0:T(8,128)(2,1)S(1)}, bf16[2,8,16,128]{3,2,1,0:T(8,128)(2,1)S(1)}, u32[]{:S(2)}, u32[]{:S(2)}) collective-permute-start(bf16[2,8,16,128]{3,2,1,0:T(8,128)(2,1)S(1)} %get-tuple-element.73), channel_id=1, source_target_pairs={{0,8},{1,9},{2,10},{3,11},{4,12},{5,13},{6,14},{7,15},{8,0},{9,1},... | collective-permute-start | bytes 196616 | tf_op jit(solution)/shard_map/ppermute | solution.py:458
  82.9 21.1 %collective-permute-start.13 = (bf16[2,8,16,128]{3,2,1,0:T(8,128)(2,1)S(1)}, bf16[2,8,16,128]{3,2,1,0:T(8,128)(2,1)S(1)}, u32[]{:S(2)}, u32[]{:S(2)}) collective-permute-start(bf16[2,8,16,128]{3,2,1,0:T(8,128)(2,1)S(1)} %get-tuple-element.74), channel_id=1, source_target_pairs={{0,5},{1,4},{2,7},{3,6},{4,1},{5,0},{6,3},{7,2},{8,13},{9,12},{10,... | collective-permute-start | bytes 196616 | tf_op jit(solution)/shard_map/ppermute | solution.py:458
  94.7 9.3 %collective-permute-start.14 = (bf16[2,8,16,128]{3,2,1,0:T(8,128)(2,1)S(1)}, bf16[2,8,16,128]{3,2,1,0:T(8,128)(2,1)S(1)}, u32[]{:S(2)}, u32[]{:S(2)}) collective-permute-start(bf16[2,8,16,128]{3,2,1,0:T(8,128)(2,1)S(1)} %get-tuple-element.75), channel_id=1, source_target_pairs={{0,4},{1,5},{2,6},{3,7},{4,0},{5,1},{6,2},{7,3},{8,12},{9,13},{10,... | collective-permute-start | bytes 196616 | tf_op jit(solution)/shard_map/ppermute | solution.py:458
  96.5 7.5 %collective-permute-start.15 = (bf16[2,8,16,128]{3,2,1,0:T(8,128)(2,1)S(1)}, bf16[2,8,16,128]{3,2,1,0:T(8,128)(2,1)S(1)}, u32[]{:S(2)}, u32[]{:S(2)}) collective-permute-start(bf16[2,8,16,128]{3,2,1,0:T(8,128)(2,1)S(1)} %get-tuple-element.76), channel_id=1, source_target_pairs={{0,1},{1,0},{2,3},{3,2},{4,5},{5,4},{6,7},{7,6},{8,9},{9,8},{10,11... | collective-permute-start | bytes 196616 | tf_op jit(solution)/shard_map/ppermute | solution.py:458

commit v2 on v1

--- a/solution.py
+++ b/solution.py
@@ -426,7 +426,7 @@
         self.inside = [o * self.inner + n for n in range(self.inner) for o in range(outer // 2)]
         self.mate = n_ch
         self.hops = [s for s in range(self.half) if s & self.mate == 0]
-        self.hops[1:] = self.hops[:0:-1]
+        self.hops[3:] = self.hops[:2:-1]
         self.n_hops = len(self.hops) + 1
         self.all_place = self.place(self.order, n_row)
         self.half_place = self.place(self.inside, n_row // 2)

time: 110 us -> 101 us (0.918); the launches traced: 108 us -> 101 us
  blocking collectives: 28.1 us -> 24.6 us
  starting transfers between devices: 35.4 us -> 31.9 us
    all_to_all x2, waiting for transfers between devices: 0.01 us -> 9.47 us  [exchange_all(): lax.all_to_all(blocks, ('row', 'ch'), split_axis=0, concat_axis=0, tiled=...]
    ppermute x16, waiting for transfers between devices: 18.7 us -> 9.28 us  [swap(): lax.ppermute(block, ('row', 'ch'), [(n, n ^ s) for n in range(self.device...]
    ppermute x16, starting transfers between devices: 24.4 us -> 20.8 us  [swap(): lax.ppermute(block, ('row', 'ch'), [(n, n ^ s) for n in range(self.device...]
    all_to_all x2, blocking collectives: 28.1 us -> 24.6 us  [exchange_half(): lax.all_to_all(blocks, ('row', 'ch'), split_axis=0, concat_axis=0, tiled=...]
  transfers between devices with their start and end apart: 18 -> 18, of which waited for: 4 -> 8; matrix products, arithmetic and copies ran while one was open for 0% -> 0% of each run, Pallas kernels for 13% -> 14%
where the time goes in v2:
time: 101 us
  starting transfers between devices  31.9 us (32%)
  Pallas kernels  25.5 us (25%)
  blocking collectives  24.6 us (24%)
  waiting for transfers between devices  18.7 us (19%)
    pallas_call x10, Pallas kernels, call(): pl.pallas_call(kernel, out_shape=outs if single else tuple(outs), in_spec...  25.5 us
    all_to_all x2, blocking collectives, exchange_half(): lax.all_to_all(blocks, ('row', 'ch'), split_axis=0, concat_axis=0, tiled=...  24.6 us
    ppermute x16, starting transfers between devices, swap(): lax.ppermute(block, ('row', 'ch'), [(n, n ^ s) for n in range(self.device...  20.8 us
    all_to_all x2, starting transfers between devices, exchange_all(): lax.all_to_all(blocks, ('row', 'ch'), split_axis=0, concat_axis=0, tiled=...  11.1 us
    all_to_all x2, waiting for transfers between devices, exchange_all(): lax.all_to_all(blocks, ('row', 'ch'), split_axis=0, concat_axis=0, tiled=...  9.47 us
    ppermute x16, waiting for transfers between devices, swap(): lax.ppermute(block, ('row', 'ch'), [(n, n ^ s) for n in range(self.device...  9.28 us
  transfers between devices with their start and end apart: 18, of which 8 were waited for; matrix products, arithmetic and copies ran while one was open for 0% of the time, Pallas kernels for 14%

profile of v2, /device:TPU:0, one launch (start us, length us, event | category | flops | bytes accessed | tf_op | source)
XLA Modules:
  0.0 100.8 jit_solution(15833490908686841718)
XLA Ops:
  0.0 4.6 %shard_map.82 = (bf16[32,8,16,128]{3,2,1,0:T(8,128)(2,1)}, bf16[8,128,256]{2,1,0:T(8,128)(2,1)S(1)}) custom-call(bf16[16,128,128]{2,1,0:T(8,128)(2,1)} %refs_2_.1, f32[1,128]{1,0:T(1,128)} %bitcast.4, f32[1,128]{1,0:T(1,128)} %bitcast.8, bf16[128,640]{1,0:T(8,128)(2,1)} %w_ref.1), custom_call_target="tpu_custom_call" | custom-call | tf_op jit(solution)/shard_map/pallas_call | solution.py:52
  4.6 7.3 %all-to-all-start = ((bf16[32,8,16,128]{3,2,1,0:T(8,128)(2,1)}), bf16[32,8,16,128]{3,2,1,0:T(8,128)(2,1)S(1)}, u32[]{:S(2)}, u32[]{:S(2)}) async-start(bf16[32,8,16,128]{3,2,1,0:T(8,128)(2,1)} %get-tuple-element.41), calls=%async_computation | async-start | bytes 2097152 | tf_op jit(solution)/shard_map/all_to_all | solution.py:447
  11.9 2.2 %shard_map.84 = (bf16[8,8,16,128]{3,2,1,0:T(8,128)(2,1)S(1)}, bf16[8,8,16,128]{3,2,1,0:T(8,128)(2,1)S(1)}) custom-call(bf16[128,640]{1,0:T(8,128)(2,1)} %w_ref.1, bf16[8,128,256]{2,1,0:T(8,128)(2,1)S(1)} %get-tuple-element.46.n_ref), custom_call_target="tpu_custom_call" | custom-call | tf_op jit(solution)/shard_map/pallas_call | solution.py:52
  14.1 0.3 collective-permute-start
  14.4 1.3 %collective-permute-done.mates_ref.refs_1_ = bf16[8,8,16,128]{3,2,1,0:T(8,128)(2,1)S(1)} collective-permute-done((bf16[8,8,16,128]{3,2,1,0:T(8,128)(2,1)S(1)}, bf16[8,8,16,128]{3,2,1,0:T(8,128)(2,1)S(1)}, u32[]{:S(2)}, u32[]{:S(2)}) %collective-permute-start) | collective-permute-done | bytes 262176 | tf_op jit(solution)/shard_map/ppermute | solution.py:458
  15.7 1.8 %collective-permute-start.1 = (bf16[2,8,16,128]{3,2,1,0:T(8,128)(2,1)S(1)}, bf16[2,8,16,128]{3,2,1,0:T(8,128)(2,1)S(1)}, u32[]{:S(2)}, u32[]{:S(2)}) collective-permute-start(bf16[2,8,16,128]{3,2,1,0:T(8,128)(2,1)S(1)} %get-tuple-element.49), channel_id=1, source_target_pairs={{0,1},{1,0},{2,3},{3,2},{4,5},{5,4},{6,7},{7,6},{8,9},{9,8},{10,11... | collective-permute-start | bytes 196616 | tf_op jit(solution)/shard_map/ppermute | solution.py:458
  17.5 1.5 %collective-permute-start.2 = (bf16[2,8,16,128]{3,2,1,0:T(8,128)(2,1)S(1)}, bf16[2,8,16,128]{3,2,1,0:T(8,128)(2,1)S(1)}, u32[]{:S(2)}, u32[]{:S(2)}) collective-permute-start(bf16[2,8,16,128]{3,2,1,0:T(8,128)(2,1)S(1)} %get-tuple-element.50), channel_id=1, source_target_pairs={{0,4},{1,5},{2,6},{3,7},{4,0},{5,1},{6,2},{7,3},{8,12},{9,13},{10,... | collective-permute-start | bytes 196616 | tf_op jit(solution)/shard_map/ppermute | solution.py:458
  19.0 1.5 %collective-permute-start.3 = (bf16[2,8,16,128]{3,2,1,0:T(8,128)(2,1)S(1)}, bf16[2,8,16,128]{3,2,1,0:T(8,128)(2,1)S(1)}, u32[]{:S(2)}, u32[]{:S(2)}) collective-permute-start(bf16[2,8,16,128]{3,2,1,0:T(8,128)(2,1)S(1)} %get-tuple-element.51), channel_id=1, source_target_pairs={{0,13},{1,12},{2,15},{3,14},{4,9},{5,8},{6,11},{7,10},{8,5},{9,4},... | collective-permute-start | bytes 196616 | tf_op jit(solution)/shard_map/ppermute | solution.py:458
  20.5 1.5 %collective-permute-start.4 = (bf16[2,8,16,128]{3,2,1,0:T(8,128)(2,1)S(1)}, bf16[2,8,16,128]{3,2,1,0:T(8,128)(2,1)S(1)}, u32[]{:S(2)}, u32[]{:S(2)}) collective-permute-start(bf16[2,8,16,128]{3,2,1,0:T(8,128)(2,1)S(1)} %get-tuple-element.52), channel_id=1, source_target_pairs={{0,12},{1,13},{2,14},{3,15},{4,8},{5,9},{6,10},{7,11},{8,4},{9,5},... | collective-permute-start | bytes 196616 | tf_op jit(solution)/shard_map/ppermute | solution.py:458
  21.9 2.4 %collective-permute-start.5 = (bf16[2,8,16,128]{3,2,1,0:T(8,128)(2,1)S(1)}, bf16[2,8,16,128]{3,2,1,0:T(8,128)(2,1)S(1)}, u32[]{:S(2)}, u32[]{:S(2)}) collective-permute-start(bf16[2,8,16,128]{3,2,1,0:T(8,128)(2,1)S(1)} %get-tuple-element.53), channel_id=1, source_target_pairs={{0,9},{1,8},{2,11},{3,10},{4,13},{5,12},{6,15},{7,14},{8,1},{9,0},... | collective-permute-start | bytes 196616 | tf_op jit(solution)/shard_map/ppermute | solution.py:458
  24.3 0.0 collective-permute-done.1.refs_2_
  24.3 0.6 collective-permute-start.6
  24.9 0.0 collective-permute-done.2.refs_3_
  24.9 0.3 collective-permute-start.7
  25.1 5.7 %shard_map.83 = (f32[16,128,128]{2,1,0:T(8,128)S(1)}, bf16[16,512,128]{2,1,0:T(8,128)(2,1)}) custom-call(bf16[16,128,128]{2,1,0:T(8,128)(2,1)} %refs_2_.1, bf16[16,128,128]{2,1,0:T(8,128)(2,1)} %refs_3_.1, f32[1,128]{1,0:T(1,128)} %bitcast.5, f32[1,128]{1,0:T(1,128)} %bitcast.9, bf16[128,640]{1,0:T(8,128)(2,1)} %w_ref.1, f32[1,128]{1,0:T(1,128)} %bitcast.11, ...), custom_call_target="tpu_custom_call" | custom-call | tf_op jit(solution)/shard_map/pallas_call | solution.py:52
  30.9 7.8 %all-to-all-done.r_ref = bf16[32,8,16,128]{3,2,1,0:T(8,128)(2,1)S(1)} async-done(((bf16[32,8,16,128]{3,2,1,0:T(8,128)(2,1)}), bf16[32,8,16,128]{3,2,1,0:T(8,128)(2,1)S(1)}, u32[]{:S(2)}, u32[]{:S(2)}) %all-to-all-start) | async-done | bytes 1048608 | tf_op jit(solution)/shard_map/all_to_all | solution.py:447
  38.7 0.0 collective-permute-done.3.refs_4_
  38.7 0.0 collective-permute-done.4.refs_5_
  38.7 0.0 collective-permute-done.5.refs_6_
  38.7 0.0 collective-permute-done.6.refs_7_
  38.7 0.0 collective-permute-done.7.refs_8_
  38.7 0.5 shard_map.86
  39.2 12.3 %all_to_all.20.t_ref = bf16[16,8,16,128]{3,2,1,0:T(8,128)(2,1)S(1)} all-to-all(bf16[16,8,16,128]{3,2,1,0:T(8,128)(2,1)S(1)} %get-tuple-element.56), channel_id=1, replica_groups={{0,8,1,9,2,10,3,11,4,12,5,13,6,14,7,15},{16,24,17,25,18,26,19,27,20,28,..., dimensions={0} | all-to-all | bytes 1048576 | tf_op jit(solution)/shard_map/all_to_all | solution.py:453
  51.5 1.2 %shard_map.87 = (bf16[16,8,16,128]{3,2,1,0:T(8,128)(2,1)S(1)}, bf16[16,8,16,128]{3,2,1,0:T(8,128)(2,1)}) custom-call(bf16[16,8,16,128]{3,2,1,0:T(8,128)(2,1)S(1)} %all_to_all.20.t_ref, f32[16,128,128]{2,1,0:T(8,128)S(1)} %get-tuple-element.57.h_ref), custom_call_target="tpu_custom_call" | custom-call | tf_op jit(solution)/shard_map/pallas_call | solution.py:52
  52.7 12.3 %all_to_all.21.gt_ref = bf16[16,8,16,128]{3,2,1,0:T(8,128)(2,1)S(1)} all-to-all(bf16[16,8,16,128]{3,2,1,0:T(8,128)(2,1)S(1)} %get-tuple-element.64), channel_id=1, replica_groups={{0,8,1,9,2,10,3,11,4,12,5,13,6,14,7,15},{16,24,17,25,18,26,19,27,20,28,..., dimensions={0} | all-to-all | bytes 1048576 | tf_op jit(solution)/shard_map/all_to_all | solution.py:453
  65.0 1.3 %shard_map.89 = (bf16[32,8,16,128]{3,2,1,0:T(8,128)(2,1)}, bf16[8,8,16,128]{3,2,1,0:T(8,128)(2,1)S(1)}, bf16[8,8,16,128]{3,2,1,0:T(8,128)(2,1)S(1)}) custom-call(bf16[16,8,16,128]{3,2,1,0:T(8,128)(2,1)S(1)} %all_to_all.21.gt_ref, bf16[16,8,16,128]{3,2,1,0:T(8,128)(2,1)S(1)} %get-tuple-element.65.l_ref, bf16[32,8,16,128]{3,2,1,0:T(8,128)(2,1)S(1)} %all-to-all-done.r_ref), custom_call_target="tpu_custom_call" | custom-call | tf_op jit(solution)/shard_map/pallas_call | solution.py:52
  66.4 3.8 %all-to-all-start.3 = ((bf16[32,8,16,128]{3,2,1,0:T(8,128)(2,1)}), bf16[32,8,16,128]{3,2,1,0:T(8,128)(2,1)S(1)}, u32[]{:S(2)}, u32[]{:S(2)}) async-start(bf16[32,8,16,128]{3,2,1,0:T(8,128)(2,1)} %get-tuple-element.66), calls=%async_computation.3 | async-start | bytes 2097152 | tf_op jit(solution)/shard_map/all_to_all | solution.py:447
  70.2 0.3 collective-permute-start.8
  70.5 1.3 %collective-permute-done.8.mates_ref.refs_1_ = bf16[8,8,16,128]{3,2,1,0:T(8,128)(2,1)S(1)} collective-permute-done((bf16[8,8,16,128]{3,2,1,0:T(8,128)(2,1)S(1)}, bf16[8,8,16,128]{3,2,1,0:T(8,128)(2,1)S(1)}, u32[]{:S(2)}, u32[]{:S(2)}) %collective-permute-start.8) | collective-permute-done | bytes 262176 | tf_op jit(solution)/shard_map/ppermute | solution.py:458
  71.8 0.0 copy-start
  71.8 0.0 copy-start.1
  71.8 1.8 %collective-permute-start.9 = (bf16[2,8,16,128]{3,2,1,0:T(8,128)(2,1)S(1)}, bf16[2,8,16,128]{3,2,1,0:T(8,128)(2,1)S(1)}, u32[]{:S(2)}, u32[]{:S(2)}) collective-permute-start(bf16[2,8,16,128]{3,2,1,0:T(8,128)(2,1)S(1)} %get-tuple-element.70), channel_id=1, source_target_pairs={{0,1},{1,0},{2,3},{3,2},{4,5},{5,4},{6,7},{7,6},{8,9},{9,8},{10,11... | collective-permute-start | bytes 196616 | tf_op jit(solution)/shard_map/ppermute | solution.py:458
  73.6 1.5 %collective-permute-start.10 = (bf16[2,8,16,128]{3,2,1,0:T(8,128)(2,1)S(1)}, bf16[2,8,16,128]{3,2,1,0:T(8,128)(2,1)S(1)}, u32[]{:S(2)}, u32[]{:S(2)}) collective-permute-start(bf16[2,8,16,128]{3,2,1,0:T(8,128)(2,1)S(1)} %get-tuple-element.71), channel_id=1, source_target_pairs={{0,4},{1,5},{2,6},{3,7},{4,0},{5,1},{6,2},{7,3},{8,12},{9,13},{10,... | collective-permute-start | bytes 196616 | tf_op jit(solution)/shard_map/ppermute | solution.py:458
  75.1 1.5 %collective-permute-start.11 = (bf16[2,8,16,128]{3,2,1,0:T(8,128)(2,1)S(1)}, bf16[2,8,16,128]{3,2,1,0:T(8,128)(2,1)S(1)}, u32[]{:S(2)}, u32[]{:S(2)}) collective-permute-start(bf16[2,8,16,128]{3,2,1,0:T(8,128)(2,1)S(1)} %get-tuple-element.72), channel_id=1, source_target_pairs={{0,13},{1,12},{2,15},{3,14},{4,9},{5,8},{6,11},{7,10},{8,5},{9,4},... | collective-permute-start | bytes 196616 | tf_op jit(solution)/shard_map/ppermute | solution.py:458
  76.6 1.5 %collective-permute-start.12 = (bf16[2,8,16,128]{3,2,1,0:T(8,128)(2,1)S(1)}, bf16[2,8,16,128]{3,2,1,0:T(8,128)(2,1)S(1)}, u32[]{:S(2)}, u32[]{:S(2)}) collective-permute-start(bf16[2,8,16,128]{3,2,1,0:T(8,128)(2,1)S(1)} %get-tuple-element.73), channel_id=1, source_target_pairs={{0,12},{1,13},{2,14},{3,15},{4,8},{5,9},{6,10},{7,11},{8,4},{9,5},... | collective-permute-start | bytes 196616 | tf_op jit(solution)/shard_map/ppermute | solution.py:458
  78.0 2.4 %collective-permute-start.13 = (bf16[2,8,16,128]{3,2,1,0:T(8,128)(2,1)S(1)}, bf16[2,8,16,128]{3,2,1,0:T(8,128)(2,1)S(1)}, u32[]{:S(2)}, u32[]{:S(2)}) collective-permute-start(bf16[2,8,16,128]{3,2,1,0:T(8,128)(2,1)S(1)} %get-tuple-element.74), channel_id=1, source_target_pairs={{0,9},{1,8},{2,11},{3,10},{4,13},{5,12},{6,15},{7,14},{8,1},{9,0},... | collective-permute-start | bytes 196616 | tf_op jit(solution)/shard_map/ppermute | solution.py:458
  80.4 0.0 collective-permute-done.9.refs_2_
  80.4 0.6 collective-permute-start.14
  81.0 0.0 collective-permute-done.10.refs_3_
  81.0 1.6 %collective-permute-start.15 = (bf16[2,8,16,128]{3,2,1,0:T(8,128)(2,1)S(1)}, bf16[2,8,16,128]{3,2,1,0:T(8,128)(2,1)S(1)}, u32[]{:S(2)}, u32[]{:S(2)}) collective-permute-start(bf16[2,8,16,128]{3,2,1,0:T(8,128)(2,1)S(1)} %get-tuple-element.76), channel_id=1, source_target_pairs={{0,5},{1,4},{2,7},{3,6},{4,1},{5,0},{6,3},{7,2},{8,13},{9,12},{10,... | collective-permute-start | bytes 196616 | tf_op jit(solution)/shard_map/ppermute | solution.py:458
  82.6 6.0 %shard_map.88 = (f32[4,128,128]{2,1,0:T(8,128)S(1)}, bf16[4,128,128]{2,1,0:T(8,128)(2,1)S(1)}, bf16[4,512,128]{2,1,0:T(8,128)(2,1)S(1)}, f32[16,128,128]{2,1,0:T...) custom-call(bf16[16,512,128]{2,1,0:T(8,128)(2,1)} %get-tuple-element.44.refs_0_.fac_hbm, ...), custom_call_target="tpu_custom_call" | custom-call | tf_op jit(solution)/shard_map/pallas_call | solution.py:52
  88.6 0.9 collective-permute-done.11.refs_4_
  89.5 1.6 %collective-permute-done.12.refs_5_ = bf16[2,8,16,128]{3,2,1,0:T(8,128)(2,1)S(1)} collective-permute-done((bf16[2,8,16,128]{3,2,1,0:T(8,128)(2,1)S(1)}, bf16[2,8,16,128]{3,2,1,0:T(8,128)(2,1)S(1)}, u32[]{:S(2)}, u32[]{:S(2)}) %collective-permute-start.12) | collective-permute-done | bytes 65568 | tf_op jit(solution)/shard_map/ppermute | solution.py:458
  91.1 2.8 %collective-permute-done.13.refs_6_ = bf16[2,8,16,128]{3,2,1,0:T(8,128)(2,1)S(1)} collective-permute-done((bf16[2,8,16,128]{3,2,1,0:T(8,128)(2,1)S(1)}, bf16[2,8,16,128]{3,2,1,0:T(8,128)(2,1)S(1)}, u32[]{:S(2)}, u32[]{:S(2)}) %collective-permute-start.13) | collective-permute-done | bytes 65568 | tf_op jit(solution)/shard_map/ppermute | solution.py:458
  94.0 1.3 %collective-permute-done.14.refs_7_ = bf16[2,8,16,128]{3,2,1,0:T(8,128)(2,1)S(1)} collective-permute-done((bf16[2,8,16,128]{3,2,1,0:T(8,128)(2,1)S(1)}, bf16[2,8,16,128]{3,2,1,0:T(8,128)(2,1)S(1)}, u32[]{:S(2)}, u32[]{:S(2)}) %collective-permute-start.14) | collective-permute-done | bytes 65568 | tf_op jit(solution)/shard_map/ppermute | solution.py:458
  95.3 0.0 collective-permute-done.15.refs_8_
  95.3 1.7 %all-to-all-done.3.r_ref = bf16[32,8,16,128]{3,2,1,0:T(8,128)(2,1)S(1)} async-done(((bf16[32,8,16,128]{3,2,1,0:T(8,128)(2,1)}), bf16[32,8,16,128]{3,2,1,0:T(8,128)(2,1)S(1)}, u32[]{:S(2)}, u32[]{:S(2)}) %all-to-all-start.3) | async-done | bytes 1048608 | tf_op jit(solution)/shard_map/all_to_all | solution.py:447
  97.0 0.0 copy-done
  97.0 0.0 copy-done.1
  97.0 3.9 %shard_map.91 = bf16[16,128,128]{2,1,0:T(8,128)(2,1)} custom-call(bf16[16,512,128]{2,1,0:T(8,128)(2,1)} %get-tuple-element.44.refs_0_.fac_hbm, bf16[16,128,128]{2,1,0:T(8,128)(2,1)} %get-tuple-element.59.nt_hbm, f32[16,128,128]{2,1,0:T(8,128)} %get-tuple-element.60.gin_hbm, bf16[4,512,128]{2,1,0:T(8,128)(2,1)S(1)} %get-tuple-element.61.fac0_ref, ...), custom_call_target="tpu_custom_call" | custom-call | tf_op jit(solution)/shard_map/pallas_call | solution.py:52
  (2 shorter events, 0.1 us)
Async XLA Ops:
  4.6 34.1 %all-to-all-start = ((bf16[32,8,16,128]{3,2,1,0:T(8,128)(2,1)}), bf16[32,8,16,128]{3,2,1,0:T(8,128)(2,1)S(1)}, u32[]{:S(2)}, u32[]{:S(2)}) async-start(bf16[32,8,16,128]{3,2,1,0:T(8,128)(2,1)} %get-tuple-element.41), calls=%async_computation | async-start | bytes 2097152 | tf_op jit(solution)/shard_map/all_to_all | solution.py:447
  14.1 1.6 %collective-permute-start = (bf16[8,8,16,128]{3,2,1,0:T(8,128)(2,1)S(1)}, bf16[8,8,16,128]{3,2,1,0:T(8,128)(2,1)S(1)}, u32[]{:S(2)}, u32[]{:S(2)}) collective-permute-start(bf16[8,8,16,128]{3,2,1,0:T(8,128)(2,1)S(1)} %get-tuple-element.48), channel_id=1, source_target_pairs={{0,2},{1,3},{2,0},{3,1},{4,6},{5,7},{6,4},{7,5},{8,10},{9,11},{10,... | collective-permute-start | bytes 786440 | tf_op jit(solution)/shard_map/ppermute | solution.py:458
  15.7 8.6 %collective-permute-start.1 = (bf16[2,8,16,128]{3,2,1,0:T(8,128)(2,1)S(1)}, bf16[2,8,16,128]{3,2,1,0:T(8,128)(2,1)S(1)}, u32[]{:S(2)}, u32[]{:S(2)}) collective-permute-start(bf16[2,8,16,128]{3,2,1,0:T(8,128)(2,1)S(1)} %get-tuple-element.49), channel_id=1, source_target_pairs={{0,1},{1,0},{2,3},{3,2},{4,5},{5,4},{6,7},{7,6},{8,9},{9,8},{10,11... | collective-permute-start | bytes 196616 | tf_op jit(solution)/shard_map/ppermute | solution.py:458
  17.5 7.3 %collective-permute-start.2 = (bf16[2,8,16,128]{3,2,1,0:T(8,128)(2,1)S(1)}, bf16[2,8,16,128]{3,2,1,0:T(8,128)(2,1)S(1)}, u32[]{:S(2)}, u32[]{:S(2)}) collective-permute-start(bf16[2,8,16,128]{3,2,1,0:T(8,128)(2,1)S(1)} %get-tuple-element.50), channel_id=1, source_target_pairs={{0,4},{1,5},{2,6},{3,7},{4,0},{5,1},{6,2},{7,3},{8,12},{9,13},{10,... | collective-permute-start | bytes 196616 | tf_op jit(solution)/shard_map/ppermute | solution.py:458
  19.0 19.7 %collective-permute-start.3 = (bf16[2,8,16,128]{3,2,1,0:T(8,128)(2,1)S(1)}, bf16[2,8,16,128]{3,2,1,0:T(8,128)(2,1)S(1)}, u32[]{:S(2)}, u32[]{:S(2)}) collective-permute-start(bf16[2,8,16,128]{3,2,1,0:T(8,128)(2,1)S(1)} %get-tuple-element.51), channel_id=1, source_target_pairs={{0,13},{1,12},{2,15},{3,14},{4,9},{5,8},{6,11},{7,10},{8,5},{9,4},... | collective-permute-start | bytes 196616 | tf_op jit(solution)/shard_map/ppermute | solution.py:458
  20.5 18.2 %collective-permute-start.4 = (bf16[2,8,16,128]{3,2,1,0:T(8,128)(2,1)S(1)}, bf16[2,8,16,128]{3,2,1,0:T(8,128)(2,1)S(1)}, u32[]{:S(2)}, u32[]{:S(2)}) collective-permute-start(bf16[2,8,16,128]{3,2,1,0:T(8,128)(2,1)S(1)} %get-tuple-element.52), channel_id=1, source_target_pairs={{0,12},{1,13},{2,14},{3,15},{4,8},{5,9},{6,10},{7,11},{8,4},{9,5},... | collective-permute-start | bytes 196616 | tf_op jit(solution)/shard_map/ppermute | solution.py:458
  21.9 16.7 %collective-permute-start.5 = (bf16[2,8,16,128]{3,2,1,0:T(8,128)(2,1)S(1)}, bf16[2,8,16,128]{3,2,1,0:T(8,128)(2,1)S(1)}, u32[]{:S(2)}, u32[]{:S(2)}) collective-permute-start(bf16[2,8,16,128]{3,2,1,0:T(8,128)(2,1)S(1)} %get-tuple-element.53), channel_id=1, source_target_pairs={{0,9},{1,8},{2,11},{3,10},{4,13},{5,12},{6,15},{7,14},{8,1},{9,0},... | collective-permute-start | bytes 196616 | tf_op jit(solution)/shard_map/ppermute | solution.py:458
  24.3 14.4 %collective-permute-start.6 = (bf16[2,8,16,128]{3,2,1,0:T(8,128)(2,1)S(1)}, bf16[2,8,16,128]{3,2,1,0:T(8,128)(2,1)S(1)}, u32[]{:S(2)}, u32[]{:S(2)}) collective-permute-start(bf16[2,8,16,128]{3,2,1,0:T(8,128)(2,1)S(1)} %get-tuple-element.54), channel_id=1, source_target_pairs={{0,8},{1,9},{2,10},{3,11},{4,12},{5,13},{6,14},{7,15},{8,0},{9,1},... | collective-permute-start | bytes 196616 | tf_op jit(solution)/shard_map/ppermute | solution.py:458
  24.9 13.8 %collective-permute-start.7 = (bf16[2,8,16,128]{3,2,1,0:T(8,128)(2,1)S(1)}, bf16[2,8,16,128]{3,2,1,0:T(8,128)(2,1)S(1)}, u32[]{:S(2)}, u32[]{:S(2)}) collective-permute-start(bf16[2,8,16,128]{3,2,1,0:T(8,128)(2,1)S(1)} %get-tuple-element.55), channel_id=1, source_target_pairs={{0,5},{1,4},{2,7},{3,6},{4,1},{5,0},{6,3},{7,2},{8,13},{9,12},{10,... | collective-permute-start | bytes 196616 | tf_op jit(solution)/shard_map/ppermute | solution.py:458
  66.4 30.6 %all-to-all-start.3 = ((bf16[32,8,16,128]{3,2,1,0:T(8,128)(2,1)}), bf16[32,8,16,128]{3,2,1,0:T(8,128)(2,1)S(1)}, u32[]{:S(2)}, u32[]{:S(2)}) async-start(bf16[32,8,16,128]{3,2,1,0:T(8,128)(2,1)} %get-tuple-element.66), calls=%async_computation.3 | async-start | bytes 2097152 | tf_op jit(solution)/shard_map/all_to_all | solution.py:447
  70.2 1.6 %collective-permute-start.8 = (bf16[8,8,16,128]{3,2,1,0:T(8,128)(2,1)S(1)}, bf16[8,8,16,128]{3,2,1,0:T(8,128)(2,1)S(1)}, u32[]{:S(2)}, u32[]{:S(2)}) collective-permute-start(bf16[8,8,16,128]{3,2,1,0:T(8,128)(2,1)S(1)} %get-tuple-element.69), channel_id=1, source_target_pairs={{0,2},{1,3},{2,0},{3,1},{4,6},{5,7},{6,4},{7,5},{8,10},{9,11},{10,... | collective-permute-start | bytes 786440 | tf_op jit(solution)/shard_map/ppermute | solution.py:458
  71.8 25.2 %copy-start = (bf16[128,640]{1,0:T(8,128)(2,1)S(1)}, bf16[128,640]{1,0:T(8,128)(2,1)}, u32[]{:S(2)}) copy-start(bf16[128,640]{1,0:T(8,128)(2,1)} %w_ref.1) | copy-start | bytes 491524
  71.8 25.2 %copy-start.1 = (f32[128]{0:T(128)S(1)}, f32[128]{0:T(128)}, u32[]{:S(2)}) copy-start(f32[128]{0:T(128)} %param.10) | copy-start | bytes 1540
  71.8 8.6 %collective-permute-start.9 = (bf16[2,8,16,128]{3,2,1,0:T(8,128)(2,1)S(1)}, bf16[2,8,16,128]{3,2,1,0:T(8,128)(2,1)S(1)}, u32[]{:S(2)}, u32[]{:S(2)}) collective-permute-start(bf16[2,8,16,128]{3,2,1,0:T(8,128)(2,1)S(1)} %get-tuple-element.70), channel_id=1, source_target_pairs={{0,1},{1,0},{2,3},{3,2},{4,5},{5,4},{6,7},{7,6},{8,9},{9,8},{10,11... | collective-permute-start | bytes 196616 | tf_op jit(solution)/shard_map/ppermute | solution.py:458
  73.6 7.4 %collective-permute-start.10 = (bf16[2,8,16,128]{3,2,1,0:T(8,128)(2,1)S(1)}, bf16[2,8,16,128]{3,2,1,0:T(8,128)(2,1)S(1)}, u32[]{:S(2)}, u32[]{:S(2)}) collective-permute-start(bf16[2,8,16,128]{3,2,1,0:T(8,128)(2,1)S(1)} %get-tuple-element.71), channel_id=1, source_target_pairs={{0,4},{1,5},{2,6},{3,7},{4,0},{5,1},{6,2},{7,3},{8,12},{9,13},{10,... | collective-permute-start | bytes 196616 | tf_op jit(solution)/shard_map/ppermute | solution.py:458
  75.1 14.4 %collective-permute-start.11 = (bf16[2,8,16,128]{3,2,1,0:T(8,128)(2,1)S(1)}, bf16[2,8,16,128]{3,2,1,0:T(8,128)(2,1)S(1)}, u32[]{:S(2)}, u32[]{:S(2)}) collective-permute-start(bf16[2,8,16,128]{3,2,1,0:T(8,128)(2,1)S(1)} %get-tuple-element.72), channel_id=1, source_target_pairs={{0,13},{1,12},{2,15},{3,14},{4,9},{5,8},{6,11},{7,10},{8,5},{9,4},... | collective-permute-start | bytes 196616 | tf_op jit(solution)/shard_map/ppermute | solution.py:458
  76.6 14.5 %collective-permute-start.12 = (bf16[2,8,16,128]{3,2,1,0:T(8,128)(2,1)S(1)}, bf16[2,8,16,128]{3,2,1,0:T(8,128)(2,1)S(1)}, u32[]{:S(2)}, u32[]{:S(2)}) collective-permute-start(bf16[2,8,16,128]{3,2,1,0:T(8,128)(2,1)S(1)} %get-tuple-element.73), channel_id=1, source_target_pairs={{0,12},{1,13},{2,14},{3,15},{4,8},{5,9},{6,10},{7,11},{8,4},{9,5},... | collective-permute-start | bytes 196616 | tf_op jit(solution)/shard_map/ppermute | solution.py:458
  78.0 15.9 %collective-permute-start.13 = (bf16[2,8,16,128]{3,2,1,0:T(8,128)(2,1)S(1)}, bf16[2,8,16,128]{3,2,1,0:T(8,128)(2,1)S(1)}, u32[]{:S(2)}, u32[]{:S(2)}) collective-permute-start(bf16[2,8,16,128]{3,2,1,0:T(8,128)(2,1)S(1)} %get-tuple-element.74), channel_id=1, source_target_pairs={{0,9},{1,8},{2,11},{3,10},{4,13},{5,12},{6,15},{7,14},{8,1},{9,0},... | collective-permute-start | bytes 196616 | tf_op jit(solution)/shard_map/ppermute | solution.py:458
  80.4 14.9 %collective-permute-start.14 = (bf16[2,8,16,128]{3,2,1,0:T(8,128)(2,1)S(1)}, bf16[2,8,16,128]{3,2,1,0:T(8,128)(2,1)S(1)}, u32[]{:S(2)}, u32[]{:S(2)}) collective-permute-start(bf16[2,8,16,128]{3,2,1,0:T(8,128)(2,1)S(1)} %get-tuple-element.75), channel_id=1, source_target_pairs={{0,8},{1,9},{2,10},{3,11},{4,12},{5,13},{6,14},{7,15},{8,0},{9,1},... | collective-permute-start | bytes 196616 | tf_op jit(solution)/shard_map/ppermute | solution.py:458
  81.0 14.3 %collective-permute-start.15 = (bf16[2,8,16,128]{3,2,1,0:T(8,128)(2,1)S(1)}, bf16[2,8,16,128]{3,2,1,0:T(8,128)(2,1)S(1)}, u32[]{:S(2)}, u32[]{:S(2)}) collective-permute-start(bf16[2,8,16,128]{3,2,1,0:T(8,128)(2,1)S(1)} %get-tuple-element.76), channel_id=1, source_target_pairs={{0,5},{1,4},{2,7},{3,6},{4,1},{5,0},{6,3},{7,2},{8,13},{9,12},{10,... | collective-permute-start | bytes 196616 | tf_op jit(solution)/shard_map/ppermute | solution.py:458

commit v3 on v2

--- a/solution.py
+++ b/solution.py
@@ -14,6 +14,7 @@
 UNROLL = 4
 BLOCK = 256
 PARTS = 4
+INSIDE_16 = (0, 11, 4, 13, 2, 14, 1, 8, 7, 9, 6, 10, 5, 12, 3, 15)
 
 
 def dot(a, b, da, db):
@@ -129,9 +130,9 @@
         fetch(p).wait()
         for n in range(0, size, 2):
             i = p * size + n
-            x = dot(eye, x_ref[pl.ds(i, 2)].reshape(2 * cols, width), 1, 1)
-            normed, _s = normalize(x, 0)
-            n_ref[p * size // 2 + n // 2] = (normed * gain + bias).astype(BF16)
+            shifted = dot(center, x_ref[pl.ds(i, 2)].reshape(2 * cols, width), 1, 1)
+            scale_inv = lax.rsqrt(jnp.mean(shifted * shifted, axis=0, keepdims=True) + EPSILON)
+            n_ref[p * size // 2 + n // 2] = (shifted * scale_inv * gain + bias).astype(BF16)
 
     def project(p):
         for n in range(0, size, 2):
@@ -146,7 +147,7 @@
         project(p - 1)
         return 0
 
-    eye = identity(width)
+    center = (identity(width).astype(F32) - 1.0 / width).astype(BF16)
     for copy in small:
         copy.wait()
     gain = column(gain_ref[...], 2 * cols)
@@ -165,7 +166,7 @@
             right_ref[to] = right.reshape(group // mine, mine, rows, cols)
             for share in range(to.start, to.stop):
                 for n, device in enumerate(lay.order):
-                    if lay.inside.index(device % lay.half) == share:
+                    if device % lay.half == share:
                         out.append(pltpu.make_async_copy(right_ref.at[share], r_hbm.at[n], out_sems.at[n]))
                         out[-1].start()
     for copy in out:
@@ -198,8 +199,8 @@
         for (to, _here), left in zip(pair, swapped(swap, [l_ref[:, here] for _to, here in pair])):
             left_ref[to] = left.reshape(group // mine, mine, rows, cols)
     for n, s in enumerate(lay.hops):
-        mine_out[n] = left_ref[lay.share(s)]
-        mate_out[n] = left_ref[lay.share(s ^ lay.mate)]
+        mine_out[n] = left_ref[lay.other(s)]
+        mate_out[n] = left_ref[lay.other(s ^ lay.mate)]
 
 
 def gate_kernel(*refs):
@@ -255,7 +256,7 @@
     ]
 
 
-def to_rows(t_ref, ts_ref):
+def to_rows(lay, t_ref, ts_ref):
     rows, width, cols = ts_ref.shape
     mine = t_ref.shape[1]
     group = BLOCK // rows
@@ -263,18 +264,18 @@
     blocks = places(width, mine, rows)
     for n in range(0, len(blocks), 2):
         pair = blocks[n : n + 2]
-        for (_to, here), block in zip(pair, swapped(swap, [t_ref[to] for to, _here in pair])):
+        for (_to, here), block in zip(pair, swapped(swap, [lay.shares(t_ref, to) for to, _here in pair])):
             ts_ref[:, here] = block.reshape(rows, group, cols)
 
 
-def tri_back_kernel(t_ref, h_ref, gt_ref, t_hbm, ts_ref, gs_ref, sem):
+def tri_back_kernel(lay, t_ref, h_ref, gt_ref, t_hbm, ts_ref, gs_ref, sem):
     rows, width, cols = h_ref.shape
     mine = t_ref.shape[1]
     group = BLOCK // rows
     copy = pltpu.make_async_copy(t_ref, t_hbm, sem)
     copy.start()
     back = permutation(group, rows)
-    to_rows(t_ref, ts_ref)
+    to_rows(lay, t_ref, ts_ref)
 
     def body(i, _):
         tri, h = ts_ref[i].astype(F32), h_ref[i]
@@ -290,11 +291,13 @@
     for n in range(0, len(blocks), 2):
         pair = blocks[n : n + 2]
         for (to, _here), block in zip(pair, swapped(back, [gs_ref[:, here] for _to, here in pair])):
-            gt_ref[to] = block.reshape(group // mine, mine, rows, cols)
+            block = block.reshape(group // mine, mine, rows, cols)
+            for share in range(to.start, to.stop):
+                gt_ref[lay.inside.index(share)] = block[share - to.start]
     copy.wait()
 
 
-def logit_kernel(*refs):
+def logit_kernel(lay, *refs):
     (fac_hbm, *sources), refs = refs[:10], refs[10:]
     (gin0_ref, nt0_ref, fac0_ref, gin_hbm, nt_hbm, s_ref), refs = refs[:6], refs[6:]
     (ts_ref, gin_ref, nt_ref, out_sems), targets, sems = refs[:4], refs[4:13], refs[13]
@@ -302,7 +305,7 @@
     rows, cols, width = x_ref.shape
     first = pl.ds(0, nt0_ref.shape[0])
     fetched([*sources, fac_hbm.at[first]], [*targets, fac0_ref], sems)
-    to_rows(t_ref, ts_ref)
+    to_rows(lay, t_ref, ts_ref)
     ogain = column(ogain_ref[...], cols)
     obias = column(obias_ref[...], cols)
 
@@ -362,14 +365,14 @@
     group = BLOCK // rows
     swap = permutation(rows, group)
     for s, source in lay.received(l_refs):
-        l_ref[lay.share(s)] = source[...]
+        l_ref[lay.other(s)] = source[...]
     for to, here in places(width, mine, rows):
         sums = []
         for share in range(to.start, to.stop):
             one, two = (
                 r_ref[n].astype(F32)
                 for n, device in enumerate(lay.order)
-                if lay.inside.index(device % lay.half) == share
+                if device % lay.half == share
             )
             sums.append((one + two).astype(BF16))
         left, right = swapped(swap, [l_ref[to], jnp.stack(sums)])
@@ -424,6 +427,8 @@
         self.inner = self.devices // outer
         self.order = [o * self.inner + n for n in range(self.inner) for o in range(outer)]
         self.inside = [o * self.inner + n for n in range(self.inner) for o in range(outer // 2)]
+        if self.half == len(INSIDE_16):
+            self.inside = list(INSIDE_16)
         self.mate = n_ch
         self.hops = [s for s in range(self.half) if s & self.mate == 0]
         self.hops[3:] = self.hops[:2:-1]
@@ -435,13 +440,12 @@
     def place(self, order, n_row):
         return [[order.index(r * self.n_ch + b) for b in range(self.n_ch)] for r in range(n_row)]
 
+    def shares(self, ref, here):
+        return jnp.stack([ref[self.inside.index(share)] for share in range(here.start, here.stop)])
+
     def other(self, s):
         me = lax.axis_index("row") * self.n_ch + lax.axis_index("ch")
         return jnp.bitwise_xor(lax.rem(me, self.half), s)
-
-    def share(self, s):
-        other = self.other(s)
-        return lax.rem(other, self.inner) * (self.half // self.inner) + lax.div(other, self.inner)
 
     def exchange_all(self, blocks):
         return lax.all_to_all(
@@ -555,7 +559,7 @@
             both_turned,
             half,
             one_here,
-            pltpu.SemaphoreType.DMA((4 + PARTS,)),
+            pltpu.SemaphoreType.DMA((4 + PARTS // 2,)),
             pltpu.SemaphoreType.DMA((lay.devices,)),
         ],
         pair_act,
@@ -603,7 +607,7 @@
     tri, left = call(functools.partial(tri_kernel, lay), [one, one], [], right, *left)
     tri = lay.exchange_half(tri)
     grad_tri, tri = call(
-        tri_back_kernel,
+        functools.partial(tri_back_kernel, lay),
         [one, pltpu.HBM(one.shape, BF16)],
         [half, half, pltpu.SemaphoreType.DMA(())],
         tri,
@@ -620,7 +624,7 @@
     grad_right = lay.exchange_all(grad_right)
     grad_left = lay.permute(*grad_left)
     grad_in_first, normed_first, fac_first, grad_in, normed_t, scale = call(
-        logit_kernel,
+        functools.partial(logit_kernel, lay),
         [
             pltpu.VMEM((rows // PARTS, width, cols), F32),
             pltpu.VMEM((rows // PARTS, width, cols), BF16),
@@ -778,6 +782,8 @@
             and group % (width // (devices // 2)) == 0
             and width % (2 * group) == 0
             and cols % 128 == 0
+            and width <= 256
+            and width & (width - 1) == 0
         ):
             return by_channel(n_row, n_ch, *args)
         return by_row(*args)

time: 101 us -> 101 us (level)
  blocking collectives: 24.6 us -> 26.1 us
  Pallas kernels: 25.5 us -> 24.4 us
    all_to_all x2, blocking collectives: 24.6 us -> 26.1 us  [exchange_half(): lax.all_to_all(blocks, ('row', 'ch'), split_axis=0, concat_axis=0, tiled=...]
    pallas_call x10, Pallas kernels: 25.5 us -> 24.4 us  [call(): pl.pallas_call(kernel, out_shape=outs if single else tuple(outs), in_spec...]
where the time goes in v3:
time: 101 us; the launch traced here: 100 us
  starting transfers between devices  31 us (31%)
  blocking collectives  26.1 us (26%)
  Pallas kernels  24.4 us (24%)
  waiting for transfers between devices  18.7 us (19%)
    all_to_all x2, blocking collectives, exchange_half(): lax.all_to_all(blocks, ('row', 'ch'), split_axis=0, concat_axis=0, tiled=...  26.1 us
    pallas_call x10, Pallas kernels, call(): pl.pallas_call(kernel, out_shape=outs if single else tuple(outs), in_spec...  24.4 us
    ppermute x16, starting transfers between devices, swap(): lax.ppermute(block, ('row', 'ch'), [(n, n ^ s) for n in range(self.device...  20.8 us
    all_to_all x2, starting transfers between devices, exchange_all(): lax.all_to_all(blocks, ('row', 'ch'), split_axis=0, concat_axis=0, tiled=...  10.2 us
    all_to_all x2, waiting for transfers between devices, exchange_all(): lax.all_to_all(blocks, ('row', 'ch'), split_axis=0, concat_axis=0, tiled=...  9.47 us
    ppermute x16, waiting for transfers between devices, swap(): lax.ppermute(block, ('row', 'ch'), [(n, n ^ s) for n in range(self.device...  9.28 us
  transfers between devices with their start and end apart: 18, of which 8 were waited for; matrix products, arithmetic and copies ran while one was open for 0% of the time, Pallas kernels for 14%

profile of v3, /device:TPU:0, one launch (start us, length us, event | category | flops | bytes accessed | tf_op | source)
XLA Modules:
  0.0 100.3 jit_solution(12832329425863354822)
XLA Ops:
  0.0 3.4 %shard_map.82 = (bf16[32,8,16,128]{3,2,1,0:T(8,128)(2,1)}, bf16[8,128,256]{2,1,0:T(8,128)(2,1)S(1)}) custom-call(bf16[16,128,128]{2,1,0:T(8,128)(2,1)} %refs_2_.1, f32[1,128]{1,0:T(1,128)} %bitcast.4, f32[1,128]{1,0:T(1,128)} %bitcast.8, bf16[128,640]{1,0:T(8,128)(2,1)} %w_ref.1), custom_call_target="tpu_custom_call" | custom-call | tf_op jit(solution)/shard_map/pallas_call | solution.py:53
  3.4 7.3 %all-to-all-start = ((bf16[32,8,16,128]{3,2,1,0:T(8,128)(2,1)}), bf16[32,8,16,128]{3,2,1,0:T(8,128)(2,1)S(1)}, u32[]{:S(2)}, u32[]{:S(2)}) async-start(bf16[32,8,16,128]{3,2,1,0:T(8,128)(2,1)} %get-tuple-element.41), calls=%async_computation | async-start | bytes 2097152 | tf_op jit(solution)/shard_map/all_to_all | solution.py:451
  10.8 2.2 %shard_map.84 = (bf16[8,8,16,128]{3,2,1,0:T(8,128)(2,1)S(1)}, bf16[8,8,16,128]{3,2,1,0:T(8,128)(2,1)S(1)}) custom-call(bf16[128,640]{1,0:T(8,128)(2,1)} %w_ref.1, bf16[8,128,256]{2,1,0:T(8,128)(2,1)S(1)} %get-tuple-element.46.n_ref), custom_call_target="tpu_custom_call" | custom-call | tf_op jit(solution)/shard_map/pallas_call | solution.py:53
  12.9 0.3 collective-permute-start
  13.3 1.3 %collective-permute-done.mates_ref.refs_1_ = bf16[8,8,16,128]{3,2,1,0:T(8,128)(2,1)S(1)} collective-permute-done((bf16[8,8,16,128]{3,2,1,0:T(8,128)(2,1)S(1)}, bf16[8,8,16,128]{3,2,1,0:T(8,128)(2,1)S(1)}, u32[]{:S(2)}, u32[]{:S(2)}) %collective-permute-start) | collective-permute-done | bytes 262176 | tf_op jit(solution)/shard_map/ppermute | solution.py:462
  14.6 1.8 %collective-permute-start.1 = (bf16[2,8,16,128]{3,2,1,0:T(8,128)(2,1)S(1)}, bf16[2,8,16,128]{3,2,1,0:T(8,128)(2,1)S(1)}, u32[]{:S(2)}, u32[]{:S(2)}) collective-permute-start(bf16[2,8,16,128]{3,2,1,0:T(8,128)(2,1)S(1)} %get-tuple-element.49), channel_id=1, source_target_pairs={{0,1},{1,0},{2,3},{3,2},{4,5},{5,4},{6,7},{7,6},{8,9},{9,8},{10,11... | collective-permute-start | bytes 196616 | tf_op jit(solution)/shard_map/ppermute | solution.py:462
  16.4 1.5 %collective-permute-start.2 = (bf16[2,8,16,128]{3,2,1,0:T(8,128)(2,1)S(1)}, bf16[2,8,16,128]{3,2,1,0:T(8,128)(2,1)S(1)}, u32[]{:S(2)}, u32[]{:S(2)}) collective-permute-start(bf16[2,8,16,128]{3,2,1,0:T(8,128)(2,1)S(1)} %get-tuple-element.50), channel_id=1, source_target_pairs={{0,4},{1,5},{2,6},{3,7},{4,0},{5,1},{6,2},{7,3},{8,12},{9,13},{10,... | collective-permute-start | bytes 196616 | tf_op jit(solution)/shard_map/ppermute | solution.py:462
  17.9 1.5 %collective-permute-start.3 = (bf16[2,8,16,128]{3,2,1,0:T(8,128)(2,1)S(1)}, bf16[2,8,16,128]{3,2,1,0:T(8,128)(2,1)S(1)}, u32[]{:S(2)}, u32[]{:S(2)}) collective-permute-start(bf16[2,8,16,128]{3,2,1,0:T(8,128)(2,1)S(1)} %get-tuple-element.51), channel_id=1, source_target_pairs={{0,13},{1,12},{2,15},{3,14},{4,9},{5,8},{6,11},{7,10},{8,5},{9,4},... | collective-permute-start | bytes 196616 | tf_op jit(solution)/shard_map/ppermute | solution.py:462
  19.3 1.5 %collective-permute-start.4 = (bf16[2,8,16,128]{3,2,1,0:T(8,128)(2,1)S(1)}, bf16[2,8,16,128]{3,2,1,0:T(8,128)(2,1)S(1)}, u32[]{:S(2)}, u32[]{:S(2)}) collective-permute-start(bf16[2,8,16,128]{3,2,1,0:T(8,128)(2,1)S(1)} %get-tuple-element.52), channel_id=1, source_target_pairs={{0,12},{1,13},{2,14},{3,15},{4,8},{5,9},{6,10},{7,11},{8,4},{9,5},... | collective-permute-start | bytes 196616 | tf_op jit(solution)/shard_map/ppermute | solution.py:462
  20.8 2.4 %collective-permute-start.5 = (bf16[2,8,16,128]{3,2,1,0:T(8,128)(2,1)S(1)}, bf16[2,8,16,128]{3,2,1,0:T(8,128)(2,1)S(1)}, u32[]{:S(2)}, u32[]{:S(2)}) collective-permute-start(bf16[2,8,16,128]{3,2,1,0:T(8,128)(2,1)S(1)} %get-tuple-element.53), channel_id=1, source_target_pairs={{0,9},{1,8},{2,11},{3,10},{4,13},{5,12},{6,15},{7,14},{8,1},{9,0},... | collective-permute-start | bytes 196616 | tf_op jit(solution)/shard_map/ppermute | solution.py:462
  23.2 0.0 collective-permute-done.1.refs_2_
  23.2 0.6 collective-permute-start.6
  23.7 0.0 collective-permute-done.2.refs_3_
  23.7 0.3 collective-permute-start.7
  24.0 5.7 %shard_map.83 = (f32[16,128,128]{2,1,0:T(8,128)S(1)}, bf16[16,512,128]{2,1,0:T(8,128)(2,1)}) custom-call(bf16[16,128,128]{2,1,0:T(8,128)(2,1)} %refs_2_.1, bf16[16,128,128]{2,1,0:T(8,128)(2,1)} %refs_3_.1, f32[1,128]{1,0:T(1,128)} %bitcast.5, f32[1,128]{1,0:T(1,128)} %bitcast.9, bf16[128,640]{1,0:T(8,128)(2,1)} %w_ref.1, f32[1,128]{1,0:T(1,128)} %bitcast.11, ...), custom_call_target="tpu_custom_call" | custom-call | tf_op jit(solution)/shard_map/pallas_call | solution.py:53
  29.7 7.8 %all-to-all-done.r_ref = bf16[32,8,16,128]{3,2,1,0:T(8,128)(2,1)S(1)} async-done(((bf16[32,8,16,128]{3,2,1,0:T(8,128)(2,1)}), bf16[32,8,16,128]{3,2,1,0:T(8,128)(2,1)S(1)}, u32[]{:S(2)}, u32[]{:S(2)}) %all-to-all-start) | async-done | bytes 1048608 | tf_op jit(solution)/shard_map/all_to_all | solution.py:451
  37.5 0.0 collective-permute-done.3.refs_4_
  37.5 0.0 collective-permute-done.4.refs_5_
  37.6 0.0 collective-permute-done.5.refs_6_
  37.6 0.0 collective-permute-done.6.refs_7_
  37.6 0.0 collective-permute-done.7.refs_8_
  37.6 0.5 shard_map.86
  38.1 13.2 %all_to_all.20.t_ref = bf16[16,8,16,128]{3,2,1,0:T(8,128)(2,1)S(1)} all-to-all(bf16[16,8,16,128]{3,2,1,0:T(8,128)(2,1)S(1)} %get-tuple-element.56), channel_id=1, replica_groups={{0,11,4,13,2,14,1,8,7,9,6,10,5,12,3,15},{16,27,20,29,18,30,17,24,23,25,..., dimensions={0} | all-to-all | bytes 1048576 | tf_op jit(solution)/shard_map/all_to_all | solution.py:457
  51.3 1.2 %shard_map.87 = (bf16[16,8,16,128]{3,2,1,0:T(8,128)(2,1)S(1)}, bf16[16,8,16,128]{3,2,1,0:T(8,128)(2,1)}) custom-call(bf16[16,8,16,128]{3,2,1,0:T(8,128)(2,1)S(1)} %all_to_all.20.t_ref, f32[16,128,128]{2,1,0:T(8,128)S(1)} %get-tuple-element.57.h_ref), custom_call_target="tpu_custom_call" | custom-call | tf_op jit(solution)/shard_map/pallas_call | solution.py:53
  52.5 12.8 %all_to_all.21.gt_ref = bf16[16,8,16,128]{3,2,1,0:T(8,128)(2,1)S(1)} all-to-all(bf16[16,8,16,128]{3,2,1,0:T(8,128)(2,1)S(1)} %get-tuple-element.64), channel_id=1, replica_groups={{0,11,4,13,2,14,1,8,7,9,6,10,5,12,3,15},{16,27,20,29,18,30,17,24,23,25,..., dimensions={0} | all-to-all | bytes 1048576 | tf_op jit(solution)/shard_map/all_to_all | solution.py:457
  65.4 1.3 %shard_map.89 = (bf16[32,8,16,128]{3,2,1,0:T(8,128)(2,1)}, bf16[8,8,16,128]{3,2,1,0:T(8,128)(2,1)S(1)}, bf16[8,8,16,128]{3,2,1,0:T(8,128)(2,1)S(1)}) custom-call(bf16[16,8,16,128]{3,2,1,0:T(8,128)(2,1)S(1)} %all_to_all.21.gt_ref, bf16[16,8,16,128]{3,2,1,0:T(8,128)(2,1)S(1)} %get-tuple-element.65.l_ref, bf16[32,8,16,128]{3,2,1,0:T(8,128)(2,1)S(1)} %all-to-all-done.r_ref), custom_call_target="tpu_custom_call" | custom-call | tf_op jit(solution)/shard_map/pallas_call | solution.py:53
  66.7 2.9 %all-to-all-start.3 = ((bf16[32,8,16,128]{3,2,1,0:T(8,128)(2,1)}), bf16[32,8,16,128]{3,2,1,0:T(8,128)(2,1)S(1)}, u32[]{:S(2)}, u32[]{:S(2)}) async-start(bf16[32,8,16,128]{3,2,1,0:T(8,128)(2,1)} %get-tuple-element.66), calls=%async_computation.3 | async-start | bytes 2097152 | tf_op jit(solution)/shard_map/all_to_all | solution.py:451
  69.6 0.3 collective-permute-start.8
  69.9 1.3 %collective-permute-done.8.mates_ref.refs_1_ = bf16[8,8,16,128]{3,2,1,0:T(8,128)(2,1)S(1)} collective-permute-done((bf16[8,8,16,128]{3,2,1,0:T(8,128)(2,1)S(1)}, bf16[8,8,16,128]{3,2,1,0:T(8,128)(2,1)S(1)}, u32[]{:S(2)}, u32[]{:S(2)}) %collective-permute-start.8) | collective-permute-done | bytes 262176 | tf_op jit(solution)/shard_map/ppermute | solution.py:462
  71.2 0.0 copy-start
  71.2 0.0 copy-start.1
  71.3 1.8 %collective-permute-start.9 = (bf16[2,8,16,128]{3,2,1,0:T(8,128)(2,1)S(1)}, bf16[2,8,16,128]{3,2,1,0:T(8,128)(2,1)S(1)}, u32[]{:S(2)}, u32[]{:S(2)}) collective-permute-start(bf16[2,8,16,128]{3,2,1,0:T(8,128)(2,1)S(1)} %get-tuple-element.70), channel_id=1, source_target_pairs={{0,1},{1,0},{2,3},{3,2},{4,5},{5,4},{6,7},{7,6},{8,9},{9,8},{10,11... | collective-permute-start | bytes 196616 | tf_op jit(solution)/shard_map/ppermute | solution.py:462
  73.1 1.5 %collective-permute-start.10 = (bf16[2,8,16,128]{3,2,1,0:T(8,128)(2,1)S(1)}, bf16[2,8,16,128]{3,2,1,0:T(8,128)(2,1)S(1)}, u32[]{:S(2)}, u32[]{:S(2)}) collective-permute-start(bf16[2,8,16,128]{3,2,1,0:T(8,128)(2,1)S(1)} %get-tuple-element.71), channel_id=1, source_target_pairs={{0,4},{1,5},{2,6},{3,7},{4,0},{5,1},{6,2},{7,3},{8,12},{9,13},{10,... | collective-permute-start | bytes 196616 | tf_op jit(solution)/shard_map/ppermute | solution.py:462
  74.6 1.5 %collective-permute-start.11 = (bf16[2,8,16,128]{3,2,1,0:T(8,128)(2,1)S(1)}, bf16[2,8,16,128]{3,2,1,0:T(8,128)(2,1)S(1)}, u32[]{:S(2)}, u32[]{:S(2)}) collective-permute-start(bf16[2,8,16,128]{3,2,1,0:T(8,128)(2,1)S(1)} %get-tuple-element.72), channel_id=1, source_target_pairs={{0,13},{1,12},{2,15},{3,14},{4,9},{5,8},{6,11},{7,10},{8,5},{9,4},... | collective-permute-start | bytes 196616 | tf_op jit(solution)/shard_map/ppermute | solution.py:462
  76.0 1.5 %collective-permute-start.12 = (bf16[2,8,16,128]{3,2,1,0:T(8,128)(2,1)S(1)}, bf16[2,8,16,128]{3,2,1,0:T(8,128)(2,1)S(1)}, u32[]{:S(2)}, u32[]{:S(2)}) collective-permute-start(bf16[2,8,16,128]{3,2,1,0:T(8,128)(2,1)S(1)} %get-tuple-element.73), channel_id=1, source_target_pairs={{0,12},{1,13},{2,14},{3,15},{4,8},{5,9},{6,10},{7,11},{8,4},{9,5},... | collective-permute-start | bytes 196616 | tf_op jit(solution)/shard_map/ppermute | solution.py:462
  77.5 2.4 %collective-permute-start.13 = (bf16[2,8,16,128]{3,2,1,0:T(8,128)(2,1)S(1)}, bf16[2,8,16,128]{3,2,1,0:T(8,128)(2,1)S(1)}, u32[]{:S(2)}, u32[]{:S(2)}) collective-permute-start(bf16[2,8,16,128]{3,2,1,0:T(8,128)(2,1)S(1)} %get-tuple-element.74), channel_id=1, source_target_pairs={{0,9},{1,8},{2,11},{3,10},{4,13},{5,12},{6,15},{7,14},{8,1},{9,0},... | collective-permute-start | bytes 196616 | tf_op jit(solution)/shard_map/ppermute | solution.py:462
  79.9 0.0 collective-permute-done.9.refs_2_
  79.9 0.6 collective-permute-start.14
  80.5 0.0 collective-permute-done.10.refs_3_
  80.5 1.6 %collective-permute-start.15 = (bf16[2,8,16,128]{3,2,1,0:T(8,128)(2,1)S(1)}, bf16[2,8,16,128]{3,2,1,0:T(8,128)(2,1)S(1)}, u32[]{:S(2)}, u32[]{:S(2)}) collective-permute-start(bf16[2,8,16,128]{3,2,1,0:T(8,128)(2,1)S(1)} %get-tuple-element.76), channel_id=1, source_target_pairs={{0,5},{1,4},{2,7},{3,6},{4,1},{5,0},{6,3},{7,2},{8,13},{9,12},{10,... | collective-permute-start | bytes 196616 | tf_op jit(solution)/shard_map/ppermute | solution.py:462
  82.0 6.0 %shard_map.88 = (f32[4,128,128]{2,1,0:T(8,128)S(1)}, bf16[4,128,128]{2,1,0:T(8,128)(2,1)S(1)}, bf16[4,512,128]{2,1,0:T(8,128)(2,1)S(1)}, f32[16,128,128]{2,1,0:T...) custom-call(bf16[16,512,128]{2,1,0:T(8,128)(2,1)} %get-tuple-element.44.refs_0_.fac_hbm, ...), custom_call_target="tpu_custom_call" | custom-call | tf_op jit(solution)/shard_map/pallas_call | solution.py:53
  88.1 0.9 collective-permute-done.11.refs_4_
  89.0 1.6 %collective-permute-done.12.refs_5_ = bf16[2,8,16,128]{3,2,1,0:T(8,128)(2,1)S(1)} collective-permute-done((bf16[2,8,16,128]{3,2,1,0:T(8,128)(2,1)S(1)}, bf16[2,8,16,128]{3,2,1,0:T(8,128)(2,1)S(1)}, u32[]{:S(2)}, u32[]{:S(2)}) %collective-permute-start.12) | collective-permute-done | bytes 65568 | tf_op jit(solution)/shard_map/ppermute | solution.py:462
  90.6 2.8 %collective-permute-done.13.refs_6_ = bf16[2,8,16,128]{3,2,1,0:T(8,128)(2,1)S(1)} collective-permute-done((bf16[2,8,16,128]{3,2,1,0:T(8,128)(2,1)S(1)}, bf16[2,8,16,128]{3,2,1,0:T(8,128)(2,1)S(1)}, u32[]{:S(2)}, u32[]{:S(2)}) %collective-permute-start.13) | collective-permute-done | bytes 65568 | tf_op jit(solution)/shard_map/ppermute | solution.py:462
  93.4 1.3 %collective-permute-done.14.refs_7_ = bf16[2,8,16,128]{3,2,1,0:T(8,128)(2,1)S(1)} collective-permute-done((bf16[2,8,16,128]{3,2,1,0:T(8,128)(2,1)S(1)}, bf16[2,8,16,128]{3,2,1,0:T(8,128)(2,1)S(1)}, u32[]{:S(2)}, u32[]{:S(2)}) %collective-permute-start.14) | collective-permute-done | bytes 65568 | tf_op jit(solution)/shard_map/ppermute | solution.py:462
  94.7 0.0 collective-permute-done.15.refs_8_
  94.7 1.7 %all-to-all-done.3.r_ref = bf16[32,8,16,128]{3,2,1,0:T(8,128)(2,1)S(1)} async-done(((bf16[32,8,16,128]{3,2,1,0:T(8,128)(2,1)}), bf16[32,8,16,128]{3,2,1,0:T(8,128)(2,1)S(1)}, u32[]{:S(2)}, u32[]{:S(2)}) %all-to-all-start.3) | async-done | bytes 1048608 | tf_op jit(solution)/shard_map/all_to_all | solution.py:451
  96.4 0.0 copy-done
  96.4 0.0 copy-done.1
  96.4 3.9 %shard_map.91 = bf16[16,128,128]{2,1,0:T(8,128)(2,1)} custom-call(bf16[16,512,128]{2,1,0:T(8,128)(2,1)} %get-tuple-element.44.refs_0_.fac_hbm, bf16[16,128,128]{2,1,0:T(8,128)(2,1)} %get-tuple-element.59.nt_hbm, f32[16,128,128]{2,1,0:T(8,128)} %get-tuple-element.60.gin_hbm, bf16[4,512,128]{2,1,0:T(8,128)(2,1)S(1)} %get-tuple-element.61.fac0_ref, ...), custom_call_target="tpu_custom_call" | custom-call | tf_op jit(solution)/shard_map/pallas_call | solution.py:53
  (2 shorter events, 0.1 us)
Async XLA Ops:
  3.4 34.1 %all-to-all-start = ((bf16[32,8,16,128]{3,2,1,0:T(8,128)(2,1)}), bf16[32,8,16,128]{3,2,1,0:T(8,128)(2,1)S(1)}, u32[]{:S(2)}, u32[]{:S(2)}) async-start(bf16[32,8,16,128]{3,2,1,0:T(8,128)(2,1)} %get-tuple-element.41), calls=%async_computation | async-start | bytes 2097152 | tf_op jit(solution)/shard_map/all_to_all | solution.py:451
  12.9 1.6 %collective-permute-start = (bf16[8,8,16,128]{3,2,1,0:T(8,128)(2,1)S(1)}, bf16[8,8,16,128]{3,2,1,0:T(8,128)(2,1)S(1)}, u32[]{:S(2)}, u32[]{:S(2)}) collective-permute-start(bf16[8,8,16,128]{3,2,1,0:T(8,128)(2,1)S(1)} %get-tuple-element.48), channel_id=1, source_target_pairs={{0,2},{1,3},{2,0},{3,1},{4,6},{5,7},{6,4},{7,5},{8,10},{9,11},{10,... | collective-permute-start | bytes 786440 | tf_op jit(solution)/shard_map/ppermute | solution.py:462
  14.6 8.6 %collective-permute-start.1 = (bf16[2,8,16,128]{3,2,1,0:T(8,128)(2,1)S(1)}, bf16[2,8,16,128]{3,2,1,0:T(8,128)(2,1)S(1)}, u32[]{:S(2)}, u32[]{:S(2)}) collective-permute-start(bf16[2,8,16,128]{3,2,1,0:T(8,128)(2,1)S(1)} %get-tuple-element.49), channel_id=1, source_target_pairs={{0,1},{1,0},{2,3},{3,2},{4,5},{5,4},{6,7},{7,6},{8,9},{9,8},{10,11... | collective-permute-start | bytes 196616 | tf_op jit(solution)/shard_map/ppermute | solution.py:462
  16.4 7.3 %collective-permute-start.2 = (bf16[2,8,16,128]{3,2,1,0:T(8,128)(2,1)S(1)}, bf16[2,8,16,128]{3,2,1,0:T(8,128)(2,1)S(1)}, u32[]{:S(2)}, u32[]{:S(2)}) collective-permute-start(bf16[2,8,16,128]{3,2,1,0:T(8,128)(2,1)S(1)} %get-tuple-element.50), channel_id=1, source_target_pairs={{0,4},{1,5},{2,6},{3,7},{4,0},{5,1},{6,2},{7,3},{8,12},{9,13},{10,... | collective-permute-start | bytes 196616 | tf_op jit(solution)/shard_map/ppermute | solution.py:462
  17.9 19.7 %collective-permute-start.3 = (bf16[2,8,16,128]{3,2,1,0:T(8,128)(2,1)S(1)}, bf16[2,8,16,128]{3,2,1,0:T(8,128)(2,1)S(1)}, u32[]{:S(2)}, u32[]{:S(2)}) collective-permute-start(bf16[2,8,16,128]{3,2,1,0:T(8,128)(2,1)S(1)} %get-tuple-element.51), channel_id=1, source_target_pairs={{0,13},{1,12},{2,15},{3,14},{4,9},{5,8},{6,11},{7,10},{8,5},{9,4},... | collective-permute-start | bytes 196616 | tf_op jit(solution)/shard_map/ppermute | solution.py:462
  19.3 18.2 %collective-permute-start.4 = (bf16[2,8,16,128]{3,2,1,0:T(8,128)(2,1)S(1)}, bf16[2,8,16,128]{3,2,1,0:T(8,128)(2,1)S(1)}, u32[]{:S(2)}, u32[]{:S(2)}) collective-permute-start(bf16[2,8,16,128]{3,2,1,0:T(8,128)(2,1)S(1)} %get-tuple-element.52), channel_id=1, source_target_pairs={{0,12},{1,13},{2,14},{3,15},{4,8},{5,9},{6,10},{7,11},{8,4},{9,5},... | collective-permute-start | bytes 196616 | tf_op jit(solution)/shard_map/ppermute | solution.py:462
  20.8 16.7 %collective-permute-start.5 = (bf16[2,8,16,128]{3,2,1,0:T(8,128)(2,1)S(1)}, bf16[2,8,16,128]{3,2,1,0:T(8,128)(2,1)S(1)}, u32[]{:S(2)}, u32[]{:S(2)}) collective-permute-start(bf16[2,8,16,128]{3,2,1,0:T(8,128)(2,1)S(1)} %get-tuple-element.53), channel_id=1, source_target_pairs={{0,9},{1,8},{2,11},{3,10},{4,13},{5,12},{6,15},{7,14},{8,1},{9,0},... | collective-permute-start | bytes 196616 | tf_op jit(solution)/shard_map/ppermute | solution.py:462
  23.2 14.4 %collective-permute-start.6 = (bf16[2,8,16,128]{3,2,1,0:T(8,128)(2,1)S(1)}, bf16[2,8,16,128]{3,2,1,0:T(8,128)(2,1)S(1)}, u32[]{:S(2)}, u32[]{:S(2)}) collective-permute-start(bf16[2,8,16,128]{3,2,1,0:T(8,128)(2,1)S(1)} %get-tuple-element.54), channel_id=1, source_target_pairs={{0,8},{1,9},{2,10},{3,11},{4,12},{5,13},{6,14},{7,15},{8,0},{9,1},... | collective-permute-start | bytes 196616 | tf_op jit(solution)/shard_map/ppermute | solution.py:462
  23.7 13.8 %collective-permute-start.7 = (bf16[2,8,16,128]{3,2,1,0:T(8,128)(2,1)S(1)}, bf16[2,8,16,128]{3,2,1,0:T(8,128)(2,1)S(1)}, u32[]{:S(2)}, u32[]{:S(2)}) collective-permute-start(bf16[2,8,16,128]{3,2,1,0:T(8,128)(2,1)S(1)} %get-tuple-element.55), channel_id=1, source_target_pairs={{0,5},{1,4},{2,7},{3,6},{4,1},{5,0},{6,3},{7,2},{8,13},{9,12},{10,... | collective-permute-start | bytes 196616 | tf_op jit(solution)/shard_map/ppermute | solution.py:462
  66.7 29.7 %all-to-all-start.3 = ((bf16[32,8,16,128]{3,2,1,0:T(8,128)(2,1)}), bf16[32,8,16,128]{3,2,1,0:T(8,128)(2,1)S(1)}, u32[]{:S(2)}, u32[]{:S(2)}) async-start(bf16[32,8,16,128]{3,2,1,0:T(8,128)(2,1)} %get-tuple-element.66), calls=%async_computation.3 | async-start | bytes 2097152 | tf_op jit(solution)/shard_map/all_to_all | solution.py:451
  69.6 1.6 %collective-permute-start.8 = (bf16[8,8,16,128]{3,2,1,0:T(8,128)(2,1)S(1)}, bf16[8,8,16,128]{3,2,1,0:T(8,128)(2,1)S(1)}, u32[]{:S(2)}, u32[]{:S(2)}) collective-permute-start(bf16[8,8,16,128]{3,2,1,0:T(8,128)(2,1)S(1)} %get-tuple-element.69), channel_id=1, source_target_pairs={{0,2},{1,3},{2,0},{3,1},{4,6},{5,7},{6,4},{7,5},{8,10},{9,11},{10,... | collective-permute-start | bytes 786440 | tf_op jit(solution)/shard_map/ppermute | solution.py:462
  71.2 25.2 %copy-start = (bf16[128,640]{1,0:T(8,128)(2,1)S(1)}, bf16[128,640]{1,0:T(8,128)(2,1)}, u32[]{:S(2)}) copy-start(bf16[128,640]{1,0:T(8,128)(2,1)} %w_ref.1) | copy-start | bytes 491524
  71.2 25.2 %copy-start.1 = (f32[128]{0:T(128)S(1)}, f32[128]{0:T(128)}, u32[]{:S(2)}) copy-start(f32[128]{0:T(128)} %param.10) | copy-start | bytes 1540
  71.3 8.6 %collective-permute-start.9 = (bf16[2,8,16,128]{3,2,1,0:T(8,128)(2,1)S(1)}, bf16[2,8,16,128]{3,2,1,0:T(8,128)(2,1)S(1)}, u32[]{:S(2)}, u32[]{:S(2)}) collective-permute-start(bf16[2,8,16,128]{3,2,1,0:T(8,128)(2,1)S(1)} %get-tuple-element.70), channel_id=1, source_target_pairs={{0,1},{1,0},{2,3},{3,2},{4,5},{5,4},{6,7},{7,6},{8,9},{9,8},{10,11... | collective-permute-start | bytes 196616 | tf_op jit(solution)/shard_map/ppermute | solution.py:462
  73.1 7.4 %collective-permute-start.10 = (bf16[2,8,16,128]{3,2,1,0:T(8,128)(2,1)S(1)}, bf16[2,8,16,128]{3,2,1,0:T(8,128)(2,1)S(1)}, u32[]{:S(2)}, u32[]{:S(2)}) collective-permute-start(bf16[2,8,16,128]{3,2,1,0:T(8,128)(2,1)S(1)} %get-tuple-element.71), channel_id=1, source_target_pairs={{0,4},{1,5},{2,6},{3,7},{4,0},{5,1},{6,2},{7,3},{8,12},{9,13},{10,... | collective-permute-start | bytes 196616 | tf_op jit(solution)/shard_map/ppermute | solution.py:462
  74.6 14.4 %collective-permute-start.11 = (bf16[2,8,16,128]{3,2,1,0:T(8,128)(2,1)S(1)}, bf16[2,8,16,128]{3,2,1,0:T(8,128)(2,1)S(1)}, u32[]{:S(2)}, u32[]{:S(2)}) collective-permute-start(bf16[2,8,16,128]{3,2,1,0:T(8,128)(2,1)S(1)} %get-tuple-element.72), channel_id=1, source_target_pairs={{0,13},{1,12},{2,15},{3,14},{4,9},{5,8},{6,11},{7,10},{8,5},{9,4},... | collective-permute-start | bytes 196616 | tf_op jit(solution)/shard_map/ppermute | solution.py:462
  76.0 14.5 %collective-permute-start.12 = (bf16[2,8,16,128]{3,2,1,0:T(8,128)(2,1)S(1)}, bf16[2,8,16,128]{3,2,1,0:T(8,128)(2,1)S(1)}, u32[]{:S(2)}, u32[]{:S(2)}) collective-permute-start(bf16[2,8,16,128]{3,2,1,0:T(8,128)(2,1)S(1)} %get-tuple-element.73), channel_id=1, source_target_pairs={{0,12},{1,13},{2,14},{3,15},{4,8},{5,9},{6,10},{7,11},{8,4},{9,5},... | collective-permute-start | bytes 196616 | tf_op jit(solution)/shard_map/ppermute | solution.py:462
  77.5 15.9 %collective-permute-start.13 = (bf16[2,8,16,128]{3,2,1,0:T(8,128)(2,1)S(1)}, bf16[2,8,16,128]{3,2,1,0:T(8,128)(2,1)S(1)}, u32[]{:S(2)}, u32[]{:S(2)}) collective-permute-start(bf16[2,8,16,128]{3,2,1,0:T(8,128)(2,1)S(1)} %get-tuple-element.74), channel_id=1, source_target_pairs={{0,9},{1,8},{2,11},{3,10},{4,13},{5,12},{6,15},{7,14},{8,1},{9,0},... | collective-permute-start | bytes 196616 | tf_op jit(solution)/shard_map/ppermute | solution.py:462
  79.9 14.9 %collective-permute-start.14 = (bf16[2,8,16,128]{3,2,1,0:T(8,128)(2,1)S(1)}, bf16[2,8,16,128]{3,2,1,0:T(8,128)(2,1)S(1)}, u32[]{:S(2)}, u32[]{:S(2)}) collective-permute-start(bf16[2,8,16,128]{3,2,1,0:T(8,128)(2,1)S(1)} %get-tuple-element.75), channel_id=1, source_target_pairs={{0,8},{1,9},{2,10},{3,11},{4,12},{5,13},{6,14},{7,15},{8,0},{9,1},... | collective-permute-start | bytes 196616 | tf_op jit(solution)/shard_map/ppermute | solution.py:462
  80.5 14.3 %collective-permute-start.15 = (bf16[2,8,16,128]{3,2,1,0:T(8,128)(2,1)S(1)}, bf16[2,8,16,128]{3,2,1,0:T(8,128)(2,1)S(1)}, u32[]{:S(2)}, u32[]{:S(2)}) collective-permute-start(bf16[2,8,16,128]{3,2,1,0:T(8,128)(2,1)S(1)} %get-tuple-element.76), channel_id=1, source_target_pairs={{0,5},{1,4},{2,7},{3,6},{4,1},{5,0},{6,3},{7,2},{8,13},{9,12},{10,... | collective-permute-start | bytes 196616 | tf_op jit(solution)/shard_map/ppermute | solution.py:462

commit v4 on v3

--- a/solution.py
+++ b/solution.py
@@ -14,7 +14,6 @@
 UNROLL = 4
 BLOCK = 256
 PARTS = 4
-INSIDE_16 = (0, 11, 4, 13, 2, 14, 1, 8, 7, 9, 6, 10, 5, 12, 3, 15)
 
 
 def dot(a, b, da, db):
@@ -286,7 +285,7 @@
         gs_ref[i] = (tri_inv * (h - first - shifted * (both * tri_inv * tri_inv))).astype(BF16)
         return 0
 
-    lax.fori_loop(0, rows, body, 0, unroll=UNROLL)
+    lax.fori_loop(0, rows, body, 0, unroll=2 * UNROLL)
     blocks = places(width, mine, rows)
     for n in range(0, len(blocks), 2):
         pair = blocks[n : n + 2]
@@ -404,16 +403,14 @@
                 result = norm_back(grad, normed, scale_inv, 0).astype(BF16)
                 out_ref[i + m] = dot(eye, result, 1, 1).astype(BF16)
 
-    def body(p, _):
+    part(0, fac0_ref, nt0_ref, gin0_ref)
+    send(0).start()
+    for p in range(1, parts):
         for copy in fetch(p):
             copy.wait()
+    for p in range(1, parts):
         part(p, fac_ref, nt_ref, gin_ref)
         send(p).start()
-        return 0
-
-    part(0, fac0_ref, nt0_ref, gin0_ref)
-    send(0).start()
-    lax.fori_loop(1, parts, body, 0)
     for p in range(parts):
         send(p).wait()
 
@@ -427,8 +424,6 @@
         self.inner = self.devices // outer
         self.order = [o * self.inner + n for n in range(self.inner) for o in range(outer)]
         self.inside = [o * self.inner + n for n in range(self.inner) for o in range(outer // 2)]
-        if self.half == len(INSIDE_16):
-            self.inside = list(INSIDE_16)
         self.mate = n_ch
         self.hops = [s for s in range(self.half) if s & self.mate == 0]
         self.hops[3:] = self.hops[:2:-1]

time: 101 us -> 100 us (0.990)
  blocking collectives: 26.1 us -> 24.6 us
    all_to_all x2, blocking collectives: 26.1 us -> 24.6 us  [exchange_half(): lax.all_to_all(blocks, ('row', 'ch'), split_axis=0, concat_axis=0, tiled=...]
where the time goes in v4:
time: 100 us; the launch traced here: 99.7 us
  starting transfers between devices  31.9 us (32%)
  blocking collectives  24.6 us (25%)
  Pallas kernels  24.3 us (24%)
  waiting for transfers between devices  18.8 us (19%)
    all_to_all x2, blocking collectives, exchange_half(): lax.all_to_all(blocks, ('row', 'ch'), split_axis=0, concat_axis=0, tiled=...  24.6 us
    pallas_call x10, Pallas kernels, call(): pl.pallas_call(kernel, out_shape=outs if single else tuple(outs), in_spec...  24.3 us
    ppermute x16, starting transfers between devices, swap(): lax.ppermute(block, ('row', 'ch'), [(n, n ^ s) for n in range(self.device...  20.8 us
    all_to_all x2, starting transfers between devices, exchange_all(): lax.all_to_all(blocks, ('row', 'ch'), split_axis=0, concat_axis=0, tiled=...  11.1 us
    all_to_all x2, waiting for transfers between devices, exchange_all(): lax.all_to_all(blocks, ('row', 'ch'), split_axis=0, concat_axis=0, tiled=...  9.47 us
    ppermute x16, waiting for transfers between devices, swap(): lax.ppermute(block, ('row', 'ch'), [(n, n ^ s) for n in range(self.device...  9.28 us
  transfers between devices with their start and end apart: 18, of which 8 were waited for; matrix products, arithmetic and copies ran while one was open for 0% of the time, Pallas kernels for 14%

profile of v4, /device:TPU:0, one launch (start us, length us, event | category | flops | bytes accessed | tf_op | source)
XLA Modules:
  0.0 99.7 jit_solution(13968650128076031154)
XLA Ops:
  0.0 3.4 %shard_map.82 = (bf16[32,8,16,128]{3,2,1,0:T(8,128)(2,1)}, bf16[8,128,256]{2,1,0:T(8,128)(2,1)S(1)}) custom-call(bf16[16,128,128]{2,1,0:T(8,128)(2,1)} %refs_2_.1, f32[1,128]{1,0:T(1,128)} %bitcast.4, f32[1,128]{1,0:T(1,128)} %bitcast.8, bf16[128,640]{1,0:T(8,128)(2,1)} %w_ref.1), custom_call_target="tpu_custom_call" | custom-call | tf_op jit(solution)/shard_map/pallas_call | solution.py:52
  3.4 7.3 %all-to-all-start = ((bf16[32,8,16,128]{3,2,1,0:T(8,128)(2,1)}), bf16[32,8,16,128]{3,2,1,0:T(8,128)(2,1)S(1)}, u32[]{:S(2)}, u32[]{:S(2)}) async-start(bf16[32,8,16,128]{3,2,1,0:T(8,128)(2,1)} %get-tuple-element.41), calls=%async_computation | async-start | bytes 2097152 | tf_op jit(solution)/shard_map/all_to_all | solution.py:446
  10.8 2.2 %shard_map.84 = (bf16[8,8,16,128]{3,2,1,0:T(8,128)(2,1)S(1)}, bf16[8,8,16,128]{3,2,1,0:T(8,128)(2,1)S(1)}) custom-call(bf16[128,640]{1,0:T(8,128)(2,1)} %w_ref.1, bf16[8,128,256]{2,1,0:T(8,128)(2,1)S(1)} %get-tuple-element.46.n_ref), custom_call_target="tpu_custom_call" | custom-call | tf_op jit(solution)/shard_map/pallas_call | solution.py:52
  12.9 0.3 collective-permute-start
  13.3 1.3 %collective-permute-done.mates_ref.refs_1_ = bf16[8,8,16,128]{3,2,1,0:T(8,128)(2,1)S(1)} collective-permute-done((bf16[8,8,16,128]{3,2,1,0:T(8,128)(2,1)S(1)}, bf16[8,8,16,128]{3,2,1,0:T(8,128)(2,1)S(1)}, u32[]{:S(2)}, u32[]{:S(2)}) %collective-permute-start) | collective-permute-done | bytes 262176 | tf_op jit(solution)/shard_map/ppermute | solution.py:457
  14.6 1.8 %collective-permute-start.1 = (bf16[2,8,16,128]{3,2,1,0:T(8,128)(2,1)S(1)}, bf16[2,8,16,128]{3,2,1,0:T(8,128)(2,1)S(1)}, u32[]{:S(2)}, u32[]{:S(2)}) collective-permute-start(bf16[2,8,16,128]{3,2,1,0:T(8,128)(2,1)S(1)} %get-tuple-element.49), channel_id=1, source_target_pairs={{0,1},{1,0},{2,3},{3,2},{4,5},{5,4},{6,7},{7,6},{8,9},{9,8},{10,11... | collective-permute-start | bytes 196616 | tf_op jit(solution)/shard_map/ppermute | solution.py:457
  16.4 1.5 %collective-permute-start.2 = (bf16[2,8,16,128]{3,2,1,0:T(8,128)(2,1)S(1)}, bf16[2,8,16,128]{3,2,1,0:T(8,128)(2,1)S(1)}, u32[]{:S(2)}, u32[]{:S(2)}) collective-permute-start(bf16[2,8,16,128]{3,2,1,0:T(8,128)(2,1)S(1)} %get-tuple-element.50), channel_id=1, source_target_pairs={{0,4},{1,5},{2,6},{3,7},{4,0},{5,1},{6,2},{7,3},{8,12},{9,13},{10,... | collective-permute-start | bytes 196616 | tf_op jit(solution)/shard_map/ppermute | solution.py:457
  17.9 1.5 %collective-permute-start.3 = (bf16[2,8,16,128]{3,2,1,0:T(8,128)(2,1)S(1)}, bf16[2,8,16,128]{3,2,1,0:T(8,128)(2,1)S(1)}, u32[]{:S(2)}, u32[]{:S(2)}) collective-permute-start(bf16[2,8,16,128]{3,2,1,0:T(8,128)(2,1)S(1)} %get-tuple-element.51), channel_id=1, source_target_pairs={{0,13},{1,12},{2,15},{3,14},{4,9},{5,8},{6,11},{7,10},{8,5},{9,4},... | collective-permute-start | bytes 196616 | tf_op jit(solution)/shard_map/ppermute | solution.py:457
  19.3 1.5 %collective-permute-start.4 = (bf16[2,8,16,128]{3,2,1,0:T(8,128)(2,1)S(1)}, bf16[2,8,16,128]{3,2,1,0:T(8,128)(2,1)S(1)}, u32[]{:S(2)}, u32[]{:S(2)}) collective-permute-start(bf16[2,8,16,128]{3,2,1,0:T(8,128)(2,1)S(1)} %get-tuple-element.52), channel_id=1, source_target_pairs={{0,12},{1,13},{2,14},{3,15},{4,8},{5,9},{6,10},{7,11},{8,4},{9,5},... | collective-permute-start | bytes 196616 | tf_op jit(solution)/shard_map/ppermute | solution.py:457
  20.8 2.4 %collective-permute-start.5 = (bf16[2,8,16,128]{3,2,1,0:T(8,128)(2,1)S(1)}, bf16[2,8,16,128]{3,2,1,0:T(8,128)(2,1)S(1)}, u32[]{:S(2)}, u32[]{:S(2)}) collective-permute-start(bf16[2,8,16,128]{3,2,1,0:T(8,128)(2,1)S(1)} %get-tuple-element.53), channel_id=1, source_target_pairs={{0,9},{1,8},{2,11},{3,10},{4,13},{5,12},{6,15},{7,14},{8,1},{9,0},... | collective-permute-start | bytes 196616 | tf_op jit(solution)/shard_map/ppermute | solution.py:457
  23.2 0.0 collective-permute-done.1.refs_2_
  23.2 0.6 collective-permute-start.6
  23.7 0.0 collective-permute-done.2.refs_3_
  23.7 0.3 collective-permute-start.7
  24.0 5.7 %shard_map.83 = (f32[16,128,128]{2,1,0:T(8,128)S(1)}, bf16[16,512,128]{2,1,0:T(8,128)(2,1)}) custom-call(bf16[16,128,128]{2,1,0:T(8,128)(2,1)} %refs_2_.1, bf16[16,128,128]{2,1,0:T(8,128)(2,1)} %refs_3_.1, f32[1,128]{1,0:T(1,128)} %bitcast.5, f32[1,128]{1,0:T(1,128)} %bitcast.9, bf16[128,640]{1,0:T(8,128)(2,1)} %w_ref.1, f32[1,128]{1,0:T(1,128)} %bitcast.11, ...), custom_call_target="tpu_custom_call" | custom-call | tf_op jit(solution)/shard_map/pallas_call | solution.py:52
  29.7 7.8 %all-to-all-done.r_ref = bf16[32,8,16,128]{3,2,1,0:T(8,128)(2,1)S(1)} async-done(((bf16[32,8,16,128]{3,2,1,0:T(8,128)(2,1)}), bf16[32,8,16,128]{3,2,1,0:T(8,128)(2,1)S(1)}, u32[]{:S(2)}, u32[]{:S(2)}) %all-to-all-start) | async-done | bytes 1048608 | tf_op jit(solution)/shard_map/all_to_all | solution.py:446
  37.5 0.0 collective-permute-done.3.refs_4_
  37.5 0.0 collective-permute-done.4.refs_5_
  37.6 0.0 collective-permute-done.5.refs_6_
  37.6 0.0 collective-permute-done.6.refs_7_
  37.6 0.0 collective-permute-done.7.refs_8_
  37.6 0.5 shard_map.86
  38.1 12.3 %all_to_all.20.t_ref = bf16[16,8,16,128]{3,2,1,0:T(8,128)(2,1)S(1)} all-to-all(bf16[16,8,16,128]{3,2,1,0:T(8,128)(2,1)S(1)} %get-tuple-element.56), channel_id=1, replica_groups={{0,8,1,9,2,10,3,11,4,12,5,13,6,14,7,15},{16,24,17,25,18,26,19,27,20,28,..., dimensions={0} | all-to-all | bytes 1048576 | tf_op jit(solution)/shard_map/all_to_all | solution.py:452
  50.4 1.2 %shard_map.87 = (bf16[16,8,16,128]{3,2,1,0:T(8,128)(2,1)S(1)}, bf16[16,8,16,128]{3,2,1,0:T(8,128)(2,1)}) custom-call(bf16[16,8,16,128]{3,2,1,0:T(8,128)(2,1)S(1)} %all_to_all.20.t_ref, f32[16,128,128]{2,1,0:T(8,128)S(1)} %get-tuple-element.57.h_ref), custom_call_target="tpu_custom_call" | custom-call | tf_op jit(solution)/shard_map/pallas_call | solution.py:52
  51.6 12.3 %all_to_all.21.gt_ref = bf16[16,8,16,128]{3,2,1,0:T(8,128)(2,1)S(1)} all-to-all(bf16[16,8,16,128]{3,2,1,0:T(8,128)(2,1)S(1)} %get-tuple-element.64), channel_id=1, replica_groups={{0,8,1,9,2,10,3,11,4,12,5,13,6,14,7,15},{16,24,17,25,18,26,19,27,20,28,..., dimensions={0} | all-to-all | bytes 1048576 | tf_op jit(solution)/shard_map/all_to_all | solution.py:452
  63.8 1.3 %shard_map.89 = (bf16[32,8,16,128]{3,2,1,0:T(8,128)(2,1)}, bf16[8,8,16,128]{3,2,1,0:T(8,128)(2,1)S(1)}, bf16[8,8,16,128]{3,2,1,0:T(8,128)(2,1)S(1)}) custom-call(bf16[16,8,16,128]{3,2,1,0:T(8,128)(2,1)S(1)} %all_to_all.21.gt_ref, bf16[16,8,16,128]{3,2,1,0:T(8,128)(2,1)S(1)} %get-tuple-element.65.l_ref, bf16[32,8,16,128]{3,2,1,0:T(8,128)(2,1)S(1)} %all-to-all-done.r_ref), custom_call_target="tpu_custom_call" | custom-call | tf_op jit(solution)/shard_map/pallas_call | solution.py:52
  65.2 3.8 %all-to-all-start.3 = ((bf16[32,8,16,128]{3,2,1,0:T(8,128)(2,1)}), bf16[32,8,16,128]{3,2,1,0:T(8,128)(2,1)S(1)}, u32[]{:S(2)}, u32[]{:S(2)}) async-start(bf16[32,8,16,128]{3,2,1,0:T(8,128)(2,1)} %get-tuple-element.66), calls=%async_computation.3 | async-start | bytes 2097152 | tf_op jit(solution)/shard_map/all_to_all | solution.py:446
  69.0 0.3 collective-permute-start.8
  69.3 1.3 %collective-permute-done.8.mates_ref.refs_1_ = bf16[8,8,16,128]{3,2,1,0:T(8,128)(2,1)S(1)} collective-permute-done((bf16[8,8,16,128]{3,2,1,0:T(8,128)(2,1)S(1)}, bf16[8,8,16,128]{3,2,1,0:T(8,128)(2,1)S(1)}, u32[]{:S(2)}, u32[]{:S(2)}) %collective-permute-start.8) | collective-permute-done | bytes 262176 | tf_op jit(solution)/shard_map/ppermute | solution.py:457
  70.6 0.0 copy-start
  70.6 0.0 copy-start.1
  70.6 1.8 %collective-permute-start.9 = (bf16[2,8,16,128]{3,2,1,0:T(8,128)(2,1)S(1)}, bf16[2,8,16,128]{3,2,1,0:T(8,128)(2,1)S(1)}, u32[]{:S(2)}, u32[]{:S(2)}) collective-permute-start(bf16[2,8,16,128]{3,2,1,0:T(8,128)(2,1)S(1)} %get-tuple-element.70), channel_id=1, source_target_pairs={{0,1},{1,0},{2,3},{3,2},{4,5},{5,4},{6,7},{7,6},{8,9},{9,8},{10,11... | collective-permute-start | bytes 196616 | tf_op jit(solution)/shard_map/ppermute | solution.py:457
  72.5 1.5 %collective-permute-start.10 = (bf16[2,8,16,128]{3,2,1,0:T(8,128)(2,1)S(1)}, bf16[2,8,16,128]{3,2,1,0:T(8,128)(2,1)S(1)}, u32[]{:S(2)}, u32[]{:S(2)}) collective-permute-start(bf16[2,8,16,128]{3,2,1,0:T(8,128)(2,1)S(1)} %get-tuple-element.71), channel_id=1, source_target_pairs={{0,4},{1,5},{2,6},{3,7},{4,0},{5,1},{6,2},{7,3},{8,12},{9,13},{10,... | collective-permute-start | bytes 196616 | tf_op jit(solution)/shard_map/ppermute | solution.py:457
  73.9 1.5 %collective-permute-start.11 = (bf16[2,8,16,128]{3,2,1,0:T(8,128)(2,1)S(1)}, bf16[2,8,16,128]{3,2,1,0:T(8,128)(2,1)S(1)}, u32[]{:S(2)}, u32[]{:S(2)}) collective-permute-start(bf16[2,8,16,128]{3,2,1,0:T(8,128)(2,1)S(1)} %get-tuple-element.72), channel_id=1, source_target_pairs={{0,13},{1,12},{2,15},{3,14},{4,9},{5,8},{6,11},{7,10},{8,5},{9,4},... | collective-permute-start | bytes 196616 | tf_op jit(solution)/shard_map/ppermute | solution.py:457
  75.4 1.5 %collective-permute-start.12 = (bf16[2,8,16,128]{3,2,1,0:T(8,128)(2,1)S(1)}, bf16[2,8,16,128]{3,2,1,0:T(8,128)(2,1)S(1)}, u32[]{:S(2)}, u32[]{:S(2)}) collective-permute-start(bf16[2,8,16,128]{3,2,1,0:T(8,128)(2,1)S(1)} %get-tuple-element.73), channel_id=1, source_target_pairs={{0,12},{1,13},{2,14},{3,15},{4,8},{5,9},{6,10},{7,11},{8,4},{9,5},... | collective-permute-start | bytes 196616 | tf_op jit(solution)/shard_map/ppermute | solution.py:457
  76.9 2.4 %collective-permute-start.13 = (bf16[2,8,16,128]{3,2,1,0:T(8,128)(2,1)S(1)}, bf16[2,8,16,128]{3,2,1,0:T(8,128)(2,1)S(1)}, u32[]{:S(2)}, u32[]{:S(2)}) collective-permute-start(bf16[2,8,16,128]{3,2,1,0:T(8,128)(2,1)S(1)} %get-tuple-element.74), channel_id=1, source_target_pairs={{0,9},{1,8},{2,11},{3,10},{4,13},{5,12},{6,15},{7,14},{8,1},{9,0},... | collective-permute-start | bytes 196616 | tf_op jit(solution)/shard_map/ppermute | solution.py:457
  79.2 0.0 collective-permute-done.9.refs_2_
  79.2 0.6 collective-permute-start.14
  79.8 0.0 collective-permute-done.10.refs_3_
  79.8 1.6 %collective-permute-start.15 = (bf16[2,8,16,128]{3,2,1,0:T(8,128)(2,1)S(1)}, bf16[2,8,16,128]{3,2,1,0:T(8,128)(2,1)S(1)}, u32[]{:S(2)}, u32[]{:S(2)}) collective-permute-start(bf16[2,8,16,128]{3,2,1,0:T(8,128)(2,1)S(1)} %get-tuple-element.76), channel_id=1, source_target_pairs={{0,5},{1,4},{2,7},{3,6},{4,1},{5,0},{6,3},{7,2},{8,13},{9,12},{10,... | collective-permute-start | bytes 196616 | tf_op jit(solution)/shard_map/ppermute | solution.py:457
  81.4 6.0 %shard_map.88 = (f32[4,128,128]{2,1,0:T(8,128)S(1)}, bf16[4,128,128]{2,1,0:T(8,128)(2,1)S(1)}, bf16[4,512,128]{2,1,0:T(8,128)(2,1)S(1)}, f32[16,128,128]{2,1,0:T...) custom-call(bf16[16,512,128]{2,1,0:T(8,128)(2,1)} %get-tuple-element.44.refs_0_.fac_hbm, ...), custom_call_target="tpu_custom_call" | custom-call | tf_op jit(solution)/shard_map/pallas_call | solution.py:52
  87.4 0.9 collective-permute-done.11.refs_4_
  88.4 1.6 %collective-permute-done.12.refs_5_ = bf16[2,8,16,128]{3,2,1,0:T(8,128)(2,1)S(1)} collective-permute-done((bf16[2,8,16,128]{3,2,1,0:T(8,128)(2,1)S(1)}, bf16[2,8,16,128]{3,2,1,0:T(8,128)(2,1)S(1)}, u32[]{:S(2)}, u32[]{:S(2)}) %collective-permute-start.12) | collective-permute-done | bytes 65568 | tf_op jit(solution)/shard_map/ppermute | solution.py:457
  89.9 2.8 %collective-permute-done.13.refs_6_ = bf16[2,8,16,128]{3,2,1,0:T(8,128)(2,1)S(1)} collective-permute-done((bf16[2,8,16,128]{3,2,1,0:T(8,128)(2,1)S(1)}, bf16[2,8,16,128]{3,2,1,0:T(8,128)(2,1)S(1)}, u32[]{:S(2)}, u32[]{:S(2)}) %collective-permute-start.13) | collective-permute-done | bytes 65568 | tf_op jit(solution)/shard_map/ppermute | solution.py:457
  92.8 1.3 %collective-permute-done.14.refs_7_ = bf16[2,8,16,128]{3,2,1,0:T(8,128)(2,1)S(1)} collective-permute-done((bf16[2,8,16,128]{3,2,1,0:T(8,128)(2,1)S(1)}, bf16[2,8,16,128]{3,2,1,0:T(8,128)(2,1)S(1)}, u32[]{:S(2)}, u32[]{:S(2)}) %collective-permute-start.14) | collective-permute-done | bytes 65568 | tf_op jit(solution)/shard_map/ppermute | solution.py:457
  94.1 0.0 collective-permute-done.15.refs_8_
  94.1 1.7 %all-to-all-done.3.r_ref = bf16[32,8,16,128]{3,2,1,0:T(8,128)(2,1)S(1)} async-done(((bf16[32,8,16,128]{3,2,1,0:T(8,128)(2,1)}), bf16[32,8,16,128]{3,2,1,0:T(8,128)(2,1)S(1)}, u32[]{:S(2)}, u32[]{:S(2)}) %all-to-all-start.3) | async-done | bytes 1048608 | tf_op jit(solution)/shard_map/all_to_all | solution.py:446
  95.8 0.0 copy-done
  95.8 0.0 copy-done.1
  95.8 3.9 %shard_map.91 = bf16[16,128,128]{2,1,0:T(8,128)(2,1)} custom-call(bf16[16,512,128]{2,1,0:T(8,128)(2,1)} %get-tuple-element.44.refs_0_.fac_hbm, bf16[16,128,128]{2,1,0:T(8,128)(2,1)} %get-tuple-element.59.nt_hbm, f32[16,128,128]{2,1,0:T(8,128)} %get-tuple-element.60.gin_hbm, bf16[4,512,128]{2,1,0:T(8,128)(2,1)S(1)} %get-tuple-element.61.fac0_ref, ...), custom_call_target="tpu_custom_call" | custom-call | tf_op jit(solution)/shard_map/pallas_call | solution.py:52
  (2 shorter events, 0.1 us)
Async XLA Ops:
  3.4 34.1 %all-to-all-start = ((bf16[32,8,16,128]{3,2,1,0:T(8,128)(2,1)}), bf16[32,8,16,128]{3,2,1,0:T(8,128)(2,1)S(1)}, u32[]{:S(2)}, u32[]{:S(2)}) async-start(bf16[32,8,16,128]{3,2,1,0:T(8,128)(2,1)} %get-tuple-element.41), calls=%async_computation | async-start | bytes 2097152 | tf_op jit(solution)/shard_map/all_to_all | solution.py:446
  12.9 1.6 %collective-permute-start = (bf16[8,8,16,128]{3,2,1,0:T(8,128)(2,1)S(1)}, bf16[8,8,16,128]{3,2,1,0:T(8,128)(2,1)S(1)}, u32[]{:S(2)}, u32[]{:S(2)}) collective-permute-start(bf16[8,8,16,128]{3,2,1,0:T(8,128)(2,1)S(1)} %get-tuple-element.48), channel_id=1, source_target_pairs={{0,2},{1,3},{2,0},{3,1},{4,6},{5,7},{6,4},{7,5},{8,10},{9,11},{10,... | collective-permute-start | bytes 786440 | tf_op jit(solution)/shard_map/ppermute | solution.py:457
  14.6 8.6 %collective-permute-start.1 = (bf16[2,8,16,128]{3,2,1,0:T(8,128)(2,1)S(1)}, bf16[2,8,16,128]{3,2,1,0:T(8,128)(2,1)S(1)}, u32[]{:S(2)}, u32[]{:S(2)}) collective-permute-start(bf16[2,8,16,128]{3,2,1,0:T(8,128)(2,1)S(1)} %get-tuple-element.49), channel_id=1, source_target_pairs={{0,1},{1,0},{2,3},{3,2},{4,5},{5,4},{6,7},{7,6},{8,9},{9,8},{10,11... | collective-permute-start | bytes 196616 | tf_op jit(solution)/shard_map/ppermute | solution.py:457
  16.4 7.3 %collective-permute-start.2 = (bf16[2,8,16,128]{3,2,1,0:T(8,128)(2,1)S(1)}, bf16[2,8,16,128]{3,2,1,0:T(8,128)(2,1)S(1)}, u32[]{:S(2)}, u32[]{:S(2)}) collective-permute-start(bf16[2,8,16,128]{3,2,1,0:T(8,128)(2,1)S(1)} %get-tuple-element.50), channel_id=1, source_target_pairs={{0,4},{1,5},{2,6},{3,7},{4,0},{5,1},{6,2},{7,3},{8,12},{9,13},{10,... | collective-permute-start | bytes 196616 | tf_op jit(solution)/shard_map/ppermute | solution.py:457
  17.9 19.7 %collective-permute-start.3 = (bf16[2,8,16,128]{3,2,1,0:T(8,128)(2,1)S(1)}, bf16[2,8,16,128]{3,2,1,0:T(8,128)(2,1)S(1)}, u32[]{:S(2)}, u32[]{:S(2)}) collective-permute-start(bf16[2,8,16,128]{3,2,1,0:T(8,128)(2,1)S(1)} %get-tuple-element.51), channel_id=1, source_target_pairs={{0,13},{1,12},{2,15},{3,14},{4,9},{5,8},{6,11},{7,10},{8,5},{9,4},... | collective-permute-start | bytes 196616 | tf_op jit(solution)/shard_map/ppermute | solution.py:457
  19.3 18.2 %collective-permute-start.4 = (bf16[2,8,16,128]{3,2,1,0:T(8,128)(2,1)S(1)}, bf16[2,8,16,128]{3,2,1,0:T(8,128)(2,1)S(1)}, u32[]{:S(2)}, u32[]{:S(2)}) collective-permute-start(bf16[2,8,16,128]{3,2,1,0:T(8,128)(2,1)S(1)} %get-tuple-element.52), channel_id=1, source_target_pairs={{0,12},{1,13},{2,14},{3,15},{4,8},{5,9},{6,10},{7,11},{8,4},{9,5},... | collective-permute-start | bytes 196616 | tf_op jit(solution)/shard_map/ppermute | solution.py:457
  20.8 16.7 %collective-permute-start.5 = (bf16[2,8,16,128]{3,2,1,0:T(8,128)(2,1)S(1)}, bf16[2,8,16,128]{3,2,1,0:T(8,128)(2,1)S(1)}, u32[]{:S(2)}, u32[]{:S(2)}) collective-permute-start(bf16[2,8,16,128]{3,2,1,0:T(8,128)(2,1)S(1)} %get-tuple-element.53), channel_id=1, source_target_pairs={{0,9},{1,8},{2,11},{3,10},{4,13},{5,12},{6,15},{7,14},{8,1},{9,0},... | collective-permute-start | bytes 196616 | tf_op jit(solution)/shard_map/ppermute | solution.py:457
  23.2 14.4 %collective-permute-start.6 = (bf16[2,8,16,128]{3,2,1,0:T(8,128)(2,1)S(1)}, bf16[2,8,16,128]{3,2,1,0:T(8,128)(2,1)S(1)}, u32[]{:S(2)}, u32[]{:S(2)}) collective-permute-start(bf16[2,8,16,128]{3,2,1,0:T(8,128)(2,1)S(1)} %get-tuple-element.54), channel_id=1, source_target_pairs={{0,8},{1,9},{2,10},{3,11},{4,12},{5,13},{6,14},{7,15},{8,0},{9,1},... | collective-permute-start | bytes 196616 | tf_op jit(solution)/shard_map/ppermute | solution.py:457
  23.7 13.8 %collective-permute-start.7 = (bf16[2,8,16,128]{3,2,1,0:T(8,128)(2,1)S(1)}, bf16[2,8,16,128]{3,2,1,0:T(8,128)(2,1)S(1)}, u32[]{:S(2)}, u32[]{:S(2)}) collective-permute-start(bf16[2,8,16,128]{3,2,1,0:T(8,128)(2,1)S(1)} %get-tuple-element.55), channel_id=1, source_target_pairs={{0,5},{1,4},{2,7},{3,6},{4,1},{5,0},{6,3},{7,2},{8,13},{9,12},{10,... | collective-permute-start | bytes 196616 | tf_op jit(solution)/shard_map/ppermute | solution.py:457
  65.2 30.6 %all-to-all-start.3 = ((bf16[32,8,16,128]{3,2,1,0:T(8,128)(2,1)}), bf16[32,8,16,128]{3,2,1,0:T(8,128)(2,1)S(1)}, u32[]{:S(2)}, u32[]{:S(2)}) async-start(bf16[32,8,16,128]{3,2,1,0:T(8,128)(2,1)} %get-tuple-element.66), calls=%async_computation.3 | async-start | bytes 2097152 | tf_op jit(solution)/shard_map/all_to_all | solution.py:446
  69.0 1.6 %collective-permute-start.8 = (bf16[8,8,16,128]{3,2,1,0:T(8,128)(2,1)S(1)}, bf16[8,8,16,128]{3,2,1,0:T(8,128)(2,1)S(1)}, u32[]{:S(2)}, u32[]{:S(2)}) collective-permute-start(bf16[8,8,16,128]{3,2,1,0:T(8,128)(2,1)S(1)} %get-tuple-element.69), channel_id=1, source_target_pairs={{0,2},{1,3},{2,0},{3,1},{4,6},{5,7},{6,4},{7,5},{8,10},{9,11},{10,... | collective-permute-start | bytes 786440 | tf_op jit(solution)/shard_map/ppermute | solution.py:457
  70.6 25.2 %copy-start = (bf16[128,640]{1,0:T(8,128)(2,1)S(1)}, bf16[128,640]{1,0:T(8,128)(2,1)}, u32[]{:S(2)}) copy-start(bf16[128,640]{1,0:T(8,128)(2,1)} %w_ref.1) | copy-start | bytes 491524
  70.6 25.2 %copy-start.1 = (f32[128]{0:T(128)S(1)}, f32[128]{0:T(128)}, u32[]{:S(2)}) copy-start(f32[128]{0:T(128)} %param.10) | copy-start | bytes 1540
  70.6 8.6 %collective-permute-start.9 = (bf16[2,8,16,128]{3,2,1,0:T(8,128)(2,1)S(1)}, bf16[2,8,16,128]{3,2,1,0:T(8,128)(2,1)S(1)}, u32[]{:S(2)}, u32[]{:S(2)}) collective-permute-start(bf16[2,8,16,128]{3,2,1,0:T(8,128)(2,1)S(1)} %get-tuple-element.70), channel_id=1, source_target_pairs={{0,1},{1,0},{2,3},{3,2},{4,5},{5,4},{6,7},{7,6},{8,9},{9,8},{10,11... | collective-permute-start | bytes 196616 | tf_op jit(solution)/shard_map/ppermute | solution.py:457
  72.5 7.4 %collective-permute-start.10 = (bf16[2,8,16,128]{3,2,1,0:T(8,128)(2,1)S(1)}, bf16[2,8,16,128]{3,2,1,0:T(8,128)(2,1)S(1)}, u32[]{:S(2)}, u32[]{:S(2)}) collective-permute-start(bf16[2,8,16,128]{3,2,1,0:T(8,128)(2,1)S(1)} %get-tuple-element.71), channel_id=1, source_target_pairs={{0,4},{1,5},{2,6},{3,7},{4,0},{5,1},{6,2},{7,3},{8,12},{9,13},{10,... | collective-permute-start | bytes 196616 | tf_op jit(solution)/shard_map/ppermute | solution.py:457
  73.9 14.4 %collective-permute-start.11 = (bf16[2,8,16,128]{3,2,1,0:T(8,128)(2,1)S(1)}, bf16[2,8,16,128]{3,2,1,0:T(8,128)(2,1)S(1)}, u32[]{:S(2)}, u32[]{:S(2)}) collective-permute-start(bf16[2,8,16,128]{3,2,1,0:T(8,128)(2,1)S(1)} %get-tuple-element.72), channel_id=1, source_target_pairs={{0,13},{1,12},{2,15},{3,14},{4,9},{5,8},{6,11},{7,10},{8,5},{9,4},... | collective-permute-start | bytes 196616 | tf_op jit(solution)/shard_map/ppermute | solution.py:457
  75.4 14.5 %collective-permute-start.12 = (bf16[2,8,16,128]{3,2,1,0:T(8,128)(2,1)S(1)}, bf16[2,8,16,128]{3,2,1,0:T(8,128)(2,1)S(1)}, u32[]{:S(2)}, u32[]{:S(2)}) collective-permute-start(bf16[2,8,16,128]{3,2,1,0:T(8,128)(2,1)S(1)} %get-tuple-element.73), channel_id=1, source_target_pairs={{0,12},{1,13},{2,14},{3,15},{4,8},{5,9},{6,10},{7,11},{8,4},{9,5},... | collective-permute-start | bytes 196616 | tf_op jit(solution)/shard_map/ppermute | solution.py:457
  76.9 15.9 %collective-permute-start.13 = (bf16[2,8,16,128]{3,2,1,0:T(8,128)(2,1)S(1)}, bf16[2,8,16,128]{3,2,1,0:T(8,128)(2,1)S(1)}, u32[]{:S(2)}, u32[]{:S(2)}) collective-permute-start(bf16[2,8,16,128]{3,2,1,0:T(8,128)(2,1)S(1)} %get-tuple-element.74), channel_id=1, source_target_pairs={{0,9},{1,8},{2,11},{3,10},{4,13},{5,12},{6,15},{7,14},{8,1},{9,0},... | collective-permute-start | bytes 196616 | tf_op jit(solution)/shard_map/ppermute | solution.py:457
  79.2 14.9 %collective-permute-start.14 = (bf16[2,8,16,128]{3,2,1,0:T(8,128)(2,1)S(1)}, bf16[2,8,16,128]{3,2,1,0:T(8,128)(2,1)S(1)}, u32[]{:S(2)}, u32[]{:S(2)}) collective-permute-start(bf16[2,8,16,128]{3,2,1,0:T(8,128)(2,1)S(1)} %get-tuple-element.75), channel_id=1, source_target_pairs={{0,8},{1,9},{2,10},{3,11},{4,12},{5,13},{6,14},{7,15},{8,0},{9,1},... | collective-permute-start | bytes 196616 | tf_op jit(solution)/shard_map/ppermute | solution.py:457
  79.8 14.3 %collective-permute-start.15 = (bf16[2,8,16,128]{3,2,1,0:T(8,128)(2,1)S(1)}, bf16[2,8,16,128]{3,2,1,0:T(8,128)(2,1)S(1)}, u32[]{:S(2)}, u32[]{:S(2)}) collective-permute-start(bf16[2,8,16,128]{3,2,1,0:T(8,128)(2,1)S(1)} %get-tuple-element.76), channel_id=1, source_target_pairs={{0,5},{1,4},{2,7},{3,6},{4,1},{5,0},{6,3},{7,2},{8,13},{9,12},{10,... | collective-permute-start | bytes 196616 | tf_op jit(solution)/shard_map/ppermute | solution.py:457

commit v5 on v4

--- a/solution.py
+++ b/solution.py
@@ -105,28 +105,32 @@
 ):
     rows, cols, width = x_ref.shape
     mine = width // lay.half
-    parts = sems.shape[0] - 4
+    parts = (sems.shape[0] - 4) // 2
     size = rows // parts
 
     def fetch(p):
-        here = pl.ds(p * size, size)
-        return pltpu.make_async_copy(x_hbm.at[here], x_ref.at[here], sems.at[4 + p])
+        copies = []
+        for n in range(2):
+            here = pl.ds(p * size + n * size // 2, size // 2)
+            copies.append(pltpu.make_async_copy(x_hbm.at[here], x_ref.at[here], sems.at[4 + 2 * p + n]))
+        return copies
 
     small = [
         pltpu.make_async_copy(gain_hbm, gain_ref, sems.at[2]),
         pltpu.make_async_copy(bias_hbm, bias_ref, sems.at[3]),
     ]
     weights = weight_copies(w_hbm, w_ref, 2, sems)
-    fetch(0).start()
-    for copy in small + weights:
+    for copy in fetch(0) + small + weights:
         copy.start()
     for p in range(1, parts):
-        fetch(p).start()
+        for copy in fetch(p):
+            copy.start()
     group = BLOCK // rows
     swap = permutation(group, rows)
 
     def normal(p):
-        fetch(p).wait()
+        for copy in fetch(p):
+            copy.wait()
         for n in range(0, size, 2):
             i = p * size + n
             shifted = dot(center, x_ref[pl.ds(i, 2)].reshape(2 * cols, width), 1, 1)
@@ -267,12 +271,22 @@
             ts_ref[:, here] = block.reshape(rows, group, cols)
 
 
-def tri_back_kernel(lay, t_ref, h_ref, gt_ref, t_hbm, ts_ref, gs_ref, sem):
+def split_copies(source, target, sems):
+    parts = sems.shape[0]
+    size = source.shape[0] // parts
+    return [
+        pltpu.make_async_copy(source.at[pl.ds(p * size, size)], target.at[pl.ds(p * size, size)], sems.at[p])
+        for p in range(parts)
+    ]
+
+
+def tri_back_kernel(lay, t_ref, h_ref, gt_ref, t_hbm, ts_ref, gs_ref, sems):
     rows, width, cols = h_ref.shape
     mine = t_ref.shape[1]
     group = BLOCK // rows
-    copy = pltpu.make_async_copy(t_ref, t_hbm, sem)
-    copy.start()
+    copies = split_copies(t_ref, t_hbm, sems)
+    for copy in copies:
+        copy.start()
     back = permutation(group, rows)
     to_rows(lay, t_ref, ts_ref)
 
@@ -293,7 +307,8 @@
             block = block.reshape(group // mine, mine, rows, cols)
             for share in range(to.start, to.stop):
                 gt_ref[lay.inside.index(share)] = block[share - to.start]
-    copy.wait()
+    for copy in copies:
+        copy.wait()
 
 
 def logit_kernel(lay, *refs):
@@ -502,8 +517,7 @@
         store_plane(t_ref, lay.half_place, c, tri.astype(BF16))
 
 
-def factor_back_kernel(lay, gt_ref, l_ref, r_ref, gr_hbm, *refs):
-    mine_out, mate_out, gl_ref, gr_ref, sems = refs
+def right_back_kernel(lay, gt_ref, l_ref, gr_hbm, gr_ref, sems):
     copies = []
     for c in range(gt_ref.shape[1]):
         right = dot(plane(gt_ref, lay.half_place, c), plane(l_ref, lay.near_place, c), 0, 0)
@@ -511,14 +525,17 @@
         here = (slice(None), c)
         copies.append(pltpu.make_async_copy(gr_ref.at[here], gr_hbm.at[here], sems.at[c]))
         copies[-1].start()
+    for copy in copies:
+        copy.wait()
+
+
+def left_back_kernel(lay, gt_ref, r_ref, mine_out, mate_out, gl_ref):
     for c in range(gt_ref.shape[1]):
         left = dot(plane(gt_ref, lay.half_place, c), plane(r_ref, lay.all_place, c), 1, 0)
         store_plane(gl_ref, lay.near_place, c, left.astype(BF16))
     for n, s in enumerate(lay.hops):
         mine_out[n] = gl_ref[lay.other(s)]
         mate_out[n] = gl_ref[lay.other(s ^ lay.mate)]
-    for copy in copies:
-        copy.wait()
 
 
 def by_channel(
@@ -554,7 +571,7 @@
             both_turned,
             half,
             one_here,
-            pltpu.SemaphoreType.DMA((4 + PARTS // 2,)),
+            pltpu.SemaphoreType.DMA((4 + PARTS,)),
             pltpu.SemaphoreType.DMA((lay.devices,)),
         ],
         pair_act,
@@ -604,17 +621,20 @@
     grad_tri, tri = call(
         functools.partial(tri_back_kernel, lay),
         [one, pltpu.HBM(one.shape, BF16)],
-        [half, half, pltpu.SemaphoreType.DMA(())],
+        [half, half, pltpu.SemaphoreType.DMA((PARTS,))],
         tri,
         h,
     )
-    grad_right, *grad_left = call(
-        functools.partial(factor_back_kernel, lay),
-        [pltpu.HBM(two_shape, BF16), some, some],
-        [one_here, pltpu.VMEM(two_shape, BF16), pltpu.SemaphoreType.DMA((mine,))],
-        lay.exchange_half(grad_tri),
+    grad_tri = lay.exchange_half(grad_tri)
+    grad_right = call(
+        functools.partial(right_back_kernel, lay),
+        pltpu.HBM(two_shape, BF16),
+        [pltpu.VMEM(two_shape, BF16), pltpu.SemaphoreType.DMA((mine,))],
+        grad_tri,
         left,
-        right,
+    )
+    grad_left = call(
+        functools.partial(left_back_kernel, lay), [some, some], [one_here], grad_tri, right
     )
     grad_right = lay.exchange_all(grad_right)
     grad_left = lay.permute(*grad_left)

time: 100 us -> 100 us (level)
    pallas_call x10 -> x11, Pallas kernels: 24.3 us -> 24.8 us  [call(): pl.pallas_call(kernel, out_shape=outs if single else tuple(outs), in_spec...]
where the time goes in v5:
time: 100 us; the launch traced here: 99.8 us
  starting transfers between devices  31.5 us (32%)
  Pallas kernels  24.8 us (25%)
  blocking collectives  24.6 us (25%)
  waiting for transfers between devices  18.7 us (19%)
    pallas_call x11, Pallas kernels, call(): pl.pallas_call(kernel, out_shape=outs if single else tuple(outs), in_spec...  24.8 us
    all_to_all x2, blocking collectives, exchange_half(): lax.all_to_all(blocks, ('row', 'ch'), split_axis=0, concat_axis=0, tiled=...  24.6 us
    ppermute x16, starting transfers between devices, swap(): lax.ppermute(block, ('row', 'ch'), [(n, n ^ s) for n in range(self.device...  20.4 us
    all_to_all x2, starting transfers between devices, exchange_all(): lax.all_to_all(blocks, ('row', 'ch'), split_axis=0, concat_axis=0, tiled=...  11.1 us
    all_to_all x2, waiting for transfers between devices, exchange_all(): lax.all_to_all(blocks, ('row', 'ch'), split_axis=0, concat_axis=0, tiled=...  9.47 us
    ppermute x16, waiting for transfers between devices, swap(): lax.ppermute(block, ('row', 'ch'), [(n, n ^ s) for n in range(self.device...  9.28 us
  transfers between devices with their start and end apart: 18, of which 8 were waited for; matrix products, arithmetic and copies ran while one was open for 0% of the time, Pallas kernels for 14%

profile of v5, /device:TPU:0, one launch (start us, length us, event | category | flops | bytes accessed | tf_op | source)
XLA Modules:
  0.0 99.8 jit_solution(16130602437547631770)
XLA Ops:
  0.0 3.5 %shard_map.82 = (bf16[32,8,16,128]{3,2,1,0:T(8,128)(2,1)}, bf16[8,128,256]{2,1,0:T(8,128)(2,1)S(1)}) custom-call(bf16[16,128,128]{2,1,0:T(8,128)(2,1)} %refs_2_.1, f32[1,128]{1,0:T(1,128)} %bitcast.4, f32[1,128]{1,0:T(1,128)} %bitcast.8, bf16[128,640]{1,0:T(8,128)(2,1)} %w_ref.1), custom_call_target="tpu_custom_call" | custom-call | tf_op jit(solution)/shard_map/pallas_call | solution.py:52
  3.5 7.3 %all-to-all-start = ((bf16[32,8,16,128]{3,2,1,0:T(8,128)(2,1)}), bf16[32,8,16,128]{3,2,1,0:T(8,128)(2,1)S(1)}, u32[]{:S(2)}, u32[]{:S(2)}) async-start(bf16[32,8,16,128]{3,2,1,0:T(8,128)(2,1)} %get-tuple-element.40), calls=%async_computation | async-start | bytes 2097152 | tf_op jit(solution)/shard_map/all_to_all | solution.py:461
  10.8 2.2 %shard_map.84 = (bf16[8,8,16,128]{3,2,1,0:T(8,128)(2,1)S(1)}, bf16[8,8,16,128]{3,2,1,0:T(8,128)(2,1)S(1)}) custom-call(bf16[128,640]{1,0:T(8,128)(2,1)} %w_ref.1, bf16[8,128,256]{2,1,0:T(8,128)(2,1)S(1)} %get-tuple-element.45.n_ref), custom_call_target="tpu_custom_call" | custom-call | tf_op jit(solution)/shard_map/pallas_call | solution.py:52
  13.0 0.3 collective-permute-start
  13.3 1.3 %collective-permute-done.mates_ref.refs_1_ = bf16[8,8,16,128]{3,2,1,0:T(8,128)(2,1)S(1)} collective-permute-done((bf16[8,8,16,128]{3,2,1,0:T(8,128)(2,1)S(1)}, bf16[8,8,16,128]{3,2,1,0:T(8,128)(2,1)S(1)}, u32[]{:S(2)}, u32[]{:S(2)}) %collective-permute-start) | collective-permute-done | bytes 262176 | tf_op jit(solution)/shard_map/ppermute | solution.py:472
  14.6 1.8 %collective-permute-start.1 = (bf16[2,8,16,128]{3,2,1,0:T(8,128)(2,1)S(1)}, bf16[2,8,16,128]{3,2,1,0:T(8,128)(2,1)S(1)}, u32[]{:S(2)}, u32[]{:S(2)}) collective-permute-start(bf16[2,8,16,128]{3,2,1,0:T(8,128)(2,1)S(1)} %get-tuple-element.48), channel_id=1, source_target_pairs={{0,1},{1,0},{2,3},{3,2},{4,5},{5,4},{6,7},{7,6},{8,9},{9,8},{10,11... | collective-permute-start | bytes 196616 | tf_op jit(solution)/shard_map/ppermute | solution.py:472
  16.4 1.5 %collective-permute-start.2 = (bf16[2,8,16,128]{3,2,1,0:T(8,128)(2,1)S(1)}, bf16[2,8,16,128]{3,2,1,0:T(8,128)(2,1)S(1)}, u32[]{:S(2)}, u32[]{:S(2)}) collective-permute-start(bf16[2,8,16,128]{3,2,1,0:T(8,128)(2,1)S(1)} %get-tuple-element.49), channel_id=1, source_target_pairs={{0,4},{1,5},{2,6},{3,7},{4,0},{5,1},{6,2},{7,3},{8,12},{9,13},{10,... | collective-permute-start | bytes 196616 | tf_op jit(solution)/shard_map/ppermute | solution.py:472
  17.9 1.5 %collective-permute-start.3 = (bf16[2,8,16,128]{3,2,1,0:T(8,128)(2,1)S(1)}, bf16[2,8,16,128]{3,2,1,0:T(8,128)(2,1)S(1)}, u32[]{:S(2)}, u32[]{:S(2)}) collective-permute-start(bf16[2,8,16,128]{3,2,1,0:T(8,128)(2,1)S(1)} %get-tuple-element.50), channel_id=1, source_target_pairs={{0,13},{1,12},{2,15},{3,14},{4,9},{5,8},{6,11},{7,10},{8,5},{9,4},... | collective-permute-start | bytes 196616 | tf_op jit(solution)/shard_map/ppermute | solution.py:472
  19.4 1.5 %collective-permute-start.4 = (bf16[2,8,16,128]{3,2,1,0:T(8,128)(2,1)S(1)}, bf16[2,8,16,128]{3,2,1,0:T(8,128)(2,1)S(1)}, u32[]{:S(2)}, u32[]{:S(2)}) collective-permute-start(bf16[2,8,16,128]{3,2,1,0:T(8,128)(2,1)S(1)} %get-tuple-element.51), channel_id=1, source_target_pairs={{0,12},{1,13},{2,14},{3,15},{4,8},{5,9},{6,10},{7,11},{8,4},{9,5},... | collective-permute-start | bytes 196616 | tf_op jit(solution)/shard_map/ppermute | solution.py:472
  20.8 2.4 %collective-permute-start.5 = (bf16[2,8,16,128]{3,2,1,0:T(8,128)(2,1)S(1)}, bf16[2,8,16,128]{3,2,1,0:T(8,128)(2,1)S(1)}, u32[]{:S(2)}, u32[]{:S(2)}) collective-permute-start(bf16[2,8,16,128]{3,2,1,0:T(8,128)(2,1)S(1)} %get-tuple-element.52), channel_id=1, source_target_pairs={{0,9},{1,8},{2,11},{3,10},{4,13},{5,12},{6,15},{7,14},{8,1},{9,0},... | collective-permute-start | bytes 196616 | tf_op jit(solution)/shard_map/ppermute | solution.py:472
  23.2 0.0 collective-permute-done.1.refs_2_
  23.2 0.6 collective-permute-start.6
  23.8 0.0 collective-permute-done.2.refs_3_
  23.8 0.3 collective-permute-start.7
  24.0 5.7 %shard_map.83 = (f32[16,128,128]{2,1,0:T(8,128)S(1)}, bf16[16,512,128]{2,1,0:T(8,128)(2,1)}) custom-call(bf16[16,128,128]{2,1,0:T(8,128)(2,1)} %refs_2_.1, bf16[16,128,128]{2,1,0:T(8,128)(2,1)} %refs_3_.1, f32[1,128]{1,0:T(1,128)} %bitcast.5, f32[1,128]{1,0:T(1,128)} %bitcast.9, bf16[128,640]{1,0:T(8,128)(2,1)} %w_ref.1, f32[1,128]{1,0:T(1,128)} %bitcast.11, ...), custom_call_target="tpu_custom_call" | custom-call | tf_op jit(solution)/shard_map/pallas_call | solution.py:52
  29.8 7.8 %all-to-all-done.r_ref = bf16[32,8,16,128]{3,2,1,0:T(8,128)(2,1)S(1)} async-done(((bf16[32,8,16,128]{3,2,1,0:T(8,128)(2,1)}), bf16[32,8,16,128]{3,2,1,0:T(8,128)(2,1)S(1)}, u32[]{:S(2)}, u32[]{:S(2)}) %all-to-all-start) | async-done | bytes 1048608 | tf_op jit(solution)/shard_map/all_to_all | solution.py:461
  37.6 0.0 collective-permute-done.3.refs_4_
  37.6 0.0 collective-permute-done.4.refs_5_
  37.6 0.0 collective-permute-done.5.refs_6_
  37.6 0.0 collective-permute-done.6.refs_7_
  37.6 0.0 collective-permute-done.7.refs_8_
  37.6 0.5 shard_map.86
  38.1 12.3 %all_to_all.20.t_ref = bf16[16,8,16,128]{3,2,1,0:T(8,128)(2,1)S(1)} all-to-all(bf16[16,8,16,128]{3,2,1,0:T(8,128)(2,1)S(1)} %get-tuple-element.55), channel_id=1, replica_groups={{0,8,1,9,2,10,3,11,4,12,5,13,6,14,7,15},{16,24,17,25,18,26,19,27,20,28,..., dimensions={0} | all-to-all | bytes 1048576 | tf_op jit(solution)/shard_map/all_to_all | solution.py:467
  50.4 1.2 %shard_map.87 = (bf16[16,8,16,128]{3,2,1,0:T(8,128)(2,1)S(1)}, bf16[16,8,16,128]{3,2,1,0:T(8,128)(2,1)}) custom-call(bf16[16,8,16,128]{3,2,1,0:T(8,128)(2,1)S(1)} %all_to_all.20.t_ref, f32[16,128,128]{2,1,0:T(8,128)S(1)} %get-tuple-element.56.h_ref), custom_call_target="tpu_custom_call" | custom-call | tf_op jit(solution)/shard_map/pallas_call | solution.py:52
  51.6 12.3 %all_to_all.21.gt_ref = bf16[16,8,16,128]{3,2,1,0:T(8,128)(2,1)S(1)} all-to-all(bf16[16,8,16,128]{3,2,1,0:T(8,128)(2,1)S(1)} %get-tuple-element.63), channel_id=1, replica_groups={{0,8,1,9,2,10,3,11,4,12,5,13,6,14,7,15},{16,24,17,25,18,26,19,27,20,28,..., dimensions={0} | all-to-all | bytes 1048576 | tf_op jit(solution)/shard_map/all_to_all | solution.py:467
  63.9 1.3 %shard_map.89 = bf16[32,8,16,128]{3,2,1,0:T(8,128)(2,1)} custom-call(bf16[16,8,16,128]{3,2,1,0:T(8,128)(2,1)S(1)} %all_to_all.21.gt_ref, bf16[16,8,16,128]{3,2,1,0:T(8,128)(2,1)S(1)} %get-tuple-element.64.l_ref), custom_call_target="tpu_custom_call" | custom-call | tf_op jit(solution)/shard_map/pallas_call | solution.py:52
  65.3 3.8 %all-to-all-start.3 = ((bf16[32,8,16,128]{3,2,1,0:T(8,128)(2,1)}), bf16[32,8,16,128]{3,2,1,0:T(8,128)(2,1)S(1)}, u32[]{:S(2)}, u32[]{:S(2)}) async-start(bf16[32,8,16,128]{3,2,1,0:T(8,128)(2,1)} %shard_map.89), calls=%async_computation.3 | async-start | bytes 2097152 | tf_op jit(solution)/shard_map/all_to_all | solution.py:461
  69.1 0.4 shard_map.90
  69.4 0.3 collective-permute-start.8
  69.8 1.3 %collective-permute-done.8.mates_ref.refs_1_ = bf16[8,8,16,128]{3,2,1,0:T(8,128)(2,1)S(1)} collective-permute-done((bf16[8,8,16,128]{3,2,1,0:T(8,128)(2,1)S(1)}, bf16[8,8,16,128]{3,2,1,0:T(8,128)(2,1)S(1)}, u32[]{:S(2)}, u32[]{:S(2)}) %collective-permute-start.8) | collective-permute-done | bytes 262176 | tf_op jit(solution)/shard_map/ppermute | solution.py:472
  71.0 0.0 copy-start
  71.0 0.0 copy-start.1
  71.1 1.8 %collective-permute-start.9 = (bf16[2,8,16,128]{3,2,1,0:T(8,128)(2,1)S(1)}, bf16[2,8,16,128]{3,2,1,0:T(8,128)(2,1)S(1)}, u32[]{:S(2)}, u32[]{:S(2)}) collective-permute-start(bf16[2,8,16,128]{3,2,1,0:T(8,128)(2,1)S(1)} %get-tuple-element.68), channel_id=1, source_target_pairs={{0,1},{1,0},{2,3},{3,2},{4,5},{5,4},{6,7},{7,6},{8,9},{9,8},{10,11... | collective-permute-start | bytes 196616 | tf_op jit(solution)/shard_map/ppermute | solution.py:472
  72.9 1.5 %collective-permute-start.10 = (bf16[2,8,16,128]{3,2,1,0:T(8,128)(2,1)S(1)}, bf16[2,8,16,128]{3,2,1,0:T(8,128)(2,1)S(1)}, u32[]{:S(2)}, u32[]{:S(2)}) collective-permute-start(bf16[2,8,16,128]{3,2,1,0:T(8,128)(2,1)S(1)} %get-tuple-element.69), channel_id=1, source_target_pairs={{0,4},{1,5},{2,6},{3,7},{4,0},{5,1},{6,2},{7,3},{8,12},{9,13},{10,... | collective-permute-start | bytes 196616 | tf_op jit(solution)/shard_map/ppermute | solution.py:472
  74.4 1.5 %collective-permute-start.11 = (bf16[2,8,16,128]{3,2,1,0:T(8,128)(2,1)S(1)}, bf16[2,8,16,128]{3,2,1,0:T(8,128)(2,1)S(1)}, u32[]{:S(2)}, u32[]{:S(2)}) collective-permute-start(bf16[2,8,16,128]{3,2,1,0:T(8,128)(2,1)S(1)} %get-tuple-element.70), channel_id=1, source_target_pairs={{0,13},{1,12},{2,15},{3,14},{4,9},{5,8},{6,11},{7,10},{8,5},{9,4},... | collective-permute-start | bytes 196616 | tf_op jit(solution)/shard_map/ppermute | solution.py:472
  75.8 1.5 %collective-permute-start.12 = (bf16[2,8,16,128]{3,2,1,0:T(8,128)(2,1)S(1)}, bf16[2,8,16,128]{3,2,1,0:T(8,128)(2,1)S(1)}, u32[]{:S(2)}, u32[]{:S(2)}) collective-permute-start(bf16[2,8,16,128]{3,2,1,0:T(8,128)(2,1)S(1)} %get-tuple-element.71), channel_id=1, source_target_pairs={{0,12},{1,13},{2,14},{3,15},{4,8},{5,9},{6,10},{7,11},{8,4},{9,5},... | collective-permute-start | bytes 196616 | tf_op jit(solution)/shard_map/ppermute | solution.py:472
  77.3 2.4 %collective-permute-start.13 = (bf16[2,8,16,128]{3,2,1,0:T(8,128)(2,1)S(1)}, bf16[2,8,16,128]{3,2,1,0:T(8,128)(2,1)S(1)}, u32[]{:S(2)}, u32[]{:S(2)}) collective-permute-start(bf16[2,8,16,128]{3,2,1,0:T(8,128)(2,1)S(1)} %get-tuple-element.72), channel_id=1, source_target_pairs={{0,9},{1,8},{2,11},{3,10},{4,13},{5,12},{6,15},{7,14},{8,1},{9,0},... | collective-permute-start | bytes 196616 | tf_op jit(solution)/shard_map/ppermute | solution.py:472
  79.7 0.0 collective-permute-done.9.refs_2_
  79.7 0.6 collective-permute-start.14
  80.2 0.0 collective-permute-done.10.refs_3_
  80.2 1.2 %collective-permute-start.15 = (bf16[2,8,16,128]{3,2,1,0:T(8,128)(2,1)S(1)}, bf16[2,8,16,128]{3,2,1,0:T(8,128)(2,1)S(1)}, u32[]{:S(2)}, u32[]{:S(2)}) collective-permute-start(bf16[2,8,16,128]{3,2,1,0:T(8,128)(2,1)S(1)} %get-tuple-element.74), channel_id=1, source_target_pairs={{0,5},{1,4},{2,7},{3,6},{4,1},{5,0},{6,3},{7,2},{8,13},{9,12},{10,... | collective-permute-start | bytes 196616 | tf_op jit(solution)/shard_map/ppermute | solution.py:472
  81.5 6.0 %shard_map.88 = (f32[4,128,128]{2,1,0:T(8,128)S(1)}, bf16[4,128,128]{2,1,0:T(8,128)(2,1)S(1)}, bf16[4,512,128]{2,1,0:T(8,128)(2,1)S(1)}, f32[16,128,128]{2,1,0:T...) custom-call(bf16[16,512,128]{2,1,0:T(8,128)(2,1)} %get-tuple-element.43.refs_0_.fac_hbm, ...), custom_call_target="tpu_custom_call" | custom-call | tf_op jit(solution)/shard_map/pallas_call | solution.py:52
  87.5 0.9 collective-permute-done.11.refs_4_
  88.4 1.6 %collective-permute-done.12.refs_5_ = bf16[2,8,16,128]{3,2,1,0:T(8,128)(2,1)S(1)} collective-permute-done((bf16[2,8,16,128]{3,2,1,0:T(8,128)(2,1)S(1)}, bf16[2,8,16,128]{3,2,1,0:T(8,128)(2,1)S(1)}, u32[]{:S(2)}, u32[]{:S(2)}) %collective-permute-start.12) | collective-permute-done | bytes 65568 | tf_op jit(solution)/shard_map/ppermute | solution.py:472
  90.0 2.8 %collective-permute-done.13.refs_6_ = bf16[2,8,16,128]{3,2,1,0:T(8,128)(2,1)S(1)} collective-permute-done((bf16[2,8,16,128]{3,2,1,0:T(8,128)(2,1)S(1)}, bf16[2,8,16,128]{3,2,1,0:T(8,128)(2,1)S(1)}, u32[]{:S(2)}, u32[]{:S(2)}) %collective-permute-start.13) | collective-permute-done | bytes 65568 | tf_op jit(solution)/shard_map/ppermute | solution.py:472
  92.8 1.3 %collective-permute-done.14.refs_7_ = bf16[2,8,16,128]{3,2,1,0:T(8,128)(2,1)S(1)} collective-permute-done((bf16[2,8,16,128]{3,2,1,0:T(8,128)(2,1)S(1)}, bf16[2,8,16,128]{3,2,1,0:T(8,128)(2,1)S(1)}, u32[]{:S(2)}, u32[]{:S(2)}) %collective-permute-start.14) | collective-permute-done | bytes 65568 | tf_op jit(solution)/shard_map/ppermute | solution.py:472
  94.2 0.0 collective-permute-done.15.refs_8_
  94.2 1.7 %all-to-all-done.3.r_ref = bf16[32,8,16,128]{3,2,1,0:T(8,128)(2,1)S(1)} async-done(((bf16[32,8,16,128]{3,2,1,0:T(8,128)(2,1)}), bf16[32,8,16,128]{3,2,1,0:T(8,128)(2,1)S(1)}, u32[]{:S(2)}, u32[]{:S(2)}) %all-to-all-start.3) | async-done | bytes 1048608 | tf_op jit(solution)/shard_map/all_to_all | solution.py:461
  95.9 0.0 copy-done
  95.9 0.0 copy-done.1
  95.9 3.9 %shard_map.92 = bf16[16,128,128]{2,1,0:T(8,128)(2,1)} custom-call(bf16[16,512,128]{2,1,0:T(8,128)(2,1)} %get-tuple-element.43.refs_0_.fac_hbm, bf16[16,128,128]{2,1,0:T(8,128)(2,1)} %get-tuple-element.58.nt_hbm, f32[16,128,128]{2,1,0:T(8,128)} %get-tuple-element.59.gin_hbm, bf16[4,512,128]{2,1,0:T(8,128)(2,1)S(1)} %get-tuple-element.60.fac0_ref, ...), custom_call_target="tpu_custom_call" | custom-call | tf_op jit(solution)/shard_map/pallas_call | solution.py:52
  (2 shorter events, 0.1 us)
Async XLA Ops:
  3.5 34.1 %all-to-all-start = ((bf16[32,8,16,128]{3,2,1,0:T(8,128)(2,1)}), bf16[32,8,16,128]{3,2,1,0:T(8,128)(2,1)S(1)}, u32[]{:S(2)}, u32[]{:S(2)}) async-start(bf16[32,8,16,128]{3,2,1,0:T(8,128)(2,1)} %get-tuple-element.40), calls=%async_computation | async-start | bytes 2097152 | tf_op jit(solution)/shard_map/all_to_all | solution.py:461
  13.0 1.6 %collective-permute-start = (bf16[8,8,16,128]{3,2,1,0:T(8,128)(2,1)S(1)}, bf16[8,8,16,128]{3,2,1,0:T(8,128)(2,1)S(1)}, u32[]{:S(2)}, u32[]{:S(2)}) collective-permute-start(bf16[8,8,16,128]{3,2,1,0:T(8,128)(2,1)S(1)} %get-tuple-element.47), channel_id=1, source_target_pairs={{0,2},{1,3},{2,0},{3,1},{4,6},{5,7},{6,4},{7,5},{8,10},{9,11},{10,... | collective-permute-start | bytes 786440 | tf_op jit(solution)/shard_map/ppermute | solution.py:472
  14.6 8.6 %collective-permute-start.1 = (bf16[2,8,16,128]{3,2,1,0:T(8,128)(2,1)S(1)}, bf16[2,8,16,128]{3,2,1,0:T(8,128)(2,1)S(1)}, u32[]{:S(2)}, u32[]{:S(2)}) collective-permute-start(bf16[2,8,16,128]{3,2,1,0:T(8,128)(2,1)S(1)} %get-tuple-element.48), channel_id=1, source_target_pairs={{0,1},{1,0},{2,3},{3,2},{4,5},{5,4},{6,7},{7,6},{8,9},{9,8},{10,11... | collective-permute-start | bytes 196616 | tf_op jit(solution)/shard_map/ppermute | solution.py:472
  16.4 7.3 %collective-permute-start.2 = (bf16[2,8,16,128]{3,2,1,0:T(8,128)(2,1)S(1)}, bf16[2,8,16,128]{3,2,1,0:T(8,128)(2,1)S(1)}, u32[]{:S(2)}, u32[]{:S(2)}) collective-permute-start(bf16[2,8,16,128]{3,2,1,0:T(8,128)(2,1)S(1)} %get-tuple-element.49), channel_id=1, source_target_pairs={{0,4},{1,5},{2,6},{3,7},{4,0},{5,1},{6,2},{7,3},{8,12},{9,13},{10,... | collective-permute-start | bytes 196616 | tf_op jit(solution)/shard_map/ppermute | solution.py:472
  17.9 19.7 %collective-permute-start.3 = (bf16[2,8,16,128]{3,2,1,0:T(8,128)(2,1)S(1)}, bf16[2,8,16,128]{3,2,1,0:T(8,128)(2,1)S(1)}, u32[]{:S(2)}, u32[]{:S(2)}) collective-permute-start(bf16[2,8,16,128]{3,2,1,0:T(8,128)(2,1)S(1)} %get-tuple-element.50), channel_id=1, source_target_pairs={{0,13},{1,12},{2,15},{3,14},{4,9},{5,8},{6,11},{7,10},{8,5},{9,4},... | collective-permute-start | bytes 196616 | tf_op jit(solution)/shard_map/ppermute | solution.py:472
  19.4 18.2 %collective-permute-start.4 = (bf16[2,8,16,128]{3,2,1,0:T(8,128)(2,1)S(1)}, bf16[2,8,16,128]{3,2,1,0:T(8,128)(2,1)S(1)}, u32[]{:S(2)}, u32[]{:S(2)}) collective-permute-start(bf16[2,8,16,128]{3,2,1,0:T(8,128)(2,1)S(1)} %get-tuple-element.51), channel_id=1, source_target_pairs={{0,12},{1,13},{2,14},{3,15},{4,8},{5,9},{6,10},{7,11},{8,4},{9,5},... | collective-permute-start | bytes 196616 | tf_op jit(solution)/shard_map/ppermute | solution.py:472
  20.8 16.7 %collective-permute-start.5 = (bf16[2,8,16,128]{3,2,1,0:T(8,128)(2,1)S(1)}, bf16[2,8,16,128]{3,2,1,0:T(8,128)(2,1)S(1)}, u32[]{:S(2)}, u32[]{:S(2)}) collective-permute-start(bf16[2,8,16,128]{3,2,1,0:T(8,128)(2,1)S(1)} %get-tuple-element.52), channel_id=1, source_target_pairs={{0,9},{1,8},{2,11},{3,10},{4,13},{5,12},{6,15},{7,14},{8,1},{9,0},... | collective-permute-start | bytes 196616 | tf_op jit(solution)/shard_map/ppermute | solution.py:472
  23.2 14.4 %collective-permute-start.6 = (bf16[2,8,16,128]{3,2,1,0:T(8,128)(2,1)S(1)}, bf16[2,8,16,128]{3,2,1,0:T(8,128)(2,1)S(1)}, u32[]{:S(2)}, u32[]{:S(2)}) collective-permute-start(bf16[2,8,16,128]{3,2,1,0:T(8,128)(2,1)S(1)} %get-tuple-element.53), channel_id=1, source_target_pairs={{0,8},{1,9},{2,10},{3,11},{4,12},{5,13},{6,14},{7,15},{8,0},{9,1},... | collective-permute-start | bytes 196616 | tf_op jit(solution)/shard_map/ppermute | solution.py:472
  23.8 13.8 %collective-permute-start.7 = (bf16[2,8,16,128]{3,2,1,0:T(8,128)(2,1)S(1)}, bf16[2,8,16,128]{3,2,1,0:T(8,128)(2,1)S(1)}, u32[]{:S(2)}, u32[]{:S(2)}) collective-permute-start(bf16[2,8,16,128]{3,2,1,0:T(8,128)(2,1)S(1)} %get-tuple-element.54), channel_id=1, source_target_pairs={{0,5},{1,4},{2,7},{3,6},{4,1},{5,0},{6,3},{7,2},{8,13},{9,12},{10,... | collective-permute-start | bytes 196616 | tf_op jit(solution)/shard_map/ppermute | solution.py:472
  65.3 30.6 %all-to-all-start.3 = ((bf16[32,8,16,128]{3,2,1,0:T(8,128)(2,1)}), bf16[32,8,16,128]{3,2,1,0:T(8,128)(2,1)S(1)}, u32[]{:S(2)}, u32[]{:S(2)}) async-start(bf16[32,8,16,128]{3,2,1,0:T(8,128)(2,1)} %shard_map.89), calls=%async_computation.3 | async-start | bytes 2097152 | tf_op jit(solution)/shard_map/all_to_all | solution.py:461
  69.4 1.6 %collective-permute-start.8 = (bf16[8,8,16,128]{3,2,1,0:T(8,128)(2,1)S(1)}, bf16[8,8,16,128]{3,2,1,0:T(8,128)(2,1)S(1)}, u32[]{:S(2)}, u32[]{:S(2)}) collective-permute-start(bf16[8,8,16,128]{3,2,1,0:T(8,128)(2,1)S(1)} %get-tuple-element.67), channel_id=1, source_target_pairs={{0,2},{1,3},{2,0},{3,1},{4,6},{5,7},{6,4},{7,5},{8,10},{9,11},{10,... | collective-permute-start | bytes 786440 | tf_op jit(solution)/shard_map/ppermute | solution.py:472
  71.0 24.8 %copy-start = (bf16[128,640]{1,0:T(8,128)(2,1)S(1)}, bf16[128,640]{1,0:T(8,128)(2,1)}, u32[]{:S(2)}) copy-start(bf16[128,640]{1,0:T(8,128)(2,1)} %w_ref.1) | copy-start | bytes 491524
  71.0 24.8 %copy-start.1 = (f32[128]{0:T(128)S(1)}, f32[128]{0:T(128)}, u32[]{:S(2)}) copy-start(f32[128]{0:T(128)} %param.10) | copy-start | bytes 1540
  71.1 8.6 %collective-permute-start.9 = (bf16[2,8,16,128]{3,2,1,0:T(8,128)(2,1)S(1)}, bf16[2,8,16,128]{3,2,1,0:T(8,128)(2,1)S(1)}, u32[]{:S(2)}, u32[]{:S(2)}) collective-permute-start(bf16[2,8,16,128]{3,2,1,0:T(8,128)(2,1)S(1)} %get-tuple-element.68), channel_id=1, source_target_pairs={{0,1},{1,0},{2,3},{3,2},{4,5},{5,4},{6,7},{7,6},{8,9},{9,8},{10,11... | collective-permute-start | bytes 196616 | tf_op jit(solution)/shard_map/ppermute | solution.py:472
  72.9 7.3 %collective-permute-start.10 = (bf16[2,8,16,128]{3,2,1,0:T(8,128)(2,1)S(1)}, bf16[2,8,16,128]{3,2,1,0:T(8,128)(2,1)S(1)}, u32[]{:S(2)}, u32[]{:S(2)}) collective-permute-start(bf16[2,8,16,128]{3,2,1,0:T(8,128)(2,1)S(1)} %get-tuple-element.69), channel_id=1, source_target_pairs={{0,4},{1,5},{2,6},{3,7},{4,0},{5,1},{6,2},{7,3},{8,12},{9,13},{10,... | collective-permute-start | bytes 196616 | tf_op jit(solution)/shard_map/ppermute | solution.py:472
  74.4 14.0 %collective-permute-start.11 = (bf16[2,8,16,128]{3,2,1,0:T(8,128)(2,1)S(1)}, bf16[2,8,16,128]{3,2,1,0:T(8,128)(2,1)S(1)}, u32[]{:S(2)}, u32[]{:S(2)}) collective-permute-start(bf16[2,8,16,128]{3,2,1,0:T(8,128)(2,1)S(1)} %get-tuple-element.70), channel_id=1, source_target_pairs={{0,13},{1,12},{2,15},{3,14},{4,9},{5,8},{6,11},{7,10},{8,5},{9,4},... | collective-permute-start | bytes 196616 | tf_op jit(solution)/shard_map/ppermute | solution.py:472
  75.8 14.2 %collective-permute-start.12 = (bf16[2,8,16,128]{3,2,1,0:T(8,128)(2,1)S(1)}, bf16[2,8,16,128]{3,2,1,0:T(8,128)(2,1)S(1)}, u32[]{:S(2)}, u32[]{:S(2)}) collective-permute-start(bf16[2,8,16,128]{3,2,1,0:T(8,128)(2,1)S(1)} %get-tuple-element.71), channel_id=1, source_target_pairs={{0,12},{1,13},{2,14},{3,15},{4,8},{5,9},{6,10},{7,11},{8,4},{9,5},... | collective-permute-start | bytes 196616 | tf_op jit(solution)/shard_map/ppermute | solution.py:472
  77.3 15.5 %collective-permute-start.13 = (bf16[2,8,16,128]{3,2,1,0:T(8,128)(2,1)S(1)}, bf16[2,8,16,128]{3,2,1,0:T(8,128)(2,1)S(1)}, u32[]{:S(2)}, u32[]{:S(2)}) collective-permute-start(bf16[2,8,16,128]{3,2,1,0:T(8,128)(2,1)S(1)} %get-tuple-element.72), channel_id=1, source_target_pairs={{0,9},{1,8},{2,11},{3,10},{4,13},{5,12},{6,15},{7,14},{8,1},{9,0},... | collective-permute-start | bytes 196616 | tf_op jit(solution)/shard_map/ppermute | solution.py:472
  79.7 14.5 %collective-permute-start.14 = (bf16[2,8,16,128]{3,2,1,0:T(8,128)(2,1)S(1)}, bf16[2,8,16,128]{3,2,1,0:T(8,128)(2,1)S(1)}, u32[]{:S(2)}, u32[]{:S(2)}) collective-permute-start(bf16[2,8,16,128]{3,2,1,0:T(8,128)(2,1)S(1)} %get-tuple-element.73), channel_id=1, source_target_pairs={{0,8},{1,9},{2,10},{3,11},{4,12},{5,13},{6,14},{7,15},{8,0},{9,1},... | collective-permute-start | bytes 196616 | tf_op jit(solution)/shard_map/ppermute | solution.py:472
  80.2 13.9 %collective-permute-start.15 = (bf16[2,8,16,128]{3,2,1,0:T(8,128)(2,1)S(1)}, bf16[2,8,16,128]{3,2,1,0:T(8,128)(2,1)S(1)}, u32[]{:S(2)}, u32[]{:S(2)}) collective-permute-start(bf16[2,8,16,128]{3,2,1,0:T(8,128)(2,1)S(1)} %get-tuple-element.74), channel_id=1, source_target_pairs={{0,5},{1,4},{2,7},{3,6},{4,1},{5,0},{6,3},{7,2},{8,13},{9,12},{10,... | collective-permute-start | bytes 196616 | tf_op jit(solution)/shard_map/ppermute | solution.py:472

commit v6 on v4

--- a/solution.py
+++ b/solution.py
@@ -316,7 +316,7 @@
         normal_out = (tri_hat * ogain + obias).astype(BF16)
         mixed = dot(normal_out, ow_ref[...], 0, 0)
         grad_logit = cot_ref[i].astype(F32) * mixed * out_gate * (1.0 - out_gate)
-        gin_ref[i] = dot(w_ref[:, 4 * width :], grad_logit.astype(BF16), 1, 1)
+        gin_ref[i] = dot(w_ref[:, 4 * width :], grad_logit.astype(BF16), 1, 1).astype(BF16)
         nt_ref[i] = normed.T.astype(BF16)
         s_ref[pl.ds(i, 1), :] = jnp.broadcast_to(scale_inv, (cols, width)).T[:1]
         return 0
@@ -338,7 +338,7 @@
     lay, fac_hbm, nt_hbm, gin_hbm, fac0_ref, nt0_ref, gin0_ref, r_ref, s_ref, gain_ref, w_ref, *refs
 ):
     l_refs, refs = refs[: lay.n_hops], refs[lay.n_hops :]
-    out_hbm, l_ref, ls_ref, rs_ref, fac_ref, nt_ref, gin_ref, out_ref, sems = refs
+    out_hbm, l_ref, ls_ref, rs_ref, fac_ref, nt_ref, gin_ref, out_ref, sems, out_sems = refs
     rows, cols, width = out_ref.shape
     mine = width // lay.half
     parts = sems.shape[1]
@@ -352,9 +352,9 @@
             pltpu.make_async_copy(gin_hbm.at[here], gin_ref.at[here], sems.at[2, p]),
         ]
 
-    def send(p):
-        here = pl.ds(p * size, size)
-        return pltpu.make_async_copy(out_ref.at[here], out_hbm.at[here], sems.at[3, p])
+    def send(n):
+        here = pl.ds(2 * n, 2)
+        return pltpu.make_async_copy(out_ref.at[here], out_hbm.at[here], out_sems.at[n])
 
     for p in range(1, parts):
         for copy in fetch(p):
@@ -397,22 +397,21 @@
                 )
             grad_in = dot(w_ref[:, : 4 * width], jnp.concatenate(blocks, axis=1), 1, 0)
             for m in range(2):
-                grad = (grad_in[:, m * cols : (m + 1) * cols] + gin_here[i + m]) * gain
+                grad = (grad_in[:, m * cols : (m + 1) * cols] + gin_here[i + m].astype(F32)) * gain
                 scale_inv = s_ref[pl.ds(i + m, 1), :]
                 normed = nt_here[i + m].astype(F32)
                 result = norm_back(grad, normed, scale_inv, 0).astype(BF16)
                 out_ref[i + m] = dot(eye, result, 1, 1).astype(BF16)
+            send(i // 2).start()
 
     part(0, fac0_ref, nt0_ref, gin0_ref)
-    send(0).start()
     for p in range(1, parts):
         for copy in fetch(p):
             copy.wait()
     for p in range(1, parts):
         part(p, fac_ref, nt_ref, gin_ref)
-        send(p).start()
-    for p in range(parts):
-        send(p).wait()
+    for n in range(rows // 2):
+        send(n).wait()
 
 
 class Layout:
@@ -422,8 +421,14 @@
         self.half = self.devices // 2
         outer = math.isqrt(n_row)
         self.inner = self.devices // outer
-        self.order = [o * self.inner + n for n in range(self.inner) for o in range(outer)]
-        self.inside = [o * self.inner + n for n in range(self.inner) for o in range(outer // 2)]
+        near = [
+            2 * n_ch * far + n_ch * core + b
+            for far in range(self.inner // (2 * n_ch))
+            for b in range(n_ch)
+            for core in range(2)
+        ]
+        self.order = [o * self.inner + n for n in near for o in range(outer)]
+        self.inside = [o * self.inner + n for n in near for o in range(outer // 2)]
         self.mate = n_ch
         self.hops = [s for s in range(self.half) if s & self.mate == 0]
         self.hops[3:] = self.hops[:2:-1]
@@ -621,16 +626,16 @@
     grad_in_first, normed_first, fac_first, grad_in, normed_t, scale = call(
         functools.partial(logit_kernel, lay),
         [
-            pltpu.VMEM((rows // PARTS, width, cols), F32),
+            pltpu.VMEM((rows // PARTS, width, cols), BF16),
             pltpu.VMEM((rows // PARTS, width, cols), BF16),
             pltpu.VMEM((rows // PARTS, 4 * width, cols), BF16),
-            pltpu.HBM((rows, width, cols), F32),
+            pltpu.HBM((rows, width, cols), BF16),
             pltpu.HBM((rows, width, cols), BF16),
             pltpu.VMEM((rows, cols), F32),
         ],
         [
             half,
-            pltpu.VMEM((rows, width, cols), F32),
+            half,
             half,
             pltpu.SemaphoreType.DMA((2,)),
             one_here,
@@ -665,9 +670,10 @@
             half,
             pltpu.VMEM((rows, 4 * width, cols), BF16),
             half,
-            pltpu.VMEM((rows, width, cols), F32),
-            half,
-            pltpu.SemaphoreType.DMA((4, PARTS)),
+            half,
+            half,
+            pltpu.SemaphoreType.DMA((3, PARTS)),
+            pltpu.SemaphoreType.DMA((rows // 2,)),
         ],
         fac,
         normed_t,
@@ -770,6 +776,7 @@
             devices & (devices - 1) == 0
             and n_row >= 4
             and n_row % outer == 0
+            and (devices // outer) % (2 * n_ch) == 0
             and outer % 2 == 0
             and width % (devices // 2) == 0
             and rows % (2 * PARTS) == 0

time: 100 us -> 99.1 us (level); the launches traced: 99.7 us -> 97.4 us
  waiting for transfers between devices: 18.8 us -> 16.2 us
    all_to_all x2, waiting for transfers between devices: 9.47 us -> 6.22 us  [exchange_all(): lax.all_to_all(blocks, ('row', 'ch'), split_axis=0, concat_axis=0, tiled=...]
  transfers between devices with their start and end apart: 18 -> 18, of which waited for: 8 -> 9; matrix products, arithmetic and copies ran while one was open for 0% -> 0% of each run, Pallas kernels for 14% -> 14%
where the time goes in v6:
time: 99.1 us; the launch traced here: 97.4 us
  starting transfers between devices  31.5 us (32%)
  blocking collectives  25.3 us (26%)
  Pallas kernels  24.2 us (24%)
  waiting for transfers between devices  16.2 us (16%)
    all_to_all x2, blocking collectives, exchange_half(): lax.all_to_all(blocks, ('row', 'ch'), split_axis=0, concat_axis=0, tiled=...  25.3 us
    pallas_call x10, Pallas kernels, call(): pl.pallas_call(kernel, out_shape=outs if single else tuple(outs), in_spec...  24.2 us
    ppermute x16, starting transfers between devices, swap(): lax.ppermute(block, ('row', 'ch'), [(n, n ^ s) for n in range(self.device...  20.1 us
    all_to_all x2, starting transfers between devices, exchange_all(): lax.all_to_all(blocks, ('row', 'ch'), split_axis=0, concat_axis=0, tiled=...  11.5 us
    ppermute x16, waiting for transfers between devices, swap(): lax.ppermute(block, ('row', 'ch'), [(n, n ^ s) for n in range(self.device...  10 us
    all_to_all x2, waiting for transfers between devices, exchange_all(): lax.all_to_all(blocks, ('row', 'ch'), split_axis=0, concat_axis=0, tiled=...  6.22 us
  transfers between devices with their start and end apart: 18, of which 9 were waited for; matrix products, arithmetic and copies ran while one was open for 0% of the time, Pallas kernels for 14%

profile of v6, /device:TPU:0, one launch (start us, length us, event | category | flops | bytes accessed | tf_op | source)
XLA Modules:
  0.0 97.4 jit_solution(10577462138722270181)
XLA Ops:
  0.0 3.4 %shard_map.82 = (bf16[32,8,16,128]{3,2,1,0:T(8,128)(2,1)}, bf16[8,128,256]{2,1,0:T(8,128)(2,1)S(1)}) custom-call(bf16[16,128,128]{2,1,0:T(8,128)(2,1)} %refs_2_.1, f32[1,128]{1,0:T(1,128)} %bitcast.4, f32[1,128]{1,0:T(1,128)} %bitcast.8, bf16[128,640]{1,0:T(8,128)(2,1)} %w_ref.1), custom_call_target="tpu_custom_call" | custom-call | tf_op jit(solution)/shard_map/pallas_call | solution.py:52
  3.4 7.3 %all-to-all-start = ((bf16[32,8,16,128]{3,2,1,0:T(8,128)(2,1)}), bf16[32,8,16,128]{3,2,1,0:T(8,128)(2,1)S(1)}, u32[]{:S(2)}, u32[]{:S(2)}) async-start(bf16[32,8,16,128]{3,2,1,0:T(8,128)(2,1)} %get-tuple-element.41), calls=%async_computation | async-start | bytes 2097152 | tf_op jit(solution)/shard_map/all_to_all | solution.py:451
  10.8 2.2 %shard_map.84 = (bf16[8,8,16,128]{3,2,1,0:T(8,128)(2,1)S(1)}, bf16[8,8,16,128]{3,2,1,0:T(8,128)(2,1)S(1)}) custom-call(bf16[128,640]{1,0:T(8,128)(2,1)} %w_ref.1, bf16[8,128,256]{2,1,0:T(8,128)(2,1)S(1)} %get-tuple-element.46.n_ref), custom_call_target="tpu_custom_call" | custom-call | tf_op jit(solution)/shard_map/pallas_call | solution.py:52
  12.9 0.3 collective-permute-start
  13.3 1.3 %collective-permute-done.mates_ref.refs_1_ = bf16[8,8,16,128]{3,2,1,0:T(8,128)(2,1)S(1)} collective-permute-done((bf16[8,8,16,128]{3,2,1,0:T(8,128)(2,1)S(1)}, bf16[8,8,16,128]{3,2,1,0:T(8,128)(2,1)S(1)}, u32[]{:S(2)}, u32[]{:S(2)}) %collective-permute-start) | collective-permute-done | bytes 262176 | tf_op jit(solution)/shard_map/ppermute | solution.py:462
  14.6 1.8 %collective-permute-start.1 = (bf16[2,8,16,128]{3,2,1,0:T(8,128)(2,1)S(1)}, bf16[2,8,16,128]{3,2,1,0:T(8,128)(2,1)S(1)}, u32[]{:S(2)}, u32[]{:S(2)}) collective-permute-start(bf16[2,8,16,128]{3,2,1,0:T(8,128)(2,1)S(1)} %get-tuple-element.49), channel_id=1, source_target_pairs={{0,1},{1,0},{2,3},{3,2},{4,5},{5,4},{6,7},{7,6},{8,9},{9,8},{10,11... | collective-permute-start | bytes 196616 | tf_op jit(solution)/shard_map/ppermute | solution.py:462
  16.4 1.5 %collective-permute-start.2 = (bf16[2,8,16,128]{3,2,1,0:T(8,128)(2,1)S(1)}, bf16[2,8,16,128]{3,2,1,0:T(8,128)(2,1)S(1)}, u32[]{:S(2)}, u32[]{:S(2)}) collective-permute-start(bf16[2,8,16,128]{3,2,1,0:T(8,128)(2,1)S(1)} %get-tuple-element.50), channel_id=1, source_target_pairs={{0,4},{1,5},{2,6},{3,7},{4,0},{5,1},{6,2},{7,3},{8,12},{9,13},{10,... | collective-permute-start | bytes 196616 | tf_op jit(solution)/shard_map/ppermute | solution.py:462
  17.9 1.5 %collective-permute-start.3 = (bf16[2,8,16,128]{3,2,1,0:T(8,128)(2,1)S(1)}, bf16[2,8,16,128]{3,2,1,0:T(8,128)(2,1)S(1)}, u32[]{:S(2)}, u32[]{:S(2)}) collective-permute-start(bf16[2,8,16,128]{3,2,1,0:T(8,128)(2,1)S(1)} %get-tuple-element.51), channel_id=1, source_target_pairs={{0,13},{1,12},{2,15},{3,14},{4,9},{5,8},{6,11},{7,10},{8,5},{9,4},... | collective-permute-start | bytes 196616 | tf_op jit(solution)/shard_map/ppermute | solution.py:462
  19.3 1.5 %collective-permute-start.4 = (bf16[2,8,16,128]{3,2,1,0:T(8,128)(2,1)S(1)}, bf16[2,8,16,128]{3,2,1,0:T(8,128)(2,1)S(1)}, u32[]{:S(2)}, u32[]{:S(2)}) collective-permute-start(bf16[2,8,16,128]{3,2,1,0:T(8,128)(2,1)S(1)} %get-tuple-element.52), channel_id=1, source_target_pairs={{0,12},{1,13},{2,14},{3,15},{4,8},{5,9},{6,10},{7,11},{8,4},{9,5},... | collective-permute-start | bytes 196616 | tf_op jit(solution)/shard_map/ppermute | solution.py:462
  20.8 2.4 %collective-permute-start.5 = (bf16[2,8,16,128]{3,2,1,0:T(8,128)(2,1)S(1)}, bf16[2,8,16,128]{3,2,1,0:T(8,128)(2,1)S(1)}, u32[]{:S(2)}, u32[]{:S(2)}) collective-permute-start(bf16[2,8,16,128]{3,2,1,0:T(8,128)(2,1)S(1)} %get-tuple-element.53), channel_id=1, source_target_pairs={{0,9},{1,8},{2,11},{3,10},{4,13},{5,12},{6,15},{7,14},{8,1},{9,0},... | collective-permute-start | bytes 196616 | tf_op jit(solution)/shard_map/ppermute | solution.py:462
  23.2 0.0 collective-permute-done.1.refs_2_
  23.2 0.6 collective-permute-start.6
  23.7 0.0 collective-permute-done.2.refs_3_
  23.7 0.3 collective-permute-start.7
  24.0 5.7 %shard_map.83 = (f32[16,128,128]{2,1,0:T(8,128)S(1)}, bf16[16,512,128]{2,1,0:T(8,128)(2,1)}) custom-call(bf16[16,128,128]{2,1,0:T(8,128)(2,1)} %refs_2_.1, bf16[16,128,128]{2,1,0:T(8,128)(2,1)} %refs_3_.1, f32[1,128]{1,0:T(1,128)} %bitcast.5, f32[1,128]{1,0:T(1,128)} %bitcast.9, bf16[128,640]{1,0:T(8,128)(2,1)} %w_ref.1, f32[1,128]{1,0:T(1,128)} %bitcast.11, ...), custom_call_target="tpu_custom_call" | custom-call | tf_op jit(solution)/shard_map/pallas_call | solution.py:52
  29.7 6.1 %all-to-all-done.r_ref = bf16[32,8,16,128]{3,2,1,0:T(8,128)(2,1)S(1)} async-done(((bf16[32,8,16,128]{3,2,1,0:T(8,128)(2,1)}), bf16[32,8,16,128]{3,2,1,0:T(8,128)(2,1)S(1)}, u32[]{:S(2)}, u32[]{:S(2)}) %all-to-all-start) | async-done | bytes 1048608 | tf_op jit(solution)/shard_map/all_to_all | solution.py:451
  35.8 0.0 collective-permute-done.3.refs_4_
  35.8 0.0 collective-permute-done.4.refs_5_
  35.8 0.0 collective-permute-done.5.refs_6_
  35.8 0.0 collective-permute-done.6.refs_7_
  35.8 0.0 collective-permute-done.7.refs_8_
  35.8 0.5 shard_map.86
  36.3 13.0 %all_to_all.20.t_ref = bf16[16,8,16,128]{3,2,1,0:T(8,128)(2,1)S(1)} all-to-all(bf16[16,8,16,128]{3,2,1,0:T(8,128)(2,1)S(1)} %get-tuple-element.56), channel_id=1, replica_groups={{0,8,2,10,1,9,3,11,4,12,6,14,5,13,7,15},{16,24,18,26,17,25,19,27,20,28,..., dimensions={0} | all-to-all | bytes 1048576 | tf_op jit(solution)/shard_map/all_to_all | solution.py:457
  49.3 1.2 %shard_map.87 = (bf16[16,8,16,128]{3,2,1,0:T(8,128)(2,1)S(1)}, bf16[16,8,16,128]{3,2,1,0:T(8,128)(2,1)}) custom-call(bf16[16,8,16,128]{3,2,1,0:T(8,128)(2,1)S(1)} %all_to_all.20.t_ref, f32[16,128,128]{2,1,0:T(8,128)S(1)} %get-tuple-element.57.h_ref), custom_call_target="tpu_custom_call" | custom-call | tf_op jit(solution)/shard_map/pallas_call | solution.py:52
  50.5 12.3 %all_to_all.21.gt_ref = bf16[16,8,16,128]{3,2,1,0:T(8,128)(2,1)S(1)} all-to-all(bf16[16,8,16,128]{3,2,1,0:T(8,128)(2,1)S(1)} %get-tuple-element.64), channel_id=1, replica_groups={{0,8,2,10,1,9,3,11,4,12,6,14,5,13,7,15},{16,24,18,26,17,25,19,27,20,28,..., dimensions={0} | all-to-all | bytes 1048576 | tf_op jit(solution)/shard_map/all_to_all | solution.py:457
  62.9 1.3 %shard_map.89 = (bf16[32,8,16,128]{3,2,1,0:T(8,128)(2,1)}, bf16[8,8,16,128]{3,2,1,0:T(8,128)(2,1)S(1)}, bf16[8,8,16,128]{3,2,1,0:T(8,128)(2,1)S(1)}) custom-call(bf16[16,8,16,128]{3,2,1,0:T(8,128)(2,1)S(1)} %all_to_all.21.gt_ref, bf16[16,8,16,128]{3,2,1,0:T(8,128)(2,1)S(1)} %get-tuple-element.65.l_ref, bf16[32,8,16,128]{3,2,1,0:T(8,128)(2,1)S(1)} %all-to-all-done.r_ref), custom_call_target="tpu_custom_call" | custom-call | tf_op jit(solution)/shard_map/pallas_call | solution.py:52
  64.2 4.2 %all-to-all-start.3 = ((bf16[32,8,16,128]{3,2,1,0:T(8,128)(2,1)}), bf16[32,8,16,128]{3,2,1,0:T(8,128)(2,1)S(1)}, u32[]{:S(2)}, u32[]{:S(2)}) async-start(bf16[32,8,16,128]{3,2,1,0:T(8,128)(2,1)} %get-tuple-element.66), calls=%async_computation.3 | async-start | bytes 2097152 | tf_op jit(solution)/shard_map/all_to_all | solution.py:451
  68.4 0.3 collective-permute-start.8
  68.7 1.3 %collective-permute-done.8.mates_ref.refs_1_ = bf16[8,8,16,128]{3,2,1,0:T(8,128)(2,1)S(1)} collective-permute-done((bf16[8,8,16,128]{3,2,1,0:T(8,128)(2,1)S(1)}, bf16[8,8,16,128]{3,2,1,0:T(8,128)(2,1)S(1)}, u32[]{:S(2)}, u32[]{:S(2)}) %collective-permute-start.8) | collective-permute-done | bytes 262176 | tf_op jit(solution)/shard_map/ppermute | solution.py:462
  70.0 0.0 copy-start
  70.0 0.0 copy-start.1
  70.0 1.8 %collective-permute-start.9 = (bf16[2,8,16,128]{3,2,1,0:T(8,128)(2,1)S(1)}, bf16[2,8,16,128]{3,2,1,0:T(8,128)(2,1)S(1)}, u32[]{:S(2)}, u32[]{:S(2)}) collective-permute-start(bf16[2,8,16,128]{3,2,1,0:T(8,128)(2,1)S(1)} %get-tuple-element.70), channel_id=1, source_target_pairs={{0,1},{1,0},{2,3},{3,2},{4,5},{5,4},{6,7},{7,6},{8,9},{9,8},{10,11... | collective-permute-start | bytes 196616 | tf_op jit(solution)/shard_map/ppermute | solution.py:462
  71.9 1.5 %collective-permute-start.10 = (bf16[2,8,16,128]{3,2,1,0:T(8,128)(2,1)S(1)}, bf16[2,8,16,128]{3,2,1,0:T(8,128)(2,1)S(1)}, u32[]{:S(2)}, u32[]{:S(2)}) collective-permute-start(bf16[2,8,16,128]{3,2,1,0:T(8,128)(2,1)S(1)} %get-tuple-element.71), channel_id=1, source_target_pairs={{0,4},{1,5},{2,6},{3,7},{4,0},{5,1},{6,2},{7,3},{8,12},{9,13},{10,... | collective-permute-start | bytes 196616 | tf_op jit(solution)/shard_map/ppermute | solution.py:462
  73.3 1.5 %collective-permute-start.11 = (bf16[2,8,16,128]{3,2,1,0:T(8,128)(2,1)S(1)}, bf16[2,8,16,128]{3,2,1,0:T(8,128)(2,1)S(1)}, u32[]{:S(2)}, u32[]{:S(2)}) collective-permute-start(bf16[2,8,16,128]{3,2,1,0:T(8,128)(2,1)S(1)} %get-tuple-element.72), channel_id=1, source_target_pairs={{0,13},{1,12},{2,15},{3,14},{4,9},{5,8},{6,11},{7,10},{8,5},{9,4},... | collective-permute-start | bytes 196616 | tf_op jit(solution)/shard_map/ppermute | solution.py:462
  74.8 1.5 %collective-permute-start.12 = (bf16[2,8,16,128]{3,2,1,0:T(8,128)(2,1)S(1)}, bf16[2,8,16,128]{3,2,1,0:T(8,128)(2,1)S(1)}, u32[]{:S(2)}, u32[]{:S(2)}) collective-permute-start(bf16[2,8,16,128]{3,2,1,0:T(8,128)(2,1)S(1)} %get-tuple-element.73), channel_id=1, source_target_pairs={{0,12},{1,13},{2,14},{3,15},{4,8},{5,9},{6,10},{7,11},{8,4},{9,5},... | collective-permute-start | bytes 196616 | tf_op jit(solution)/shard_map/ppermute | solution.py:462
  76.2 2.4 %collective-permute-start.13 = (bf16[2,8,16,128]{3,2,1,0:T(8,128)(2,1)S(1)}, bf16[2,8,16,128]{3,2,1,0:T(8,128)(2,1)S(1)}, u32[]{:S(2)}, u32[]{:S(2)}) collective-permute-start(bf16[2,8,16,128]{3,2,1,0:T(8,128)(2,1)S(1)} %get-tuple-element.74), channel_id=1, source_target_pairs={{0,9},{1,8},{2,11},{3,10},{4,13},{5,12},{6,15},{7,14},{8,1},{9,0},... | collective-permute-start | bytes 196616 | tf_op jit(solution)/shard_map/ppermute | solution.py:462
  78.6 0.0 collective-permute-done.9.refs_2_
  78.6 0.8 collective-permute-start.14
  79.4 0.8 collective-permute-done.10.refs_3_
  80.2 0.7 collective-permute-start.15
  80.8 5.8 %shard_map.88 = (bf16[4,128,128]{2,1,0:T(8,128)(2,1)S(1)}, bf16[4,128,128]{2,1,0:T(8,128)(2,1)S(1)}, bf16[4,512,128]{2,1,0:T(8,128)(2,1)S(1)}, bf16[16,128,128]{...) custom-call(bf16[16,512,128]{2,1,0:T(8,128)(2,1)} %get-tuple-element.44.refs_0_.fac_hbm, ...), custom_call_target="tpu_custom_call" | custom-call | tf_op jit(solution)/shard_map/pallas_call | solution.py:52
  86.6 1.1 %collective-permute-done.11.refs_4_ = bf16[2,8,16,128]{3,2,1,0:T(8,128)(2,1)S(1)} collective-permute-done((bf16[2,8,16,128]{3,2,1,0:T(8,128)(2,1)S(1)}, bf16[2,8,16,128]{3,2,1,0:T(8,128)(2,1)S(1)}, u32[]{:S(2)}, u32[]{:S(2)}) %collective-permute-start.11) | collective-permute-done | bytes 65568 | tf_op jit(solution)/shard_map/ppermute | solution.py:462
  87.7 1.6 %collective-permute-done.12.refs_5_ = bf16[2,8,16,128]{3,2,1,0:T(8,128)(2,1)S(1)} collective-permute-done((bf16[2,8,16,128]{3,2,1,0:T(8,128)(2,1)S(1)}, bf16[2,8,16,128]{3,2,1,0:T(8,128)(2,1)S(1)}, u32[]{:S(2)}, u32[]{:S(2)}) %collective-permute-start.12) | collective-permute-done | bytes 65568 | tf_op jit(solution)/shard_map/ppermute | solution.py:462
  89.3 2.7 %collective-permute-done.13.refs_6_ = bf16[2,8,16,128]{3,2,1,0:T(8,128)(2,1)S(1)} collective-permute-done((bf16[2,8,16,128]{3,2,1,0:T(8,128)(2,1)S(1)}, bf16[2,8,16,128]{3,2,1,0:T(8,128)(2,1)S(1)}, u32[]{:S(2)}, u32[]{:S(2)}) %collective-permute-start.13) | collective-permute-done | bytes 65568 | tf_op jit(solution)/shard_map/ppermute | solution.py:462
  92.1 1.2 %collective-permute-done.14.refs_7_ = bf16[2,8,16,128]{3,2,1,0:T(8,128)(2,1)S(1)} collective-permute-done((bf16[2,8,16,128]{3,2,1,0:T(8,128)(2,1)S(1)}, bf16[2,8,16,128]{3,2,1,0:T(8,128)(2,1)S(1)}, u32[]{:S(2)}, u32[]{:S(2)}) %collective-permute-start.14) | collective-permute-done | bytes 65568 | tf_op jit(solution)/shard_map/ppermute | solution.py:462
  93.3 0.0 collective-permute-done.15.refs_8_
  93.3 0.2 all-to-all-done.3.r_ref
  93.4 0.0 copy-done
  93.4 0.0 copy-done.1
  93.4 4.0 %shard_map.91 = bf16[16,128,128]{2,1,0:T(8,128)(2,1)} custom-call(bf16[16,512,128]{2,1,0:T(8,128)(2,1)} %get-tuple-element.44.refs_0_.fac_hbm, bf16[16,128,128]{2,1,0:T(8,128)(2,1)} %get-tuple-element.59.nt_hbm, bf16[16,128,128]{2,1,0:T(8,128)(2,1)} %get-tuple-element.60.gin_hbm, bf16[4,512,128]{2,1,0:T(8,128)(2,1)S(1)} %get-tuple-element.61.fac0_ref, ...), custom_call_target="tpu_custom_call" | custom-call | tf_op jit(solution)/shard_map/pallas_call | solution.py:52
  (2 shorter events, 0.1 us)
Async XLA Ops:
  3.4 32.4 %all-to-all-start = ((bf16[32,8,16,128]{3,2,1,0:T(8,128)(2,1)}), bf16[32,8,16,128]{3,2,1,0:T(8,128)(2,1)S(1)}, u32[]{:S(2)}, u32[]{:S(2)}) async-start(bf16[32,8,16,128]{3,2,1,0:T(8,128)(2,1)} %get-tuple-element.41), calls=%async_computation | async-start | bytes 2097152 | tf_op jit(solution)/shard_map/all_to_all | solution.py:451
  12.9 1.6 %collective-permute-start = (bf16[8,8,16,128]{3,2,1,0:T(8,128)(2,1)S(1)}, bf16[8,8,16,128]{3,2,1,0:T(8,128)(2,1)S(1)}, u32[]{:S(2)}, u32[]{:S(2)}) collective-permute-start(bf16[8,8,16,128]{3,2,1,0:T(8,128)(2,1)S(1)} %get-tuple-element.48), channel_id=1, source_target_pairs={{0,2},{1,3},{2,0},{3,1},{4,6},{5,7},{6,4},{7,5},{8,10},{9,11},{10,... | collective-permute-start | bytes 786440 | tf_op jit(solution)/shard_map/ppermute | solution.py:462
  14.6 8.6 %collective-permute-start.1 = (bf16[2,8,16,128]{3,2,1,0:T(8,128)(2,1)S(1)}, bf16[2,8,16,128]{3,2,1,0:T(8,128)(2,1)S(1)}, u32[]{:S(2)}, u32[]{:S(2)}) collective-permute-start(bf16[2,8,16,128]{3,2,1,0:T(8,128)(2,1)S(1)} %get-tuple-element.49), channel_id=1, source_target_pairs={{0,1},{1,0},{2,3},{3,2},{4,5},{5,4},{6,7},{7,6},{8,9},{9,8},{10,11... | collective-permute-start | bytes 196616 | tf_op jit(solution)/shard_map/ppermute | solution.py:462
  16.4 7.3 %collective-permute-start.2 = (bf16[2,8,16,128]{3,2,1,0:T(8,128)(2,1)S(1)}, bf16[2,8,16,128]{3,2,1,0:T(8,128)(2,1)S(1)}, u32[]{:S(2)}, u32[]{:S(2)}) collective-permute-start(bf16[2,8,16,128]{3,2,1,0:T(8,128)(2,1)S(1)} %get-tuple-element.50), channel_id=1, source_target_pairs={{0,4},{1,5},{2,6},{3,7},{4,0},{5,1},{6,2},{7,3},{8,12},{9,13},{10,... | collective-permute-start | bytes 196616 | tf_op jit(solution)/shard_map/ppermute | solution.py:462
  17.9 17.9 %collective-permute-start.3 = (bf16[2,8,16,128]{3,2,1,0:T(8,128)(2,1)S(1)}, bf16[2,8,16,128]{3,2,1,0:T(8,128)(2,1)S(1)}, u32[]{:S(2)}, u32[]{:S(2)}) collective-permute-start(bf16[2,8,16,128]{3,2,1,0:T(8,128)(2,1)S(1)} %get-tuple-element.51), channel_id=1, source_target_pairs={{0,13},{1,12},{2,15},{3,14},{4,9},{5,8},{6,11},{7,10},{8,5},{9,4},... | collective-permute-start | bytes 196616 | tf_op jit(solution)/shard_map/ppermute | solution.py:462
  19.3 16.5 %collective-permute-start.4 = (bf16[2,8,16,128]{3,2,1,0:T(8,128)(2,1)S(1)}, bf16[2,8,16,128]{3,2,1,0:T(8,128)(2,1)S(1)}, u32[]{:S(2)}, u32[]{:S(2)}) collective-permute-start(bf16[2,8,16,128]{3,2,1,0:T(8,128)(2,1)S(1)} %get-tuple-element.52), channel_id=1, source_target_pairs={{0,12},{1,13},{2,14},{3,15},{4,8},{5,9},{6,10},{7,11},{8,4},{9,5},... | collective-permute-start | bytes 196616 | tf_op jit(solution)/shard_map/ppermute | solution.py:462
  20.8 15.0 %collective-permute-start.5 = (bf16[2,8,16,128]{3,2,1,0:T(8,128)(2,1)S(1)}, bf16[2,8,16,128]{3,2,1,0:T(8,128)(2,1)S(1)}, u32[]{:S(2)}, u32[]{:S(2)}) collective-permute-start(bf16[2,8,16,128]{3,2,1,0:T(8,128)(2,1)S(1)} %get-tuple-element.53), channel_id=1, source_target_pairs={{0,9},{1,8},{2,11},{3,10},{4,13},{5,12},{6,15},{7,14},{8,1},{9,0},... | collective-permute-start | bytes 196616 | tf_op jit(solution)/shard_map/ppermute | solution.py:462
  23.2 12.7 %collective-permute-start.6 = (bf16[2,8,16,128]{3,2,1,0:T(8,128)(2,1)S(1)}, bf16[2,8,16,128]{3,2,1,0:T(8,128)(2,1)S(1)}, u32[]{:S(2)}, u32[]{:S(2)}) collective-permute-start(bf16[2,8,16,128]{3,2,1,0:T(8,128)(2,1)S(1)} %get-tuple-element.54), channel_id=1, source_target_pairs={{0,8},{1,9},{2,10},{3,11},{4,12},{5,13},{6,14},{7,15},{8,0},{9,1},... | collective-permute-start | bytes 196616 | tf_op jit(solution)/shard_map/ppermute | solution.py:462
  23.7 12.1 %collective-permute-start.7 = (bf16[2,8,16,128]{3,2,1,0:T(8,128)(2,1)S(1)}, bf16[2,8,16,128]{3,2,1,0:T(8,128)(2,1)S(1)}, u32[]{:S(2)}, u32[]{:S(2)}) collective-permute-start(bf16[2,8,16,128]{3,2,1,0:T(8,128)(2,1)S(1)} %get-tuple-element.55), channel_id=1, source_target_pairs={{0,5},{1,4},{2,7},{3,6},{4,1},{5,0},{6,3},{7,2},{8,13},{9,12},{10,... | collective-permute-start | bytes 196616 | tf_op jit(solution)/shard_map/ppermute | solution.py:462
  64.2 29.2 %all-to-all-start.3 = ((bf16[32,8,16,128]{3,2,1,0:T(8,128)(2,1)}), bf16[32,8,16,128]{3,2,1,0:T(8,128)(2,1)S(1)}, u32[]{:S(2)}, u32[]{:S(2)}) async-start(bf16[32,8,16,128]{3,2,1,0:T(8,128)(2,1)} %get-tuple-element.66), calls=%async_computation.3 | async-start | bytes 2097152 | tf_op jit(solution)/shard_map/all_to_all | solution.py:451
  68.4 1.6 %collective-permute-start.8 = (bf16[8,8,16,128]{3,2,1,0:T(8,128)(2,1)S(1)}, bf16[8,8,16,128]{3,2,1,0:T(8,128)(2,1)S(1)}, u32[]{:S(2)}, u32[]{:S(2)}) collective-permute-start(bf16[8,8,16,128]{3,2,1,0:T(8,128)(2,1)S(1)} %get-tuple-element.69), channel_id=1, source_target_pairs={{0,2},{1,3},{2,0},{3,1},{4,6},{5,7},{6,4},{7,5},{8,10},{9,11},{10,... | collective-permute-start | bytes 786440 | tf_op jit(solution)/shard_map/ppermute | solution.py:462
  70.0 23.5 %copy-start = (bf16[128,640]{1,0:T(8,128)(2,1)S(1)}, bf16[128,640]{1,0:T(8,128)(2,1)}, u32[]{:S(2)}) copy-start(bf16[128,640]{1,0:T(8,128)(2,1)} %w_ref.1) | copy-start | bytes 491524
  70.0 23.5 %copy-start.1 = (f32[128]{0:T(128)S(1)}, f32[128]{0:T(128)}, u32[]{:S(2)}) copy-start(f32[128]{0:T(128)} %param.10) | copy-start | bytes 1540
  70.0 8.6 %collective-permute-start.9 = (bf16[2,8,16,128]{3,2,1,0:T(8,128)(2,1)S(1)}, bf16[2,8,16,128]{3,2,1,0:T(8,128)(2,1)S(1)}, u32[]{:S(2)}, u32[]{:S(2)}) collective-permute-start(bf16[2,8,16,128]{3,2,1,0:T(8,128)(2,1)S(1)} %get-tuple-element.70), channel_id=1, source_target_pairs={{0,1},{1,0},{2,3},{3,2},{4,5},{5,4},{6,7},{7,6},{8,9},{9,8},{10,11... | collective-permute-start | bytes 196616 | tf_op jit(solution)/shard_map/ppermute | solution.py:462
  71.9 8.3 %collective-permute-start.10 = (bf16[2,8,16,128]{3,2,1,0:T(8,128)(2,1)S(1)}, bf16[2,8,16,128]{3,2,1,0:T(8,128)(2,1)S(1)}, u32[]{:S(2)}, u32[]{:S(2)}) collective-permute-start(bf16[2,8,16,128]{3,2,1,0:T(8,128)(2,1)S(1)} %get-tuple-element.71), channel_id=1, source_target_pairs={{0,4},{1,5},{2,6},{3,7},{4,0},{5,1},{6,2},{7,3},{8,12},{9,13},{10,... | collective-permute-start | bytes 196616 | tf_op jit(solution)/shard_map/ppermute | solution.py:462
  73.3 14.4 %collective-permute-start.11 = (bf16[2,8,16,128]{3,2,1,0:T(8,128)(2,1)S(1)}, bf16[2,8,16,128]{3,2,1,0:T(8,128)(2,1)S(1)}, u32[]{:S(2)}, u32[]{:S(2)}) collective-permute-start(bf16[2,8,16,128]{3,2,1,0:T(8,128)(2,1)S(1)} %get-tuple-element.72), channel_id=1, source_target_pairs={{0,13},{1,12},{2,15},{3,14},{4,9},{5,8},{6,11},{7,10},{8,5},{9,4},... | collective-permute-start | bytes 196616 | tf_op jit(solution)/shard_map/ppermute | solution.py:462
  74.8 14.6 %collective-permute-start.12 = (bf16[2,8,16,128]{3,2,1,0:T(8,128)(2,1)S(1)}, bf16[2,8,16,128]{3,2,1,0:T(8,128)(2,1)S(1)}, u32[]{:S(2)}, u32[]{:S(2)}) collective-permute-start(bf16[2,8,16,128]{3,2,1,0:T(8,128)(2,1)S(1)} %get-tuple-element.73), channel_id=1, source_target_pairs={{0,12},{1,13},{2,14},{3,15},{4,8},{5,9},{6,10},{7,11},{8,4},{9,5},... | collective-permute-start | bytes 196616 | tf_op jit(solution)/shard_map/ppermute | solution.py:462
  76.2 15.8 %collective-permute-start.13 = (bf16[2,8,16,128]{3,2,1,0:T(8,128)(2,1)S(1)}, bf16[2,8,16,128]{3,2,1,0:T(8,128)(2,1)S(1)}, u32[]{:S(2)}, u32[]{:S(2)}) collective-permute-start(bf16[2,8,16,128]{3,2,1,0:T(8,128)(2,1)S(1)} %get-tuple-element.74), channel_id=1, source_target_pairs={{0,9},{1,8},{2,11},{3,10},{4,13},{5,12},{6,15},{7,14},{8,1},{9,0},... | collective-permute-start | bytes 196616 | tf_op jit(solution)/shard_map/ppermute | solution.py:462
  78.6 14.7 %collective-permute-start.14 = (bf16[2,8,16,128]{3,2,1,0:T(8,128)(2,1)S(1)}, bf16[2,8,16,128]{3,2,1,0:T(8,128)(2,1)S(1)}, u32[]{:S(2)}, u32[]{:S(2)}) collective-permute-start(bf16[2,8,16,128]{3,2,1,0:T(8,128)(2,1)S(1)} %get-tuple-element.75), channel_id=1, source_target_pairs={{0,8},{1,9},{2,10},{3,11},{4,12},{5,13},{6,14},{7,15},{8,0},{9,1},... | collective-permute-start | bytes 196616 | tf_op jit(solution)/shard_map/ppermute | solution.py:462
  80.2 13.1 %collective-permute-start.15 = (bf16[2,8,16,128]{3,2,1,0:T(8,128)(2,1)S(1)}, bf16[2,8,16,128]{3,2,1,0:T(8,128)(2,1)S(1)}, u32[]{:S(2)}, u32[]{:S(2)}) collective-permute-start(bf16[2,8,16,128]{3,2,1,0:T(8,128)(2,1)S(1)} %get-tuple-element.76), channel_id=1, source_target_pairs={{0,5},{1,4},{2,7},{3,6},{4,1},{5,0},{6,3},{7,2},{8,13},{9,12},{10,... | collective-permute-start | bytes 196616 | tf_op jit(solution)/shard_map/ppermute | solution.py:462

commit v7 on v6

--- a/solution.py
+++ b/solution.py
@@ -369,11 +369,11 @@
         sums = []
         for share in range(to.start, to.stop):
             one, two = (
-                r_ref[n].astype(F32)
+                r_ref[n]
                 for n, device in enumerate(lay.order)
                 if device % lay.half == share
             )
-            sums.append((one + two).astype(BF16))
+            sums.append(one + two)
         left, right = swapped(swap, [l_ref[to], jnp.stack(sums)])
         ls_ref[:, here] = left.reshape(rows, group, cols)
         rs_ref[:, here] = right.reshape(rows, group, cols)
@@ -423,8 +423,8 @@
         self.inner = self.devices // outer
         near = [
             2 * n_ch * far + n_ch * core + b
+            for b in range(n_ch)
             for far in range(self.inner // (2 * n_ch))
-            for b in range(n_ch)
             for core in range(2)
         ]
         self.order = [o * self.inner + n for n in near for o in range(outer)]

time: 99.1 us -> 99 us (level)
  starting transfers between devices: 31.5 us -> 34.2 us
  waiting for transfers between devices: 16.2 us -> 13.8 us
    ppermute x16, starting transfers between devices: 20.1 us -> 23.2 us  [swap(): lax.ppermute(block, ('row', 'ch'), [(n, n ^ s) for n in range(self.device...]
    ppermute x16, waiting for transfers between devices: 10 us -> 8.62 us  [swap(): lax.ppermute(block, ('row', 'ch'), [(n, n ^ s) for n in range(self.device...]
    all_to_all x2, waiting for transfers between devices: 6.22 us -> 5.16 us  [exchange_all(): lax.all_to_all(blocks, ('row', 'ch'), split_axis=0, concat_axis=0, tiled=...]
  transfers between devices with their start and end apart: 18 -> 18, of which waited for: 9 -> 7; matrix products, arithmetic and copies ran while one was open for 0% -> 0% of each run, Pallas kernels for 14% -> 14%
where the time goes in v7:
time: 99 us; the launch traced here: 97.7 us
  starting transfers between devices  34.2 us (35%)
  blocking collectives  25.4 us (26%)
  Pallas kernels  24.2 us (24%)
  waiting for transfers between devices  13.8 us (14%)
    all_to_all x2, blocking collectives, exchange_half(): lax.all_to_all(blocks, ('row', 'ch'), split_axis=0, concat_axis=0, tiled=...  25.4 us
    pallas_call x10, Pallas kernels, call(): pl.pallas_call(kernel, out_shape=outs if single else tuple(outs), in_spec...  24.2 us
    ppermute x16, starting transfers between devices, swap(): lax.ppermute(block, ('row', 'ch'), [(n, n ^ s) for n in range(self.device...  23.2 us
    all_to_all x2, starting transfers between devices, exchange_all(): lax.all_to_all(blocks, ('row', 'ch'), split_axis=0, concat_axis=0, tiled=...  11 us
    ppermute x16, waiting for transfers between devices, swap(): lax.ppermute(block, ('row', 'ch'), [(n, n ^ s) for n in range(self.device...  8.62 us
    all_to_all x2, waiting for transfers between devices, exchange_all(): lax.all_to_all(blocks, ('row', 'ch'), split_axis=0, concat_axis=0, tiled=...  5.16 us
  transfers between devices with their start and end apart: 18, of which 7 were waited for; matrix products, arithmetic and copies ran while one was open for 0% of the time, Pallas kernels for 14%

profile of v7, /device:TPU:0, one launch (start us, length us, event | category | flops | bytes accessed | tf_op | source)
XLA Modules:
  0.0 97.7 jit_solution(884792578029818951)
XLA Ops:
  0.0 3.5 %shard_map.82 = (bf16[32,8,16,128]{3,2,1,0:T(8,128)(2,1)}, bf16[8,128,256]{2,1,0:T(8,128)(2,1)S(1)}) custom-call(bf16[16,128,128]{2,1,0:T(8,128)(2,1)} %refs_2_.1, f32[1,128]{1,0:T(1,128)} %bitcast.4, f32[1,128]{1,0:T(1,128)} %bitcast.8, bf16[128,640]{1,0:T(8,128)(2,1)} %w_ref.1), custom_call_target="tpu_custom_call" | custom-call | tf_op jit(solution)/shard_map/pallas_call | solution.py:52
  3.5 7.3 %all-to-all-start = ((bf16[32,8,16,128]{3,2,1,0:T(8,128)(2,1)}), bf16[32,8,16,128]{3,2,1,0:T(8,128)(2,1)S(1)}, u32[]{:S(2)}, u32[]{:S(2)}) async-start(bf16[32,8,16,128]{3,2,1,0:T(8,128)(2,1)} %get-tuple-element.41), calls=%async_computation | async-start | bytes 2097152 | tf_op jit(solution)/shard_map/all_to_all | solution.py:451
  10.8 2.2 %shard_map.84 = (bf16[8,8,16,128]{3,2,1,0:T(8,128)(2,1)S(1)}, bf16[8,8,16,128]{3,2,1,0:T(8,128)(2,1)S(1)}) custom-call(bf16[128,640]{1,0:T(8,128)(2,1)} %w_ref.1, bf16[8,128,256]{2,1,0:T(8,128)(2,1)S(1)} %get-tuple-element.46.n_ref), custom_call_target="tpu_custom_call" | custom-call | tf_op jit(solution)/shard_map/pallas_call | solution.py:52
  13.0 0.3 collective-permute-start
  13.3 1.3 %collective-permute-done.mates_ref.refs_1_ = bf16[8,8,16,128]{3,2,1,0:T(8,128)(2,1)S(1)} collective-permute-done((bf16[8,8,16,128]{3,2,1,0:T(8,128)(2,1)S(1)}, bf16[8,8,16,128]{3,2,1,0:T(8,128)(2,1)S(1)}, u32[]{:S(2)}, u32[]{:S(2)}) %collective-permute-start) | collective-permute-done | bytes 262176 | tf_op jit(solution)/shard_map/ppermute | solution.py:462
  14.6 1.8 %collective-permute-start.1 = (bf16[2,8,16,128]{3,2,1,0:T(8,128)(2,1)S(1)}, bf16[2,8,16,128]{3,2,1,0:T(8,128)(2,1)S(1)}, u32[]{:S(2)}, u32[]{:S(2)}) collective-permute-start(bf16[2,8,16,128]{3,2,1,0:T(8,128)(2,1)S(1)} %get-tuple-element.49), channel_id=1, source_target_pairs={{0,1},{1,0},{2,3},{3,2},{4,5},{5,4},{6,7},{7,6},{8,9},{9,8},{10,11... | collective-permute-start | bytes 196616 | tf_op jit(solution)/shard_map/ppermute | solution.py:462
  16.4 1.5 %collective-permute-start.2 = (bf16[2,8,16,128]{3,2,1,0:T(8,128)(2,1)S(1)}, bf16[2,8,16,128]{3,2,1,0:T(8,128)(2,1)S(1)}, u32[]{:S(2)}, u32[]{:S(2)}) collective-permute-start(bf16[2,8,16,128]{3,2,1,0:T(8,128)(2,1)S(1)} %get-tuple-element.50), channel_id=1, source_target_pairs={{0,4},{1,5},{2,6},{3,7},{4,0},{5,1},{6,2},{7,3},{8,12},{9,13},{10,... | collective-permute-start | bytes 196616 | tf_op jit(solution)/shard_map/ppermute | solution.py:462
  17.9 1.5 %collective-permute-start.3 = (bf16[2,8,16,128]{3,2,1,0:T(8,128)(2,1)S(1)}, bf16[2,8,16,128]{3,2,1,0:T(8,128)(2,1)S(1)}, u32[]{:S(2)}, u32[]{:S(2)}) collective-permute-start(bf16[2,8,16,128]{3,2,1,0:T(8,128)(2,1)S(1)} %get-tuple-element.51), channel_id=1, source_target_pairs={{0,13},{1,12},{2,15},{3,14},{4,9},{5,8},{6,11},{7,10},{8,5},{9,4},... | collective-permute-start | bytes 196616 | tf_op jit(solution)/shard_map/ppermute | solution.py:462
  19.4 1.5 %collective-permute-start.4 = (bf16[2,8,16,128]{3,2,1,0:T(8,128)(2,1)S(1)}, bf16[2,8,16,128]{3,2,1,0:T(8,128)(2,1)S(1)}, u32[]{:S(2)}, u32[]{:S(2)}) collective-permute-start(bf16[2,8,16,128]{3,2,1,0:T(8,128)(2,1)S(1)} %get-tuple-element.52), channel_id=1, source_target_pairs={{0,12},{1,13},{2,14},{3,15},{4,8},{5,9},{6,10},{7,11},{8,4},{9,5},... | collective-permute-start | bytes 196616 | tf_op jit(solution)/shard_map/ppermute | solution.py:462
  20.8 2.4 %collective-permute-start.5 = (bf16[2,8,16,128]{3,2,1,0:T(8,128)(2,1)S(1)}, bf16[2,8,16,128]{3,2,1,0:T(8,128)(2,1)S(1)}, u32[]{:S(2)}, u32[]{:S(2)}) collective-permute-start(bf16[2,8,16,128]{3,2,1,0:T(8,128)(2,1)S(1)} %get-tuple-element.53), channel_id=1, source_target_pairs={{0,9},{1,8},{2,11},{3,10},{4,13},{5,12},{6,15},{7,14},{8,1},{9,0},... | collective-permute-start | bytes 196616 | tf_op jit(solution)/shard_map/ppermute | solution.py:462
  23.2 0.0 collective-permute-done.1.refs_2_
  23.2 0.6 collective-permute-start.6
  23.8 0.0 collective-permute-done.2.refs_3_
  23.8 1.2 %collective-permute-start.7 = (bf16[2,8,16,128]{3,2,1,0:T(8,128)(2,1)S(1)}, bf16[2,8,16,128]{3,2,1,0:T(8,128)(2,1)S(1)}, u32[]{:S(2)}, u32[]{:S(2)}) collective-permute-start(bf16[2,8,16,128]{3,2,1,0:T(8,128)(2,1)S(1)} %get-tuple-element.55), channel_id=1, source_target_pairs={{0,5},{1,4},{2,7},{3,6},{4,1},{5,0},{6,3},{7,2},{8,13},{9,12},{10,... | collective-permute-start | bytes 196616 | tf_op jit(solution)/shard_map/ppermute | solution.py:462
  24.9 5.7 %shard_map.83 = (f32[16,128,128]{2,1,0:T(8,128)S(1)}, bf16[16,512,128]{2,1,0:T(8,128)(2,1)}) custom-call(bf16[16,128,128]{2,1,0:T(8,128)(2,1)} %refs_2_.1, bf16[16,128,128]{2,1,0:T(8,128)(2,1)} %refs_3_.1, f32[1,128]{1,0:T(1,128)} %bitcast.5, f32[1,128]{1,0:T(1,128)} %bitcast.9, bf16[128,640]{1,0:T(8,128)(2,1)} %w_ref.1, f32[1,128]{1,0:T(1,128)} %bitcast.11, ...), custom_call_target="tpu_custom_call" | custom-call | tf_op jit(solution)/shard_map/pallas_call | solution.py:52
  30.7 5.2 %all-to-all-done.r_ref = bf16[32,8,16,128]{3,2,1,0:T(8,128)(2,1)S(1)} async-done(((bf16[32,8,16,128]{3,2,1,0:T(8,128)(2,1)}), bf16[32,8,16,128]{3,2,1,0:T(8,128)(2,1)S(1)}, u32[]{:S(2)}, u32[]{:S(2)}) %all-to-all-start) | async-done | bytes 1048608 | tf_op jit(solution)/shard_map/all_to_all | solution.py:451
  35.8 0.0 collective-permute-done.3.refs_4_
  35.8 0.0 collective-permute-done.4.refs_5_
  35.8 0.0 collective-permute-done.5.refs_6_
  35.8 0.3 collective-permute-done.6.refs_7_
  36.2 0.0 collective-permute-done.7.refs_8_
  36.2 0.5 shard_map.86
  36.6 13.2 %all_to_all.20.t_ref = bf16[16,8,16,128]{3,2,1,0:T(8,128)(2,1)S(1)} all-to-all(bf16[16,8,16,128]{3,2,1,0:T(8,128)(2,1)S(1)} %get-tuple-element.56), channel_id=1, replica_groups={{0,8,2,10,4,12,6,14,1,9,3,11,5,13,7,15},{16,24,18,26,20,28,22,30,17,25,..., dimensions={0} | all-to-all | bytes 1048576 | tf_op jit(solution)/shard_map/all_to_all | solution.py:457
  49.8 1.2 %shard_map.87 = (bf16[16,8,16,128]{3,2,1,0:T(8,128)(2,1)S(1)}, bf16[16,8,16,128]{3,2,1,0:T(8,128)(2,1)}) custom-call(bf16[16,8,16,128]{3,2,1,0:T(8,128)(2,1)S(1)} %all_to_all.20.t_ref, f32[16,128,128]{2,1,0:T(8,128)S(1)} %get-tuple-element.57.h_ref), custom_call_target="tpu_custom_call" | custom-call | tf_op jit(solution)/shard_map/pallas_call | solution.py:52
  51.0 12.3 %all_to_all.21.gt_ref = bf16[16,8,16,128]{3,2,1,0:T(8,128)(2,1)S(1)} all-to-all(bf16[16,8,16,128]{3,2,1,0:T(8,128)(2,1)S(1)} %get-tuple-element.64), channel_id=1, replica_groups={{0,8,2,10,4,12,6,14,1,9,3,11,5,13,7,15},{16,24,18,26,20,28,22,30,17,25,..., dimensions={0} | all-to-all | bytes 1048576 | tf_op jit(solution)/shard_map/all_to_all | solution.py:457
  63.3 1.3 %shard_map.89 = (bf16[32,8,16,128]{3,2,1,0:T(8,128)(2,1)}, bf16[8,8,16,128]{3,2,1,0:T(8,128)(2,1)S(1)}, bf16[8,8,16,128]{3,2,1,0:T(8,128)(2,1)S(1)}) custom-call(bf16[16,8,16,128]{3,2,1,0:T(8,128)(2,1)S(1)} %all_to_all.21.gt_ref, bf16[16,8,16,128]{3,2,1,0:T(8,128)(2,1)S(1)} %get-tuple-element.65.l_ref, bf16[32,8,16,128]{3,2,1,0:T(8,128)(2,1)S(1)} %all-to-all-done.r_ref), custom_call_target="tpu_custom_call" | custom-call | tf_op jit(solution)/shard_map/pallas_call | solution.py:52
  64.6 3.7 %all-to-all-start.3 = ((bf16[32,8,16,128]{3,2,1,0:T(8,128)(2,1)}), bf16[32,8,16,128]{3,2,1,0:T(8,128)(2,1)S(1)}, u32[]{:S(2)}, u32[]{:S(2)}) async-start(bf16[32,8,16,128]{3,2,1,0:T(8,128)(2,1)} %get-tuple-element.66), calls=%async_computation.3 | async-start | bytes 2097152 | tf_op jit(solution)/shard_map/all_to_all | solution.py:451
  68.4 0.3 collective-permute-start.8
  68.7 1.3 %collective-permute-done.8.mates_ref.refs_1_ = bf16[8,8,16,128]{3,2,1,0:T(8,128)(2,1)S(1)} collective-permute-done((bf16[8,8,16,128]{3,2,1,0:T(8,128)(2,1)S(1)}, bf16[8,8,16,128]{3,2,1,0:T(8,128)(2,1)S(1)}, u32[]{:S(2)}, u32[]{:S(2)}) %collective-permute-start.8) | collective-permute-done | bytes 262176 | tf_op jit(solution)/shard_map/ppermute | solution.py:462
  70.0 0.0 copy-start
  70.0 0.0 copy-start.1
  70.0 1.8 %collective-permute-start.9 = (bf16[2,8,16,128]{3,2,1,0:T(8,128)(2,1)S(1)}, bf16[2,8,16,128]{3,2,1,0:T(8,128)(2,1)S(1)}, u32[]{:S(2)}, u32[]{:S(2)}) collective-permute-start(bf16[2,8,16,128]{3,2,1,0:T(8,128)(2,1)S(1)} %get-tuple-element.70), channel_id=1, source_target_pairs={{0,1},{1,0},{2,3},{3,2},{4,5},{5,4},{6,7},{7,6},{8,9},{9,8},{10,11... | collective-permute-start | bytes 196616 | tf_op jit(solution)/shard_map/ppermute | solution.py:462
  71.8 1.5 %collective-permute-start.10 = (bf16[2,8,16,128]{3,2,1,0:T(8,128)(2,1)S(1)}, bf16[2,8,16,128]{3,2,1,0:T(8,128)(2,1)S(1)}, u32[]{:S(2)}, u32[]{:S(2)}) collective-permute-start(bf16[2,8,16,128]{3,2,1,0:T(8,128)(2,1)S(1)} %get-tuple-element.71), channel_id=1, source_target_pairs={{0,4},{1,5},{2,6},{3,7},{4,0},{5,1},{6,2},{7,3},{8,12},{9,13},{10,... | collective-permute-start | bytes 196616 | tf_op jit(solution)/shard_map/ppermute | solution.py:462
  73.3 1.5 %collective-permute-start.11 = (bf16[2,8,16,128]{3,2,1,0:T(8,128)(2,1)S(1)}, bf16[2,8,16,128]{3,2,1,0:T(8,128)(2,1)S(1)}, u32[]{:S(2)}, u32[]{:S(2)}) collective-permute-start(bf16[2,8,16,128]{3,2,1,0:T(8,128)(2,1)S(1)} %get-tuple-element.72), channel_id=1, source_target_pairs={{0,13},{1,12},{2,15},{3,14},{4,9},{5,8},{6,11},{7,10},{8,5},{9,4},... | collective-permute-start | bytes 196616 | tf_op jit(solution)/shard_map/ppermute | solution.py:462
  74.8 1.5 %collective-permute-start.12 = (bf16[2,8,16,128]{3,2,1,0:T(8,128)(2,1)S(1)}, bf16[2,8,16,128]{3,2,1,0:T(8,128)(2,1)S(1)}, u32[]{:S(2)}, u32[]{:S(2)}) collective-permute-start(bf16[2,8,16,128]{3,2,1,0:T(8,128)(2,1)S(1)} %get-tuple-element.73), channel_id=1, source_target_pairs={{0,12},{1,13},{2,14},{3,15},{4,8},{5,9},{6,10},{7,11},{8,4},{9,5},... | collective-permute-start | bytes 196616 | tf_op jit(solution)/shard_map/ppermute | solution.py:462
  76.2 2.4 %collective-permute-start.13 = (bf16[2,8,16,128]{3,2,1,0:T(8,128)(2,1)S(1)}, bf16[2,8,16,128]{3,2,1,0:T(8,128)(2,1)S(1)}, u32[]{:S(2)}, u32[]{:S(2)}) collective-permute-start(bf16[2,8,16,128]{3,2,1,0:T(8,128)(2,1)S(1)} %get-tuple-element.74), channel_id=1, source_target_pairs={{0,9},{1,8},{2,11},{3,10},{4,13},{5,12},{6,15},{7,14},{8,1},{9,0},... | collective-permute-start | bytes 196616 | tf_op jit(solution)/shard_map/ppermute | solution.py:462
  78.6 0.0 collective-permute-done.9.refs_2_
  78.6 0.8 collective-permute-start.14
  79.4 0.0 collective-permute-done.10.refs_3_
  79.4 2.9 %collective-permute-start.15 = (bf16[2,8,16,128]{3,2,1,0:T(8,128)(2,1)S(1)}, bf16[2,8,16,128]{3,2,1,0:T(8,128)(2,1)S(1)}, u32[]{:S(2)}, u32[]{:S(2)}) collective-permute-start(bf16[2,8,16,128]{3,2,1,0:T(8,128)(2,1)S(1)} %get-tuple-element.76), channel_id=1, source_target_pairs={{0,5},{1,4},{2,7},{3,6},{4,1},{5,0},{6,3},{7,2},{8,13},{9,12},{10,... | collective-permute-start | bytes 196616 | tf_op jit(solution)/shard_map/ppermute | solution.py:462
  82.2 5.8 %shard_map.88 = (bf16[4,128,128]{2,1,0:T(8,128)(2,1)S(1)}, bf16[4,128,128]{2,1,0:T(8,128)(2,1)S(1)}, bf16[4,512,128]{2,1,0:T(8,128)(2,1)S(1)}, bf16[16,128,128]{...) custom-call(bf16[16,512,128]{2,1,0:T(8,128)(2,1)} %get-tuple-element.44.refs_0_.fac_hbm, ...), custom_call_target="tpu_custom_call" | custom-call | tf_op jit(solution)/shard_map/pallas_call | solution.py:52
  88.0 0.0 collective-permute-done.11.refs_4_
  88.0 1.2 %collective-permute-done.12.refs_5_ = bf16[2,8,16,128]{3,2,1,0:T(8,128)(2,1)S(1)} collective-permute-done((bf16[2,8,16,128]{3,2,1,0:T(8,128)(2,1)S(1)}, bf16[2,8,16,128]{3,2,1,0:T(8,128)(2,1)S(1)}, u32[]{:S(2)}, u32[]{:S(2)}) %collective-permute-start.12) | collective-permute-done | bytes 65568 | tf_op jit(solution)/shard_map/ppermute | solution.py:462
  89.2 3.8 %collective-permute-done.13.refs_6_ = bf16[2,8,16,128]{3,2,1,0:T(8,128)(2,1)S(1)} collective-permute-done((bf16[2,8,16,128]{3,2,1,0:T(8,128)(2,1)S(1)}, bf16[2,8,16,128]{3,2,1,0:T(8,128)(2,1)S(1)}, u32[]{:S(2)}, u32[]{:S(2)}) %collective-permute-start.13) | collective-permute-done | bytes 65568 | tf_op jit(solution)/shard_map/ppermute | solution.py:462
  93.0 0.8 collective-permute-done.14.refs_7_
  93.8 0.0 collective-permute-done.15.refs_8_
  93.8 0.0 all-to-all-done.3.r_ref
  93.8 0.0 copy-done
  93.8 0.0 copy-done.1
  93.8 4.0 %shard_map.91 = bf16[16,128,128]{2,1,0:T(8,128)(2,1)} custom-call(bf16[16,512,128]{2,1,0:T(8,128)(2,1)} %get-tuple-element.44.refs_0_.fac_hbm, bf16[16,128,128]{2,1,0:T(8,128)(2,1)} %get-tuple-element.59.nt_hbm, bf16[16,128,128]{2,1,0:T(8,128)(2,1)} %get-tuple-element.60.gin_hbm, bf16[4,512,128]{2,1,0:T(8,128)(2,1)S(1)} %get-tuple-element.61.fac0_ref, ...), custom_call_target="tpu_custom_call" | custom-call | tf_op jit(solution)/shard_map/pallas_call | solution.py:52
  (2 shorter events, 0.1 us)
Async XLA Ops:
  3.5 32.4 %all-to-all-start = ((bf16[32,8,16,128]{3,2,1,0:T(8,128)(2,1)}), bf16[32,8,16,128]{3,2,1,0:T(8,128)(2,1)S(1)}, u32[]{:S(2)}, u32[]{:S(2)}) async-start(bf16[32,8,16,128]{3,2,1,0:T(8,128)(2,1)} %get-tuple-element.41), calls=%async_computation | async-start | bytes 2097152 | tf_op jit(solution)/shard_map/all_to_all | solution.py:451
  13.0 1.6 %collective-permute-start = (bf16[8,8,16,128]{3,2,1,0:T(8,128)(2,1)S(1)}, bf16[8,8,16,128]{3,2,1,0:T(8,128)(2,1)S(1)}, u32[]{:S(2)}, u32[]{:S(2)}) collective-permute-start(bf16[8,8,16,128]{3,2,1,0:T(8,128)(2,1)S(1)} %get-tuple-element.48), channel_id=1, source_target_pairs={{0,2},{1,3},{2,0},{3,1},{4,6},{5,7},{6,4},{7,5},{8,10},{9,11},{10,... | collective-permute-start | bytes 786440 | tf_op jit(solution)/shard_map/ppermute | solution.py:462
  14.6 8.6 %collective-permute-start.1 = (bf16[2,8,16,128]{3,2,1,0:T(8,128)(2,1)S(1)}, bf16[2,8,16,128]{3,2,1,0:T(8,128)(2,1)S(1)}, u32[]{:S(2)}, u32[]{:S(2)}) collective-permute-start(bf16[2,8,16,128]{3,2,1,0:T(8,128)(2,1)S(1)} %get-tuple-element.49), channel_id=1, source_target_pairs={{0,1},{1,0},{2,3},{3,2},{4,5},{5,4},{6,7},{7,6},{8,9},{9,8},{10,11... | collective-permute-start | bytes 196616 | tf_op jit(solution)/shard_map/ppermute | solution.py:462
  16.4 7.3 %collective-permute-start.2 = (bf16[2,8,16,128]{3,2,1,0:T(8,128)(2,1)S(1)}, bf16[2,8,16,128]{3,2,1,0:T(8,128)(2,1)S(1)}, u32[]{:S(2)}, u32[]{:S(2)}) collective-permute-start(bf16[2,8,16,128]{3,2,1,0:T(8,128)(2,1)S(1)} %get-tuple-element.50), channel_id=1, source_target_pairs={{0,4},{1,5},{2,6},{3,7},{4,0},{5,1},{6,2},{7,3},{8,12},{9,13},{10,... | collective-permute-start | bytes 196616 | tf_op jit(solution)/shard_map/ppermute | solution.py:462
  17.9 17.9 %collective-permute-start.3 = (bf16[2,8,16,128]{3,2,1,0:T(8,128)(2,1)S(1)}, bf16[2,8,16,128]{3,2,1,0:T(8,128)(2,1)S(1)}, u32[]{:S(2)}, u32[]{:S(2)}) collective-permute-start(bf16[2,8,16,128]{3,2,1,0:T(8,128)(2,1)S(1)} %get-tuple-element.51), channel_id=1, source_target_pairs={{0,13},{1,12},{2,15},{3,14},{4,9},{5,8},{6,11},{7,10},{8,5},{9,4},... | collective-permute-start | bytes 196616 | tf_op jit(solution)/shard_map/ppermute | solution.py:462
  19.4 16.5 %collective-permute-start.4 = (bf16[2,8,16,128]{3,2,1,0:T(8,128)(2,1)S(1)}, bf16[2,8,16,128]{3,2,1,0:T(8,128)(2,1)S(1)}, u32[]{:S(2)}, u32[]{:S(2)}) collective-permute-start(bf16[2,8,16,128]{3,2,1,0:T(8,128)(2,1)S(1)} %get-tuple-element.52), channel_id=1, source_target_pairs={{0,12},{1,13},{2,14},{3,15},{4,8},{5,9},{6,10},{7,11},{8,4},{9,5},... | collective-permute-start | bytes 196616 | tf_op jit(solution)/shard_map/ppermute | solution.py:462
  20.8 15.0 %collective-permute-start.5 = (bf16[2,8,16,128]{3,2,1,0:T(8,128)(2,1)S(1)}, bf16[2,8,16,128]{3,2,1,0:T(8,128)(2,1)S(1)}, u32[]{:S(2)}, u32[]{:S(2)}) collective-permute-start(bf16[2,8,16,128]{3,2,1,0:T(8,128)(2,1)S(1)} %get-tuple-element.53), channel_id=1, source_target_pairs={{0,9},{1,8},{2,11},{3,10},{4,13},{5,12},{6,15},{7,14},{8,1},{9,0},... | collective-permute-start | bytes 196616 | tf_op jit(solution)/shard_map/ppermute | solution.py:462
  23.2 13.0 %collective-permute-start.6 = (bf16[2,8,16,128]{3,2,1,0:T(8,128)(2,1)S(1)}, bf16[2,8,16,128]{3,2,1,0:T(8,128)(2,1)S(1)}, u32[]{:S(2)}, u32[]{:S(2)}) collective-permute-start(bf16[2,8,16,128]{3,2,1,0:T(8,128)(2,1)S(1)} %get-tuple-element.54), channel_id=1, source_target_pairs={{0,8},{1,9},{2,10},{3,11},{4,12},{5,13},{6,14},{7,15},{8,0},{9,1},... | collective-permute-start | bytes 196616 | tf_op jit(solution)/shard_map/ppermute | solution.py:462
  23.8 12.4 %collective-permute-start.7 = (bf16[2,8,16,128]{3,2,1,0:T(8,128)(2,1)S(1)}, bf16[2,8,16,128]{3,2,1,0:T(8,128)(2,1)S(1)}, u32[]{:S(2)}, u32[]{:S(2)}) collective-permute-start(bf16[2,8,16,128]{3,2,1,0:T(8,128)(2,1)S(1)} %get-tuple-element.55), channel_id=1, source_target_pairs={{0,5},{1,4},{2,7},{3,6},{4,1},{5,0},{6,3},{7,2},{8,13},{9,12},{10,... | collective-permute-start | bytes 196616 | tf_op jit(solution)/shard_map/ppermute | solution.py:462
  64.6 29.1 %all-to-all-start.3 = ((bf16[32,8,16,128]{3,2,1,0:T(8,128)(2,1)}), bf16[32,8,16,128]{3,2,1,0:T(8,128)(2,1)S(1)}, u32[]{:S(2)}, u32[]{:S(2)}) async-start(bf16[32,8,16,128]{3,2,1,0:T(8,128)(2,1)} %get-tuple-element.66), calls=%async_computation.3 | async-start | bytes 2097152 | tf_op jit(solution)/shard_map/all_to_all | solution.py:451
  68.4 1.6 %collective-permute-start.8 = (bf16[8,8,16,128]{3,2,1,0:T(8,128)(2,1)S(1)}, bf16[8,8,16,128]{3,2,1,0:T(8,128)(2,1)S(1)}, u32[]{:S(2)}, u32[]{:S(2)}) collective-permute-start(bf16[8,8,16,128]{3,2,1,0:T(8,128)(2,1)S(1)} %get-tuple-element.69), channel_id=1, source_target_pairs={{0,2},{1,3},{2,0},{3,1},{4,6},{5,7},{6,4},{7,5},{8,10},{9,11},{10,... | collective-permute-start | bytes 786440 | tf_op jit(solution)/shard_map/ppermute | solution.py:462
  70.0 23.8 %copy-start = (bf16[128,640]{1,0:T(8,128)(2,1)S(1)}, bf16[128,640]{1,0:T(8,128)(2,1)}, u32[]{:S(2)}) copy-start(bf16[128,640]{1,0:T(8,128)(2,1)} %w_ref.1) | copy-start | bytes 491524
  70.0 23.8 %copy-start.1 = (f32[128]{0:T(128)S(1)}, f32[128]{0:T(128)}, u32[]{:S(2)}) copy-start(f32[128]{0:T(128)} %param.10) | copy-start | bytes 1540
  70.0 8.6 %collective-permute-start.9 = (bf16[2,8,16,128]{3,2,1,0:T(8,128)(2,1)S(1)}, bf16[2,8,16,128]{3,2,1,0:T(8,128)(2,1)S(1)}, u32[]{:S(2)}, u32[]{:S(2)}) collective-permute-start(bf16[2,8,16,128]{3,2,1,0:T(8,128)(2,1)S(1)} %get-tuple-element.70), channel_id=1, source_target_pairs={{0,1},{1,0},{2,3},{3,2},{4,5},{5,4},{6,7},{7,6},{8,9},{9,8},{10,11... | collective-permute-start | bytes 196616 | tf_op jit(solution)/shard_map/ppermute | solution.py:462
  71.8 7.5 %collective-permute-start.10 = (bf16[2,8,16,128]{3,2,1,0:T(8,128)(2,1)S(1)}, bf16[2,8,16,128]{3,2,1,0:T(8,128)(2,1)S(1)}, u32[]{:S(2)}, u32[]{:S(2)}) collective-permute-start(bf16[2,8,16,128]{3,2,1,0:T(8,128)(2,1)S(1)} %get-tuple-element.71), channel_id=1, source_target_pairs={{0,4},{1,5},{2,6},{3,7},{4,0},{5,1},{6,2},{7,3},{8,12},{9,13},{10,... | collective-permute-start | bytes 196616 | tf_op jit(solution)/shard_map/ppermute | solution.py:462
  73.3 14.7 %collective-permute-start.11 = (bf16[2,8,16,128]{3,2,1,0:T(8,128)(2,1)S(1)}, bf16[2,8,16,128]{3,2,1,0:T(8,128)(2,1)S(1)}, u32[]{:S(2)}, u32[]{:S(2)}) collective-permute-start(bf16[2,8,16,128]{3,2,1,0:T(8,128)(2,1)S(1)} %get-tuple-element.72), channel_id=1, source_target_pairs={{0,13},{1,12},{2,15},{3,14},{4,9},{5,8},{6,11},{7,10},{8,5},{9,4},... | collective-permute-start | bytes 196616 | tf_op jit(solution)/shard_map/ppermute | solution.py:462
  74.8 14.5 %collective-permute-start.12 = (bf16[2,8,16,128]{3,2,1,0:T(8,128)(2,1)S(1)}, bf16[2,8,16,128]{3,2,1,0:T(8,128)(2,1)S(1)}, u32[]{:S(2)}, u32[]{:S(2)}) collective-permute-start(bf16[2,8,16,128]{3,2,1,0:T(8,128)(2,1)S(1)} %get-tuple-element.73), channel_id=1, source_target_pairs={{0,12},{1,13},{2,14},{3,15},{4,8},{5,9},{6,10},{7,11},{8,4},{9,5},... | collective-permute-start | bytes 196616 | tf_op jit(solution)/shard_map/ppermute | solution.py:462
  76.2 16.8 %collective-permute-start.13 = (bf16[2,8,16,128]{3,2,1,0:T(8,128)(2,1)S(1)}, bf16[2,8,16,128]{3,2,1,0:T(8,128)(2,1)S(1)}, u32[]{:S(2)}, u32[]{:S(2)}) collective-permute-start(bf16[2,8,16,128]{3,2,1,0:T(8,128)(2,1)S(1)} %get-tuple-element.74), channel_id=1, source_target_pairs={{0,9},{1,8},{2,11},{3,10},{4,13},{5,12},{6,15},{7,14},{8,1},{9,0},... | collective-permute-start | bytes 196616 | tf_op jit(solution)/shard_map/ppermute | solution.py:462
  78.6 15.2 %collective-permute-start.14 = (bf16[2,8,16,128]{3,2,1,0:T(8,128)(2,1)S(1)}, bf16[2,8,16,128]{3,2,1,0:T(8,128)(2,1)S(1)}, u32[]{:S(2)}, u32[]{:S(2)}) collective-permute-start(bf16[2,8,16,128]{3,2,1,0:T(8,128)(2,1)S(1)} %get-tuple-element.75), channel_id=1, source_target_pairs={{0,8},{1,9},{2,10},{3,11},{4,12},{5,13},{6,14},{7,15},{8,0},{9,1},... | collective-permute-start | bytes 196616 | tf_op jit(solution)/shard_map/ppermute | solution.py:462
  79.4 14.4 %collective-permute-start.15 = (bf16[2,8,16,128]{3,2,1,0:T(8,128)(2,1)S(1)}, bf16[2,8,16,128]{3,2,1,0:T(8,128)(2,1)S(1)}, u32[]{:S(2)}, u32[]{:S(2)}) collective-permute-start(bf16[2,8,16,128]{3,2,1,0:T(8,128)(2,1)S(1)} %get-tuple-element.76), channel_id=1, source_target_pairs={{0,5},{1,4},{2,7},{3,6},{4,1},{5,0},{6,3},{7,2},{8,13},{9,12},{10,... | collective-permute-start | bytes 196616 | tf_op jit(solution)/shard_map/ppermute | solution.py:462

commit v8 on v7

--- a/solution.py
+++ b/solution.py
@@ -421,14 +421,14 @@
         self.half = self.devices // 2
         outer = math.isqrt(n_row)
         self.inner = self.devices // outer
-        near = [
-            2 * n_ch * far + n_ch * core + b
-            for b in range(n_ch)
-            for far in range(self.inner // (2 * n_ch))
-            for core in range(2)
+        rest = [
+            2 * n_ch * far + b for b in range(n_ch) for far in range(self.inner // (2 * n_ch))
         ]
-        self.order = [o * self.inner + n for n in near for o in range(outer)]
-        self.inside = [o * self.inner + n for n in near for o in range(outer // 2)]
+
+        def spread(parts):
+            return [o * self.inner + n + n_ch * core for n in rest for o in range(parts) for core in range(2)]
+
+        self.order, self.inside = spread(outer), spread(outer // 2)
         self.mate = n_ch
         self.hops = [s for s in range(self.half) if s & self.mate == 0]
         self.hops[3:] = self.hops[:2:-1]

time: 99 us -> 103 us (1.040)
  waiting for transfers between devices: 13.8 us -> 19.8 us
  starting transfers between devices: 34.2 us -> 31.5 us
    all_to_all x2, waiting for transfers between devices: 5.16 us -> 12.1 us  [exchange_all(): lax.all_to_all(blocks, ('row', 'ch'), split_axis=0, concat_axis=0, tiled=...]
    ppermute x16, starting transfers between devices: 23.2 us -> 21.6 us  [swap(): lax.ppermute(block, ('row', 'ch'), [(n, n ^ s) for n in range(self.device...]
    all_to_all x2, starting transfers between devices: 11 us -> 9.96 us  [exchange_all(): lax.all_to_all(blocks, ('row', 'ch'), split_axis=0, concat_axis=0, tiled=...]
  transfers between devices with their start and end apart: 18 -> 18, of which waited for: 7 -> 8; matrix products, arithmetic and copies ran while one was open for 0% -> 0% of each run, Pallas kernels for 14% -> 13%
where the time goes in v8:
time: 103 us; the launch traced here: 102 us
  starting transfers between devices  31.5 us (31%)
  blocking collectives  26.3 us (26%)
  Pallas kernels  24.2 us (23%)
  waiting for transfers between devices  19.8 us (19%)
    all_to_all x2, blocking collectives, exchange_half(): lax.all_to_all(blocks, ('row', 'ch'), split_axis=0, concat_axis=0, tiled=...  26.3 us
    pallas_call x10, Pallas kernels, call(): pl.pallas_call(kernel, out_shape=outs if single else tuple(outs), in_spec...  24.2 us
    ppermute x16, starting transfers between devices, swap(): lax.ppermute(block, ('row', 'ch'), [(n, n ^ s) for n in range(self.device...  21.6 us
    all_to_all x2, waiting for transfers between devices, exchange_all(): lax.all_to_all(blocks, ('row', 'ch'), split_axis=0, concat_axis=0, tiled=...  12.1 us
    all_to_all x2, starting transfers between devices, exchange_all(): lax.all_to_all(blocks, ('row', 'ch'), split_axis=0, concat_axis=0, tiled=...  9.96 us
    ppermute x16, waiting for transfers between devices, swap(): lax.ppermute(block, ('row', 'ch'), [(n, n ^ s) for n in range(self.device...  7.73 us
  transfers between devices with their start and end apart: 18, of which 8 were waited for; matrix products, arithmetic and copies ran while one was open for 0% of the time, Pallas kernels for 13%

profile of v8, /device:TPU:0, one launch (start us, length us, event | category | flops | bytes accessed | tf_op | source)
XLA Modules:
  0.0 102.0 jit_solution(1482639440274614443)
XLA Ops:
  0.0 3.5 %shard_map.82 = (bf16[32,8,16,128]{3,2,1,0:T(8,128)(2,1)}, bf16[8,128,256]{2,1,0:T(8,128)(2,1)S(1)}) custom-call(bf16[16,128,128]{2,1,0:T(8,128)(2,1)} %refs_2_.1, f32[1,128]{1,0:T(1,128)} %bitcast.4, f32[1,128]{1,0:T(1,128)} %bitcast.8, bf16[128,640]{1,0:T(8,128)(2,1)} %w_ref.1), custom_call_target="tpu_custom_call" | custom-call | tf_op jit(solution)/shard_map/pallas_call | solution.py:52
  3.5 7.3 %all-to-all-start = ((bf16[32,8,16,128]{3,2,1,0:T(8,128)(2,1)}), bf16[32,8,16,128]{3,2,1,0:T(8,128)(2,1)S(1)}, u32[]{:S(2)}, u32[]{:S(2)}) async-start(bf16[32,8,16,128]{3,2,1,0:T(8,128)(2,1)} %get-tuple-element.41), calls=%async_computation | async-start | bytes 2097152 | tf_op jit(solution)/shard_map/all_to_all | solution.py:451
  10.8 2.2 %shard_map.84 = (bf16[8,8,16,128]{3,2,1,0:T(8,128)(2,1)S(1)}, bf16[8,8,16,128]{3,2,1,0:T(8,128)(2,1)S(1)}) custom-call(bf16[128,640]{1,0:T(8,128)(2,1)} %w_ref.1, bf16[8,128,256]{2,1,0:T(8,128)(2,1)S(1)} %get-tuple-element.46.n_ref), custom_call_target="tpu_custom_call" | custom-call | tf_op jit(solution)/shard_map/pallas_call | solution.py:52
  13.0 0.3 collective-permute-start
  13.3 1.3 %collective-permute-done.mates_ref.refs_1_ = bf16[8,8,16,128]{3,2,1,0:T(8,128)(2,1)S(1)} collective-permute-done((bf16[8,8,16,128]{3,2,1,0:T(8,128)(2,1)S(1)}, bf16[8,8,16,128]{3,2,1,0:T(8,128)(2,1)S(1)}, u32[]{:S(2)}, u32[]{:S(2)}) %collective-permute-start) | collective-permute-done | bytes 262176 | tf_op jit(solution)/shard_map/ppermute | solution.py:462
  14.6 1.8 %collective-permute-start.1 = (bf16[2,8,16,128]{3,2,1,0:T(8,128)(2,1)S(1)}, bf16[2,8,16,128]{3,2,1,0:T(8,128)(2,1)S(1)}, u32[]{:S(2)}, u32[]{:S(2)}) collective-permute-start(bf16[2,8,16,128]{3,2,1,0:T(8,128)(2,1)S(1)} %get-tuple-element.49), channel_id=1, source_target_pairs={{0,1},{1,0},{2,3},{3,2},{4,5},{5,4},{6,7},{7,6},{8,9},{9,8},{10,11... | collective-permute-start | bytes 196616 | tf_op jit(solution)/shard_map/ppermute | solution.py:462
  16.4 1.5 %collective-permute-start.2 = (bf16[2,8,16,128]{3,2,1,0:T(8,128)(2,1)S(1)}, bf16[2,8,16,128]{3,2,1,0:T(8,128)(2,1)S(1)}, u32[]{:S(2)}, u32[]{:S(2)}) collective-permute-start(bf16[2,8,16,128]{3,2,1,0:T(8,128)(2,1)S(1)} %get-tuple-element.50), channel_id=1, source_target_pairs={{0,4},{1,5},{2,6},{3,7},{4,0},{5,1},{6,2},{7,3},{8,12},{9,13},{10,... | collective-permute-start | bytes 196616 | tf_op jit(solution)/shard_map/ppermute | solution.py:462
  17.9 1.5 %collective-permute-start.3 = (bf16[2,8,16,128]{3,2,1,0:T(8,128)(2,1)S(1)}, bf16[2,8,16,128]{3,2,1,0:T(8,128)(2,1)S(1)}, u32[]{:S(2)}, u32[]{:S(2)}) collective-permute-start(bf16[2,8,16,128]{3,2,1,0:T(8,128)(2,1)S(1)} %get-tuple-element.51), channel_id=1, source_target_pairs={{0,13},{1,12},{2,15},{3,14},{4,9},{5,8},{6,11},{7,10},{8,5},{9,4},... | collective-permute-start | bytes 196616 | tf_op jit(solution)/shard_map/ppermute | solution.py:462
  19.4 1.5 %collective-permute-start.4 = (bf16[2,8,16,128]{3,2,1,0:T(8,128)(2,1)S(1)}, bf16[2,8,16,128]{3,2,1,0:T(8,128)(2,1)S(1)}, u32[]{:S(2)}, u32[]{:S(2)}) collective-permute-start(bf16[2,8,16,128]{3,2,1,0:T(8,128)(2,1)S(1)} %get-tuple-element.52), channel_id=1, source_target_pairs={{0,12},{1,13},{2,14},{3,15},{4,8},{5,9},{6,10},{7,11},{8,4},{9,5},... | collective-permute-start | bytes 196616 | tf_op jit(solution)/shard_map/ppermute | solution.py:462
  20.8 2.4 %collective-permute-start.5 = (bf16[2,8,16,128]{3,2,1,0:T(8,128)(2,1)S(1)}, bf16[2,8,16,128]{3,2,1,0:T(8,128)(2,1)S(1)}, u32[]{:S(2)}, u32[]{:S(2)}) collective-permute-start(bf16[2,8,16,128]{3,2,1,0:T(8,128)(2,1)S(1)} %get-tuple-element.53), channel_id=1, source_target_pairs={{0,9},{1,8},{2,11},{3,10},{4,13},{5,12},{6,15},{7,14},{8,1},{9,0},... | collective-permute-start | bytes 196616 | tf_op jit(solution)/shard_map/ppermute | solution.py:462
  23.2 0.0 collective-permute-done.1.refs_2_
  23.2 0.6 collective-permute-start.6
  23.7 0.0 collective-permute-done.2.refs_3_
  23.7 0.4 collective-permute-start.7
  24.1 5.7 %shard_map.83 = (f32[16,128,128]{2,1,0:T(8,128)S(1)}, bf16[16,512,128]{2,1,0:T(8,128)(2,1)}) custom-call(bf16[16,128,128]{2,1,0:T(8,128)(2,1)} %refs_2_.1, bf16[16,128,128]{2,1,0:T(8,128)(2,1)} %refs_3_.1, f32[1,128]{1,0:T(1,128)} %bitcast.5, f32[1,128]{1,0:T(1,128)} %bitcast.9, bf16[128,640]{1,0:T(8,128)(2,1)} %w_ref.1, f32[1,128]{1,0:T(1,128)} %bitcast.11, ...), custom_call_target="tpu_custom_call" | custom-call | tf_op jit(solution)/shard_map/pallas_call | solution.py:52
  29.9 8.5 %all-to-all-done.r_ref = bf16[32,8,16,128]{3,2,1,0:T(8,128)(2,1)S(1)} async-done(((bf16[32,8,16,128]{3,2,1,0:T(8,128)(2,1)}), bf16[32,8,16,128]{3,2,1,0:T(8,128)(2,1)S(1)}, u32[]{:S(2)}, u32[]{:S(2)}) %all-to-all-start) | async-done | bytes 1048608 | tf_op jit(solution)/shard_map/all_to_all | solution.py:451
  38.4 0.0 collective-permute-done.3.refs_4_
  38.4 0.0 collective-permute-done.4.refs_5_
  38.4 0.0 collective-permute-done.5.refs_6_
  38.4 0.0 collective-permute-done.6.refs_7_
  38.4 0.0 collective-permute-done.7.refs_8_
  38.4 0.5 shard_map.86
  38.9 13.2 %all_to_all.20.t_ref = bf16[16,8,16,128]{3,2,1,0:T(8,128)(2,1)S(1)} all-to-all(bf16[16,8,16,128]{3,2,1,0:T(8,128)(2,1)S(1)} %get-tuple-element.56), channel_id=1, replica_groups={{0,2,8,10,4,6,12,14,1,3,9,11,5,7,13,15},{16,18,24,26,20,22,28,30,17,19,..., dimensions={0} | all-to-all | bytes 1048576 | tf_op jit(solution)/shard_map/all_to_all | solution.py:457
  52.0 1.2 %shard_map.87 = (bf16[16,8,16,128]{3,2,1,0:T(8,128)(2,1)S(1)}, bf16[16,8,16,128]{3,2,1,0:T(8,128)(2,1)}) custom-call(bf16[16,8,16,128]{3,2,1,0:T(8,128)(2,1)S(1)} %all_to_all.20.t_ref, f32[16,128,128]{2,1,0:T(8,128)S(1)} %get-tuple-element.57.h_ref), custom_call_target="tpu_custom_call" | custom-call | tf_op jit(solution)/shard_map/pallas_call | solution.py:52
  53.2 13.2 %all_to_all.21.gt_ref = bf16[16,8,16,128]{3,2,1,0:T(8,128)(2,1)S(1)} all-to-all(bf16[16,8,16,128]{3,2,1,0:T(8,128)(2,1)S(1)} %get-tuple-element.64), channel_id=1, replica_groups={{0,2,8,10,4,6,12,14,1,3,9,11,5,7,13,15},{16,18,24,26,20,22,28,30,17,19,..., dimensions={0} | all-to-all | bytes 1048576 | tf_op jit(solution)/shard_map/all_to_all | solution.py:457
  66.4 1.3 %shard_map.89 = (bf16[32,8,16,128]{3,2,1,0:T(8,128)(2,1)}, bf16[8,8,16,128]{3,2,1,0:T(8,128)(2,1)S(1)}, bf16[8,8,16,128]{3,2,1,0:T(8,128)(2,1)S(1)}) custom-call(bf16[16,8,16,128]{3,2,1,0:T(8,128)(2,1)S(1)} %all_to_all.21.gt_ref, bf16[16,8,16,128]{3,2,1,0:T(8,128)(2,1)S(1)} %get-tuple-element.65.l_ref, bf16[32,8,16,128]{3,2,1,0:T(8,128)(2,1)S(1)} %all-to-all-done.r_ref), custom_call_target="tpu_custom_call" | custom-call | tf_op jit(solution)/shard_map/pallas_call | solution.py:52
  67.8 2.7 %all-to-all-start.3 = ((bf16[32,8,16,128]{3,2,1,0:T(8,128)(2,1)}), bf16[32,8,16,128]{3,2,1,0:T(8,128)(2,1)S(1)}, u32[]{:S(2)}, u32[]{:S(2)}) async-start(bf16[32,8,16,128]{3,2,1,0:T(8,128)(2,1)} %get-tuple-element.66), calls=%async_computation.3 | async-start | bytes 2097152 | tf_op jit(solution)/shard_map/all_to_all | solution.py:451
  70.4 0.2 collective-permute-start.8
  70.6 1.4 %collective-permute-done.8.mates_ref.refs_1_ = bf16[8,8,16,128]{3,2,1,0:T(8,128)(2,1)S(1)} collective-permute-done((bf16[8,8,16,128]{3,2,1,0:T(8,128)(2,1)S(1)}, bf16[8,8,16,128]{3,2,1,0:T(8,128)(2,1)S(1)}, u32[]{:S(2)}, u32[]{:S(2)}) %collective-permute-start.8) | collective-permute-done | bytes 262176 | tf_op jit(solution)/shard_map/ppermute | solution.py:462
  72.0 0.0 copy-start
  72.0 0.0 copy-start.1
  72.1 1.7 %collective-permute-start.9 = (bf16[2,8,16,128]{3,2,1,0:T(8,128)(2,1)S(1)}, bf16[2,8,16,128]{3,2,1,0:T(8,128)(2,1)S(1)}, u32[]{:S(2)}, u32[]{:S(2)}) collective-permute-start(bf16[2,8,16,128]{3,2,1,0:T(8,128)(2,1)S(1)} %get-tuple-element.70), channel_id=1, source_target_pairs={{0,1},{1,0},{2,3},{3,2},{4,5},{5,4},{6,7},{7,6},{8,9},{9,8},{10,11... | collective-permute-start | bytes 196616 | tf_op jit(solution)/shard_map/ppermute | solution.py:462
  73.8 1.5 %collective-permute-start.10 = (bf16[2,8,16,128]{3,2,1,0:T(8,128)(2,1)S(1)}, bf16[2,8,16,128]{3,2,1,0:T(8,128)(2,1)S(1)}, u32[]{:S(2)}, u32[]{:S(2)}) collective-permute-start(bf16[2,8,16,128]{3,2,1,0:T(8,128)(2,1)S(1)} %get-tuple-element.71), channel_id=1, source_target_pairs={{0,4},{1,5},{2,6},{3,7},{4,0},{5,1},{6,2},{7,3},{8,12},{9,13},{10,... | collective-permute-start | bytes 196616 | tf_op jit(solution)/shard_map/ppermute | solution.py:462
  75.3 1.5 %collective-permute-start.11 = (bf16[2,8,16,128]{3,2,1,0:T(8,128)(2,1)S(1)}, bf16[2,8,16,128]{3,2,1,0:T(8,128)(2,1)S(1)}, u32[]{:S(2)}, u32[]{:S(2)}) collective-permute-start(bf16[2,8,16,128]{3,2,1,0:T(8,128)(2,1)S(1)} %get-tuple-element.72), channel_id=1, source_target_pairs={{0,13},{1,12},{2,15},{3,14},{4,9},{5,8},{6,11},{7,10},{8,5},{9,4},... | collective-permute-start | bytes 196616 | tf_op jit(solution)/shard_map/ppermute | solution.py:462
  76.7 1.4 %collective-permute-start.12 = (bf16[2,8,16,128]{3,2,1,0:T(8,128)(2,1)S(1)}, bf16[2,8,16,128]{3,2,1,0:T(8,128)(2,1)S(1)}, u32[]{:S(2)}, u32[]{:S(2)}) collective-permute-start(bf16[2,8,16,128]{3,2,1,0:T(8,128)(2,1)S(1)} %get-tuple-element.73), channel_id=1, source_target_pairs={{0,12},{1,13},{2,14},{3,15},{4,8},{5,9},{6,10},{7,11},{8,4},{9,5},... | collective-permute-start | bytes 196616 | tf_op jit(solution)/shard_map/ppermute | solution.py:462
  78.2 2.4 %collective-permute-start.13 = (bf16[2,8,16,128]{3,2,1,0:T(8,128)(2,1)S(1)}, bf16[2,8,16,128]{3,2,1,0:T(8,128)(2,1)S(1)}, u32[]{:S(2)}, u32[]{:S(2)}) collective-permute-start(bf16[2,8,16,128]{3,2,1,0:T(8,128)(2,1)S(1)} %get-tuple-element.74), channel_id=1, source_target_pairs={{0,9},{1,8},{2,11},{3,10},{4,13},{5,12},{6,15},{7,14},{8,1},{9,0},... | collective-permute-start | bytes 196616 | tf_op jit(solution)/shard_map/ppermute | solution.py:462
  80.6 0.0 collective-permute-done.9.refs_2_
  80.6 0.5 collective-permute-start.14
  81.1 0.0 collective-permute-done.10.refs_3_
  81.1 2.5 %collective-permute-start.15 = (bf16[2,8,16,128]{3,2,1,0:T(8,128)(2,1)S(1)}, bf16[2,8,16,128]{3,2,1,0:T(8,128)(2,1)S(1)}, u32[]{:S(2)}, u32[]{:S(2)}) collective-permute-start(bf16[2,8,16,128]{3,2,1,0:T(8,128)(2,1)S(1)} %get-tuple-element.76), channel_id=1, source_target_pairs={{0,5},{1,4},{2,7},{3,6},{4,1},{5,0},{6,3},{7,2},{8,13},{9,12},{10,... | collective-permute-start | bytes 196616 | tf_op jit(solution)/shard_map/ppermute | solution.py:462
  83.6 5.8 %shard_map.88 = (bf16[4,128,128]{2,1,0:T(8,128)(2,1)S(1)}, bf16[4,128,128]{2,1,0:T(8,128)(2,1)S(1)}, bf16[4,512,128]{2,1,0:T(8,128)(2,1)S(1)}, bf16[16,128,128]{...) custom-call(bf16[16,512,128]{2,1,0:T(8,128)(2,1)} %get-tuple-element.44.refs_0_.fac_hbm, ...), custom_call_target="tpu_custom_call" | custom-call | tf_op jit(solution)/shard_map/pallas_call | solution.py:52
  89.4 0.3 collective-permute-done.11.refs_4_
  89.6 1.5 %collective-permute-done.12.refs_5_ = bf16[2,8,16,128]{3,2,1,0:T(8,128)(2,1)S(1)} collective-permute-done((bf16[2,8,16,128]{3,2,1,0:T(8,128)(2,1)S(1)}, bf16[2,8,16,128]{3,2,1,0:T(8,128)(2,1)S(1)}, u32[]{:S(2)}, u32[]{:S(2)}) %collective-permute-start.12) | collective-permute-done | bytes 65568 | tf_op jit(solution)/shard_map/ppermute | solution.py:462
  91.1 2.4 %collective-permute-done.13.refs_6_ = bf16[2,8,16,128]{3,2,1,0:T(8,128)(2,1)S(1)} collective-permute-done((bf16[2,8,16,128]{3,2,1,0:T(8,128)(2,1)S(1)}, bf16[2,8,16,128]{3,2,1,0:T(8,128)(2,1)S(1)}, u32[]{:S(2)}, u32[]{:S(2)}) %collective-permute-start.13) | collective-permute-done | bytes 65568 | tf_op jit(solution)/shard_map/ppermute | solution.py:462
  93.5 0.9 collective-permute-done.14.refs_7_
  94.4 0.0 collective-permute-done.15.refs_8_
  94.4 3.6 %all-to-all-done.3.r_ref = bf16[32,8,16,128]{3,2,1,0:T(8,128)(2,1)S(1)} async-done(((bf16[32,8,16,128]{3,2,1,0:T(8,128)(2,1)}), bf16[32,8,16,128]{3,2,1,0:T(8,128)(2,1)S(1)}, u32[]{:S(2)}, u32[]{:S(2)}) %all-to-all-start.3) | async-done | bytes 1048608 | tf_op jit(solution)/shard_map/all_to_all | solution.py:451
  98.0 0.0 copy-done
  98.0 0.0 copy-done.1
  98.0 4.0 %shard_map.91 = bf16[16,128,128]{2,1,0:T(8,128)(2,1)} custom-call(bf16[16,512,128]{2,1,0:T(8,128)(2,1)} %get-tuple-element.44.refs_0_.fac_hbm, bf16[16,128,128]{2,1,0:T(8,128)(2,1)} %get-tuple-element.59.nt_hbm, bf16[16,128,128]{2,1,0:T(8,128)(2,1)} %get-tuple-element.60.gin_hbm, bf16[4,512,128]{2,1,0:T(8,128)(2,1)S(1)} %get-tuple-element.61.fac0_ref, ...), custom_call_target="tpu_custom_call" | custom-call | tf_op jit(solution)/shard_map/pallas_call | solution.py:52
  (2 shorter events, 0.1 us)
Async XLA Ops:
  3.5 34.9 %all-to-all-start = ((bf16[32,8,16,128]{3,2,1,0:T(8,128)(2,1)}), bf16[32,8,16,128]{3,2,1,0:T(8,128)(2,1)S(1)}, u32[]{:S(2)}, u32[]{:S(2)}) async-start(bf16[32,8,16,128]{3,2,1,0:T(8,128)(2,1)} %get-tuple-element.41), calls=%async_computation | async-start | bytes 2097152 | tf_op jit(solution)/shard_map/all_to_all | solution.py:451
  13.0 1.6 %collective-permute-start = (bf16[8,8,16,128]{3,2,1,0:T(8,128)(2,1)S(1)}, bf16[8,8,16,128]{3,2,1,0:T(8,128)(2,1)S(1)}, u32[]{:S(2)}, u32[]{:S(2)}) collective-permute-start(bf16[8,8,16,128]{3,2,1,0:T(8,128)(2,1)S(1)} %get-tuple-element.48), channel_id=1, source_target_pairs={{0,2},{1,3},{2,0},{3,1},{4,6},{5,7},{6,4},{7,5},{8,10},{9,11},{10,... | collective-permute-start | bytes 786440 | tf_op jit(solution)/shard_map/ppermute | solution.py:462
  14.6 8.6 %collective-permute-start.1 = (bf16[2,8,16,128]{3,2,1,0:T(8,128)(2,1)S(1)}, bf16[2,8,16,128]{3,2,1,0:T(8,128)(2,1)S(1)}, u32[]{:S(2)}, u32[]{:S(2)}) collective-permute-start(bf16[2,8,16,128]{3,2,1,0:T(8,128)(2,1)S(1)} %get-tuple-element.49), channel_id=1, source_target_pairs={{0,1},{1,0},{2,3},{3,2},{4,5},{5,4},{6,7},{7,6},{8,9},{9,8},{10,11... | collective-permute-start | bytes 196616 | tf_op jit(solution)/shard_map/ppermute | solution.py:462
  16.4 7.3 %collective-permute-start.2 = (bf16[2,8,16,128]{3,2,1,0:T(8,128)(2,1)S(1)}, bf16[2,8,16,128]{3,2,1,0:T(8,128)(2,1)S(1)}, u32[]{:S(2)}, u32[]{:S(2)}) collective-permute-start(bf16[2,8,16,128]{3,2,1,0:T(8,128)(2,1)S(1)} %get-tuple-element.50), channel_id=1, source_target_pairs={{0,4},{1,5},{2,6},{3,7},{4,0},{5,1},{6,2},{7,3},{8,12},{9,13},{10,... | collective-permute-start | bytes 196616 | tf_op jit(solution)/shard_map/ppermute | solution.py:462
  17.9 20.5 %collective-permute-start.3 = (bf16[2,8,16,128]{3,2,1,0:T(8,128)(2,1)S(1)}, bf16[2,8,16,128]{3,2,1,0:T(8,128)(2,1)S(1)}, u32[]{:S(2)}, u32[]{:S(2)}) collective-permute-start(bf16[2,8,16,128]{3,2,1,0:T(8,128)(2,1)S(1)} %get-tuple-element.51), channel_id=1, source_target_pairs={{0,13},{1,12},{2,15},{3,14},{4,9},{5,8},{6,11},{7,10},{8,5},{9,4},... | collective-permute-start | bytes 196616 | tf_op jit(solution)/shard_map/ppermute | solution.py:462
  19.4 19.0 %collective-permute-start.4 = (bf16[2,8,16,128]{3,2,1,0:T(8,128)(2,1)S(1)}, bf16[2,8,16,128]{3,2,1,0:T(8,128)(2,1)S(1)}, u32[]{:S(2)}, u32[]{:S(2)}) collective-permute-start(bf16[2,8,16,128]{3,2,1,0:T(8,128)(2,1)S(1)} %get-tuple-element.52), channel_id=1, source_target_pairs={{0,12},{1,13},{2,14},{3,15},{4,8},{5,9},{6,10},{7,11},{8,4},{9,5},... | collective-permute-start | bytes 196616 | tf_op jit(solution)/shard_map/ppermute | solution.py:462
  20.8 17.6 %collective-permute-start.5 = (bf16[2,8,16,128]{3,2,1,0:T(8,128)(2,1)S(1)}, bf16[2,8,16,128]{3,2,1,0:T(8,128)(2,1)S(1)}, u32[]{:S(2)}, u32[]{:S(2)}) collective-permute-start(bf16[2,8,16,128]{3,2,1,0:T(8,128)(2,1)S(1)} %get-tuple-element.53), channel_id=1, source_target_pairs={{0,9},{1,8},{2,11},{3,10},{4,13},{5,12},{6,15},{7,14},{8,1},{9,0},... | collective-permute-start | bytes 196616 | tf_op jit(solution)/shard_map/ppermute | solution.py:462
  23.2 15.2 %collective-permute-start.6 = (bf16[2,8,16,128]{3,2,1,0:T(8,128)(2,1)S(1)}, bf16[2,8,16,128]{3,2,1,0:T(8,128)(2,1)S(1)}, u32[]{:S(2)}, u32[]{:S(2)}) collective-permute-start(bf16[2,8,16,128]{3,2,1,0:T(8,128)(2,1)S(1)} %get-tuple-element.54), channel_id=1, source_target_pairs={{0,8},{1,9},{2,10},{3,11},{4,12},{5,13},{6,14},{7,15},{8,0},{9,1},... | collective-permute-start | bytes 196616 | tf_op jit(solution)/shard_map/ppermute | solution.py:462
  23.7 14.6 %collective-permute-start.7 = (bf16[2,8,16,128]{3,2,1,0:T(8,128)(2,1)S(1)}, bf16[2,8,16,128]{3,2,1,0:T(8,128)(2,1)S(1)}, u32[]{:S(2)}, u32[]{:S(2)}) collective-permute-start(bf16[2,8,16,128]{3,2,1,0:T(8,128)(2,1)S(1)} %get-tuple-element.55), channel_id=1, source_target_pairs={{0,5},{1,4},{2,7},{3,6},{4,1},{5,0},{6,3},{7,2},{8,13},{9,12},{10,... | collective-permute-start | bytes 196616 | tf_op jit(solution)/shard_map/ppermute | solution.py:462
  67.8 30.3 %all-to-all-start.3 = ((bf16[32,8,16,128]{3,2,1,0:T(8,128)(2,1)}), bf16[32,8,16,128]{3,2,1,0:T(8,128)(2,1)S(1)}, u32[]{:S(2)}, u32[]{:S(2)}) async-start(bf16[32,8,16,128]{3,2,1,0:T(8,128)(2,1)} %get-tuple-element.66), calls=%async_computation.3 | async-start | bytes 2097152 | tf_op jit(solution)/shard_map/all_to_all | solution.py:451
  70.4 1.6 %collective-permute-start.8 = (bf16[8,8,16,128]{3,2,1,0:T(8,128)(2,1)S(1)}, bf16[8,8,16,128]{3,2,1,0:T(8,128)(2,1)S(1)}, u32[]{:S(2)}, u32[]{:S(2)}) collective-permute-start(bf16[8,8,16,128]{3,2,1,0:T(8,128)(2,1)S(1)} %get-tuple-element.69), channel_id=1, source_target_pairs={{0,2},{1,3},{2,0},{3,1},{4,6},{5,7},{6,4},{7,5},{8,10},{9,11},{10,... | collective-permute-start | bytes 786440 | tf_op jit(solution)/shard_map/ppermute | solution.py:462
  72.0 26.0 %copy-start = (bf16[128,640]{1,0:T(8,128)(2,1)S(1)}, bf16[128,640]{1,0:T(8,128)(2,1)}, u32[]{:S(2)}) copy-start(bf16[128,640]{1,0:T(8,128)(2,1)} %w_ref.1) | copy-start | bytes 491524
  72.0 26.0 %copy-start.1 = (f32[128]{0:T(128)S(1)}, f32[128]{0:T(128)}, u32[]{:S(2)}) copy-start(f32[128]{0:T(128)} %param.10) | copy-start | bytes 1540
  72.1 8.6 %collective-permute-start.9 = (bf16[2,8,16,128]{3,2,1,0:T(8,128)(2,1)S(1)}, bf16[2,8,16,128]{3,2,1,0:T(8,128)(2,1)S(1)}, u32[]{:S(2)}, u32[]{:S(2)}) collective-permute-start(bf16[2,8,16,128]{3,2,1,0:T(8,128)(2,1)S(1)} %get-tuple-element.70), channel_id=1, source_target_pairs={{0,1},{1,0},{2,3},{3,2},{4,5},{5,4},{6,7},{7,6},{8,9},{9,8},{10,11... | collective-permute-start | bytes 196616 | tf_op jit(solution)/shard_map/ppermute | solution.py:462
  73.8 7.4 %collective-permute-start.10 = (bf16[2,8,16,128]{3,2,1,0:T(8,128)(2,1)S(1)}, bf16[2,8,16,128]{3,2,1,0:T(8,128)(2,1)S(1)}, u32[]{:S(2)}, u32[]{:S(2)}) collective-permute-start(bf16[2,8,16,128]{3,2,1,0:T(8,128)(2,1)S(1)} %get-tuple-element.71), channel_id=1, source_target_pairs={{0,4},{1,5},{2,6},{3,7},{4,0},{5,1},{6,2},{7,3},{8,12},{9,13},{10,... | collective-permute-start | bytes 196616 | tf_op jit(solution)/shard_map/ppermute | solution.py:462
  75.3 14.4 %collective-permute-start.11 = (bf16[2,8,16,128]{3,2,1,0:T(8,128)(2,1)S(1)}, bf16[2,8,16,128]{3,2,1,0:T(8,128)(2,1)S(1)}, u32[]{:S(2)}, u32[]{:S(2)}) collective-permute-start(bf16[2,8,16,128]{3,2,1,0:T(8,128)(2,1)S(1)} %get-tuple-element.72), channel_id=1, source_target_pairs={{0,13},{1,12},{2,15},{3,14},{4,9},{5,8},{6,11},{7,10},{8,5},{9,4},... | collective-permute-start | bytes 196616 | tf_op jit(solution)/shard_map/ppermute | solution.py:462
  76.7 14.4 %collective-permute-start.12 = (bf16[2,8,16,128]{3,2,1,0:T(8,128)(2,1)S(1)}, bf16[2,8,16,128]{3,2,1,0:T(8,128)(2,1)S(1)}, u32[]{:S(2)}, u32[]{:S(2)}) collective-permute-start(bf16[2,8,16,128]{3,2,1,0:T(8,128)(2,1)S(1)} %get-tuple-element.73), channel_id=1, source_target_pairs={{0,12},{1,13},{2,14},{3,15},{4,8},{5,9},{6,10},{7,11},{8,4},{9,5},... | collective-permute-start | bytes 196616 | tf_op jit(solution)/shard_map/ppermute | solution.py:462
  78.2 15.4 %collective-permute-start.13 = (bf16[2,8,16,128]{3,2,1,0:T(8,128)(2,1)S(1)}, bf16[2,8,16,128]{3,2,1,0:T(8,128)(2,1)S(1)}, u32[]{:S(2)}, u32[]{:S(2)}) collective-permute-start(bf16[2,8,16,128]{3,2,1,0:T(8,128)(2,1)S(1)} %get-tuple-element.74), channel_id=1, source_target_pairs={{0,9},{1,8},{2,11},{3,10},{4,13},{5,12},{6,15},{7,14},{8,1},{9,0},... | collective-permute-start | bytes 196616 | tf_op jit(solution)/shard_map/ppermute | solution.py:462
  80.6 13.8 %collective-permute-start.14 = (bf16[2,8,16,128]{3,2,1,0:T(8,128)(2,1)S(1)}, bf16[2,8,16,128]{3,2,1,0:T(8,128)(2,1)S(1)}, u32[]{:S(2)}, u32[]{:S(2)}) collective-permute-start(bf16[2,8,16,128]{3,2,1,0:T(8,128)(2,1)S(1)} %get-tuple-element.75), channel_id=1, source_target_pairs={{0,8},{1,9},{2,10},{3,11},{4,12},{5,13},{6,14},{7,15},{8,0},{9,1},... | collective-permute-start | bytes 196616 | tf_op jit(solution)/shard_map/ppermute | solution.py:462
  81.1 13.3 %collective-permute-start.15 = (bf16[2,8,16,128]{3,2,1,0:T(8,128)(2,1)S(1)}, bf16[2,8,16,128]{3,2,1,0:T(8,128)(2,1)S(1)}, u32[]{:S(2)}, u32[]{:S(2)}) collective-permute-start(bf16[2,8,16,128]{3,2,1,0:T(8,128)(2,1)S(1)} %get-tuple-element.76), channel_id=1, source_target_pairs={{0,5},{1,4},{2,7},{3,6},{4,1},{5,0},{6,3},{7,2},{8,13},{9,12},{10,... | collective-permute-start | bytes 196616 | tf_op jit(solution)/shard_map/ppermute | solution.py:462

commit v9 on v7

--- a/solution.py
+++ b/solution.py
@@ -267,12 +267,10 @@
             ts_ref[:, here] = block.reshape(rows, group, cols)
 
 
-def tri_back_kernel(lay, t_ref, h_ref, gt_ref, t_hbm, ts_ref, gs_ref, sem):
+def tri_back_kernel(lay, t_ref, h_ref, gt_ref, ts_ref, gs_ref):
     rows, width, cols = h_ref.shape
     mine = t_ref.shape[1]
     group = BLOCK // rows
-    copy = pltpu.make_async_copy(t_ref, t_hbm, sem)
-    copy.start()
     back = permutation(group, rows)
     to_rows(lay, t_ref, ts_ref)
 
@@ -293,14 +291,13 @@
             block = block.reshape(group // mine, mine, rows, cols)
             for share in range(to.start, to.stop):
                 gt_ref[lay.inside.index(share)] = block[share - to.start]
-    copy.wait()
 
 
 def logit_kernel(lay, *refs):
-    (fac_hbm, *sources), refs = refs[:10], refs[10:]
+    (fac_hbm, *sources), t_ref, refs = refs[:9], refs[9], refs[10:]
     (gin0_ref, nt0_ref, fac0_ref, gin_hbm, nt_hbm, s_ref), refs = refs[:6], refs[6:]
-    (ts_ref, gin_ref, nt_ref, out_sems), targets, sems = refs[:4], refs[4:13], refs[13]
-    t_ref, x_ref, cot_ref, gain_ref, bias_ref, w_ref, ogain_ref, obias_ref, ow_ref = targets
+    (ts_ref, gin_ref, nt_ref, out_sems), targets, sems = refs[:4], refs[4:12], refs[12]
+    x_ref, cot_ref, gain_ref, bias_ref, w_ref, ogain_ref, obias_ref, ow_ref = targets
     rows, cols, width = x_ref.shape
     first = pl.ds(0, nt0_ref.shape[0])
     fetched([*sources, fac_hbm.at[first]], [*targets, fac0_ref], sems)
@@ -606,13 +603,7 @@
     right, h, fac = lax.optimization_barrier((right, h, fac))
     tri, left = call(functools.partial(tri_kernel, lay), [one, one], [], right, *left)
     tri = lay.exchange_half(tri)
-    grad_tri, tri = call(
-        functools.partial(tri_back_kernel, lay),
-        [one, pltpu.HBM(one.shape, BF16)],
-        [half, half, pltpu.SemaphoreType.DMA(())],
-        tri,
-        h,
-    )
+    grad_tri = call(functools.partial(tri_back_kernel, lay), one, [half, half], tri, h)
     grad_right, *grad_left = call(
         functools.partial(factor_back_kernel, lay),
         [pltpu.HBM(two_shape, BF16), some, some],
@@ -638,7 +629,6 @@
             half,
             half,
             pltpu.SemaphoreType.DMA((2,)),
-            one_here,
             half,
             half,
             row,
@@ -647,10 +637,9 @@
             row,
             row,
             out_weight_here,
-            pltpu.SemaphoreType.DMA((10,)),
+            pltpu.SemaphoreType.DMA((9,)),
         ],
         fac,
-        tri,
         pair_act,
         cotangent,
         in_gain,
@@ -659,7 +648,8 @@
         out_gain,
         out_bias,
         out_weight,
-        hbm=10,
+        tri,
+        hbm=9,
     )
     return call(
         functools.partial(pair_kernel, lay),

time: 99 us -> 99 us (level)
  no operation moved by 1% of the time
where the time goes in v9:
time: 99 us; the launch traced here: 97.7 us
  starting transfers between devices  34.2 us (35%)
  blocking collectives  25.4 us (26%)
  Pallas kernels  24 us (24%)
  waiting for transfers between devices  13.9 us (14%)
    all_to_all x2, blocking collectives, exchange_half(): lax.all_to_all(blocks, ('row', 'ch'), split_axis=0, concat_axis=0, tiled=...  25.4 us
    pallas_call x10, Pallas kernels, call(): pl.pallas_call(kernel, out_shape=outs if single else tuple(outs), in_spec...  24 us
    ppermute x16, starting transfers between devices, swap(): lax.ppermute(block, ('row', 'ch'), [(n, n ^ s) for n in range(self.device...  23.2 us
    all_to_all x2, starting transfers between devices, exchange_all(): lax.all_to_all(blocks, ('row', 'ch'), split_axis=0, concat_axis=0, tiled=...  11 us
    ppermute x16, waiting for transfers between devices, swap(): lax.ppermute(block, ('row', 'ch'), [(n, n ^ s) for n in range(self.device...  8.79 us
    all_to_all x2, waiting for transfers between devices, exchange_all(): lax.all_to_all(blocks, ('row', 'ch'), split_axis=0, concat_axis=0, tiled=...  5.16 us
  transfers between devices with their start and end apart: 18, of which 7 were waited for; matrix products, arithmetic and copies ran while one was open for 0% of the time, Pallas kernels for 14%

profile of v9, /device:TPU:0, one launch (start us, length us, event | category | flops | bytes accessed | tf_op | source)
XLA Modules:
  0.0 97.7 jit_solution(14005049327726415766)
XLA Ops:
  0.0 3.4 %shard_map.82 = (bf16[32,8,16,128]{3,2,1,0:T(8,128)(2,1)}, bf16[8,128,256]{2,1,0:T(8,128)(2,1)S(1)}) custom-call(bf16[16,128,128]{2,1,0:T(8,128)(2,1)} %refs_1_.3, f32[1,128]{1,0:T(1,128)} %bitcast.4, f32[1,128]{1,0:T(1,128)} %bitcast.8, bf16[128,640]{1,0:T(8,128)(2,1)} %w_ref.1), custom_call_target="tpu_custom_call" | custom-call | tf_op jit(solution)/shard_map/pallas_call | solution.py:52
  3.4 7.3 %all-to-all-start = ((bf16[32,8,16,128]{3,2,1,0:T(8,128)(2,1)}), bf16[32,8,16,128]{3,2,1,0:T(8,128)(2,1)S(1)}, u32[]{:S(2)}, u32[]{:S(2)}) async-start(bf16[32,8,16,128]{3,2,1,0:T(8,128)(2,1)} %get-tuple-element.39), calls=%async_computation | async-start | bytes 2097152 | tf_op jit(solution)/shard_map/all_to_all | solution.py:448
  10.8 2.2 %shard_map.84 = (bf16[8,8,16,128]{3,2,1,0:T(8,128)(2,1)S(1)}, bf16[8,8,16,128]{3,2,1,0:T(8,128)(2,1)S(1)}) custom-call(bf16[128,640]{1,0:T(8,128)(2,1)} %w_ref.1, bf16[8,128,256]{2,1,0:T(8,128)(2,1)S(1)} %get-tuple-element.44.n_ref), custom_call_target="tpu_custom_call" | custom-call | tf_op jit(solution)/shard_map/pallas_call | solution.py:52
  12.9 0.3 collective-permute-start
  13.3 1.3 %collective-permute-done.mates_ref.refs_1_ = bf16[8,8,16,128]{3,2,1,0:T(8,128)(2,1)S(1)} collective-permute-done((bf16[8,8,16,128]{3,2,1,0:T(8,128)(2,1)S(1)}, bf16[8,8,16,128]{3,2,1,0:T(8,128)(2,1)S(1)}, u32[]{:S(2)}, u32[]{:S(2)}) %collective-permute-start) | collective-permute-done | bytes 262176 | tf_op jit(solution)/shard_map/ppermute | solution.py:459
  14.6 1.8 %collective-permute-start.1 = (bf16[2,8,16,128]{3,2,1,0:T(8,128)(2,1)S(1)}, bf16[2,8,16,128]{3,2,1,0:T(8,128)(2,1)S(1)}, u32[]{:S(2)}, u32[]{:S(2)}) collective-permute-start(bf16[2,8,16,128]{3,2,1,0:T(8,128)(2,1)S(1)} %get-tuple-element.47), channel_id=1, source_target_pairs={{0,1},{1,0},{2,3},{3,2},{4,5},{5,4},{6,7},{7,6},{8,9},{9,8},{10,11... | collective-permute-start | bytes 196616 | tf_op jit(solution)/shard_map/ppermute | solution.py:459
  16.4 1.5 %collective-permute-start.2 = (bf16[2,8,16,128]{3,2,1,0:T(8,128)(2,1)S(1)}, bf16[2,8,16,128]{3,2,1,0:T(8,128)(2,1)S(1)}, u32[]{:S(2)}, u32[]{:S(2)}) collective-permute-start(bf16[2,8,16,128]{3,2,1,0:T(8,128)(2,1)S(1)} %get-tuple-element.48), channel_id=1, source_target_pairs={{0,4},{1,5},{2,6},{3,7},{4,0},{5,1},{6,2},{7,3},{8,12},{9,13},{10,... | collective-permute-start | bytes 196616 | tf_op jit(solution)/shard_map/ppermute | solution.py:459
  17.9 1.5 %collective-permute-start.3 = (bf16[2,8,16,128]{3,2,1,0:T(8,128)(2,1)S(1)}, bf16[2,8,16,128]{3,2,1,0:T(8,128)(2,1)S(1)}, u32[]{:S(2)}, u32[]{:S(2)}) collective-permute-start(bf16[2,8,16,128]{3,2,1,0:T(8,128)(2,1)S(1)} %get-tuple-element.49), channel_id=1, source_target_pairs={{0,13},{1,12},{2,15},{3,14},{4,9},{5,8},{6,11},{7,10},{8,5},{9,4},... | collective-permute-start | bytes 196616 | tf_op jit(solution)/shard_map/ppermute | solution.py:459
  19.3 1.5 %collective-permute-start.4 = (bf16[2,8,16,128]{3,2,1,0:T(8,128)(2,1)S(1)}, bf16[2,8,16,128]{3,2,1,0:T(8,128)(2,1)S(1)}, u32[]{:S(2)}, u32[]{:S(2)}) collective-permute-start(bf16[2,8,16,128]{3,2,1,0:T(8,128)(2,1)S(1)} %get-tuple-element.50), channel_id=1, source_target_pairs={{0,12},{1,13},{2,14},{3,15},{4,8},{5,9},{6,10},{7,11},{8,4},{9,5},... | collective-permute-start | bytes 196616 | tf_op jit(solution)/shard_map/ppermute | solution.py:459
  20.8 2.4 %collective-permute-start.5 = (bf16[2,8,16,128]{3,2,1,0:T(8,128)(2,1)S(1)}, bf16[2,8,16,128]{3,2,1,0:T(8,128)(2,1)S(1)}, u32[]{:S(2)}, u32[]{:S(2)}) collective-permute-start(bf16[2,8,16,128]{3,2,1,0:T(8,128)(2,1)S(1)} %get-tuple-element.51), channel_id=1, source_target_pairs={{0,9},{1,8},{2,11},{3,10},{4,13},{5,12},{6,15},{7,14},{8,1},{9,0},... | collective-permute-start | bytes 196616 | tf_op jit(solution)/shard_map/ppermute | solution.py:459
  23.2 0.0 collective-permute-done.1.refs_2_
  23.2 0.6 collective-permute-start.6
  23.7 0.0 collective-permute-done.2.refs_3_
  23.7 1.2 %collective-permute-start.7 = (bf16[2,8,16,128]{3,2,1,0:T(8,128)(2,1)S(1)}, bf16[2,8,16,128]{3,2,1,0:T(8,128)(2,1)S(1)}, u32[]{:S(2)}, u32[]{:S(2)}) collective-permute-start(bf16[2,8,16,128]{3,2,1,0:T(8,128)(2,1)S(1)} %get-tuple-element.53), channel_id=1, source_target_pairs={{0,5},{1,4},{2,7},{3,6},{4,1},{5,0},{6,3},{7,2},{8,13},{9,12},{10,... | collective-permute-start | bytes 196616 | tf_op jit(solution)/shard_map/ppermute | solution.py:459
  24.9 5.7 %shard_map.83 = (f32[16,128,128]{2,1,0:T(8,128)S(1)}, bf16[16,512,128]{2,1,0:T(8,128)(2,1)}) custom-call(bf16[16,128,128]{2,1,0:T(8,128)(2,1)} %refs_1_.3, bf16[16,128,128]{2,1,0:T(8,128)(2,1)} %refs_2_.1, f32[1,128]{1,0:T(1,128)} %bitcast.5, f32[1,128]{1,0:T(1,128)} %bitcast.9, bf16[128,640]{1,0:T(8,128)(2,1)} %w_ref.1, f32[1,128]{1,0:T(1,128)} %bitcast.11, ...), custom_call_target="tpu_custom_call" | custom-call | tf_op jit(solution)/shard_map/pallas_call | solution.py:52
  30.7 5.2 %all-to-all-done.r_ref = bf16[32,8,16,128]{3,2,1,0:T(8,128)(2,1)S(1)} async-done(((bf16[32,8,16,128]{3,2,1,0:T(8,128)(2,1)}), bf16[32,8,16,128]{3,2,1,0:T(8,128)(2,1)S(1)}, u32[]{:S(2)}, u32[]{:S(2)}) %all-to-all-start) | async-done | bytes 1048608 | tf_op jit(solution)/shard_map/all_to_all | solution.py:448
  35.8 0.0 collective-permute-done.3.refs_4_
  35.8 0.0 collective-permute-done.4.refs_5_
  35.8 0.0 collective-permute-done.5.refs_6_
  35.8 0.3 collective-permute-done.6.refs_7_
  36.1 0.0 collective-permute-done.7.refs_8_
  36.1 0.5 shard_map.86
  36.6 13.1 %all_to_all.20.refs_9_.t_ref = bf16[16,8,16,128]{3,2,1,0:T(8,128)(2,1)S(1)} all-to-all(bf16[16,8,16,128]{3,2,1,0:T(8,128)(2,1)S(1)} %get-tuple-element.54), channel_id=1, replica_groups={{0,8,2,10,4,12,6,14,1,9,3,11,5,13,7,15},{16,24,18,26,20,28,22,30,17,25,..., dimensions={0} | all-to-all | bytes 1048576 | tf_op jit(solution)/shard_map/all_to_all | solution.py:454
  49.8 1.2 %shard_map.88 = bf16[16,8,16,128]{3,2,1,0:T(8,128)(2,1)S(1)} custom-call(bf16[16,8,16,128]{3,2,1,0:T(8,128)(2,1)S(1)} %all_to_all.20.refs_9_.t_ref, f32[16,128,128]{2,1,0:T(8,128)S(1)} %get-tuple-element.60.h_ref), custom_call_target="tpu_custom_call" | custom-call | tf_op jit(solution)/shard_map/pallas_call | solution.py:52
  51.0 12.3 %all_to_all.21.gt_ref = bf16[16,8,16,128]{3,2,1,0:T(8,128)(2,1)S(1)} all-to-all(bf16[16,8,16,128]{3,2,1,0:T(8,128)(2,1)S(1)} %shard_map.88), channel_id=1, replica_groups={{0,8,2,10,4,12,6,14,1,9,3,11,5,13,7,15},{16,24,18,26,20,28,22,30,17,25,..., dimensions={0} | all-to-all | bytes 1048576 | tf_op jit(solution)/shard_map/all_to_all | solution.py:454
  63.2 1.4 %shard_map.89 = (bf16[32,8,16,128]{3,2,1,0:T(8,128)(2,1)}, bf16[8,8,16,128]{3,2,1,0:T(8,128)(2,1)S(1)}, bf16[8,8,16,128]{3,2,1,0:T(8,128)(2,1)S(1)}) custom-call(bf16[16,8,16,128]{3,2,1,0:T(8,128)(2,1)S(1)} %all_to_all.21.gt_ref, bf16[16,8,16,128]{3,2,1,0:T(8,128)(2,1)S(1)} %get-tuple-element.61.l_ref, bf16[32,8,16,128]{3,2,1,0:T(8,128)(2,1)S(1)} %all-to-all-done.r_ref), custom_call_target="tpu_custom_call" | custom-call | tf_op jit(solution)/shard_map/pallas_call | solution.py:52
  64.6 3.7 %all-to-all-start.3 = ((bf16[32,8,16,128]{3,2,1,0:T(8,128)(2,1)}), bf16[32,8,16,128]{3,2,1,0:T(8,128)(2,1)S(1)}, u32[]{:S(2)}, u32[]{:S(2)}) async-start(bf16[32,8,16,128]{3,2,1,0:T(8,128)(2,1)} %get-tuple-element.62), calls=%async_computation.3 | async-start | bytes 2097152 | tf_op jit(solution)/shard_map/all_to_all | solution.py:448
  68.3 0.3 collective-permute-start.8
  68.7 1.3 %collective-permute-done.8.mates_ref.refs_1_ = bf16[8,8,16,128]{3,2,1,0:T(8,128)(2,1)S(1)} collective-permute-done((bf16[8,8,16,128]{3,2,1,0:T(8,128)(2,1)S(1)}, bf16[8,8,16,128]{3,2,1,0:T(8,128)(2,1)S(1)}, u32[]{:S(2)}, u32[]{:S(2)}) %collective-permute-start.8) | collective-permute-done | bytes 262176 | tf_op jit(solution)/shard_map/ppermute | solution.py:459
  69.9 0.0 copy-start
  69.9 0.0 copy-start.1
  70.0 1.8 %collective-permute-start.9 = (bf16[2,8,16,128]{3,2,1,0:T(8,128)(2,1)S(1)}, bf16[2,8,16,128]{3,2,1,0:T(8,128)(2,1)S(1)}, u32[]{:S(2)}, u32[]{:S(2)}) collective-permute-start(bf16[2,8,16,128]{3,2,1,0:T(8,128)(2,1)S(1)} %get-tuple-element.66), channel_id=1, source_target_pairs={{0,1},{1,0},{2,3},{3,2},{4,5},{5,4},{6,7},{7,6},{8,9},{9,8},{10,11... | collective-permute-start | bytes 196616 | tf_op jit(solution)/shard_map/ppermute | solution.py:459
  71.8 1.5 %collective-permute-start.10 = (bf16[2,8,16,128]{3,2,1,0:T(8,128)(2,1)S(1)}, bf16[2,8,16,128]{3,2,1,0:T(8,128)(2,1)S(1)}, u32[]{:S(2)}, u32[]{:S(2)}) collective-permute-start(bf16[2,8,16,128]{3,2,1,0:T(8,128)(2,1)S(1)} %get-tuple-element.67), channel_id=1, source_target_pairs={{0,4},{1,5},{2,6},{3,7},{4,0},{5,1},{6,2},{7,3},{8,12},{9,13},{10,... | collective-permute-start | bytes 196616 | tf_op jit(solution)/shard_map/ppermute | solution.py:459
  73.3 1.5 %collective-permute-start.11 = (bf16[2,8,16,128]{3,2,1,0:T(8,128)(2,1)S(1)}, bf16[2,8,16,128]{3,2,1,0:T(8,128)(2,1)S(1)}, u32[]{:S(2)}, u32[]{:S(2)}) collective-permute-start(bf16[2,8,16,128]{3,2,1,0:T(8,128)(2,1)S(1)} %get-tuple-element.68), channel_id=1, source_target_pairs={{0,13},{1,12},{2,15},{3,14},{4,9},{5,8},{6,11},{7,10},{8,5},{9,4},... | collective-permute-start | bytes 196616 | tf_op jit(solution)/shard_map/ppermute | solution.py:459
  74.7 1.5 %collective-permute-start.12 = (bf16[2,8,16,128]{3,2,1,0:T(8,128)(2,1)S(1)}, bf16[2,8,16,128]{3,2,1,0:T(8,128)(2,1)S(1)}, u32[]{:S(2)}, u32[]{:S(2)}) collective-permute-start(bf16[2,8,16,128]{3,2,1,0:T(8,128)(2,1)S(1)} %get-tuple-element.69), channel_id=1, source_target_pairs={{0,12},{1,13},{2,14},{3,15},{4,8},{5,9},{6,10},{7,11},{8,4},{9,5},... | collective-permute-start | bytes 196616 | tf_op jit(solution)/shard_map/ppermute | solution.py:459
  76.2 2.4 %collective-permute-start.13 = (bf16[2,8,16,128]{3,2,1,0:T(8,128)(2,1)S(1)}, bf16[2,8,16,128]{3,2,1,0:T(8,128)(2,1)S(1)}, u32[]{:S(2)}, u32[]{:S(2)}) collective-permute-start(bf16[2,8,16,128]{3,2,1,0:T(8,128)(2,1)S(1)} %get-tuple-element.70), channel_id=1, source_target_pairs={{0,9},{1,8},{2,11},{3,10},{4,13},{5,12},{6,15},{7,14},{8,1},{9,0},... | collective-permute-start | bytes 196616 | tf_op jit(solution)/shard_map/ppermute | solution.py:459
  78.6 0.0 collective-permute-done.9.refs_2_
  78.6 0.8 collective-permute-start.14
  79.3 0.0 collective-permute-done.10.refs_3_
  79.3 2.9 %collective-permute-start.15 = (bf16[2,8,16,128]{3,2,1,0:T(8,128)(2,1)S(1)}, bf16[2,8,16,128]{3,2,1,0:T(8,128)(2,1)S(1)}, u32[]{:S(2)}, u32[]{:S(2)}) collective-permute-start(bf16[2,8,16,128]{3,2,1,0:T(8,128)(2,1)S(1)} %get-tuple-element.72), channel_id=1, source_target_pairs={{0,5},{1,4},{2,7},{3,6},{4,1},{5,0},{6,3},{7,2},{8,13},{9,12},{10,... | collective-permute-start | bytes 196616 | tf_op jit(solution)/shard_map/ppermute | solution.py:459
  82.2 5.6 %shard_map.87 = (bf16[4,128,128]{2,1,0:T(8,128)(2,1)S(1)}, bf16[4,128,128]{2,1,0:T(8,128)(2,1)S(1)}, bf16[4,512,128]{2,1,0:T(8,128)(2,1)S(1)}, bf16[16,128,128]{...) custom-call(bf16[16,512,128]{2,1,0:T(8,128)(2,1)} %get-tuple-element.42.refs_0_.fac_hbm, ...), custom_call_target="tpu_custom_call" | custom-call | tf_op jit(solution)/shard_map/pallas_call | solution.py:52
  87.8 0.0 collective-permute-done.11.refs_4_
  87.9 1.3 %collective-permute-done.12.refs_5_ = bf16[2,8,16,128]{3,2,1,0:T(8,128)(2,1)S(1)} collective-permute-done((bf16[2,8,16,128]{3,2,1,0:T(8,128)(2,1)S(1)}, bf16[2,8,16,128]{3,2,1,0:T(8,128)(2,1)S(1)}, u32[]{:S(2)}, u32[]{:S(2)}) %collective-permute-start.12) | collective-permute-done | bytes 65568 | tf_op jit(solution)/shard_map/ppermute | solution.py:459
  89.2 3.8 %collective-permute-done.13.refs_6_ = bf16[2,8,16,128]{3,2,1,0:T(8,128)(2,1)S(1)} collective-permute-done((bf16[2,8,16,128]{3,2,1,0:T(8,128)(2,1)S(1)}, bf16[2,8,16,128]{3,2,1,0:T(8,128)(2,1)S(1)}, u32[]{:S(2)}, u32[]{:S(2)}) %collective-permute-start.13) | collective-permute-done | bytes 65568 | tf_op jit(solution)/shard_map/ppermute | solution.py:459
  93.0 0.8 collective-permute-done.14.refs_7_
  93.7 0.0 collective-permute-done.15.refs_8_
  93.7 0.0 all-to-all-done.3.r_ref
  93.7 0.0 copy-done
  93.7 0.0 copy-done.1
  93.7 4.0 %shard_map.91 = bf16[16,128,128]{2,1,0:T(8,128)(2,1)} custom-call(bf16[16,512,128]{2,1,0:T(8,128)(2,1)} %get-tuple-element.42.refs_0_.fac_hbm, bf16[16,128,128]{2,1,0:T(8,128)(2,1)} %get-tuple-element.55.nt_hbm, bf16[16,128,128]{2,1,0:T(8,128)(2,1)} %get-tuple-element.56.gin_hbm, bf16[4,512,128]{2,1,0:T(8,128)(2,1)S(1)} %get-tuple-element.57.fac0_ref, ...), custom_call_target="tpu_custom_call" | custom-call | tf_op jit(solution)/shard_map/pallas_call | solution.py:52
  (2 shorter events, 0.1 us)
Async XLA Ops:
  3.4 32.4 %all-to-all-start = ((bf16[32,8,16,128]{3,2,1,0:T(8,128)(2,1)}), bf16[32,8,16,128]{3,2,1,0:T(8,128)(2,1)S(1)}, u32[]{:S(2)}, u32[]{:S(2)}) async-start(bf16[32,8,16,128]{3,2,1,0:T(8,128)(2,1)} %get-tuple-element.39), calls=%async_computation | async-start | bytes 2097152 | tf_op jit(solution)/shard_map/all_to_all | solution.py:448
  12.9 1.6 %collective-permute-start = (bf16[8,8,16,128]{3,2,1,0:T(8,128)(2,1)S(1)}, bf16[8,8,16,128]{3,2,1,0:T(8,128)(2,1)S(1)}, u32[]{:S(2)}, u32[]{:S(2)}) collective-permute-start(bf16[8,8,16,128]{3,2,1,0:T(8,128)(2,1)S(1)} %get-tuple-element.46), channel_id=1, source_target_pairs={{0,2},{1,3},{2,0},{3,1},{4,6},{5,7},{6,4},{7,5},{8,10},{9,11},{10,... | collective-permute-start | bytes 786440 | tf_op jit(solution)/shard_map/ppermute | solution.py:459
  14.6 8.6 %collective-permute-start.1 = (bf16[2,8,16,128]{3,2,1,0:T(8,128)(2,1)S(1)}, bf16[2,8,16,128]{3,2,1,0:T(8,128)(2,1)S(1)}, u32[]{:S(2)}, u32[]{:S(2)}) collective-permute-start(bf16[2,8,16,128]{3,2,1,0:T(8,128)(2,1)S(1)} %get-tuple-element.47), channel_id=1, source_target_pairs={{0,1},{1,0},{2,3},{3,2},{4,5},{5,4},{6,7},{7,6},{8,9},{9,8},{10,11... | collective-permute-start | bytes 196616 | tf_op jit(solution)/shard_map/ppermute | solution.py:459
  16.4 7.3 %collective-permute-start.2 = (bf16[2,8,16,128]{3,2,1,0:T(8,128)(2,1)S(1)}, bf16[2,8,16,128]{3,2,1,0:T(8,128)(2,1)S(1)}, u32[]{:S(2)}, u32[]{:S(2)}) collective-permute-start(bf16[2,8,16,128]{3,2,1,0:T(8,128)(2,1)S(1)} %get-tuple-element.48), channel_id=1, source_target_pairs={{0,4},{1,5},{2,6},{3,7},{4,0},{5,1},{6,2},{7,3},{8,12},{9,13},{10,... | collective-permute-start | bytes 196616 | tf_op jit(solution)/shard_map/ppermute | solution.py:459
  17.9 17.9 %collective-permute-start.3 = (bf16[2,8,16,128]{3,2,1,0:T(8,128)(2,1)S(1)}, bf16[2,8,16,128]{3,2,1,0:T(8,128)(2,1)S(1)}, u32[]{:S(2)}, u32[]{:S(2)}) collective-permute-start(bf16[2,8,16,128]{3,2,1,0:T(8,128)(2,1)S(1)} %get-tuple-element.49), channel_id=1, source_target_pairs={{0,13},{1,12},{2,15},{3,14},{4,9},{5,8},{6,11},{7,10},{8,5},{9,4},... | collective-permute-start | bytes 196616 | tf_op jit(solution)/shard_map/ppermute | solution.py:459
  19.3 16.5 %collective-permute-start.4 = (bf16[2,8,16,128]{3,2,1,0:T(8,128)(2,1)S(1)}, bf16[2,8,16,128]{3,2,1,0:T(8,128)(2,1)S(1)}, u32[]{:S(2)}, u32[]{:S(2)}) collective-permute-start(bf16[2,8,16,128]{3,2,1,0:T(8,128)(2,1)S(1)} %get-tuple-element.50), channel_id=1, source_target_pairs={{0,12},{1,13},{2,14},{3,15},{4,8},{5,9},{6,10},{7,11},{8,4},{9,5},... | collective-permute-start | bytes 196616 | tf_op jit(solution)/shard_map/ppermute | solution.py:459
  20.8 15.0 %collective-permute-start.5 = (bf16[2,8,16,128]{3,2,1,0:T(8,128)(2,1)S(1)}, bf16[2,8,16,128]{3,2,1,0:T(8,128)(2,1)S(1)}, u32[]{:S(2)}, u32[]{:S(2)}) collective-permute-start(bf16[2,8,16,128]{3,2,1,0:T(8,128)(2,1)S(1)} %get-tuple-element.51), channel_id=1, source_target_pairs={{0,9},{1,8},{2,11},{3,10},{4,13},{5,12},{6,15},{7,14},{8,1},{9,0},... | collective-permute-start | bytes 196616 | tf_op jit(solution)/shard_map/ppermute | solution.py:459
  23.2 13.0 %collective-permute-start.6 = (bf16[2,8,16,128]{3,2,1,0:T(8,128)(2,1)S(1)}, bf16[2,8,16,128]{3,2,1,0:T(8,128)(2,1)S(1)}, u32[]{:S(2)}, u32[]{:S(2)}) collective-permute-start(bf16[2,8,16,128]{3,2,1,0:T(8,128)(2,1)S(1)} %get-tuple-element.52), channel_id=1, source_target_pairs={{0,8},{1,9},{2,10},{3,11},{4,12},{5,13},{6,14},{7,15},{8,0},{9,1},... | collective-permute-start | bytes 196616 | tf_op jit(solution)/shard_map/ppermute | solution.py:459
  23.7 12.4 %collective-permute-start.7 = (bf16[2,8,16,128]{3,2,1,0:T(8,128)(2,1)S(1)}, bf16[2,8,16,128]{3,2,1,0:T(8,128)(2,1)S(1)}, u32[]{:S(2)}, u32[]{:S(2)}) collective-permute-start(bf16[2,8,16,128]{3,2,1,0:T(8,128)(2,1)S(1)} %get-tuple-element.53), channel_id=1, source_target_pairs={{0,5},{1,4},{2,7},{3,6},{4,1},{5,0},{6,3},{7,2},{8,13},{9,12},{10,... | collective-permute-start | bytes 196616 | tf_op jit(solution)/shard_map/ppermute | solution.py:459
  64.6 29.1 %all-to-all-start.3 = ((bf16[32,8,16,128]{3,2,1,0:T(8,128)(2,1)}), bf16[32,8,16,128]{3,2,1,0:T(8,128)(2,1)S(1)}, u32[]{:S(2)}, u32[]{:S(2)}) async-start(bf16[32,8,16,128]{3,2,1,0:T(8,128)(2,1)} %get-tuple-element.62), calls=%async_computation.3 | async-start | bytes 2097152 | tf_op jit(solution)/shard_map/all_to_all | solution.py:448
  68.3 1.6 %collective-permute-start.8 = (bf16[8,8,16,128]{3,2,1,0:T(8,128)(2,1)S(1)}, bf16[8,8,16,128]{3,2,1,0:T(8,128)(2,1)S(1)}, u32[]{:S(2)}, u32[]{:S(2)}) collective-permute-start(bf16[8,8,16,128]{3,2,1,0:T(8,128)(2,1)S(1)} %get-tuple-element.65), channel_id=1, source_target_pairs={{0,2},{1,3},{2,0},{3,1},{4,6},{5,7},{6,4},{7,5},{8,10},{9,11},{10,... | collective-permute-start | bytes 786440 | tf_op jit(solution)/shard_map/ppermute | solution.py:459
  69.9 23.8 %copy-start = (bf16[128,640]{1,0:T(8,128)(2,1)S(1)}, bf16[128,640]{1,0:T(8,128)(2,1)}, u32[]{:S(2)}) copy-start(bf16[128,640]{1,0:T(8,128)(2,1)} %w_ref.1) | copy-start | bytes 491524
  69.9 23.8 %copy-start.1 = (f32[128]{0:T(128)S(1)}, f32[128]{0:T(128)}, u32[]{:S(2)}) copy-start(f32[128]{0:T(128)} %param.10) | copy-start | bytes 1540
  70.0 8.6 %collective-permute-start.9 = (bf16[2,8,16,128]{3,2,1,0:T(8,128)(2,1)S(1)}, bf16[2,8,16,128]{3,2,1,0:T(8,128)(2,1)S(1)}, u32[]{:S(2)}, u32[]{:S(2)}) collective-permute-start(bf16[2,8,16,128]{3,2,1,0:T(8,128)(2,1)S(1)} %get-tuple-element.66), channel_id=1, source_target_pairs={{0,1},{1,0},{2,3},{3,2},{4,5},{5,4},{6,7},{7,6},{8,9},{9,8},{10,11... | collective-permute-start | bytes 196616 | tf_op jit(solution)/shard_map/ppermute | solution.py:459
  71.8 7.5 %collective-permute-start.10 = (bf16[2,8,16,128]{3,2,1,0:T(8,128)(2,1)S(1)}, bf16[2,8,16,128]{3,2,1,0:T(8,128)(2,1)S(1)}, u32[]{:S(2)}, u32[]{:S(2)}) collective-permute-start(bf16[2,8,16,128]{3,2,1,0:T(8,128)(2,1)S(1)} %get-tuple-element.67), channel_id=1, source_target_pairs={{0,4},{1,5},{2,6},{3,7},{4,0},{5,1},{6,2},{7,3},{8,12},{9,13},{10,... | collective-permute-start | bytes 196616 | tf_op jit(solution)/shard_map/ppermute | solution.py:459
  73.3 14.6 %collective-permute-start.11 = (bf16[2,8,16,128]{3,2,1,0:T(8,128)(2,1)S(1)}, bf16[2,8,16,128]{3,2,1,0:T(8,128)(2,1)S(1)}, u32[]{:S(2)}, u32[]{:S(2)}) collective-permute-start(bf16[2,8,16,128]{3,2,1,0:T(8,128)(2,1)S(1)} %get-tuple-element.68), channel_id=1, source_target_pairs={{0,13},{1,12},{2,15},{3,14},{4,9},{5,8},{6,11},{7,10},{8,5},{9,4},... | collective-permute-start | bytes 196616 | tf_op jit(solution)/shard_map/ppermute | solution.py:459
  74.7 14.5 %collective-permute-start.12 = (bf16[2,8,16,128]{3,2,1,0:T(8,128)(2,1)S(1)}, bf16[2,8,16,128]{3,2,1,0:T(8,128)(2,1)S(1)}, u32[]{:S(2)}, u32[]{:S(2)}) collective-permute-start(bf16[2,8,16,128]{3,2,1,0:T(8,128)(2,1)S(1)} %get-tuple-element.69), channel_id=1, source_target_pairs={{0,12},{1,13},{2,14},{3,15},{4,8},{5,9},{6,10},{7,11},{8,4},{9,5},... | collective-permute-start | bytes 196616 | tf_op jit(solution)/shard_map/ppermute | solution.py:459
  76.2 16.8 %collective-permute-start.13 = (bf16[2,8,16,128]{3,2,1,0:T(8,128)(2,1)S(1)}, bf16[2,8,16,128]{3,2,1,0:T(8,128)(2,1)S(1)}, u32[]{:S(2)}, u32[]{:S(2)}) collective-permute-start(bf16[2,8,16,128]{3,2,1,0:T(8,128)(2,1)S(1)} %get-tuple-element.70), channel_id=1, source_target_pairs={{0,9},{1,8},{2,11},{3,10},{4,13},{5,12},{6,15},{7,14},{8,1},{9,0},... | collective-permute-start | bytes 196616 | tf_op jit(solution)/shard_map/ppermute | solution.py:459
  78.6 15.2 %collective-permute-start.14 = (bf16[2,8,16,128]{3,2,1,0:T(8,128)(2,1)S(1)}, bf16[2,8,16,128]{3,2,1,0:T(8,128)(2,1)S(1)}, u32[]{:S(2)}, u32[]{:S(2)}) collective-permute-start(bf16[2,8,16,128]{3,2,1,0:T(8,128)(2,1)S(1)} %get-tuple-element.71), channel_id=1, source_target_pairs={{0,8},{1,9},{2,10},{3,11},{4,12},{5,13},{6,14},{7,15},{8,0},{9,1},... | collective-permute-start | bytes 196616 | tf_op jit(solution)/shard_map/ppermute | solution.py:459
  79.3 14.4 %collective-permute-start.15 = (bf16[2,8,16,128]{3,2,1,0:T(8,128)(2,1)S(1)}, bf16[2,8,16,128]{3,2,1,0:T(8,128)(2,1)S(1)}, u32[]{:S(2)}, u32[]{:S(2)}) collective-permute-start(bf16[2,8,16,128]{3,2,1,0:T(8,128)(2,1)S(1)} %get-tuple-element.72), channel_id=1, source_target_pairs={{0,5},{1,4},{2,7},{3,6},{4,1},{5,0},{6,3},{7,2},{8,13},{9,12},{10,... | collective-permute-start | bytes 196616 | tf_op jit(solution)/shard_map/ppermute | solution.py:459

commit v10 on v9

--- a/solution.py
+++ b/solution.py
@@ -428,7 +428,7 @@
         self.inside = [o * self.inner + n for n in near for o in range(outer // 2)]
         self.mate = n_ch
         self.hops = [s for s in range(self.half) if s & self.mate == 0]
-        self.hops[3:] = self.hops[:2:-1]
+        self.hops[3:] = sorted(self.hops[3:], key=lambda s: (s < self.inner, s % n_ch == 0, -s))
         self.n_hops = len(self.hops) + 1
         self.all_place = self.place(self.order, n_row)
         self.half_place = self.place(self.inside, n_row // 2)

time: 99 us -> 99.3 us (level)
  no operation moved by 1% of the time
where the time goes in v10:
time: 99.3 us; the launch traced here: 97.6 us
  starting transfers between devices  34.5 us (35%)
  blocking collectives  25.7 us (26%)
  Pallas kernels  24 us (24%)
  waiting for transfers between devices  13.3 us (13%)
    all_to_all x2, blocking collectives, exchange_half(): lax.all_to_all(blocks, ('row', 'ch'), split_axis=0, concat_axis=0, tiled=...  25.7 us
    pallas_call x10, Pallas kernels, call(): pl.pallas_call(kernel, out_shape=outs if single else tuple(outs), in_spec...  24 us
    ppermute x16, starting transfers between devices, swap(): lax.ppermute(block, ('row', 'ch'), [(n, n ^ s) for n in range(self.device...  23.2 us
    all_to_all x2, starting transfers between devices, exchange_all(): lax.all_to_all(blocks, ('row', 'ch'), split_axis=0, concat_axis=0, tiled=...  11.3 us
    ppermute x16, waiting for transfers between devices, swap(): lax.ppermute(block, ('row', 'ch'), [(n, n ^ s) for n in range(self.device...  7.99 us
    all_to_all x2, waiting for transfers between devices, exchange_all(): lax.all_to_all(blocks, ('row', 'ch'), split_axis=0, concat_axis=0, tiled=...  5.3 us
  transfers between devices with their start and end apart: 18, of which 7 were waited for; matrix products, arithmetic and copies ran while one was open for 0% of the time, Pallas kernels for 14%

profile of v10, /device:TPU:0, one launch (start us, length us, event | category | flops | bytes accessed | tf_op | source)
XLA Modules:
  0.0 97.6 jit_solution(5044759973858711361)
XLA Ops:
  0.0 3.4 %shard_map.82 = (bf16[32,8,16,128]{3,2,1,0:T(8,128)(2,1)}, bf16[8,128,256]{2,1,0:T(8,128)(2,1)S(1)}) custom-call(bf16[16,128,128]{2,1,0:T(8,128)(2,1)} %refs_1_.3, f32[1,128]{1,0:T(1,128)} %bitcast.4, f32[1,128]{1,0:T(1,128)} %bitcast.8, bf16[128,640]{1,0:T(8,128)(2,1)} %w_ref.1), custom_call_target="tpu_custom_call" | custom-call | tf_op jit(solution)/shard_map/pallas_call | solution.py:52
  3.4 7.3 %all-to-all-start = ((bf16[32,8,16,128]{3,2,1,0:T(8,128)(2,1)}), bf16[32,8,16,128]{3,2,1,0:T(8,128)(2,1)S(1)}, u32[]{:S(2)}, u32[]{:S(2)}) async-start(bf16[32,8,16,128]{3,2,1,0:T(8,128)(2,1)} %get-tuple-element.39), calls=%async_computation | async-start | bytes 2097152 | tf_op jit(solution)/shard_map/all_to_all | solution.py:448
  10.8 2.2 %shard_map.84 = (bf16[8,8,16,128]{3,2,1,0:T(8,128)(2,1)S(1)}, bf16[8,8,16,128]{3,2,1,0:T(8,128)(2,1)S(1)}) custom-call(bf16[128,640]{1,0:T(8,128)(2,1)} %w_ref.1, bf16[8,128,256]{2,1,0:T(8,128)(2,1)S(1)} %get-tuple-element.44.n_ref), custom_call_target="tpu_custom_call" | custom-call | tf_op jit(solution)/shard_map/pallas_call | solution.py:52
  12.9 0.3 collective-permute-start
  13.3 1.3 %collective-permute-done.mates_ref.refs_1_ = bf16[8,8,16,128]{3,2,1,0:T(8,128)(2,1)S(1)} collective-permute-done((bf16[8,8,16,128]{3,2,1,0:T(8,128)(2,1)S(1)}, bf16[8,8,16,128]{3,2,1,0:T(8,128)(2,1)S(1)}, u32[]{:S(2)}, u32[]{:S(2)}) %collective-permute-start) | collective-permute-done | bytes 262176 | tf_op jit(solution)/shard_map/ppermute | solution.py:459
  14.6 1.8 %collective-permute-start.1 = (bf16[2,8,16,128]{3,2,1,0:T(8,128)(2,1)S(1)}, bf16[2,8,16,128]{3,2,1,0:T(8,128)(2,1)S(1)}, u32[]{:S(2)}, u32[]{:S(2)}) collective-permute-start(bf16[2,8,16,128]{3,2,1,0:T(8,128)(2,1)S(1)} %get-tuple-element.47), channel_id=1, source_target_pairs={{0,1},{1,0},{2,3},{3,2},{4,5},{5,4},{6,7},{7,6},{8,9},{9,8},{10,11... | collective-permute-start | bytes 196616 | tf_op jit(solution)/shard_map/ppermute | solution.py:459
  16.4 1.5 %collective-permute-start.2 = (bf16[2,8,16,128]{3,2,1,0:T(8,128)(2,1)S(1)}, bf16[2,8,16,128]{3,2,1,0:T(8,128)(2,1)S(1)}, u32[]{:S(2)}, u32[]{:S(2)}) collective-permute-start(bf16[2,8,16,128]{3,2,1,0:T(8,128)(2,1)S(1)} %get-tuple-element.48), channel_id=1, source_target_pairs={{0,4},{1,5},{2,6},{3,7},{4,0},{5,1},{6,2},{7,3},{8,12},{9,13},{10,... | collective-permute-start | bytes 196616 | tf_op jit(solution)/shard_map/ppermute | solution.py:459
  17.9 1.5 %collective-permute-start.3 = (bf16[2,8,16,128]{3,2,1,0:T(8,128)(2,1)S(1)}, bf16[2,8,16,128]{3,2,1,0:T(8,128)(2,1)S(1)}, u32[]{:S(2)}, u32[]{:S(2)}) collective-permute-start(bf16[2,8,16,128]{3,2,1,0:T(8,128)(2,1)S(1)} %get-tuple-element.49), channel_id=1, source_target_pairs={{0,13},{1,12},{2,15},{3,14},{4,9},{5,8},{6,11},{7,10},{8,5},{9,4},... | collective-permute-start | bytes 196616 | tf_op jit(solution)/shard_map/ppermute | solution.py:459
  19.3 1.5 %collective-permute-start.4 = (bf16[2,8,16,128]{3,2,1,0:T(8,128)(2,1)S(1)}, bf16[2,8,16,128]{3,2,1,0:T(8,128)(2,1)S(1)}, u32[]{:S(2)}, u32[]{:S(2)}) collective-permute-start(bf16[2,8,16,128]{3,2,1,0:T(8,128)(2,1)S(1)} %get-tuple-element.50), channel_id=1, source_target_pairs={{0,9},{1,8},{2,11},{3,10},{4,13},{5,12},{6,15},{7,14},{8,1},{9,0},... | collective-permute-start | bytes 196616 | tf_op jit(solution)/shard_map/ppermute | solution.py:459
  20.8 2.4 %collective-permute-start.5 = (bf16[2,8,16,128]{3,2,1,0:T(8,128)(2,1)S(1)}, bf16[2,8,16,128]{3,2,1,0:T(8,128)(2,1)S(1)}, u32[]{:S(2)}, u32[]{:S(2)}) collective-permute-start(bf16[2,8,16,128]{3,2,1,0:T(8,128)(2,1)S(1)} %get-tuple-element.51), channel_id=1, source_target_pairs={{0,12},{1,13},{2,14},{3,15},{4,8},{5,9},{6,10},{7,11},{8,4},{9,5},... | collective-permute-start | bytes 196616 | tf_op jit(solution)/shard_map/ppermute | solution.py:459
  23.2 0.0 collective-permute-done.1.refs_2_
  23.2 0.6 collective-permute-start.6
  23.7 0.0 collective-permute-done.2.refs_3_
  23.7 1.2 %collective-permute-start.7 = (bf16[2,8,16,128]{3,2,1,0:T(8,128)(2,1)S(1)}, bf16[2,8,16,128]{3,2,1,0:T(8,128)(2,1)S(1)}, u32[]{:S(2)}, u32[]{:S(2)}) collective-permute-start(bf16[2,8,16,128]{3,2,1,0:T(8,128)(2,1)S(1)} %get-tuple-element.53), channel_id=1, source_target_pairs={{0,5},{1,4},{2,7},{3,6},{4,1},{5,0},{6,3},{7,2},{8,13},{9,12},{10,... | collective-permute-start | bytes 196616 | tf_op jit(solution)/shard_map/ppermute | solution.py:459
  24.9 5.7 %shard_map.83 = (f32[16,128,128]{2,1,0:T(8,128)S(1)}, bf16[16,512,128]{2,1,0:T(8,128)(2,1)}) custom-call(bf16[16,128,128]{2,1,0:T(8,128)(2,1)} %refs_1_.3, bf16[16,128,128]{2,1,0:T(8,128)(2,1)} %refs_2_.1, f32[1,128]{1,0:T(1,128)} %bitcast.5, f32[1,128]{1,0:T(1,128)} %bitcast.9, bf16[128,640]{1,0:T(8,128)(2,1)} %w_ref.1, f32[1,128]{1,0:T(1,128)} %bitcast.11, ...), custom_call_target="tpu_custom_call" | custom-call | tf_op jit(solution)/shard_map/pallas_call | solution.py:52
  30.7 5.2 %all-to-all-done.r_ref = bf16[32,8,16,128]{3,2,1,0:T(8,128)(2,1)S(1)} async-done(((bf16[32,8,16,128]{3,2,1,0:T(8,128)(2,1)}), bf16[32,8,16,128]{3,2,1,0:T(8,128)(2,1)S(1)}, u32[]{:S(2)}, u32[]{:S(2)}) %all-to-all-start) | async-done | bytes 1048608 | tf_op jit(solution)/shard_map/all_to_all | solution.py:448
  35.8 0.0 collective-permute-done.3.refs_4_
  35.8 0.0 collective-permute-done.4.refs_5_
  35.8 0.0 collective-permute-done.5.refs_6_
  35.8 0.0 collective-permute-done.6.refs_7_
  35.8 0.0 collective-permute-done.7.refs_8_
  35.8 0.5 shard_map.86
  36.3 13.5 %all_to_all.20.refs_9_.t_ref = bf16[16,8,16,128]{3,2,1,0:T(8,128)(2,1)S(1)} all-to-all(bf16[16,8,16,128]{3,2,1,0:T(8,128)(2,1)S(1)} %get-tuple-element.54), channel_id=1, replica_groups={{0,8,2,10,4,12,6,14,1,9,3,11,5,13,7,15},{16,24,18,26,20,28,22,30,17,25,..., dimensions={0} | all-to-all | bytes 1048576 | tf_op jit(solution)/shard_map/all_to_all | solution.py:454
  49.8 1.2 %shard_map.88 = bf16[16,8,16,128]{3,2,1,0:T(8,128)(2,1)S(1)} custom-call(bf16[16,8,16,128]{3,2,1,0:T(8,128)(2,1)S(1)} %all_to_all.20.refs_9_.t_ref, f32[16,128,128]{2,1,0:T(8,128)S(1)} %get-tuple-element.60.h_ref), custom_call_target="tpu_custom_call" | custom-call | tf_op jit(solution)/shard_map/pallas_call | solution.py:52
  51.0 12.3 %all_to_all.21.gt_ref = bf16[16,8,16,128]{3,2,1,0:T(8,128)(2,1)S(1)} all-to-all(bf16[16,8,16,128]{3,2,1,0:T(8,128)(2,1)S(1)} %shard_map.88), channel_id=1, replica_groups={{0,8,2,10,4,12,6,14,1,9,3,11,5,13,7,15},{16,24,18,26,20,28,22,30,17,25,..., dimensions={0} | all-to-all | bytes 1048576 | tf_op jit(solution)/shard_map/all_to_all | solution.py:454
  63.2 1.4 %shard_map.89 = (bf16[32,8,16,128]{3,2,1,0:T(8,128)(2,1)}, bf16[8,8,16,128]{3,2,1,0:T(8,128)(2,1)S(1)}, bf16[8,8,16,128]{3,2,1,0:T(8,128)(2,1)S(1)}) custom-call(bf16[16,8,16,128]{3,2,1,0:T(8,128)(2,1)S(1)} %all_to_all.21.gt_ref, bf16[16,8,16,128]{3,2,1,0:T(8,128)(2,1)S(1)} %get-tuple-element.61.l_ref, bf16[32,8,16,128]{3,2,1,0:T(8,128)(2,1)S(1)} %all-to-all-done.r_ref), custom_call_target="tpu_custom_call" | custom-call | tf_op jit(solution)/shard_map/pallas_call | solution.py:52
  64.6 4.0 %all-to-all-start.3 = ((bf16[32,8,16,128]{3,2,1,0:T(8,128)(2,1)}), bf16[32,8,16,128]{3,2,1,0:T(8,128)(2,1)S(1)}, u32[]{:S(2)}, u32[]{:S(2)}) async-start(bf16[32,8,16,128]{3,2,1,0:T(8,128)(2,1)} %get-tuple-element.62), calls=%async_computation.3 | async-start | bytes 2097152 | tf_op jit(solution)/shard_map/all_to_all | solution.py:448
  68.6 0.3 collective-permute-start.8
  68.9 1.3 %collective-permute-done.8.mates_ref.refs_1_ = bf16[8,8,16,128]{3,2,1,0:T(8,128)(2,1)S(1)} collective-permute-done((bf16[8,8,16,128]{3,2,1,0:T(8,128)(2,1)S(1)}, bf16[8,8,16,128]{3,2,1,0:T(8,128)(2,1)S(1)}, u32[]{:S(2)}, u32[]{:S(2)}) %collective-permute-start.8) | collective-permute-done | bytes 262176 | tf_op jit(solution)/shard_map/ppermute | solution.py:459
  70.2 0.0 copy-start
  70.2 0.0 copy-start.1
  70.2 1.8 %collective-permute-start.9 = (bf16[2,8,16,128]{3,2,1,0:T(8,128)(2,1)S(1)}, bf16[2,8,16,128]{3,2,1,0:T(8,128)(2,1)S(1)}, u32[]{:S(2)}, u32[]{:S(2)}) collective-permute-start(bf16[2,8,16,128]{3,2,1,0:T(8,128)(2,1)S(1)} %get-tuple-element.66), channel_id=1, source_target_pairs={{0,1},{1,0},{2,3},{3,2},{4,5},{5,4},{6,7},{7,6},{8,9},{9,8},{10,11... | collective-permute-start | bytes 196616 | tf_op jit(solution)/shard_map/ppermute | solution.py:459
  72.1 1.5 %collective-permute-start.10 = (bf16[2,8,16,128]{3,2,1,0:T(8,128)(2,1)S(1)}, bf16[2,8,16,128]{3,2,1,0:T(8,128)(2,1)S(1)}, u32[]{:S(2)}, u32[]{:S(2)}) collective-permute-start(bf16[2,8,16,128]{3,2,1,0:T(8,128)(2,1)S(1)} %get-tuple-element.67), channel_id=1, source_target_pairs={{0,4},{1,5},{2,6},{3,7},{4,0},{5,1},{6,2},{7,3},{8,12},{9,13},{10,... | collective-permute-start | bytes 196616 | tf_op jit(solution)/shard_map/ppermute | solution.py:459
  73.5 1.5 %collective-permute-start.11 = (bf16[2,8,16,128]{3,2,1,0:T(8,128)(2,1)S(1)}, bf16[2,8,16,128]{3,2,1,0:T(8,128)(2,1)S(1)}, u32[]{:S(2)}, u32[]{:S(2)}) collective-permute-start(bf16[2,8,16,128]{3,2,1,0:T(8,128)(2,1)S(1)} %get-tuple-element.68), channel_id=1, source_target_pairs={{0,13},{1,12},{2,15},{3,14},{4,9},{5,8},{6,11},{7,10},{8,5},{9,4},... | collective-permute-start | bytes 196616 | tf_op jit(solution)/shard_map/ppermute | solution.py:459
  75.0 1.5 %collective-permute-start.12 = (bf16[2,8,16,128]{3,2,1,0:T(8,128)(2,1)S(1)}, bf16[2,8,16,128]{3,2,1,0:T(8,128)(2,1)S(1)}, u32[]{:S(2)}, u32[]{:S(2)}) collective-permute-start(bf16[2,8,16,128]{3,2,1,0:T(8,128)(2,1)S(1)} %get-tuple-element.69), channel_id=1, source_target_pairs={{0,9},{1,8},{2,11},{3,10},{4,13},{5,12},{6,15},{7,14},{8,1},{9,0},... | collective-permute-start | bytes 196616 | tf_op jit(solution)/shard_map/ppermute | solution.py:459
  76.5 2.4 %collective-permute-start.13 = (bf16[2,8,16,128]{3,2,1,0:T(8,128)(2,1)S(1)}, bf16[2,8,16,128]{3,2,1,0:T(8,128)(2,1)S(1)}, u32[]{:S(2)}, u32[]{:S(2)}) collective-permute-start(bf16[2,8,16,128]{3,2,1,0:T(8,128)(2,1)S(1)} %get-tuple-element.70), channel_id=1, source_target_pairs={{0,12},{1,13},{2,14},{3,15},{4,8},{5,9},{6,10},{7,11},{8,4},{9,5},... | collective-permute-start | bytes 196616 | tf_op jit(solution)/shard_map/ppermute | solution.py:459
  78.8 0.0 collective-permute-done.9.refs_2_
  78.8 0.8 collective-permute-start.14
  79.6 0.0 collective-permute-done.10.refs_3_
  79.6 2.9 %collective-permute-start.15 = (bf16[2,8,16,128]{3,2,1,0:T(8,128)(2,1)S(1)}, bf16[2,8,16,128]{3,2,1,0:T(8,128)(2,1)S(1)}, u32[]{:S(2)}, u32[]{:S(2)}) collective-permute-start(bf16[2,8,16,128]{3,2,1,0:T(8,128)(2,1)S(1)} %get-tuple-element.72), channel_id=1, source_target_pairs={{0,5},{1,4},{2,7},{3,6},{4,1},{5,0},{6,3},{7,2},{8,13},{9,12},{10,... | collective-permute-start | bytes 196616 | tf_op jit(solution)/shard_map/ppermute | solution.py:459
  82.5 5.6 %shard_map.87 = (bf16[4,128,128]{2,1,0:T(8,128)(2,1)S(1)}, bf16[4,128,128]{2,1,0:T(8,128)(2,1)S(1)}, bf16[4,512,128]{2,1,0:T(8,128)(2,1)S(1)}, bf16[16,128,128]{...) custom-call(bf16[16,512,128]{2,1,0:T(8,128)(2,1)} %get-tuple-element.42.refs_0_.fac_hbm, ...), custom_call_target="tpu_custom_call" | custom-call | tf_op jit(solution)/shard_map/pallas_call | solution.py:52
  88.1 0.0 collective-permute-done.11.refs_4_
  88.1 1.7 %collective-permute-done.12.refs_5_ = bf16[2,8,16,128]{3,2,1,0:T(8,128)(2,1)S(1)} collective-permute-done((bf16[2,8,16,128]{3,2,1,0:T(8,128)(2,1)S(1)}, bf16[2,8,16,128]{3,2,1,0:T(8,128)(2,1)S(1)}, u32[]{:S(2)}, u32[]{:S(2)}) %collective-permute-start.12) | collective-permute-done | bytes 65568 | tf_op jit(solution)/shard_map/ppermute | solution.py:459
  89.8 2.4 %collective-permute-done.13.refs_6_ = bf16[2,8,16,128]{3,2,1,0:T(8,128)(2,1)S(1)} collective-permute-done((bf16[2,8,16,128]{3,2,1,0:T(8,128)(2,1)S(1)}, bf16[2,8,16,128]{3,2,1,0:T(8,128)(2,1)S(1)}, u32[]{:S(2)}, u32[]{:S(2)}) %collective-permute-start.13) | collective-permute-done | bytes 65568 | tf_op jit(solution)/shard_map/ppermute | solution.py:459
  92.3 1.2 %collective-permute-done.14.refs_7_ = bf16[2,8,16,128]{3,2,1,0:T(8,128)(2,1)S(1)} collective-permute-done((bf16[2,8,16,128]{3,2,1,0:T(8,128)(2,1)S(1)}, bf16[2,8,16,128]{3,2,1,0:T(8,128)(2,1)S(1)}, u32[]{:S(2)}, u32[]{:S(2)}) %collective-permute-start.14) | collective-permute-done | bytes 65568 | tf_op jit(solution)/shard_map/ppermute | solution.py:459
  93.5 0.0 collective-permute-done.15.refs_8_
  93.5 0.2 all-to-all-done.3.r_ref
  93.7 0.0 copy-done
  93.7 0.0 copy-done.1
  93.7 4.0 %shard_map.91 = bf16[16,128,128]{2,1,0:T(8,128)(2,1)} custom-call(bf16[16,512,128]{2,1,0:T(8,128)(2,1)} %get-tuple-element.42.refs_0_.fac_hbm, bf16[16,128,128]{2,1,0:T(8,128)(2,1)} %get-tuple-element.55.nt_hbm, bf16[16,128,128]{2,1,0:T(8,128)(2,1)} %get-tuple-element.56.gin_hbm, bf16[4,512,128]{2,1,0:T(8,128)(2,1)S(1)} %get-tuple-element.57.fac0_ref, ...), custom_call_target="tpu_custom_call" | custom-call | tf_op jit(solution)/shard_map/pallas_call | solution.py:52
  (2 shorter events, 0.1 us)
Async XLA Ops:
  3.4 32.4 %all-to-all-start = ((bf16[32,8,16,128]{3,2,1,0:T(8,128)(2,1)}), bf16[32,8,16,128]{3,2,1,0:T(8,128)(2,1)S(1)}, u32[]{:S(2)}, u32[]{:S(2)}) async-start(bf16[32,8,16,128]{3,2,1,0:T(8,128)(2,1)} %get-tuple-element.39), calls=%async_computation | async-start | bytes 2097152 | tf_op jit(solution)/shard_map/all_to_all | solution.py:448
  12.9 1.6 %collective-permute-start = (bf16[8,8,16,128]{3,2,1,0:T(8,128)(2,1)S(1)}, bf16[8,8,16,128]{3,2,1,0:T(8,128)(2,1)S(1)}, u32[]{:S(2)}, u32[]{:S(2)}) collective-permute-start(bf16[8,8,16,128]{3,2,1,0:T(8,128)(2,1)S(1)} %get-tuple-element.46), channel_id=1, source_target_pairs={{0,2},{1,3},{2,0},{3,1},{4,6},{5,7},{6,4},{7,5},{8,10},{9,11},{10,... | collective-permute-start | bytes 786440 | tf_op jit(solution)/shard_map/ppermute | solution.py:459
  14.6 8.6 %collective-permute-start.1 = (bf16[2,8,16,128]{3,2,1,0:T(8,128)(2,1)S(1)}, bf16[2,8,16,128]{3,2,1,0:T(8,128)(2,1)S(1)}, u32[]{:S(2)}, u32[]{:S(2)}) collective-permute-start(bf16[2,8,16,128]{3,2,1,0:T(8,128)(2,1)S(1)} %get-tuple-element.47), channel_id=1, source_target_pairs={{0,1},{1,0},{2,3},{3,2},{4,5},{5,4},{6,7},{7,6},{8,9},{9,8},{10,11... | collective-permute-start | bytes 196616 | tf_op jit(solution)/shard_map/ppermute | solution.py:459
  16.4 7.3 %collective-permute-start.2 = (bf16[2,8,16,128]{3,2,1,0:T(8,128)(2,1)S(1)}, bf16[2,8,16,128]{3,2,1,0:T(8,128)(2,1)S(1)}, u32[]{:S(2)}, u32[]{:S(2)}) collective-permute-start(bf16[2,8,16,128]{3,2,1,0:T(8,128)(2,1)S(1)} %get-tuple-element.48), channel_id=1, source_target_pairs={{0,4},{1,5},{2,6},{3,7},{4,0},{5,1},{6,2},{7,3},{8,12},{9,13},{10,... | collective-permute-start | bytes 196616 | tf_op jit(solution)/shard_map/ppermute | solution.py:459
  17.9 17.9 %collective-permute-start.3 = (bf16[2,8,16,128]{3,2,1,0:T(8,128)(2,1)S(1)}, bf16[2,8,16,128]{3,2,1,0:T(8,128)(2,1)S(1)}, u32[]{:S(2)}, u32[]{:S(2)}) collective-permute-start(bf16[2,8,16,128]{3,2,1,0:T(8,128)(2,1)S(1)} %get-tuple-element.49), channel_id=1, source_target_pairs={{0,13},{1,12},{2,15},{3,14},{4,9},{5,8},{6,11},{7,10},{8,5},{9,4},... | collective-permute-start | bytes 196616 | tf_op jit(solution)/shard_map/ppermute | solution.py:459
  19.3 16.5 %collective-permute-start.4 = (bf16[2,8,16,128]{3,2,1,0:T(8,128)(2,1)S(1)}, bf16[2,8,16,128]{3,2,1,0:T(8,128)(2,1)S(1)}, u32[]{:S(2)}, u32[]{:S(2)}) collective-permute-start(bf16[2,8,16,128]{3,2,1,0:T(8,128)(2,1)S(1)} %get-tuple-element.50), channel_id=1, source_target_pairs={{0,9},{1,8},{2,11},{3,10},{4,13},{5,12},{6,15},{7,14},{8,1},{9,0},... | collective-permute-start | bytes 196616 | tf_op jit(solution)/shard_map/ppermute | solution.py:459
  20.8 15.0 %collective-permute-start.5 = (bf16[2,8,16,128]{3,2,1,0:T(8,128)(2,1)S(1)}, bf16[2,8,16,128]{3,2,1,0:T(8,128)(2,1)S(1)}, u32[]{:S(2)}, u32[]{:S(2)}) collective-permute-start(bf16[2,8,16,128]{3,2,1,0:T(8,128)(2,1)S(1)} %get-tuple-element.51), channel_id=1, source_target_pairs={{0,12},{1,13},{2,14},{3,15},{4,8},{5,9},{6,10},{7,11},{8,4},{9,5},... | collective-permute-start | bytes 196616 | tf_op jit(solution)/shard_map/ppermute | solution.py:459
  23.2 12.7 %collective-permute-start.6 = (bf16[2,8,16,128]{3,2,1,0:T(8,128)(2,1)S(1)}, bf16[2,8,16,128]{3,2,1,0:T(8,128)(2,1)S(1)}, u32[]{:S(2)}, u32[]{:S(2)}) collective-permute-start(bf16[2,8,16,128]{3,2,1,0:T(8,128)(2,1)S(1)} %get-tuple-element.52), channel_id=1, source_target_pairs={{0,8},{1,9},{2,10},{3,11},{4,12},{5,13},{6,14},{7,15},{8,0},{9,1},... | collective-permute-start | bytes 196616 | tf_op jit(solution)/shard_map/ppermute | solution.py:459
  23.7 12.1 %collective-permute-start.7 = (bf16[2,8,16,128]{3,2,1,0:T(8,128)(2,1)S(1)}, bf16[2,8,16,128]{3,2,1,0:T(8,128)(2,1)S(1)}, u32[]{:S(2)}, u32[]{:S(2)}) collective-permute-start(bf16[2,8,16,128]{3,2,1,0:T(8,128)(2,1)S(1)} %get-tuple-element.53), channel_id=1, source_target_pairs={{0,5},{1,4},{2,7},{3,6},{4,1},{5,0},{6,3},{7,2},{8,13},{9,12},{10,... | collective-permute-start | bytes 196616 | tf_op jit(solution)/shard_map/ppermute | solution.py:459
  64.6 29.1 %all-to-all-start.3 = ((bf16[32,8,16,128]{3,2,1,0:T(8,128)(2,1)}), bf16[32,8,16,128]{3,2,1,0:T(8,128)(2,1)S(1)}, u32[]{:S(2)}, u32[]{:S(2)}) async-start(bf16[32,8,16,128]{3,2,1,0:T(8,128)(2,1)} %get-tuple-element.62), calls=%async_computation.3 | async-start | bytes 2097152 | tf_op jit(solution)/shard_map/all_to_all | solution.py:448
  68.6 1.6 %collective-permute-start.8 = (bf16[8,8,16,128]{3,2,1,0:T(8,128)(2,1)S(1)}, bf16[8,8,16,128]{3,2,1,0:T(8,128)(2,1)S(1)}, u32[]{:S(2)}, u32[]{:S(2)}) collective-permute-start(bf16[8,8,16,128]{3,2,1,0:T(8,128)(2,1)S(1)} %get-tuple-element.65), channel_id=1, source_target_pairs={{0,2},{1,3},{2,0},{3,1},{4,6},{5,7},{6,4},{7,5},{8,10},{9,11},{10,... | collective-permute-start | bytes 786440 | tf_op jit(solution)/shard_map/ppermute | solution.py:459
  70.2 23.5 %copy-start = (bf16[128,640]{1,0:T(8,128)(2,1)S(1)}, bf16[128,640]{1,0:T(8,128)(2,1)}, u32[]{:S(2)}) copy-start(bf16[128,640]{1,0:T(8,128)(2,1)} %w_ref.1) | copy-start | bytes 491524
  70.2 23.5 %copy-start.1 = (f32[128]{0:T(128)S(1)}, f32[128]{0:T(128)}, u32[]{:S(2)}) copy-start(f32[128]{0:T(128)} %param.10) | copy-start | bytes 1540
  70.2 8.6 %collective-permute-start.9 = (bf16[2,8,16,128]{3,2,1,0:T(8,128)(2,1)S(1)}, bf16[2,8,16,128]{3,2,1,0:T(8,128)(2,1)S(1)}, u32[]{:S(2)}, u32[]{:S(2)}) collective-permute-start(bf16[2,8,16,128]{3,2,1,0:T(8,128)(2,1)S(1)} %get-tuple-element.66), channel_id=1, source_target_pairs={{0,1},{1,0},{2,3},{3,2},{4,5},{5,4},{6,7},{7,6},{8,9},{9,8},{10,11... | collective-permute-start | bytes 196616 | tf_op jit(solution)/shard_map/ppermute | solution.py:459
  72.1 7.5 %collective-permute-start.10 = (bf16[2,8,16,128]{3,2,1,0:T(8,128)(2,1)S(1)}, bf16[2,8,16,128]{3,2,1,0:T(8,128)(2,1)S(1)}, u32[]{:S(2)}, u32[]{:S(2)}) collective-permute-start(bf16[2,8,16,128]{3,2,1,0:T(8,128)(2,1)S(1)} %get-tuple-element.67), channel_id=1, source_target_pairs={{0,4},{1,5},{2,6},{3,7},{4,0},{5,1},{6,2},{7,3},{8,12},{9,13},{10,... | collective-permute-start | bytes 196616 | tf_op jit(solution)/shard_map/ppermute | solution.py:459
  73.5 14.6 %collective-permute-start.11 = (bf16[2,8,16,128]{3,2,1,0:T(8,128)(2,1)S(1)}, bf16[2,8,16,128]{3,2,1,0:T(8,128)(2,1)S(1)}, u32[]{:S(2)}, u32[]{:S(2)}) collective-permute-start(bf16[2,8,16,128]{3,2,1,0:T(8,128)(2,1)S(1)} %get-tuple-element.68), channel_id=1, source_target_pairs={{0,13},{1,12},{2,15},{3,14},{4,9},{5,8},{6,11},{7,10},{8,5},{9,4},... | collective-permute-start | bytes 196616 | tf_op jit(solution)/shard_map/ppermute | solution.py:459
  75.0 14.8 %collective-permute-start.12 = (bf16[2,8,16,128]{3,2,1,0:T(8,128)(2,1)S(1)}, bf16[2,8,16,128]{3,2,1,0:T(8,128)(2,1)S(1)}, u32[]{:S(2)}, u32[]{:S(2)}) collective-permute-start(bf16[2,8,16,128]{3,2,1,0:T(8,128)(2,1)S(1)} %get-tuple-element.69), channel_id=1, source_target_pairs={{0,9},{1,8},{2,11},{3,10},{4,13},{5,12},{6,15},{7,14},{8,1},{9,0},... | collective-permute-start | bytes 196616 | tf_op jit(solution)/shard_map/ppermute | solution.py:459
  76.5 15.8 %collective-permute-start.13 = (bf16[2,8,16,128]{3,2,1,0:T(8,128)(2,1)S(1)}, bf16[2,8,16,128]{3,2,1,0:T(8,128)(2,1)S(1)}, u32[]{:S(2)}, u32[]{:S(2)}) collective-permute-start(bf16[2,8,16,128]{3,2,1,0:T(8,128)(2,1)S(1)} %get-tuple-element.70), channel_id=1, source_target_pairs={{0,12},{1,13},{2,14},{3,15},{4,8},{5,9},{6,10},{7,11},{8,4},{9,5},... | collective-permute-start | bytes 196616 | tf_op jit(solution)/shard_map/ppermute | solution.py:459
  78.8 14.7 %collective-permute-start.14 = (bf16[2,8,16,128]{3,2,1,0:T(8,128)(2,1)S(1)}, bf16[2,8,16,128]{3,2,1,0:T(8,128)(2,1)S(1)}, u32[]{:S(2)}, u32[]{:S(2)}) collective-permute-start(bf16[2,8,16,128]{3,2,1,0:T(8,128)(2,1)S(1)} %get-tuple-element.71), channel_id=1, source_target_pairs={{0,8},{1,9},{2,10},{3,11},{4,12},{5,13},{6,14},{7,15},{8,0},{9,1},... | collective-permute-start | bytes 196616 | tf_op jit(solution)/shard_map/ppermute | solution.py:459
  79.6 13.9 %collective-permute-start.15 = (bf16[2,8,16,128]{3,2,1,0:T(8,128)(2,1)S(1)}, bf16[2,8,16,128]{3,2,1,0:T(8,128)(2,1)S(1)}, u32[]{:S(2)}, u32[]{:S(2)}) collective-permute-start(bf16[2,8,16,128]{3,2,1,0:T(8,128)(2,1)S(1)} %get-tuple-element.72), channel_id=1, source_target_pairs={{0,5},{1,4},{2,7},{3,6},{4,1},{5,0},{6,3},{7,2},{8,13},{9,12},{10,... | collective-permute-start | bytes 196616 | tf_op jit(solution)/shard_map/ppermute | solution.py:459

commit v11 on v9

--- a/solution.py
+++ b/solution.py
@@ -283,7 +283,7 @@
         gs_ref[i] = (tri_inv * (h - first - shifted * (both * tri_inv * tri_inv))).astype(BF16)
         return 0
 
-    lax.fori_loop(0, rows, body, 0, unroll=2 * UNROLL)
+    lax.fori_loop(0, rows, body, 0, unroll=4 * UNROLL)
     blocks = places(width, mine, rows)
     for n in range(0, len(blocks), 2):
         pair = blocks[n : n + 2]

time: 99 us -> 98.9 us (level)
  no operation moved by 1% of the time
where the time goes in v11:
time: 98.9 us; the launch traced here: 97.6 us
  starting transfers between devices  34.2 us (35%)
  blocking collectives  25.4 us (26%)
  Pallas kernels  23.9 us (24%)
  waiting for transfers between devices  13.9 us (14%)
    all_to_all x2, blocking collectives, exchange_half(): lax.all_to_all(blocks, ('row', 'ch'), split_axis=0, concat_axis=0, tiled=...  25.4 us
    pallas_call x10, Pallas kernels, call(): pl.pallas_call(kernel, out_shape=outs if single else tuple(outs), in_spec...  23.9 us
    ppermute x16, starting transfers between devices, swap(): lax.ppermute(block, ('row', 'ch'), [(n, n ^ s) for n in range(self.device...  23.2 us
    all_to_all x2, starting transfers between devices, exchange_all(): lax.all_to_all(blocks, ('row', 'ch'), split_axis=0, concat_axis=0, tiled=...  11 us
    ppermute x16, waiting for transfers between devices, swap(): lax.ppermute(block, ('row', 'ch'), [(n, n ^ s) for n in range(self.device...  8.79 us
    all_to_all x2, waiting for transfers between devices, exchange_all(): lax.all_to_all(blocks, ('row', 'ch'), split_axis=0, concat_axis=0, tiled=...  5.16 us
  transfers between devices with their start and end apart: 18, of which 7 were waited for; matrix products, arithmetic and copies ran while one was open for 0% of the time, Pallas kernels for 14%

profile of v11, /device:TPU:0, one launch (start us, length us, event | category | flops | bytes accessed | tf_op | source)
XLA Modules:
  0.0 97.6 jit_solution(3611072684286839985)
XLA Ops:
  0.0 3.4 %shard_map.82 = (bf16[32,8,16,128]{3,2,1,0:T(8,128)(2,1)}, bf16[8,128,256]{2,1,0:T(8,128)(2,1)S(1)}) custom-call(bf16[16,128,128]{2,1,0:T(8,128)(2,1)} %refs_1_.3, f32[1,128]{1,0:T(1,128)} %bitcast.4, f32[1,128]{1,0:T(1,128)} %bitcast.8, bf16[128,640]{1,0:T(8,128)(2,1)} %w_ref.1), custom_call_target="tpu_custom_call" | custom-call | tf_op jit(solution)/shard_map/pallas_call | solution.py:52
  3.4 7.3 %all-to-all-start = ((bf16[32,8,16,128]{3,2,1,0:T(8,128)(2,1)}), bf16[32,8,16,128]{3,2,1,0:T(8,128)(2,1)S(1)}, u32[]{:S(2)}, u32[]{:S(2)}) async-start(bf16[32,8,16,128]{3,2,1,0:T(8,128)(2,1)} %get-tuple-element.39), calls=%async_computation | async-start | bytes 2097152 | tf_op jit(solution)/shard_map/all_to_all | solution.py:448
  10.8 2.2 %shard_map.84 = (bf16[8,8,16,128]{3,2,1,0:T(8,128)(2,1)S(1)}, bf16[8,8,16,128]{3,2,1,0:T(8,128)(2,1)S(1)}) custom-call(bf16[128,640]{1,0:T(8,128)(2,1)} %w_ref.1, bf16[8,128,256]{2,1,0:T(8,128)(2,1)S(1)} %get-tuple-element.44.n_ref), custom_call_target="tpu_custom_call" | custom-call | tf_op jit(solution)/shard_map/pallas_call | solution.py:52
  12.9 0.3 collective-permute-start
  13.3 1.3 %collective-permute-done.mates_ref.refs_1_ = bf16[8,8,16,128]{3,2,1,0:T(8,128)(2,1)S(1)} collective-permute-done((bf16[8,8,16,128]{3,2,1,0:T(8,128)(2,1)S(1)}, bf16[8,8,16,128]{3,2,1,0:T(8,128)(2,1)S(1)}, u32[]{:S(2)}, u32[]{:S(2)}) %collective-permute-start) | collective-permute-done | bytes 262176 | tf_op jit(solution)/shard_map/ppermute | solution.py:459
  14.6 1.8 %collective-permute-start.1 = (bf16[2,8,16,128]{3,2,1,0:T(8,128)(2,1)S(1)}, bf16[2,8,16,128]{3,2,1,0:T(8,128)(2,1)S(1)}, u32[]{:S(2)}, u32[]{:S(2)}) collective-permute-start(bf16[2,8,16,128]{3,2,1,0:T(8,128)(2,1)S(1)} %get-tuple-element.47), channel_id=1, source_target_pairs={{0,1},{1,0},{2,3},{3,2},{4,5},{5,4},{6,7},{7,6},{8,9},{9,8},{10,11... | collective-permute-start | bytes 196616 | tf_op jit(solution)/shard_map/ppermute | solution.py:459
  16.4 1.5 %collective-permute-start.2 = (bf16[2,8,16,128]{3,2,1,0:T(8,128)(2,1)S(1)}, bf16[2,8,16,128]{3,2,1,0:T(8,128)(2,1)S(1)}, u32[]{:S(2)}, u32[]{:S(2)}) collective-permute-start(bf16[2,8,16,128]{3,2,1,0:T(8,128)(2,1)S(1)} %get-tuple-element.48), channel_id=1, source_target_pairs={{0,4},{1,5},{2,6},{3,7},{4,0},{5,1},{6,2},{7,3},{8,12},{9,13},{10,... | collective-permute-start | bytes 196616 | tf_op jit(solution)/shard_map/ppermute | solution.py:459
  17.9 1.5 %collective-permute-start.3 = (bf16[2,8,16,128]{3,2,1,0:T(8,128)(2,1)S(1)}, bf16[2,8,16,128]{3,2,1,0:T(8,128)(2,1)S(1)}, u32[]{:S(2)}, u32[]{:S(2)}) collective-permute-start(bf16[2,8,16,128]{3,2,1,0:T(8,128)(2,1)S(1)} %get-tuple-element.49), channel_id=1, source_target_pairs={{0,13},{1,12},{2,15},{3,14},{4,9},{5,8},{6,11},{7,10},{8,5},{9,4},... | collective-permute-start | bytes 196616 | tf_op jit(solution)/shard_map/ppermute | solution.py:459
  19.3 1.5 %collective-permute-start.4 = (bf16[2,8,16,128]{3,2,1,0:T(8,128)(2,1)S(1)}, bf16[2,8,16,128]{3,2,1,0:T(8,128)(2,1)S(1)}, u32[]{:S(2)}, u32[]{:S(2)}) collective-permute-start(bf16[2,8,16,128]{3,2,1,0:T(8,128)(2,1)S(1)} %get-tuple-element.50), channel_id=1, source_target_pairs={{0,12},{1,13},{2,14},{3,15},{4,8},{5,9},{6,10},{7,11},{8,4},{9,5},... | collective-permute-start | bytes 196616 | tf_op jit(solution)/shard_map/ppermute | solution.py:459
  20.8 2.4 %collective-permute-start.5 = (bf16[2,8,16,128]{3,2,1,0:T(8,128)(2,1)S(1)}, bf16[2,8,16,128]{3,2,1,0:T(8,128)(2,1)S(1)}, u32[]{:S(2)}, u32[]{:S(2)}) collective-permute-start(bf16[2,8,16,128]{3,2,1,0:T(8,128)(2,1)S(1)} %get-tuple-element.51), channel_id=1, source_target_pairs={{0,9},{1,8},{2,11},{3,10},{4,13},{5,12},{6,15},{7,14},{8,1},{9,0},... | collective-permute-start | bytes 196616 | tf_op jit(solution)/shard_map/ppermute | solution.py:459
  23.2 0.0 collective-permute-done.1.refs_2_
  23.2 0.6 collective-permute-start.6
  23.7 0.0 collective-permute-done.2.refs_3_
  23.7 1.2 %collective-permute-start.7 = (bf16[2,8,16,128]{3,2,1,0:T(8,128)(2,1)S(1)}, bf16[2,8,16,128]{3,2,1,0:T(8,128)(2,1)S(1)}, u32[]{:S(2)}, u32[]{:S(2)}) collective-permute-start(bf16[2,8,16,128]{3,2,1,0:T(8,128)(2,1)S(1)} %get-tuple-element.53), channel_id=1, source_target_pairs={{0,5},{1,4},{2,7},{3,6},{4,1},{5,0},{6,3},{7,2},{8,13},{9,12},{10,... | collective-permute-start | bytes 196616 | tf_op jit(solution)/shard_map/ppermute | solution.py:459
  24.9 5.7 %shard_map.83 = (f32[16,128,128]{2,1,0:T(8,128)S(1)}, bf16[16,512,128]{2,1,0:T(8,128)(2,1)}) custom-call(bf16[16,128,128]{2,1,0:T(8,128)(2,1)} %refs_1_.3, bf16[16,128,128]{2,1,0:T(8,128)(2,1)} %refs_2_.1, f32[1,128]{1,0:T(1,128)} %bitcast.5, f32[1,128]{1,0:T(1,128)} %bitcast.9, bf16[128,640]{1,0:T(8,128)(2,1)} %w_ref.1, f32[1,128]{1,0:T(1,128)} %bitcast.11, ...), custom_call_target="tpu_custom_call" | custom-call | tf_op jit(solution)/shard_map/pallas_call | solution.py:52
  30.7 5.2 %all-to-all-done.r_ref = bf16[32,8,16,128]{3,2,1,0:T(8,128)(2,1)S(1)} async-done(((bf16[32,8,16,128]{3,2,1,0:T(8,128)(2,1)}), bf16[32,8,16,128]{3,2,1,0:T(8,128)(2,1)S(1)}, u32[]{:S(2)}, u32[]{:S(2)}) %all-to-all-start) | async-done | bytes 1048608 | tf_op jit(solution)/shard_map/all_to_all | solution.py:448
  35.8 0.0 collective-permute-done.3.refs_4_
  35.8 0.0 collective-permute-done.4.refs_5_
  35.8 0.0 collective-permute-done.5.refs_6_
  35.8 0.3 collective-permute-done.6.refs_7_
  36.1 0.0 collective-permute-done.7.refs_8_
  36.1 0.5 shard_map.86
  36.6 13.1 %all_to_all.20.refs_9_.t_ref = bf16[16,8,16,128]{3,2,1,0:T(8,128)(2,1)S(1)} all-to-all(bf16[16,8,16,128]{3,2,1,0:T(8,128)(2,1)S(1)} %get-tuple-element.54), channel_id=1, replica_groups={{0,8,2,10,4,12,6,14,1,9,3,11,5,13,7,15},{16,24,18,26,20,28,22,30,17,25,..., dimensions={0} | all-to-all | bytes 1048576 | tf_op jit(solution)/shard_map/all_to_all | solution.py:454
  49.8 1.1 %shard_map.88 = bf16[16,8,16,128]{3,2,1,0:T(8,128)(2,1)S(1)} custom-call(bf16[16,8,16,128]{3,2,1,0:T(8,128)(2,1)S(1)} %all_to_all.20.refs_9_.t_ref, f32[16,128,128]{2,1,0:T(8,128)S(1)} %get-tuple-element.60.h_ref), custom_call_target="tpu_custom_call" | custom-call | tf_op jit(solution)/shard_map/pallas_call | solution.py:52
  50.8 12.3 %all_to_all.21.gt_ref = bf16[16,8,16,128]{3,2,1,0:T(8,128)(2,1)S(1)} all-to-all(bf16[16,8,16,128]{3,2,1,0:T(8,128)(2,1)S(1)} %shard_map.88), channel_id=1, replica_groups={{0,8,2,10,4,12,6,14,1,9,3,11,5,13,7,15},{16,24,18,26,20,28,22,30,17,25,..., dimensions={0} | all-to-all | bytes 1048576 | tf_op jit(solution)/shard_map/all_to_all | solution.py:454
  63.1 1.4 %shard_map.89 = (bf16[32,8,16,128]{3,2,1,0:T(8,128)(2,1)}, bf16[8,8,16,128]{3,2,1,0:T(8,128)(2,1)S(1)}, bf16[8,8,16,128]{3,2,1,0:T(8,128)(2,1)S(1)}) custom-call(bf16[16,8,16,128]{3,2,1,0:T(8,128)(2,1)S(1)} %all_to_all.21.gt_ref, bf16[16,8,16,128]{3,2,1,0:T(8,128)(2,1)S(1)} %get-tuple-element.61.l_ref, bf16[32,8,16,128]{3,2,1,0:T(8,128)(2,1)S(1)} %all-to-all-done.r_ref), custom_call_target="tpu_custom_call" | custom-call | tf_op jit(solution)/shard_map/pallas_call | solution.py:52
  64.5 3.7 %all-to-all-start.3 = ((bf16[32,8,16,128]{3,2,1,0:T(8,128)(2,1)}), bf16[32,8,16,128]{3,2,1,0:T(8,128)(2,1)S(1)}, u32[]{:S(2)}, u32[]{:S(2)}) async-start(bf16[32,8,16,128]{3,2,1,0:T(8,128)(2,1)} %get-tuple-element.62), calls=%async_computation.3 | async-start | bytes 2097152 | tf_op jit(solution)/shard_map/all_to_all | solution.py:448
  68.2 0.3 collective-permute-start.8
  68.5 1.3 %collective-permute-done.8.mates_ref.refs_1_ = bf16[8,8,16,128]{3,2,1,0:T(8,128)(2,1)S(1)} collective-permute-done((bf16[8,8,16,128]{3,2,1,0:T(8,128)(2,1)S(1)}, bf16[8,8,16,128]{3,2,1,0:T(8,128)(2,1)S(1)}, u32[]{:S(2)}, u32[]{:S(2)}) %collective-permute-start.8) | collective-permute-done | bytes 262176 | tf_op jit(solution)/shard_map/ppermute | solution.py:459
  69.8 0.0 copy-start
  69.8 0.0 copy-start.1
  69.9 1.8 %collective-permute-start.9 = (bf16[2,8,16,128]{3,2,1,0:T(8,128)(2,1)S(1)}, bf16[2,8,16,128]{3,2,1,0:T(8,128)(2,1)S(1)}, u32[]{:S(2)}, u32[]{:S(2)}) collective-permute-start(bf16[2,8,16,128]{3,2,1,0:T(8,128)(2,1)S(1)} %get-tuple-element.66), channel_id=1, source_target_pairs={{0,1},{1,0},{2,3},{3,2},{4,5},{5,4},{6,7},{7,6},{8,9},{9,8},{10,11... | collective-permute-start | bytes 196616 | tf_op jit(solution)/shard_map/ppermute | solution.py:459
  71.7 1.5 %collective-permute-start.10 = (bf16[2,8,16,128]{3,2,1,0:T(8,128)(2,1)S(1)}, bf16[2,8,16,128]{3,2,1,0:T(8,128)(2,1)S(1)}, u32[]{:S(2)}, u32[]{:S(2)}) collective-permute-start(bf16[2,8,16,128]{3,2,1,0:T(8,128)(2,1)S(1)} %get-tuple-element.67), channel_id=1, source_target_pairs={{0,4},{1,5},{2,6},{3,7},{4,0},{5,1},{6,2},{7,3},{8,12},{9,13},{10,... | collective-permute-start | bytes 196616 | tf_op jit(solution)/shard_map/ppermute | solution.py:459
  73.2 1.5 %collective-permute-start.11 = (bf16[2,8,16,128]{3,2,1,0:T(8,128)(2,1)S(1)}, bf16[2,8,16,128]{3,2,1,0:T(8,128)(2,1)S(1)}, u32[]{:S(2)}, u32[]{:S(2)}) collective-permute-start(bf16[2,8,16,128]{3,2,1,0:T(8,128)(2,1)S(1)} %get-tuple-element.68), channel_id=1, source_target_pairs={{0,13},{1,12},{2,15},{3,14},{4,9},{5,8},{6,11},{7,10},{8,5},{9,4},... | collective-permute-start | bytes 196616 | tf_op jit(solution)/shard_map/ppermute | solution.py:459
  74.6 1.5 %collective-permute-start.12 = (bf16[2,8,16,128]{3,2,1,0:T(8,128)(2,1)S(1)}, bf16[2,8,16,128]{3,2,1,0:T(8,128)(2,1)S(1)}, u32[]{:S(2)}, u32[]{:S(2)}) collective-permute-start(bf16[2,8,16,128]{3,2,1,0:T(8,128)(2,1)S(1)} %get-tuple-element.69), channel_id=1, source_target_pairs={{0,12},{1,13},{2,14},{3,15},{4,8},{5,9},{6,10},{7,11},{8,4},{9,5},... | collective-permute-start | bytes 196616 | tf_op jit(solution)/shard_map/ppermute | solution.py:459
  76.1 2.4 %collective-permute-start.13 = (bf16[2,8,16,128]{3,2,1,0:T(8,128)(2,1)S(1)}, bf16[2,8,16,128]{3,2,1,0:T(8,128)(2,1)S(1)}, u32[]{:S(2)}, u32[]{:S(2)}) collective-permute-start(bf16[2,8,16,128]{3,2,1,0:T(8,128)(2,1)S(1)} %get-tuple-element.70), channel_id=1, source_target_pairs={{0,9},{1,8},{2,11},{3,10},{4,13},{5,12},{6,15},{7,14},{8,1},{9,0},... | collective-permute-start | bytes 196616 | tf_op jit(solution)/shard_map/ppermute | solution.py:459
  78.4 0.0 collective-permute-done.9.refs_2_
  78.5 0.8 collective-permute-start.14
  79.2 0.0 collective-permute-done.10.refs_3_
  79.2 2.9 %collective-permute-start.15 = (bf16[2,8,16,128]{3,2,1,0:T(8,128)(2,1)S(1)}, bf16[2,8,16,128]{3,2,1,0:T(8,128)(2,1)S(1)}, u32[]{:S(2)}, u32[]{:S(2)}) collective-permute-start(bf16[2,8,16,128]{3,2,1,0:T(8,128)(2,1)S(1)} %get-tuple-element.72), channel_id=1, source_target_pairs={{0,5},{1,4},{2,7},{3,6},{4,1},{5,0},{6,3},{7,2},{8,13},{9,12},{10,... | collective-permute-start | bytes 196616 | tf_op jit(solution)/shard_map/ppermute | solution.py:459
  82.1 5.6 %shard_map.87 = (bf16[4,128,128]{2,1,0:T(8,128)(2,1)S(1)}, bf16[4,128,128]{2,1,0:T(8,128)(2,1)S(1)}, bf16[4,512,128]{2,1,0:T(8,128)(2,1)S(1)}, bf16[16,128,128]{...) custom-call(bf16[16,512,128]{2,1,0:T(8,128)(2,1)} %get-tuple-element.42.refs_0_.fac_hbm, ...), custom_call_target="tpu_custom_call" | custom-call | tf_op jit(solution)/shard_map/pallas_call | solution.py:52
  87.7 0.0 collective-permute-done.11.refs_4_
  87.7 1.3 %collective-permute-done.12.refs_5_ = bf16[2,8,16,128]{3,2,1,0:T(8,128)(2,1)S(1)} collective-permute-done((bf16[2,8,16,128]{3,2,1,0:T(8,128)(2,1)S(1)}, bf16[2,8,16,128]{3,2,1,0:T(8,128)(2,1)S(1)}, u32[]{:S(2)}, u32[]{:S(2)}) %collective-permute-start.12) | collective-permute-done | bytes 65568 | tf_op jit(solution)/shard_map/ppermute | solution.py:459
  89.1 3.8 %collective-permute-done.13.refs_6_ = bf16[2,8,16,128]{3,2,1,0:T(8,128)(2,1)S(1)} collective-permute-done((bf16[2,8,16,128]{3,2,1,0:T(8,128)(2,1)S(1)}, bf16[2,8,16,128]{3,2,1,0:T(8,128)(2,1)S(1)}, u32[]{:S(2)}, u32[]{:S(2)}) %collective-permute-start.13) | collective-permute-done | bytes 65568 | tf_op jit(solution)/shard_map/ppermute | solution.py:459
  92.8 0.8 collective-permute-done.14.refs_7_
  93.6 0.0 collective-permute-done.15.refs_8_
  93.6 0.0 all-to-all-done.3.r_ref
  93.6 0.0 copy-done
  93.6 0.0 copy-done.1
  93.6 4.0 %shard_map.91 = bf16[16,128,128]{2,1,0:T(8,128)(2,1)} custom-call(bf16[16,512,128]{2,1,0:T(8,128)(2,1)} %get-tuple-element.42.refs_0_.fac_hbm, bf16[16,128,128]{2,1,0:T(8,128)(2,1)} %get-tuple-element.55.nt_hbm, bf16[16,128,128]{2,1,0:T(8,128)(2,1)} %get-tuple-element.56.gin_hbm, bf16[4,512,128]{2,1,0:T(8,128)(2,1)S(1)} %get-tuple-element.57.fac0_ref, ...), custom_call_target="tpu_custom_call" | custom-call | tf_op jit(solution)/shard_map/pallas_call | solution.py:52
  (2 shorter events, 0.1 us)
Async XLA Ops:
  3.4 32.4 %all-to-all-start = ((bf16[32,8,16,128]{3,2,1,0:T(8,128)(2,1)}), bf16[32,8,16,128]{3,2,1,0:T(8,128)(2,1)S(1)}, u32[]{:S(2)}, u32[]{:S(2)}) async-start(bf16[32,8,16,128]{3,2,1,0:T(8,128)(2,1)} %get-tuple-element.39), calls=%async_computation | async-start | bytes 2097152 | tf_op jit(solution)/shard_map/all_to_all | solution.py:448
  12.9 1.6 %collective-permute-start = (bf16[8,8,16,128]{3,2,1,0:T(8,128)(2,1)S(1)}, bf16[8,8,16,128]{3,2,1,0:T(8,128)(2,1)S(1)}, u32[]{:S(2)}, u32[]{:S(2)}) collective-permute-start(bf16[8,8,16,128]{3,2,1,0:T(8,128)(2,1)S(1)} %get-tuple-element.46), channel_id=1, source_target_pairs={{0,2},{1,3},{2,0},{3,1},{4,6},{5,7},{6,4},{7,5},{8,10},{9,11},{10,... | collective-permute-start | bytes 786440 | tf_op jit(solution)/shard_map/ppermute | solution.py:459
  14.6 8.6 %collective-permute-start.1 = (bf16[2,8,16,128]{3,2,1,0:T(8,128)(2,1)S(1)}, bf16[2,8,16,128]{3,2,1,0:T(8,128)(2,1)S(1)}, u32[]{:S(2)}, u32[]{:S(2)}) collective-permute-start(bf16[2,8,16,128]{3,2,1,0:T(8,128)(2,1)S(1)} %get-tuple-element.47), channel_id=1, source_target_pairs={{0,1},{1,0},{2,3},{3,2},{4,5},{5,4},{6,7},{7,6},{8,9},{9,8},{10,11... | collective-permute-start | bytes 196616 | tf_op jit(solution)/shard_map/ppermute | solution.py:459
  16.4 7.3 %collective-permute-start.2 = (bf16[2,8,16,128]{3,2,1,0:T(8,128)(2,1)S(1)}, bf16[2,8,16,128]{3,2,1,0:T(8,128)(2,1)S(1)}, u32[]{:S(2)}, u32[]{:S(2)}) collective-permute-start(bf16[2,8,16,128]{3,2,1,0:T(8,128)(2,1)S(1)} %get-tuple-element.48), channel_id=1, source_target_pairs={{0,4},{1,5},{2,6},{3,7},{4,0},{5,1},{6,2},{7,3},{8,12},{9,13},{10,... | collective-permute-start | bytes 196616 | tf_op jit(solution)/shard_map/ppermute | solution.py:459
  17.9 17.9 %collective-permute-start.3 = (bf16[2,8,16,128]{3,2,1,0:T(8,128)(2,1)S(1)}, bf16[2,8,16,128]{3,2,1,0:T(8,128)(2,1)S(1)}, u32[]{:S(2)}, u32[]{:S(2)}) collective-permute-start(bf16[2,8,16,128]{3,2,1,0:T(8,128)(2,1)S(1)} %get-tuple-element.49), channel_id=1, source_target_pairs={{0,13},{1,12},{2,15},{3,14},{4,9},{5,8},{6,11},{7,10},{8,5},{9,4},... | collective-permute-start | bytes 196616 | tf_op jit(solution)/shard_map/ppermute | solution.py:459
  19.3 16.5 %collective-permute-start.4 = (bf16[2,8,16,128]{3,2,1,0:T(8,128)(2,1)S(1)}, bf16[2,8,16,128]{3,2,1,0:T(8,128)(2,1)S(1)}, u32[]{:S(2)}, u32[]{:S(2)}) collective-permute-start(bf16[2,8,16,128]{3,2,1,0:T(8,128)(2,1)S(1)} %get-tuple-element.50), channel_id=1, source_target_pairs={{0,12},{1,13},{2,14},{3,15},{4,8},{5,9},{6,10},{7,11},{8,4},{9,5},... | collective-permute-start | bytes 196616 | tf_op jit(solution)/shard_map/ppermute | solution.py:459
  20.8 15.0 %collective-permute-start.5 = (bf16[2,8,16,128]{3,2,1,0:T(8,128)(2,1)S(1)}, bf16[2,8,16,128]{3,2,1,0:T(8,128)(2,1)S(1)}, u32[]{:S(2)}, u32[]{:S(2)}) collective-permute-start(bf16[2,8,16,128]{3,2,1,0:T(8,128)(2,1)S(1)} %get-tuple-element.51), channel_id=1, source_target_pairs={{0,9},{1,8},{2,11},{3,10},{4,13},{5,12},{6,15},{7,14},{8,1},{9,0},... | collective-permute-start | bytes 196616 | tf_op jit(solution)/shard_map/ppermute | solution.py:459
  23.2 13.0 %collective-permute-start.6 = (bf16[2,8,16,128]{3,2,1,0:T(8,128)(2,1)S(1)}, bf16[2,8,16,128]{3,2,1,0:T(8,128)(2,1)S(1)}, u32[]{:S(2)}, u32[]{:S(2)}) collective-permute-start(bf16[2,8,16,128]{3,2,1,0:T(8,128)(2,1)S(1)} %get-tuple-element.52), channel_id=1, source_target_pairs={{0,8},{1,9},{2,10},{3,11},{4,12},{5,13},{6,14},{7,15},{8,0},{9,1},... | collective-permute-start | bytes 196616 | tf_op jit(solution)/shard_map/ppermute | solution.py:459
  23.7 12.4 %collective-permute-start.7 = (bf16[2,8,16,128]{3,2,1,0:T(8,128)(2,1)S(1)}, bf16[2,8,16,128]{3,2,1,0:T(8,128)(2,1)S(1)}, u32[]{:S(2)}, u32[]{:S(2)}) collective-permute-start(bf16[2,8,16,128]{3,2,1,0:T(8,128)(2,1)S(1)} %get-tuple-element.53), channel_id=1, source_target_pairs={{0,5},{1,4},{2,7},{3,6},{4,1},{5,0},{6,3},{7,2},{8,13},{9,12},{10,... | collective-permute-start | bytes 196616 | tf_op jit(solution)/shard_map/ppermute | solution.py:459
  64.5 29.1 %all-to-all-start.3 = ((bf16[32,8,16,128]{3,2,1,0:T(8,128)(2,1)}), bf16[32,8,16,128]{3,2,1,0:T(8,128)(2,1)S(1)}, u32[]{:S(2)}, u32[]{:S(2)}) async-start(bf16[32,8,16,128]{3,2,1,0:T(8,128)(2,1)} %get-tuple-element.62), calls=%async_computation.3 | async-start | bytes 2097152 | tf_op jit(solution)/shard_map/all_to_all | solution.py:448
  68.2 1.6 %collective-permute-start.8 = (bf16[8,8,16,128]{3,2,1,0:T(8,128)(2,1)S(1)}, bf16[8,8,16,128]{3,2,1,0:T(8,128)(2,1)S(1)}, u32[]{:S(2)}, u32[]{:S(2)}) collective-permute-start(bf16[8,8,16,128]{3,2,1,0:T(8,128)(2,1)S(1)} %get-tuple-element.65), channel_id=1, source_target_pairs={{0,2},{1,3},{2,0},{3,1},{4,6},{5,7},{6,4},{7,5},{8,10},{9,11},{10,... | collective-permute-start | bytes 786440 | tf_op jit(solution)/shard_map/ppermute | solution.py:459
  69.8 23.8 %copy-start = (bf16[128,640]{1,0:T(8,128)(2,1)S(1)}, bf16[128,640]{1,0:T(8,128)(2,1)}, u32[]{:S(2)}) copy-start(bf16[128,640]{1,0:T(8,128)(2,1)} %w_ref.1) | copy-start | bytes 491524
  69.8 23.8 %copy-start.1 = (f32[128]{0:T(128)S(1)}, f32[128]{0:T(128)}, u32[]{:S(2)}) copy-start(f32[128]{0:T(128)} %param.10) | copy-start | bytes 1540
  69.9 8.6 %collective-permute-start.9 = (bf16[2,8,16,128]{3,2,1,0:T(8,128)(2,1)S(1)}, bf16[2,8,16,128]{3,2,1,0:T(8,128)(2,1)S(1)}, u32[]{:S(2)}, u32[]{:S(2)}) collective-permute-start(bf16[2,8,16,128]{3,2,1,0:T(8,128)(2,1)S(1)} %get-tuple-element.66), channel_id=1, source_target_pairs={{0,1},{1,0},{2,3},{3,2},{4,5},{5,4},{6,7},{7,6},{8,9},{9,8},{10,11... | collective-permute-start | bytes 196616 | tf_op jit(solution)/shard_map/ppermute | solution.py:459
  71.7 7.5 %collective-permute-start.10 = (bf16[2,8,16,128]{3,2,1,0:T(8,128)(2,1)S(1)}, bf16[2,8,16,128]{3,2,1,0:T(8,128)(2,1)S(1)}, u32[]{:S(2)}, u32[]{:S(2)}) collective-permute-start(bf16[2,8,16,128]{3,2,1,0:T(8,128)(2,1)S(1)} %get-tuple-element.67), channel_id=1, source_target_pairs={{0,4},{1,5},{2,6},{3,7},{4,0},{5,1},{6,2},{7,3},{8,12},{9,13},{10,... | collective-permute-start | bytes 196616 | tf_op jit(solution)/shard_map/ppermute | solution.py:459
  73.2 14.6 %collective-permute-start.11 = (bf16[2,8,16,128]{3,2,1,0:T(8,128)(2,1)S(1)}, bf16[2,8,16,128]{3,2,1,0:T(8,128)(2,1)S(1)}, u32[]{:S(2)}, u32[]{:S(2)}) collective-permute-start(bf16[2,8,16,128]{3,2,1,0:T(8,128)(2,1)S(1)} %get-tuple-element.68), channel_id=1, source_target_pairs={{0,13},{1,12},{2,15},{3,14},{4,9},{5,8},{6,11},{7,10},{8,5},{9,4},... | collective-permute-start | bytes 196616 | tf_op jit(solution)/shard_map/ppermute | solution.py:459
  74.6 14.5 %collective-permute-start.12 = (bf16[2,8,16,128]{3,2,1,0:T(8,128)(2,1)S(1)}, bf16[2,8,16,128]{3,2,1,0:T(8,128)(2,1)S(1)}, u32[]{:S(2)}, u32[]{:S(2)}) collective-permute-start(bf16[2,8,16,128]{3,2,1,0:T(8,128)(2,1)S(1)} %get-tuple-element.69), channel_id=1, source_target_pairs={{0,12},{1,13},{2,14},{3,15},{4,8},{5,9},{6,10},{7,11},{8,4},{9,5},... | collective-permute-start | bytes 196616 | tf_op jit(solution)/shard_map/ppermute | solution.py:459
  76.1 16.8 %collective-permute-start.13 = (bf16[2,8,16,128]{3,2,1,0:T(8,128)(2,1)S(1)}, bf16[2,8,16,128]{3,2,1,0:T(8,128)(2,1)S(1)}, u32[]{:S(2)}, u32[]{:S(2)}) collective-permute-start(bf16[2,8,16,128]{3,2,1,0:T(8,128)(2,1)S(1)} %get-tuple-element.70), channel_id=1, source_target_pairs={{0,9},{1,8},{2,11},{3,10},{4,13},{5,12},{6,15},{7,14},{8,1},{9,0},... | collective-permute-start | bytes 196616 | tf_op jit(solution)/shard_map/ppermute | solution.py:459
  78.5 15.2 %collective-permute-start.14 = (bf16[2,8,16,128]{3,2,1,0:T(8,128)(2,1)S(1)}, bf16[2,8,16,128]{3,2,1,0:T(8,128)(2,1)S(1)}, u32[]{:S(2)}, u32[]{:S(2)}) collective-permute-start(bf16[2,8,16,128]{3,2,1,0:T(8,128)(2,1)S(1)} %get-tuple-element.71), channel_id=1, source_target_pairs={{0,8},{1,9},{2,10},{3,11},{4,12},{5,13},{6,14},{7,15},{8,0},{9,1},... | collective-permute-start | bytes 196616 | tf_op jit(solution)/shard_map/ppermute | solution.py:459
  79.2 14.4 %collective-permute-start.15 = (bf16[2,8,16,128]{3,2,1,0:T(8,128)(2,1)S(1)}, bf16[2,8,16,128]{3,2,1,0:T(8,128)(2,1)S(1)}, u32[]{:S(2)}, u32[]{:S(2)}) collective-permute-start(bf16[2,8,16,128]{3,2,1,0:T(8,128)(2,1)S(1)} %get-tuple-element.72), channel_id=1, source_target_pairs={{0,5},{1,4},{2,7},{3,6},{4,1},{5,0},{6,3},{7,2},{8,13},{9,12},{10,... | collective-permute-start | bytes 196616 | tf_op jit(solution)/shard_map/ppermute | solution.py:459
